TPU v7x, 128 devices: a whole 4x4x4 slice. The times are simulated.
128 devices in a mesh: trow: 8 (over x_lo, z), tcol: 16 (over y, x_hi, core).
Axes of the slice: x: 4 (x_hi: 2, x_lo: 2; x = x_hi * 2 + x_lo), y: 4, z: 4, core: 2. Of those that a mesh axis runs over, the one named last changes fastest.
Arguments:
- signal: bfloat16 [256, 32768], P(None, ('tcol', 'trow')), may hold values from -6 to 6
- left_factors: bfloat16 [16, 16, 2048, 256], P('trow', 'tcol'), may hold values from -0.09375 to 0.09375
- right_factors: bfloat16 [16, 16, 2048, 256], P('trow', 'tcol'), may hold values from -0.125 to 0.125
- dense_diagonal: bfloat16 [16, 2048, 2048], P('tcol'), may hold values from -0.125 to 0.125
- buckets: int32 [16, 16], P('trow', 'tcol'), may hold values from 0 to 4
Outputs:
- first_out: bfloat16 [256, 32768], P(None, ('trow', 'tcol'))
- second_out: bfloat16 [256, 32768], P(None, ('tcol', 'trow'))
Inputs may be any that keep to these rules, and one draw needn't show every extreme that they name: A tile's rank is 16 times two to the power of its bucket; factor columns past the rank are not part of the tile, and the diagonal tiles' buckets are unused.
All inputs are finite; a program needn't handle non-finite values.
Results may differ from a plain program's by a relative error of at most 0.022.
Values may be sent and summed in bfloat16 or wider, within the bound.
No kernel may reach another device: no remote copies, remote signals or barrier semaphores. Data moves between devices by JAX's collectives and lax.ppermute only.
A program may use at most 128 MiB of HBM per device.

v0:
```python
import jax
import jax.numpy as jnp
from jax import lax
from jax.sharding import PartitionSpec as P


def body(signal, left_factors, right_factors, dense_diagonal, buckets):
    row_index = lax.axis_index("trow")
    col_index = lax.axis_index("tcol")
    left_tiles = left_factors[:, 0]
    right_tiles = right_factors[:, 0]
    diagonal_tile = dense_diagonal[0]
    tile_buckets = buckets[:, 0]
    tiles_here = left_tiles.shape[0]
    columns = signal.shape[0]
    tile_size = left_tiles.shape[1]
    full_rank = left_tiles.shape[2]
    global_rows = row_index * tiles_here + jnp.arange(tiles_here, dtype=jnp.int32)
    off_diagonal = (global_rows != col_index).astype(jnp.float32)
    is_owner = row_index == col_index // tiles_here
    local_slot = col_index % tiles_here
    kept_ranks = jnp.left_shift(jnp.int32(16), tile_buckets)
    rank_mask = (
        (jnp.arange(full_rank, dtype=jnp.int32)[None, :] < kept_ranks[:, None]).astype(jnp.float32)
        * off_diagonal[:, None]
    )[:, None, :]
    shard_piece = lax.all_gather(signal, "trow", axis=1, tiled=True)
    diag_sum = jnp.zeros((columns, tile_size), jnp.float32)
    increment = jnp.einsum(
        "kn,tnr->tkr", shard_piece, right_tiles, preferred_element_type=jnp.float32
    )
    diag_sum = lax.cond(
        is_owner,
        lambda: lax.dot_general(
            shard_piece, diagonal_tile, (((1,), (1,)), ((), ())), preferred_element_type=jnp.float32
        ),
        lambda: diag_sum,
    )
    coeff_sum, diag_sum = (increment, diag_sum)
    coefficients = (coeff_sum * rank_mask).astype(jnp.bfloat16)
    partial_term = jnp.einsum(
        "tkr,tbr->tkb", coefficients, left_tiles, preferred_element_type=jnp.float32
    )
    slot_pick = (jnp.arange(tiles_here, dtype=jnp.int32) == local_slot).astype(jnp.float32)[
        :, None, None
    ]
    partial_term = partial_term + slot_pick * diag_sum[None]
    term_flat = jnp.transpose(partial_term, (1, 0, 2)).reshape(columns, tiles_here * tile_size)
    first_out = lax.psum_scatter(
        term_flat.astype(jnp.bfloat16), "tcol", scatter_dimension=1, tiled=True
    )
    gathered = lax.all_gather(first_out, "tcol", axis=1, tiled=True)
    block_tiles = jnp.transpose(gathered.reshape(columns, tiles_here, tile_size), (1, 0, 2))
    back_coeffs = jnp.einsum(
        "tkb,tbr->tkr", block_tiles, left_tiles, preferred_element_type=jnp.float32
    )
    back_coeffs = (back_coeffs * rank_mask).astype(jnp.bfloat16)
    second_term = jnp.einsum(
        "tkr,tbr->kb", back_coeffs, right_tiles, preferred_element_type=jnp.float32
    )
    own_block = lax.dynamic_index_in_dim(block_tiles, local_slot, 0, keepdims=False)
    owned_term = lax.cond(
        is_owner,
        lambda: second_term + jnp.dot(own_block, diagonal_tile, preferred_element_type=jnp.float32),
        lambda: second_term,
    )
    second_out = lax.psum_scatter(
        owned_term.astype(jnp.bfloat16), "trow", scatter_dimension=1, tiled=True
    )
    return (first_out, second_out)


def solution(mesh):
    in_specs = (
        P(None, ("tcol", "trow")),
        P("trow", "tcol", None, None),
        P("trow", "tcol", None, None),
        P("tcol", None, None),
        P("trow", "tcol"),
    )
    out_specs = (P(None, ("trow", "tcol")), P(None, ("tcol", "trow")))
    return jax.shard_map(body, mesh=mesh, in_specs=in_specs, out_specs=out_specs, check_vma=False)
```

profile of v0, /device:TPU:0, one launch (start us, length us, event | category | flops | bytes accessed | tf_op | source)
XLA Modules:
  0.0 250.5 jit_solution(13569567383582425134)
XLA Ops:
  7.2 0.0 copy-start
  7.2 0.0 all-gather.3.cloned.1.call-start
  7.2 0.7 all-gather.3.cloned.1.call-update
  7.9 0.0 reduce-scatter.3.cloned.1.call-start
  8.0 0.7 shift-left_bitcast_fusion
  8.7 0.1 compare_select_fusion
  8.7 40.9 %all-gather.3.cloned.1.call-done = bf16[256,2048]{1,0:T(8,128)(2,1)} async-done(((bf16[256,256]{1,0:T(8,128)(2,1)}), bf16[256,2048]{1,0:T(8,128)(2,1)}) %all-gather.3.cloned.1.call-update) | async-done | bytes 1048592 | tf_op jit(solution)/shard_map/all_gather | solution.py:27
  49.6 7.4 %conditional.2 = (f32[256,2048]{1,0:T(8,128)}) conditional(s32[]{:T(128)} %convert_element_type.38, () %tuple.22, (bf16[256,2048]{1,0:T(8,128)(2,1)}, bf16[2048,2048]{1,0:T(8,128)(2,1)}) %tuple.41), branch_computations={%region_0.1_spmd, %region_1.2_spmd} | conditional | flops 2147483648 | bytes 11534344 | solution.py:32
  49.6 7.4 %fusion.31 = f32[256,2048]{1,0:T(8,128)} fusion(bf16[256,2048]{1,0:T(8,128)(2,1)} %get-tuple-element.46, bf16[2048,2048]{1,0:T(8,128)(2,1)} %get-tuple-element.47), kind=kOutput, calls=%fused_computation.24 | convolution fusion | flops 2147483648 | bytes 11534336 | tf_op jit(solution)/shard_map/cond/branch_1_fun/dot_general | solution.py:34
  57.0 0.0 copy-done
  57.0 5.2 %fusion.3 = bf16[256,2,2048]{2,0,1:T(8,128)(2,1)} fusion(bf16[2,1,2048,256]{3,2,1,0:T(8,128)(2,1)S(1)} %copy-done, f32[256,2048]{1,0:T(8,128)} %get-tuple-element.60, f32[2]{0:T(128)S(1)} %compare_convert_fusion, bf16[2,1,2048,256]{3,2,1,0:T(8,128)(2,1)} %param.11, bf16[256,2048]{1,0:T(8,128)(2,1)} %all-gather.3.cloned.1.call-done, ...), kind=kOutput, calls=%fused_computation.5 | convolution fusion | flops 1077149696 | bytes 9439240 | tf_op jit(solution)/shard_map/tkr,tbr->tkb/dot_general | solution.py:41
  62.2 4.0 %copy.7 = bf16[256,2,2048]{0,2,1:T(8,128)(2,1)} copy(bf16[256,2,2048]{2,0,1:T(8,128)(2,1)} %fusion.3) | data formatting | bytes 4194304 | tf_op jit(solution)/shard_map/convert_element_type | solution.py:50
  66.2 0.0 reduce-scatter.3.cloned.1.call-update
  66.2 0.0 all-gather.5.cloned.1.call-start
  66.3 70.6 %reduce-scatter.3.cloned.1.call-done = bf16[256,256]{0,1:T(8,128)(2,1)} async-done(((bf16[256,4096]{0,1:T(8,128)(2,1)}), bf16[256,256]{0,1:T(8,128)(2,1)}) %reduce-scatter.3.cloned.1.call-update) | async-done | bytes 131088 | tf_op jit(solution)/shard_map/reduce_scatter | solution.py:49
  136.9 0.0 all-gather.5.cloned.1.call-update
  136.9 0.0 reduce-scatter.5.cloned.1.call-start
  137.0 49.3 %all-gather.5.cloned.1.call-done = bf16[256,4096]{0,1:T(8,128)(2,1)} async-done(((bf16[256,256]{0,1:T(8,128)(2,1)}), bf16[256,4096]{0,1:T(8,128)(2,1)}) %all-gather.5.cloned.1.call-update) | async-done | bytes 2097168 | tf_op jit(solution)/shard_map/all_gather | solution.py:52
  186.3 4.9 %convolution_bitcast_fusion = f32[256,2048]{1,0:T(8,128)} fusion(bf16[2,1,2048,256]{3,2,1,0:T(8,128)(2,1)} %param.11, bf16[2,256,2048]{1,2,0:T(8,128)(2,1)} %bitcast.47, bf16[2,1,2048,256]{3,2,1,0:T(8,128)(2,1)S(1)} %copy-done, f32[2,256]{1,0:T(2,128)S(1)} %compare_select_fusion), kind=kOutput, calls=%fused_computation.6 | convolution fusion | flops 1074003968 | bytes 8390656 | tf_op jit(solution)/shard_map/tkr,tbr->kb/dot_general | solution.py:58
  191.2 11.9 %conditional.3 = (f32[256,2048]{1,0:T(8,128)}) conditional(s32[]{:T(128)} %convert_element_type.38, f32[256,2048]{1,0:T(8,128)} %convolution_bitcast_fusion, (s32[]{:T(128)}, bf16[256,2,2048]{0,2,1:T(8,128)(2,1)}, bf16[2048,2048]{1,0:T(8,128)(2,1)}, f32[256,2048]{1,0:T(8,128)}) %tuple.42), branch_computations={%region_3.4_spmd, %region_4.5_spmd} | conditional | flops 2148007936 | bytes 17825838 | solution.py:62
  191.2 4.0 %copy.8 = bf16[256,2,2048]{2,0,1:T(8,128)(2,1)} copy(bf16[256,2,2048]{0,2,1:T(8,128)(2,1)} %get-tuple-element.55) | data formatting | bytes 4194304 | tf_op jit(solution)/shard_map
  195.2 7.9 %convolution_add_fusion = f32[256,2048]{1,0:T(8,128)} fusion(f32[256,2048]{1,0:T(8,128)} %get-tuple-element.48, bf16[2048,2048]{1,0:T(8,128)(2,1)} %get-tuple-element.51, bf16[256,2,2048]{2,0,1:T(8,128)(2,1)} %copy.8, s32[]{:T(128)S(6)} %select_n.14), kind=kOutput, calls=%fused_computation | convolution fusion | flops 2148007936 | bytes 13631492 | tf_op jit(solution)/shard_map/cond/branch_1_fun/dot_general | solution.py:64
  203.1 0.0 copy-start.1
  203.1 2.8 %convert_element_type.42 = bf16[256,2048]{1,0:T(8,128)(2,1)} convert(f32[256,2048]{1,0:T(8,128)} %get-tuple-element.61) | non-fusion elementwise | flops 524288 | bytes 3145728 | tf_op jit(solution)/shard_map/convert_element_type | solution.py:68
  205.9 0.0 reduce-scatter.5.cloned.1.call-update
  205.9 0.0 copy-done.1
  205.9 0.8 copy.9
  206.7 37.3 %reduce-scatter.5.cloned.1.call-done = bf16[256,256]{1,0:T(8,128)(2,1)} async-done(((bf16[256,2048]{1,0:T(8,128)(2,1)}), bf16[256,256]{1,0:T(8,128)(2,1)}) %reduce-scatter.5.cloned.1.call-update) | async-done | bytes 131088 | tf_op jit(solution)/shard_map/reduce_scatter | solution.py:67
  (2 shorter events, 0.0 us)
Async XLA Ops:
  7.2 49.9 %copy-start = (bf16[2,1,2048,256]{3,2,1,0:T(8,128)(2,1)S(1)}, bf16[2,1,2048,256]{3,2,1,0:T(8,128)(2,1)}, u32[]{:S(2)}) copy-start(bf16[2,1,2048,256]{3,2,1,0:T(8,128)(2,1)} %param.10) | copy-start | bytes 6291460
  7.2 42.4 %all-gather.3.cloned.1.call-start = ((), (), s32[]{:S(2)}) async-start(), calls=%async_computation.2 | async-start | bytes 1179648 | tf_op jit(solution)/shard_map/all_gather | solution.py:27
  7.9 129.0 %reduce-scatter.3.cloned.1.call-start = ((), (), s32[]{:S(2)}) async-start(), calls=%async_computation.3 | async-start | bytes 2228224 | tf_op jit(solution)/shard_map/reduce_scatter | solution.py:49
  66.2 120.1 %all-gather.5.cloned.1.call-start = ((), (), s32[]{:S(2)}) async-start(), calls=%async_computation.4 | async-start | bytes 2228224 | tf_op jit(solution)/shard_map/all_gather | solution.py:52
  136.9 107.0 %reduce-scatter.5.cloned.1.call-start = ((), (), s32[]{:S(2)}) async-start(), calls=%async_computation.5 | async-start | bytes 1179648 | tf_op jit(solution)/shard_map/reduce_scatter | solution.py:67
  203.1 2.8 %copy-start.1 = (bf16[256,256]{0,1:T(8,128)(2,1)S(1)}, bf16[256,256]{0,1:T(8,128)(2,1)}, u32[]{:S(2)}) copy-start(bf16[256,256]{0,1:T(8,128)(2,1)} %reduce-scatter.3.cloned.1.call-done) | copy-start | bytes 393220
Sparse Core Ops, SparseCore 0:
  9.6 39.9 all-gather.2
  66.3 70.5 reduce-scatter.2
  139.7 46.5 all-gather.4
  206.0 37.8 reduce-scatter.4
where the time goes:
time: 251 us; the launch traced here: 250 us
  waiting for transfers between devices  199 us (79%)
  matrix products  25.4 us (10%)
  between operations  13.8 us (5%)
  local copies, waits for them, and re-layouts  8.76 us (3%)
  other arithmetic  3.5 us (1%)
    reduce_scatter x1, waiting for transfers between devices, body(): lax.psum_scatter(term_flat.astype(jnp.bfloat16), 'tcol', scatter_dimensio...  70.6 us
    all_gather x1, waiting for transfers between devices, body(): gathered = lax.all_gather(first_out, 'tcol', axis=1, tiled=True)  49.3 us
    all_gather x1, waiting for transfers between devices, body(): shard_piece = lax.all_gather(signal, 'trow', axis=1, tiled=True)  40.9 us
    reduce_scatter x1, waiting for transfers between devices, body(): lax.psum_scatter(owned_term.astype(jnp.bfloat16), 'trow', scatter_dimensi...  37.3 us
    dot_general x1, matrix products, body(): jnp.dot(own_block, diagonal_tile, preferred_element_type=jnp.float32)  7.94 us
    dot_general x1, matrix products, body(): lax.dot_general(shard_piece, diagonal_tile, (((1,), (1,)), ((), ())), pre...  7.4 us
    dot_general x1, matrix products, body(): jnp.einsum('tkr,tbr->tkb', coefficients, left_tiles, preferred_element_ty...  5.21 us
  transfers between devices with their start and end apart: 4, of which 4 were waited for; matrix products, arithmetic and copies ran while one was open for 1% of the time, Pallas kernels for 0%

commit v1 on v0

v1 whole, which is shorter than its diff:
```python
import functools

import jax
import jax.numpy as jnp
from jax import lax
from jax.experimental import pallas as pl
from jax.experimental.pallas import tpu as pltpu
from jax.sharding import PartitionSpec as P

CHUNKS = 1
PIECE = 256
F32 = jnp.float32
BF16 = jnp.bfloat16
REL = [(d, x) for d in range(4) for x in range(2)]
VMEM = pl.BlockSpec(memory_space=pltpu.VMEM)
SMEM = pl.BlockSpec(memory_space=pltpu.SMEM)


def dot(a, b):
    return lax.dot_general(a, b, (((1,), (0,)), ((), ())), preferred_element_type=F32)


def dot_t(a, b):
    return lax.dot_general(a, b, (((1,), (1,)), ((), ())), preferred_element_type=F32)


def total(parts):
    return functools.reduce(lambda a, b: a + b, parts)


def row_piece(info, rel):
    return (info[0] ^ rel[1]) * 4 + (info[1] ^ rel[0])


def half_piece(info, rel):
    return (info[2] ^ rel[0]) * 2 + (info[3] ^ rel[1])


def rows_of(piece):
    return pl.ds(pl.multiple_of(piece * PIECE, PIECE), PIECE)


def masked(values, rank):
    columns = lax.broadcasted_iota(jnp.int32, values.shape, 1)
    return jnp.where(columns < rank, values, 0.0)


def coeff_kernel(info, *refs):
    x, right, out = refs[:8], refs[8], refs[9]
    for t in range(2):
        acc = total(dot(x[n][...], right[t, rows_of(row_piece(info, rel)), :]) for n, rel in enumerate(REL))
        out[t] = masked(acc, info[4 + t]).astype(BF16)


def diag_kernel(info, *refs):
    x, dense, out = refs[:8], refs[8], refs[9]
    acc = total(dot_t(x[n][...], dense[:, rows_of(row_piece(info, rel))]) for n, rel in enumerate(REL))
    out[...] = acc.astype(BF16)


def term_kernel(info, own, mate, left_own, left_mate, *outs):
    for out, rel in zip(outs, REL):
        piece = half_piece(info, rel)
        tile = piece // 4
        acc = dot_t(own[tile], left_own[piece]) + dot_t(mate[tile], left_mate[piece])
        out[...] = acc.astype(BF16)


def back_kernel(info, *refs):
    y, left_own, left_mate, own, mate = refs[:8], refs[8], refs[9], refs[10], refs[11]
    for half in range(2):
        tile = (info[2] // 2) ^ half
        for left, out in ((left_mate, mate), (left_own, own)):
            out[tile] = total(
                dot(y[n][...], left[half_piece(info, rel)]) for n, rel in enumerate(REL) if rel[0] // 2 == half
            ).astype(out.dtype)


def second_kernel(info, own, mate, right, y_diag, dense, *outs):
    coeff = [masked(own[t] + mate[t].astype(F32), info[4 + t]).astype(BF16) for t in range(2)]
    for out, rel in zip(outs, REL):
        rows = rows_of(row_piece(info, rel))
        acc = dot_t(coeff[0], right[0, rows, :]) + dot_t(coeff[1], right[1, rows, :])
        out[...] = (acc + dot(y_diag[...], dense[:, rows])).astype(BF16)


def call(kernel, name, info, operands, outs, flops, moved):
    return pl.pallas_call(
        kernel,
        name=name,
        out_shape=outs,
        in_specs=[SMEM] + [VMEM] * len(operands),
        out_specs=[VMEM] * len(outs),
        cost_estimate=pl.CostEstimate(flops=flops, bytes_accessed=moved, transcendentals=0),
    )(info, *operands)


def swap(x, axis, bits):
    size = lax.axis_size(axis)
    return lax.ppermute(x, axis, [(i, i ^ bits) for i in range(size)])


def gather(own, axis, ring, side):
    got = {(0, 0): own}
    got[(0, 1)] = swap(own, axis, side)
    for d in (1, 3, 2):
        got[(d, 0)] = swap(own, axis, d * ring)
    for d in (1, 3, 2):
        got[(d, 1)] = swap(got[(0, 1)], axis, d * ring)
    return [got[rel] for rel in REL]


def scatter(pieces, axis, ring, side, extra=()):
    piece = dict(zip(REL, pieces))
    far = [piece[(0, 1)]] + [swap(piece[(d, 1)], axis, d * ring) for d in (1, 3, 2)]
    near = [piece[(0, 0)]] + [swap(piece[(d, 0)], axis, d * ring) for d in (1, 3, 2)]
    crossed = swap(total(v.astype(F32) for v in far).astype(BF16), axis, side)
    return total(v.astype(F32) for v in near + [crossed] + list(extra)).astype(BF16)


def body(signal, left_factors, right_factors, dense_diagonal, buckets):
    trow = lax.axis_index("trow")
    tcol = lax.axis_index("tcol")
    core = tcol % 2
    tile_rows = trow * 2 + jnp.arange(2, dtype=jnp.int32)
    ranks = jnp.where(tile_rows == tcol, 0, jnp.left_shift(jnp.int32(16), buckets[:, 0]))
    info = jnp.concatenate([jnp.stack([trow // 4, trow % 4, tcol // 4, (tcol // 2) % 2]), ranks]).astype(jnp.int32)

    right = right_factors[:, 0]
    left = left_factors.reshape(2, 4, 2, PIECE, PIECE)
    left_own = lax.dynamic_index_in_dim(left, core, 2, keepdims=False).reshape(8, PIECE, PIECE)
    left_sent = lax.dynamic_index_in_dim(left, 1 - core, 2, keepdims=False).reshape(8, PIECE, PIECE)
    left_mate = swap(left_sent, "tcol", 1)
    dense = lax.dynamic_slice_in_dim(dense_diagonal[0], trow * PIECE, PIECE, 0)
    to_owner = [(a * 16 + b, (b // 2) * 16 + (b % 2) * 8 + a) for a in range(8) for b in range(16)]
    from_owner = [(d, s) for s, d in to_owner]

    count = signal.shape[0] // CHUNKS
    unit = 2 * count * PIECE * PIECE
    size = count * PIECE * 2
    piece = jax.ShapeDtypeStruct((count, PIECE), BF16)
    pair = jax.ShapeDtypeStruct((2, count, PIECE), BF16)
    pair_wide = jax.ShapeDtypeStruct((2, count, PIECE), F32)
    firsts, seconds = [], []
    for c in range(CHUNKS):
        x = gather(signal[c * count : (c + 1) * count], "trow", 1, 4)
        (coeff,) = call(coeff_kernel, "coeff", info, [*x, right], [pair], 16 * unit, 10 * size + 2**21)
        coeff_mate = swap(coeff, "tcol", 1)
        (diag,) = call(diag_kernel, "diag", info, [*x, dense], [piece], 8 * unit, 9 * size + 2**20)
        diag = lax.ppermute(diag, ("trow", "tcol"), to_owner)
        terms = call(
            term_kernel, "term", info, [coeff, coeff_mate, left_own, left_mate], [piece] * 8, 16 * unit, 12 * size + 2**21
        )
        first = scatter(terms, "tcol", 4, 2, [diag])
        y = gather(first, "tcol", 4, 2)
        y_diag = lax.ppermute(first, ("trow", "tcol"), from_owner)
        own, mate = call(
            back_kernel, "back", info, [*y, left_own, left_mate], [pair_wide, pair], 16 * unit, 14 * size + 2**21
        )
        mate = swap(mate, "tcol", 1)
        terms = call(
            second_kernel, "second", info, [own, mate, right, y_diag, dense], [piece] * 8, 24 * unit, 15 * size + 3 * 2**20
        )
        second = scatter(terms, "trow", 1, 4)
        firsts.append(first)
        seconds.append(second)
    return (jnp.concatenate(firsts, 0), jnp.concatenate(seconds, 0))


def solution(mesh):
    in_specs = (
        P(None, ("tcol", "trow")),
        P("trow", "tcol", None, None),
        P("trow", "tcol", None, None),
        P("tcol", None, None),
        P("trow", "tcol"),
    )
    out_specs = (P(None, ("trow", "tcol")), P(None, ("tcol", "trow")))
    return jax.shard_map(body, mesh=mesh, in_specs=in_specs, out_specs=out_specs, check_vma=False)
```

time: 251 us -> 123 us (0.49)
  waiting for transfers between devices: 199 us -> 34.1 us
  starting transfers between devices: 0.16 us -> 57.4 us
  matrix products: 25.4 us -> 0 us
  Pallas kernels: 0 us -> 17 us
  between operations: 13.8 us -> 0.85 us
    reduce_scatter x2 -> x0, waiting for transfers between devices: 108 us -> none  [the longest x1 70.6 us: body(): lax.psum_scatter(term_flat.astype(jnp.bfloat16), 'tcol', scatter_dimensio...]
    all_gather x2 -> x0, waiting for transfers between devices: 90.2 us -> none  [the longest x1 49.3 us: body(): gathered = lax.all_gather(first_out, 'tcol', axis=1, tiled=True)]
    ppermute x0 -> x33, starting transfers between devices: none -> 57.4 us  [the longest x31 54.3 us: swap(): return lax.ppermute(x, axis, [(i, i ^ bits) for i in range(size)])]
    ppermute x0 -> x33, waiting for transfers between devices: none -> 34.1 us  [the longest x31 34.1 us: swap(): return lax.ppermute(x, axis, [(i, i ^ bits) for i in range(size)])]
    dot_general x4 -> x0, matrix products: 25.4 us -> none  [the longest x1 7.94 us: body(): jnp.dot(own_block, diagonal_tile, preferred_element_type=jnp.float32)]
    pallas_call x0 -> x5, Pallas kernels: none -> 17 us  [call(): pl.pallas_call(kernel, name=name, out_shape=outs, in_specs=[SMEM] + [VMEM...]
    dynamic_slice x0 -> x2, local copies, waits for them, and re-layouts: none -> 5.12 us  [the longest x1 2.8 us: body(): lax.dynamic_index_in_dim(left, 1 - core, 2, keepdims=False)]
    another operation x1 -> x0, local copies, waits for them, and re-layouts: 4 us -> none
  transfers between devices with their start and end apart: 4 -> 33, of which waited for: 4 -> 18; matrix products, arithmetic and copies ran while one was open for 1% -> 3% of each run, Pallas kernels for 0% -> 5%
where the time goes in v1:
time: 123 us; the launch traced here: 121 us
  starting transfers between devices  57.4 us (47%)
  waiting for transfers between devices  34.1 us (28%)
  Pallas kernels  17 us (14%)
  local copies, waits for them, and re-layouts  8.93 us (7%)
  other arithmetic  2.81 us (2%)
    ppermute x31, starting transfers between devices, swap(): return lax.ppermute(x, axis, [(i, i ^ bits) for i in range(size)])  54.3 us
    ppermute x31, waiting for transfers between devices, swap(): return lax.ppermute(x, axis, [(i, i ^ bits) for i in range(size)])  34.1 us
    pallas_call x5, Pallas kernels, call(): pl.pallas_call(kernel, name=name, out_shape=outs, in_specs=[SMEM] + [VMEM...  17 us
    unnamed x52, local copies, waits for them, and re-layouts  3.17 us
    dynamic_slice x1, local copies, waits for them, and re-layouts, body(): lax.dynamic_index_in_dim(left, 1 - core, 2, keepdims=False)  2.8 us
  transfers between devices with their start and end apart: 33, of which 18 were waited for; matrix products, arithmetic and copies ran while one was open for 3% of the time, Pallas kernels for 5%

profile of v1, /device:TPU:0, one launch (start us, length us, event | category | flops | bytes accessed | tf_op | source)
XLA Modules:
  0.0 121.1 jit_solution(10706983551628282754)
XLA Ops:
  0.7 2.8 %constant_dynamic-slice_fusion = (bf16[2,4,1,256,256]{4,3,2,1,0:T(8,128)(2,1)S(1)}, bf16[2,4,1,256,256]{4,3,2,1,0:T(8,128)(2,1)}) fusion(bf16[2,4,2,256,256]{4,3,2,1,0:T(8,128)(2,1)} %bitcast.20, s32[]{:T(128)S(6)} %select_n.47, s32[]{:T(128)S(6)} %select_n.46), kind=kLoop, calls=%fused_computation.6 | loop fusion | bytes 4194312 | tf_op jit(solution)/shard_map/jit(dynamic_index_in_dim)/dynamic_slice | solution.py:132
  3.5 1.6 %collective-permute-start = (bf16[256,256]{1,0:T(8,128)(2,1)S(1)}, bf16[256,256]{1,0:T(8,128)(2,1)S(1)}, u32[]{:S(2)}, u32[]{:S(2)}) collective-permute-start(bf16[256,256]{1,0:T(8,128)(2,1)S(1)} %copy-done.1), channel_id=1, source_target_pairs={{0,64},{16,80},{32,96},{48,112},{64,0},{80,16},{96,32},{112,48},{1... | collective-permute-start | bytes 393224 | tf_op jit(solution)/shard_map/ppermute | solution.py:100
  5.1 1.9 %collective-permute-start.1 = (bf16[256,256]{1,0:T(8,128)(2,1)S(1)}, bf16[256,256]{1,0:T(8,128)(2,1)S(1)}, u32[]{:S(2)}, u32[]{:S(2)}) collective-permute-start(bf16[256,256]{1,0:T(8,128)(2,1)S(1)} %copy-done.1), channel_id=1, source_target_pairs={{0,16},{16,0},{32,48},{48,32},{64,80},{80,64},{96,112},{112,96},{1... | collective-permute-start | bytes 393224 | tf_op jit(solution)/shard_map/ppermute | solution.py:100
  7.0 3.6 %collective-permute-start.3 = (bf16[256,256]{1,0:T(8,128)(2,1)S(1)}, bf16[256,256]{1,0:T(8,128)(2,1)S(1)}, u32[]{:S(2)}, u32[]{:S(2)}) collective-permute-start(bf16[256,256]{1,0:T(8,128)(2,1)S(1)} %copy-done.1), channel_id=1, source_target_pairs={{0,32},{16,48},{32,0},{48,16},{64,96},{80,112},{96,64},{112,80},{1... | collective-permute-start | bytes 393224 | tf_op jit(solution)/shard_map/ppermute | solution.py:100
  11.4 3.9 %collective-permute-start.4 = (bf16[256,256]{1,0:T(8,128)(2,1)S(1)}, bf16[256,256]{1,0:T(8,128)(2,1)S(1)}, u32[]{:S(2)}, u32[]{:S(2)}) collective-permute-start(bf16[256,256]{1,0:T(8,128)(2,1)S(1)} %collective-permute-done.refs_1_), channel_id=1, source_target_pairs={{0,32},{16,48},{32,0},{48,16},{64,96},{80,112},{96,64},{112,80},{1... | collective-permute-start | bytes 393224 | tf_op jit(solution)/shard_map/ppermute | solution.py:100
  15.3 2.4 %collective-permute-done.3.refs_4_ = bf16[256,256]{1,0:T(8,128)(2,1)S(1)} collective-permute-done((bf16[256,256]{1,0:T(8,128)(2,1)S(1)}, bf16[256,256]{1,0:T(8,128)(2,1)S(1)}, u32[]{:S(2)}, u32[]{:S(2)}) %collective-permute-start.3) | collective-permute-done | bytes 131104 | tf_op jit(solution)/shard_map/ppermute | solution.py:100
  19.6 3.1 %collective-permute-done.4.refs_5_ = bf16[256,256]{1,0:T(8,128)(2,1)S(1)} collective-permute-done((bf16[256,256]{1,0:T(8,128)(2,1)S(1)}, bf16[256,256]{1,0:T(8,128)(2,1)S(1)}, u32[]{:S(2)}, u32[]{:S(2)}) %collective-permute-start.4) | collective-permute-done | bytes 131104 | tf_op jit(solution)/shard_map/ppermute | solution.py:100
  22.7 2.5 %collective-permute-done.6.refs_7_ = bf16[256,256]{1,0:T(8,128)(2,1)S(1)} collective-permute-done((bf16[256,256]{1,0:T(8,128)(2,1)S(1)}, bf16[256,256]{1,0:T(8,128)(2,1)S(1)}, u32[]{:S(2)}, u32[]{:S(2)}) %collective-permute-start.6) | collective-permute-done | bytes 131104 | tf_op jit(solution)/shard_map/ppermute | solution.py:100
  25.9 3.5 %coeff.1.own = bf16[2,256,256]{2,1,0:T(8,128)(2,1)} custom-call(s32[6]{0:T(128)} %concatenate.3.info, bf16[256,256]{1,0:T(8,128)(2,1)} %refs_0_.3, bf16[256,256]{1,0:T(8,128)(2,1)} %copy-done.2, bf16[256,256]{1,0:T(8,128)(2,1)} %copy-done.3, bf16[256,256]{1,0:T(8,128)(2,1)} %copy-done.6, bf16[256,256]{1,0:T(8,128)(2,1)} %copy-done.4, ...), custom_call_target="tpu_custom_call" | custom-call | flops 536870912 | bytes 3407872 | tf_op jit(solution)/shard_map/coeff/pallas_call | solution.py:88
  29.4 1.7 %collective-permute-done.7.mate = bf16[2,256,256]{2,1,0:T(8,128)(2,1)S(1)} collective-permute-done((bf16[2,256,256]{2,1,0:T(8,128)(2,1)}, bf16[2,256,256]{2,1,0:T(8,128)(2,1)S(1)}, u32[]{:S(2)}, u32[]{:S(2)}) %collective-permute-start.7) | collective-permute-done | bytes 262176 | tf_op jit(solution)/shard_map/ppermute | solution.py:100
  32.3 3.2 %term.1 = (bf16[256,256]{1,0:T(8,128)(2,1)}, bf16[256,256]{1,0:T(8,128)(2,1)}, bf16[256,256]{1,0:T(8,128)(2,1)}, bf16[256,256]{1,0:T(8,128)(2,1)}, bf16[256,256]...) custom-call(s32[6]{0:T(128)} %concatenate.3.info, ...), custom_call_target="tpu_custom_call" | custom-call | flops 536870912 | bytes 3670016 | tf_op jit(solution)/shard_map/term/pallas_call | solution.py:88
  37.0 2.2 %collective-permute-start.13 = (bf16[256,256]{1,0:T(8,128)(2,1)}, bf16[256,256]{1,0:T(8,128)(2,1)S(1)}, u32[]{:S(2)}, u32[]{:S(2)}) collective-permute-start(bf16[256,256]{1,0:T(8,128)(2,1)} %get-tuple-element.26), channel_id=1, source_target_pairs={{0,12},{1,13},{2,14},{3,15},{4,8},{5,9},{6,10},{7,11},{8,4},{9,5},... | collective-permute-start | bytes 393224 | tf_op jit(solution)/shard_map/ppermute | solution.py:100
  40.0 2.3 %dynamic-slice_bitcast_fusion.refs_8_.dense = bf16[256,2048]{1,0:T(8,128)(2,1)} fusion(bf16[1,2048,2048]{2,1,0:T(8,128)(2,1)} %param.8, s32[]{:T(128)S(6)} %select_n.48), kind=kLoop, calls=%fused_computation | loop fusion | bytes 2097156 | tf_op jit(solution)/shard_map/dynamic_slice | solution.py:134
  42.4 2.8 %diag.1 = bf16[256,256]{1,0:T(8,128)(2,1)} custom-call(s32[6]{0:T(128)} %concatenate.3.info, bf16[256,256]{1,0:T(8,128)(2,1)} %refs_0_.3, bf16[256,256]{1,0:T(8,128)(2,1)} %copy-done.2, bf16[256,256]{1,0:T(8,128)(2,1)} %copy-done.3, bf16[256,256]{1,0:T(8,128)(2,1)} %copy-done.6, bf16[256,256]{1,0:T(8,128)(2,1)} %copy-done.4, bf16[256,256]{1,0:T(8,128)(2,1)} %copy-done.7, ...), custom_call_target="tpu_custom_call" | custom-call | flops 268435456 | bytes 2228224 | tf_op jit(solution)/shard_map/diag/pallas_call | solution.py:88
  46.7 3.1 %collective-permute-start.10 = (bf16[256,256]{1,0:T(8,128)(2,1)S(1)}, bf16[256,256]{1,0:T(8,128)(2,1)S(1)}, u32[]{:S(2)}, u32[]{:S(2)}) collective-permute-start(bf16[256,256]{1,0:T(8,128)(2,1)S(1)} %copy-done.25), channel_id=1, source_target_pairs={{0,12},{1,13},{2,14},{3,15},{4,8},{5,9},{6,10},{7,11},{8,4},{9,5},... | collective-permute-start | bytes 393224 | tf_op jit(solution)/shard_map/ppermute | solution.py:100
  50.9 3.3 %collective-permute-start.15 = (bf16[256,256]{1,0:T(8,128)(2,1)S(1)}, bf16[256,256]{1,0:T(8,128)(2,1)S(1)}, u32[]{:S(2)}, u32[]{:S(2)}) collective-permute-start(bf16[256,256]{1,0:T(8,128)(2,1)S(1)} %add_convert_fusion.3), channel_id=1, source_target_pairs={{0,2},{1,3},{2,0},{3,1},{4,6},{5,7},{6,4},{7,5},{8,10},{9,11},{10,... | collective-permute-start | bytes 393224 | tf_op jit(solution)/shard_map/ppermute | solution.py:100
  54.2 7.5 %collective-permute-done.10 = bf16[256,256]{1,0:T(8,128)(2,1)S(1)} collective-permute-done((bf16[256,256]{1,0:T(8,128)(2,1)S(1)}, bf16[256,256]{1,0:T(8,128)(2,1)S(1)}, u32[]{:S(2)}, u32[]{:S(2)}) %collective-permute-start.10) | collective-permute-done | bytes 131104 | tf_op jit(solution)/shard_map/ppermute | solution.py:100
  63.0 6.4 %collective-permute-start.20 = (bf16[256,256]{1,0:T(8,128)(2,1)S(1)}, bf16[256,256]{1,0:T(8,128)(2,1)S(1)}, u32[]{:S(2)}, u32[]{:S(2)}) collective-permute-start(bf16[256,256]{1,0:T(8,128)(2,1)S(1)} %add_convert_fusion.2.refs_0_), channel_id=1, source_target_pairs={{0,8},{1,9},{2,10},{3,11},{4,12},{5,13},{6,14},{7,15},{8,0},{9,1},... | collective-permute-start | bytes 393224 | tf_op jit(solution)/shard_map/ppermute | solution.py:100
  70.5 3.6 %collective-permute-start.21 = (bf16[256,256]{1,0:T(8,128)(2,1)S(1)}, bf16[256,256]{1,0:T(8,128)(2,1)S(1)}, u32[]{:S(2)}, u32[]{:S(2)}) collective-permute-start(bf16[256,256]{1,0:T(8,128)(2,1)S(1)} %collective-permute-done.17.refs_1_), channel_id=1, source_target_pairs={{0,8},{1,9},{2,10},{3,11},{4,12},{5,13},{6,14},{7,15},{8,0},{9,1},... | collective-permute-start | bytes 393224 | tf_op jit(solution)/shard_map/ppermute | solution.py:100
  74.5 2.3 %collective-permute-done.22.refs_6_ = bf16[256,256]{1,0:T(8,128)(2,1)S(1)} collective-permute-done((bf16[256,256]{1,0:T(8,128)(2,1)S(1)}, bf16[256,256]{1,0:T(8,128)(2,1)S(1)}, u32[]{:S(2)}, u32[]{:S(2)}) %collective-permute-start.22) | collective-permute-done | bytes 131104 | tf_op jit(solution)/shard_map/ppermute | solution.py:100
  76.8 2.9 %collective-permute-done.21.refs_5_ = bf16[256,256]{1,0:T(8,128)(2,1)S(1)} collective-permute-done((bf16[256,256]{1,0:T(8,128)(2,1)S(1)}, bf16[256,256]{1,0:T(8,128)(2,1)S(1)}, u32[]{:S(2)}, u32[]{:S(2)}) %collective-permute-start.21) | collective-permute-done | bytes 131104 | tf_op jit(solution)/shard_map/ppermute | solution.py:100
  79.7 1.7 %collective-permute-done.23.refs_7_ = bf16[256,256]{1,0:T(8,128)(2,1)S(1)} collective-permute-done((bf16[256,256]{1,0:T(8,128)(2,1)S(1)}, bf16[256,256]{1,0:T(8,128)(2,1)S(1)}, u32[]{:S(2)}, u32[]{:S(2)}) %collective-permute-start.23) | collective-permute-done | bytes 131104 | tf_op jit(solution)/shard_map/ppermute | solution.py:100
  82.1 3.6 %back.1 = (f32[2,256,256]{2,1,0:T(8,128)}, bf16[2,256,256]{2,1,0:T(8,128)(2,1)}) custom-call(s32[6]{0:T(128)} %concatenate.3.info, bf16[256,256]{1,0:T(8,128)(2,1)} %copy-done.9, bf16[256,256]{1,0:T(8,128)(2,1)} %copy-done.15, bf16[256,256]{1,0:T(8,128)(2,1)} %copy-done.16, bf16[256,256]{1,0:T(8,128)(2,1)} %copy-done.19, bf16[256,256]{1,0:T(8,128)(2,1)} %copy-done.17, ...), custom_call_target="tpu_custom_call" | custom-call | flops 536870912 | bytes 3932160 | tf_op jit(solution)/shard_map/back/pallas_call | solution.py:88
  88.2 3.9 %second.1 = (bf16[256,256]{1,0:T(8,128)(2,1)}, bf16[256,256]{1,0:T(8,128)(2,1)}, bf16[256,256]{1,0:T(8,128)(2,1)}, bf16[256,256]{1,0:T(8,128)(2,1)}, bf16[256,25...) custom-call(s32[6]{0:T(128)} %concatenate.3.info, ...), custom_call_target="tpu_custom_call" | custom-call | flops 805306368 | bytes 5111808 | tf_op jit(solution)/shard_map/second/pallas_call | solution.py:88
  92.1 7.2 %collective-permute-start.29 = (bf16[256,256]{1,0:T(8,128)(2,1)}, bf16[256,256]{1,0:T(8,128)(2,1)S(1)}, u32[]{:S(2)}, u32[]{:S(2)}) collective-permute-start(bf16[256,256]{1,0:T(8,128)(2,1)} %get-tuple-element.35), channel_id=1, source_target_pairs={{0,16},{16,0},{32,48},{48,32},{64,80},{80,64},{96,112},{112,96},{1... | collective-permute-start | bytes 393224 | tf_op jit(solution)/shard_map/ppermute | solution.py:100
  99.3 5.4 %collective-permute-start.30 = (bf16[256,256]{1,0:T(8,128)(2,1)}, bf16[256,256]{1,0:T(8,128)(2,1)S(1)}, u32[]{:S(2)}, u32[]{:S(2)}) collective-permute-start(bf16[256,256]{1,0:T(8,128)(2,1)} %get-tuple-element.36), channel_id=1, source_target_pairs={{0,48},{16,32},{32,16},{48,0},{64,112},{80,96},{96,80},{112,64},{1... | collective-permute-start | bytes 393224 | tf_op jit(solution)/shard_map/ppermute | solution.py:100
  105.5 3.2 %collective-permute-start.27 = (bf16[256,256]{1,0:T(8,128)(2,1)}, bf16[256,256]{1,0:T(8,128)(2,1)S(1)}, u32[]{:S(2)}, u32[]{:S(2)}) collective-permute-start(bf16[256,256]{1,0:T(8,128)(2,1)} %get-tuple-element.32), channel_id=1, source_target_pairs={{0,48},{16,32},{32,16},{48,0},{64,112},{80,96},{96,80},{112,64},{1... | collective-permute-start | bytes 393224 | tf_op jit(solution)/shard_map/ppermute | solution.py:100
  109.3 1.8 %collective-permute-done.30 = bf16[256,256]{1,0:T(8,128)(2,1)S(1)} collective-permute-done((bf16[256,256]{1,0:T(8,128)(2,1)}, bf16[256,256]{1,0:T(8,128)(2,1)S(1)}, u32[]{:S(2)}, u32[]{:S(2)}) %collective-permute-start.30) | collective-permute-done | bytes 131104 | tf_op jit(solution)/shard_map/ppermute | solution.py:100
  113.1 1.7 %collective-permute-start.32 = (bf16[256,256]{1,0:T(8,128)(2,1)S(1)}, bf16[256,256]{1,0:T(8,128)(2,1)S(1)}, u32[]{:S(2)}, u32[]{:S(2)}) collective-permute-start(bf16[256,256]{1,0:T(8,128)(2,1)S(1)} %add_convert_fusion.1), channel_id=1, source_target_pairs={{0,64},{16,80},{32,96},{48,112},{64,0},{80,16},{96,32},{112,48},{1... | collective-permute-start | bytes 393224 | tf_op jit(solution)/shard_map/ppermute | solution.py:100
  114.9 2.0 %collective-permute-done.27 = bf16[256,256]{1,0:T(8,128)(2,1)S(1)} collective-permute-done((bf16[256,256]{1,0:T(8,128)(2,1)}, bf16[256,256]{1,0:T(8,128)(2,1)S(1)}, u32[]{:S(2)}, u32[]{:S(2)}) %collective-permute-start.27) | collective-permute-done | bytes 131104 | tf_op jit(solution)/shard_map/ppermute | solution.py:100
  117.7 1.8 %collective-permute-done.32 = bf16[256,256]{1,0:T(8,128)(2,1)S(1)} collective-permute-done((bf16[256,256]{1,0:T(8,128)(2,1)S(1)}, bf16[256,256]{1,0:T(8,128)(2,1)S(1)}, u32[]{:S(2)}, u32[]{:S(2)}) %collective-permute-start.32) | collective-permute-done | bytes 131104 | tf_op jit(solution)/shard_map/ppermute | solution.py:100
  119.4 1.6 %add_convert_fusion = bf16[256,256]{1,0:T(8,128)(2,1)} fusion(bf16[256,256]{1,0:T(8,128)(2,1)S(1)} %collective-permute-done.32, bf16[256,256]{1,0:T(8,128)(2,1)S(1)} %collective-permute-done.28, bf16[256,256]{1,0:T(8,128)(2,1)S(1)} %collective-permute-done.27, bf16[256,256]{1,0:T(8,128)(2,1)S(1)} %collective-permute-done.26, ...), kind=kLoop, calls=%fused_computation.1 | loop fusion | flops 655360 | bytes 786432 | tf_op jit(solution)/shard_map/convert_element_type | solution.py:118
  (99 shorter events, 19.6 us)
Async XLA Ops:
  3.5 27.7 %collective-permute-start.8 = (bf16[8,256,256]{2,1,0:T(8,128)(2,1)S(1)}, bf16[8,256,256]{2,1,0:T(8,128)(2,1)S(1)}, u32[]{:S(2)}, u32[]{:S(2)}) collective-permute-start(bf16[8,256,256]{2,1,0:T(8,128)(2,1)S(1)} %bitcast.21), channel_id=1, source_target_pairs={{0,1},{1,0},{2,3},{3,2},{4,5},{5,4},{6,7},{7,6},{8,9},{9,8},{10,11... | collective-permute-start | bytes 3145736 | tf_op jit(solution)/shard_map/ppermute | solution.py:100
  3.5 7.1 %collective-permute-start = (bf16[256,256]{1,0:T(8,128)(2,1)S(1)}, bf16[256,256]{1,0:T(8,128)(2,1)S(1)}, u32[]{:S(2)}, u32[]{:S(2)}) collective-permute-start(bf16[256,256]{1,0:T(8,128)(2,1)S(1)} %copy-done.1), channel_id=1, source_target_pairs={{0,64},{16,80},{32,96},{48,112},{64,0},{80,16},{96,32},{112,48},{1... | collective-permute-start | bytes 393224 | tf_op jit(solution)/shard_map/ppermute | solution.py:100
  5.1 6.3 %collective-permute-start.1 = (bf16[256,256]{1,0:T(8,128)(2,1)S(1)}, bf16[256,256]{1,0:T(8,128)(2,1)S(1)}, u32[]{:S(2)}, u32[]{:S(2)}) collective-permute-start(bf16[256,256]{1,0:T(8,128)(2,1)S(1)} %copy-done.1), channel_id=1, source_target_pairs={{0,16},{16,0},{32,48},{48,32},{64,80},{80,64},{96,112},{112,96},{1... | collective-permute-start | bytes 393224 | tf_op jit(solution)/shard_map/ppermute | solution.py:100
  7.0 10.7 %collective-permute-start.3 = (bf16[256,256]{1,0:T(8,128)(2,1)S(1)}, bf16[256,256]{1,0:T(8,128)(2,1)S(1)}, u32[]{:S(2)}, u32[]{:S(2)}) collective-permute-start(bf16[256,256]{1,0:T(8,128)(2,1)S(1)} %copy-done.1), channel_id=1, source_target_pairs={{0,32},{16,48},{32,0},{48,16},{64,96},{80,112},{96,64},{112,80},{1... | collective-permute-start | bytes 393224 | tf_op jit(solution)/shard_map/ppermute | solution.py:100
  10.6 9.0 %collective-permute-start.5 = (bf16[256,256]{1,0:T(8,128)(2,1)S(1)}, bf16[256,256]{1,0:T(8,128)(2,1)S(1)}, u32[]{:S(2)}, u32[]{:S(2)}) collective-permute-start(bf16[256,256]{1,0:T(8,128)(2,1)S(1)} %copy-done.1), channel_id=1, source_target_pairs={{0,48},{16,32},{32,16},{48,0},{64,112},{80,96},{96,80},{112,64},{1... | collective-permute-start | bytes 393224 | tf_op jit(solution)/shard_map/ppermute | solution.py:100
  10.6 9.0 %collective-permute-start.2 = (bf16[256,256]{1,0:T(8,128)(2,1)S(1)}, bf16[256,256]{1,0:T(8,128)(2,1)S(1)}, u32[]{:S(2)}, u32[]{:S(2)}) collective-permute-start(bf16[256,256]{1,0:T(8,128)(2,1)S(1)} %collective-permute-done.refs_1_), channel_id=1, source_target_pairs={{0,16},{16,0},{32,48},{48,32},{64,80},{80,64},{96,112},{112,96},{1... | collective-permute-start | bytes 393224 | tf_op jit(solution)/shard_map/ppermute | solution.py:100
  11.4 11.3 %collective-permute-start.4 = (bf16[256,256]{1,0:T(8,128)(2,1)S(1)}, bf16[256,256]{1,0:T(8,128)(2,1)S(1)}, u32[]{:S(2)}, u32[]{:S(2)}) collective-permute-start(bf16[256,256]{1,0:T(8,128)(2,1)S(1)} %collective-permute-done.refs_1_), channel_id=1, source_target_pairs={{0,32},{16,48},{32,0},{48,16},{64,96},{80,112},{96,64},{112,80},{1... | collective-permute-start | bytes 393224 | tf_op jit(solution)/shard_map/ppermute | solution.py:100
  17.7 7.6 %collective-permute-start.6 = (bf16[256,256]{1,0:T(8,128)(2,1)S(1)}, bf16[256,256]{1,0:T(8,128)(2,1)S(1)}, u32[]{:S(2)}, u32[]{:S(2)}) collective-permute-start(bf16[256,256]{1,0:T(8,128)(2,1)S(1)} %collective-permute-done.refs_1_), channel_id=1, source_target_pairs={{0,48},{16,32},{32,16},{48,0},{64,112},{80,96},{96,80},{112,64},{1... | collective-permute-start | bytes 393224 | tf_op jit(solution)/shard_map/ppermute | solution.py:100
  29.4 1.7 %collective-permute-start.7 = (bf16[2,256,256]{2,1,0:T(8,128)(2,1)}, bf16[2,256,256]{2,1,0:T(8,128)(2,1)S(1)}, u32[]{:S(2)}, u32[]{:S(2)}) collective-permute-start(bf16[2,256,256]{2,1,0:T(8,128)(2,1)} %coeff.1.own), channel_id=1, source_target_pairs={{0,1},{1,0},{2,3},{3,2},{4,5},{5,4},{6,7},{7,6},{8,9},{9,8},{10,11... | collective-permute-start | bytes 786440 | tf_op jit(solution)/shard_map/ppermute | solution.py:100
  35.4 14.3 %collective-permute-start.12 = (bf16[256,256]{1,0:T(8,128)(2,1)}, bf16[256,256]{1,0:T(8,128)(2,1)S(1)}, u32[]{:S(2)}, u32[]{:S(2)}) collective-permute-start(bf16[256,256]{1,0:T(8,128)(2,1)} %get-tuple-element.25), channel_id=1, source_target_pairs={{0,4},{1,5},{2,6},{3,7},{4,0},{5,1},{6,2},{7,3},{8,12},{9,13},{10,... | collective-permute-start | bytes 393224 | tf_op jit(solution)/shard_map/ppermute | solution.py:100
  37.0 13.8 %collective-permute-start.13 = (bf16[256,256]{1,0:T(8,128)(2,1)}, bf16[256,256]{1,0:T(8,128)(2,1)S(1)}, u32[]{:S(2)}, u32[]{:S(2)}) collective-permute-start(bf16[256,256]{1,0:T(8,128)(2,1)} %get-tuple-element.26), channel_id=1, source_target_pairs={{0,12},{1,13},{2,14},{3,15},{4,8},{5,9},{6,10},{7,11},{8,4},{9,5},... | collective-permute-start | bytes 393224 | tf_op jit(solution)/shard_map/ppermute | solution.py:100
  39.2 11.6 %collective-permute-start.14 = (bf16[256,256]{1,0:T(8,128)(2,1)}, bf16[256,256]{1,0:T(8,128)(2,1)S(1)}, u32[]{:S(2)}, u32[]{:S(2)}) collective-permute-start(bf16[256,256]{1,0:T(8,128)(2,1)} %get-tuple-element.27), channel_id=1, source_target_pairs={{0,8},{1,9},{2,10},{3,11},{4,12},{5,13},{6,14},{7,15},{8,0},{9,1},... | collective-permute-start | bytes 393224 | tf_op jit(solution)/shard_map/ppermute | solution.py:100
  45.2 9.0 %collective-permute-start.16 = (bf16[256,256]{1,0:T(8,128)(2,1)}, bf16[256,256]{1,0:T(8,128)(2,1)S(1)}, u32[]{:S(2)}, u32[]{:S(2)}) collective-permute-start(bf16[256,256]{1,0:T(8,128)(2,1)} %diag.1), channel_id=1, source_target_pairs={{0,0},{1,8},{2,16},{3,24},{4,32},{5,40},{6,48},{7,56},{8,64},{9,72... | collective-permute-start | bytes 393224 | tf_op jit(solution)/shard_map/ppermute | solution.py:150
  46.7 15.0 %collective-permute-start.10 = (bf16[256,256]{1,0:T(8,128)(2,1)S(1)}, bf16[256,256]{1,0:T(8,128)(2,1)S(1)}, u32[]{:S(2)}, u32[]{:S(2)}) collective-permute-start(bf16[256,256]{1,0:T(8,128)(2,1)S(1)} %copy-done.25), channel_id=1, source_target_pairs={{0,12},{1,13},{2,14},{3,15},{4,8},{5,9},{6,10},{7,11},{8,4},{9,5},... | collective-permute-start | bytes 393224 | tf_op jit(solution)/shard_map/ppermute | solution.py:100
  49.8 11.9 %collective-permute-start.11 = (bf16[256,256]{1,0:T(8,128)(2,1)S(1)}, bf16[256,256]{1,0:T(8,128)(2,1)S(1)}, u32[]{:S(2)}, u32[]{:S(2)}) collective-permute-start(bf16[256,256]{1,0:T(8,128)(2,1)S(1)} %copy-done.24), channel_id=1, source_target_pairs={{0,8},{1,9},{2,10},{3,11},{4,12},{5,13},{6,14},{7,15},{8,0},{9,1},... | collective-permute-start | bytes 393224 | tf_op jit(solution)/shard_map/ppermute | solution.py:100
  50.8 11.7 %collective-permute-start.9 = (bf16[256,256]{1,0:T(8,128)(2,1)S(1)}, bf16[256,256]{1,0:T(8,128)(2,1)S(1)}, u32[]{:S(2)}, u32[]{:S(2)}) collective-permute-start(bf16[256,256]{1,0:T(8,128)(2,1)S(1)} %copy-done.23), channel_id=1, source_target_pairs={{0,4},{1,5},{2,6},{3,7},{4,0},{5,1},{6,2},{7,3},{8,12},{9,13},{10,... | collective-permute-start | bytes 393224 | tf_op jit(solution)/shard_map/ppermute | solution.py:100
  50.9 11.5 %collective-permute-start.15 = (bf16[256,256]{1,0:T(8,128)(2,1)S(1)}, bf16[256,256]{1,0:T(8,128)(2,1)S(1)}, u32[]{:S(2)}, u32[]{:S(2)}) collective-permute-start(bf16[256,256]{1,0:T(8,128)(2,1)S(1)} %add_convert_fusion.3), channel_id=1, source_target_pairs={{0,2},{1,3},{2,0},{3,1},{4,6},{5,7},{6,4},{7,5},{8,10},{9,11},{10,... | collective-permute-start | bytes 393224 | tf_op jit(solution)/shard_map/ppermute | solution.py:100
  62.6 7.1 %collective-permute-start.17 = (bf16[256,256]{1,0:T(8,128)(2,1)S(1)}, bf16[256,256]{1,0:T(8,128)(2,1)S(1)}, u32[]{:S(2)}, u32[]{:S(2)}) collective-permute-start(bf16[256,256]{1,0:T(8,128)(2,1)S(1)} %add_convert_fusion.2.refs_0_), channel_id=1, source_target_pairs={{0,2},{1,3},{2,0},{3,1},{4,6},{5,7},{6,4},{7,5},{8,10},{9,11},{10,... | collective-permute-start | bytes 393224 | tf_op jit(solution)/shard_map/ppermute | solution.py:100
  62.7 11.5 %collective-permute-start.18 = (bf16[256,256]{1,0:T(8,128)(2,1)S(1)}, bf16[256,256]{1,0:T(8,128)(2,1)S(1)}, u32[]{:S(2)}, u32[]{:S(2)}) collective-permute-start(bf16[256,256]{1,0:T(8,128)(2,1)S(1)} %add_convert_fusion.2.refs_0_), channel_id=1, source_target_pairs={{0,4},{1,5},{2,6},{3,7},{4,0},{5,1},{6,2},{7,3},{8,12},{9,13},{10,... | collective-permute-start | bytes 393224 | tf_op jit(solution)/shard_map/ppermute | solution.py:100
  63.0 11.5 %collective-permute-start.20 = (bf16[256,256]{1,0:T(8,128)(2,1)S(1)}, bf16[256,256]{1,0:T(8,128)(2,1)S(1)}, u32[]{:S(2)}, u32[]{:S(2)}) collective-permute-start(bf16[256,256]{1,0:T(8,128)(2,1)S(1)} %add_convert_fusion.2.refs_0_), channel_id=1, source_target_pairs={{0,8},{1,9},{2,10},{3,11},{4,12},{5,13},{6,14},{7,15},{8,0},{9,1},... | collective-permute-start | bytes 393224 | tf_op jit(solution)/shard_map/ppermute | solution.py:100
  69.5 7.3 %collective-permute-start.22 = (bf16[256,256]{1,0:T(8,128)(2,1)S(1)}, bf16[256,256]{1,0:T(8,128)(2,1)S(1)}, u32[]{:S(2)}, u32[]{:S(2)}) collective-permute-start(bf16[256,256]{1,0:T(8,128)(2,1)S(1)} %add_convert_fusion.2.refs_0_), channel_id=1, source_target_pairs={{0,12},{1,13},{2,14},{3,15},{4,8},{5,9},{6,10},{7,11},{8,4},{9,5},... | collective-permute-start | bytes 393224 | tf_op jit(solution)/shard_map/ppermute | solution.py:100
  69.7 7.1 %collective-permute-start.19 = (bf16[256,256]{1,0:T(8,128)(2,1)S(1)}, bf16[256,256]{1,0:T(8,128)(2,1)S(1)}, u32[]{:S(2)}, u32[]{:S(2)}) collective-permute-start(bf16[256,256]{1,0:T(8,128)(2,1)S(1)} %collective-permute-done.17.refs_1_), channel_id=1, source_target_pairs={{0,4},{1,5},{2,6},{3,7},{4,0},{5,1},{6,2},{7,3},{8,12},{9,13},{10,... | collective-permute-start | bytes 393224 | tf_op jit(solution)/shard_map/ppermute | solution.py:100
  70.5 9.1 %collective-permute-start.21 = (bf16[256,256]{1,0:T(8,128)(2,1)S(1)}, bf16[256,256]{1,0:T(8,128)(2,1)S(1)}, u32[]{:S(2)}, u32[]{:S(2)}) collective-permute-start(bf16[256,256]{1,0:T(8,128)(2,1)S(1)} %collective-permute-done.17.refs_1_), channel_id=1, source_target_pairs={{0,8},{1,9},{2,10},{3,11},{4,12},{5,13},{6,14},{7,15},{8,0},{9,1},... | collective-permute-start | bytes 393224 | tf_op jit(solution)/shard_map/ppermute | solution.py:100
  74.2 7.2 %collective-permute-start.23 = (bf16[256,256]{1,0:T(8,128)(2,1)S(1)}, bf16[256,256]{1,0:T(8,128)(2,1)S(1)}, u32[]{:S(2)}, u32[]{:S(2)}) collective-permute-start(bf16[256,256]{1,0:T(8,128)(2,1)S(1)} %collective-permute-done.17.refs_1_), channel_id=1, source_target_pairs={{0,12},{1,13},{2,14},{3,15},{4,8},{5,9},{6,10},{7,11},{8,4},{9,5},... | collective-permute-start | bytes 393224 | tf_op jit(solution)/shard_map/ppermute | solution.py:100
  85.7 1.7 %collective-permute-start.24 = (bf16[2,256,256]{2,1,0:T(8,128)(2,1)}, bf16[2,256,256]{2,1,0:T(8,128)(2,1)S(1)}, u32[]{:S(2)}, u32[]{:S(2)}) collective-permute-start(bf16[2,256,256]{2,1,0:T(8,128)(2,1)} %get-tuple-element.29), channel_id=1, source_target_pairs={{0,1},{1,0},{2,3},{3,2},{4,5},{5,4},{6,7},{7,6},{8,9},{9,8},{10,11... | collective-permute-start | bytes 786440 | tf_op jit(solution)/shard_map/ppermute | solution.py:100
  92.1 16.6 %collective-permute-start.29 = (bf16[256,256]{1,0:T(8,128)(2,1)}, bf16[256,256]{1,0:T(8,128)(2,1)S(1)}, u32[]{:S(2)}, u32[]{:S(2)}) collective-permute-start(bf16[256,256]{1,0:T(8,128)(2,1)} %get-tuple-element.35), channel_id=1, source_target_pairs={{0,16},{16,0},{32,48},{48,32},{64,80},{80,64},{96,112},{112,96},{1... | collective-permute-start | bytes 393224 | tf_op jit(solution)/shard_map/ppermute | solution.py:100
  99.3 11.9 %collective-permute-start.30 = (bf16[256,256]{1,0:T(8,128)(2,1)}, bf16[256,256]{1,0:T(8,128)(2,1)S(1)}, u32[]{:S(2)}, u32[]{:S(2)}) collective-permute-start(bf16[256,256]{1,0:T(8,128)(2,1)} %get-tuple-element.36), channel_id=1, source_target_pairs={{0,48},{16,32},{32,16},{48,0},{64,112},{80,96},{96,80},{112,64},{1... | collective-permute-start | bytes 393224 | tf_op jit(solution)/shard_map/ppermute | solution.py:100
  104.6 7.5 %collective-permute-start.31 = (bf16[256,256]{1,0:T(8,128)(2,1)}, bf16[256,256]{1,0:T(8,128)(2,1)S(1)}, u32[]{:S(2)}, u32[]{:S(2)}) collective-permute-start(bf16[256,256]{1,0:T(8,128)(2,1)} %get-tuple-element.37), channel_id=1, source_target_pairs={{0,32},{16,48},{32,0},{48,16},{64,96},{80,112},{96,64},{112,80},{1... | collective-permute-start | bytes 393224 | tf_op jit(solution)/shard_map/ppermute | solution.py:100
  104.7 10.2 %collective-permute-start.26 = (bf16[256,256]{1,0:T(8,128)(2,1)}, bf16[256,256]{1,0:T(8,128)(2,1)S(1)}, u32[]{:S(2)}, u32[]{:S(2)}) collective-permute-start(bf16[256,256]{1,0:T(8,128)(2,1)} %get-tuple-element.31), channel_id=1, source_target_pairs={{0,16},{16,0},{32,48},{48,32},{64,80},{80,64},{96,112},{112,96},{1... | collective-permute-start | bytes 393224 | tf_op jit(solution)/shard_map/ppermute | solution.py:100
  105.5 11.4 %collective-permute-start.27 = (bf16[256,256]{1,0:T(8,128)(2,1)}, bf16[256,256]{1,0:T(8,128)(2,1)S(1)}, u32[]{:S(2)}, u32[]{:S(2)}) collective-permute-start(bf16[256,256]{1,0:T(8,128)(2,1)} %get-tuple-element.32), channel_id=1, source_target_pairs={{0,48},{16,32},{32,16},{48,0},{64,112},{80,96},{96,80},{112,64},{1... | collective-permute-start | bytes 393224 | tf_op jit(solution)/shard_map/ppermute | solution.py:100
  108.7 8.9 %collective-permute-start.28 = (bf16[256,256]{1,0:T(8,128)(2,1)}, bf16[256,256]{1,0:T(8,128)(2,1)S(1)}, u32[]{:S(2)}, u32[]{:S(2)}) collective-permute-start(bf16[256,256]{1,0:T(8,128)(2,1)} %get-tuple-element.33), channel_id=1, source_target_pairs={{0,32},{16,48},{32,0},{48,16},{64,96},{80,112},{96,64},{112,80},{1... | collective-permute-start | bytes 393224 | tf_op jit(solution)/shard_map/ppermute | solution.py:100
  113.1 6.3 %collective-permute-start.32 = (bf16[256,256]{1,0:T(8,128)(2,1)S(1)}, bf16[256,256]{1,0:T(8,128)(2,1)S(1)}, u32[]{:S(2)}, u32[]{:S(2)}) collective-permute-start(bf16[256,256]{1,0:T(8,128)(2,1)S(1)} %add_convert_fusion.1), channel_id=1, source_target_pairs={{0,64},{16,80},{32,96},{48,112},{64,0},{80,16},{96,32},{112,48},{1... | collective-permute-start | bytes 393224 | tf_op jit(solution)/shard_map/ppermute | solution.py:100
  (27 other events, 196.5 us)

commit v2 on v1

v2 whole, which is shorter than its diff:
```python
import functools

import jax
import jax.numpy as jnp
from jax import lax
from jax.experimental import pallas as pl
from jax.experimental.pallas import tpu as pltpu
from jax.sharding import PartitionSpec as P

PIECE = 256
F32 = jnp.float32
BF16 = jnp.bfloat16
REL = [(d, x) for d in range(4) for x in range(2)]
VMEM = pl.BlockSpec(memory_space=pltpu.VMEM)
SMEM = pl.BlockSpec(memory_space=pltpu.SMEM)


def dot(a, b):
    return lax.dot_general(a, b, (((1,), (0,)), ((), ())), preferred_element_type=F32)


def dot_t(a, b):
    return lax.dot_general(a, b, (((1,), (1,)), ((), ())), preferred_element_type=F32)


def total(parts):
    return functools.reduce(lambda a, b: a + b, parts)


def row_piece(info, rel):
    return (info[0] ^ rel[1]) * 4 + (info[1] ^ rel[0])


def half_piece(info, rel):
    return (info[2] ^ rel[0]) * 2 + (info[3] ^ rel[1])


def rows_of(piece):
    return pl.ds(pl.multiple_of(piece * PIECE, PIECE), PIECE)


def left_rows(info, piece):
    return rows_of((piece % 4) * 2 + info[6])


def masked(values, rank):
    columns = lax.broadcasted_iota(jnp.int32, values.shape, 1)
    return jnp.where(columns < rank, values, 0.0)


def coeff_kernel(info, *refs):
    x, right, out = refs[:8], refs[8], refs[9]
    for t in range(2):
        acc = total(dot(x[n][...], right[t, rows_of(row_piece(info, rel)), :]) for n, rel in enumerate(REL))
        out[t] = masked(acc, info[4 + t]).astype(BF16)


def diag_kernel(for_mate, info, *refs):
    x, dense, out = refs[:8], refs[8], refs[9]
    parity = info[6] ^ for_mate

    @pl.when(info[7] == 1)
    def _():
        for q in range(4):
            rows = rows_of(2 * q + parity)
            acc = total(dot_t(x[n][...], dense[rows, rows_of(row_piece(info, rel))]) for n, rel in enumerate(REL))
            out[q] = acc.astype(out.dtype)


def term_kernel(info, own, mate, left_own, left_mate, dense_own, dense_mate, *outs):
    core = info[6]
    for out, rel in zip(outs, REL):
        piece = half_piece(info, rel)
        tile = piece // 4
        rows = left_rows(info, piece)
        acc = dot_t(own[tile], left_own[tile, rows, :]) + dot_t(mate[tile], left_mate[tile, rows, :])

        @pl.when(info[7] == 0)
        def _():
            out[...] = acc.astype(BF16)

        @pl.when(jnp.logical_and(info[7] == 1, tile == core))
        def _():
            out[...] = (acc + dense_own[piece % 4].astype(F32)).astype(BF16)

        @pl.when(jnp.logical_and(info[7] == 1, tile != core))
        def _():
            out[...] = (acc + dense_mate[piece % 4].astype(F32)).astype(BF16)


def pack_kernel(info, *refs):
    y, out = refs[:8], refs[8]
    for n, rel in enumerate(REL):
        piece = half_piece(info, rel)

        @pl.when(jnp.logical_and(info[7] == 1, piece // 4 != info[6]))
        def _():
            out[piece % 4] = y[n][...]


def back_kernel(info, *refs):
    y, left_own, left_mate, own, mate = refs[:8], refs[8], refs[9], refs[10], refs[11]
    for half in range(2):
        tile = (info[2] // 2) ^ half
        for left, out in ((left_mate, mate), (left_own, own)):
            out[tile] = total(
                dot(y[n][...], left[tile, left_rows(info, half_piece(info, rel)), :])
                for n, rel in enumerate(REL)
                if rel[0] // 2 == half
            ).astype(out.dtype)


def diag_back_kernel(info, *refs):
    y, dense, out = refs[:8], refs[8], refs[9]
    for half in range(2):

        @pl.when(jnp.logical_and(info[7] == 1, (info[2] // 2) ^ half == info[6]))
        def _():
            for p in range(8):
                out[p] = total(
                    dot(y[n][...], dense[left_rows(info, half_piece(info, rel)), p * PIECE : (p + 1) * PIECE])
                    for n, rel in enumerate(REL)
                    if rel[0] // 2 == half
                )


def second_kernel(info, own, mate, right, dense_sum, y_mate, dense, *outs):
    coeff = [masked(own[t] + mate[t].astype(F32), info[4 + t]).astype(BF16) for t in range(2)]
    for out, rel in zip(outs, REL):
        piece = row_piece(info, rel)
        rows = rows_of(piece)
        acc = dot_t(coeff[0], right[0, rows, :]) + dot_t(coeff[1], right[1, rows, :])

        @pl.when(info[7] == 0)
        def _():
            out[...] = acc.astype(BF16)

        @pl.when(info[7] == 1)
        def _():
            rest = total(dot(y_mate[q], dense[rows_of(2 * q + 1 - info[6]), rows]) for q in range(4))
            out[...] = (acc + dense_sum[piece] + rest).astype(BF16)


def call(kernel, name, info, operands, outs, flops, moved):
    return pl.pallas_call(
        kernel,
        name=name,
        out_shape=outs,
        in_specs=[SMEM] + [VMEM] * len(operands),
        out_specs=[VMEM] * len(outs),
        compiler_params=pltpu.CompilerParams(vmem_limit_bytes=16 * 2**20),
        cost_estimate=pl.CostEstimate(flops=flops, bytes_accessed=moved, transcendentals=0),
    )(info, *operands)


def swap(x, axis, bits):
    size = lax.axis_size(axis)
    return lax.ppermute(x, axis, [(i, i ^ bits) for i in range(size)])


def gather(own, axis, ring, side):
    got = {(0, 0): own}
    got[(0, 1)] = swap(own, axis, side)
    got[(2, 0)] = swap(own, axis, 2 * ring)
    got[(1, 0)] = swap(own, axis, ring)
    got[(3, 0)] = swap(own, axis, 3 * ring)
    got[(1, 1)] = swap(got[(0, 1)], axis, ring)
    got[(3, 1)] = swap(got[(0, 1)], axis, 3 * ring)
    got[(2, 1)] = swap(got[(2, 0)], axis, side)
    return [got[rel] for rel in REL]


def add(*parts):
    return total(v.astype(F32) for v in parts).astype(BF16)


def scatter(pieces, axis, ring, side):
    piece = dict(zip(REL, pieces))
    far_1 = swap(piece[(1, 1)], axis, ring)
    far_3 = swap(piece[(3, 1)], axis, 3 * ring)
    far_2 = swap(piece[(2, 1)], axis, side)
    near_1 = swap(piece[(1, 0)], axis, ring)
    near_3 = swap(piece[(3, 0)], axis, 3 * ring)
    near_2 = swap(add(piece[(2, 0)], far_2), axis, 2 * ring)
    crossed = swap(add(piece[(0, 1)], far_1, far_3), axis, side)
    return add(piece[(0, 0)], near_1, near_3, near_2, crossed)


def body(signal, left_factors, right_factors, dense_diagonal, buckets):
    trow = lax.axis_index("trow")
    tcol = lax.axis_index("tcol")
    tile_rows = trow * 2 + jnp.arange(2, dtype=jnp.int32)
    ranks = jnp.where(tile_rows == tcol, 0, jnp.left_shift(jnp.int32(16), buckets[:, 0]))
    place = jnp.stack([trow // 4, trow % 4, tcol // 4, (tcol // 2) % 2])
    owner = (trow == tcol // 2).astype(jnp.int32)
    info = jnp.concatenate([place, ranks, jnp.stack([tcol % 2, owner])]).astype(jnp.int32)

    right = right_factors[:, 0]
    left = left_factors[:, 0]
    dense = dense_diagonal[0]
    left_mate = swap(left, "tcol", 1)
    owners = [((b // 2) * 16 + b, (b // 2) * 16 + (b ^ 1)) for b in range(16)]

    count = signal.shape[0]
    unit = 2 * count * PIECE * PIECE
    size = count * PIECE * 2
    piece = jax.ShapeDtypeStruct((count, PIECE), BF16)
    pair = jax.ShapeDtypeStruct((2, count, PIECE), BF16)
    pair_wide = jax.ShapeDtypeStruct((2, count, PIECE), F32)
    four = jax.ShapeDtypeStruct((4, count, PIECE), BF16)
    eight_wide = jax.ShapeDtypeStruct((8, count, PIECE), F32)

    x = gather(signal, "trow", 1, 4)
    (coeff,) = call(coeff_kernel, "coeff", info, [*x, right], [pair], 16 * unit, 10 * size + 2**21)
    coeff_mate = swap(coeff, "tcol", 1)
    (dense_sent,) = call(functools.partial(diag_kernel, 1), "diag_mate", info, [*x, dense], [four], 32 * unit, 12 * size + 2**23)
    dense_mate = lax.ppermute(dense_sent, ("trow", "tcol"), owners)
    (dense_own,) = call(functools.partial(diag_kernel, 0), "diag_own", info, [*x, dense], [four], 32 * unit, 12 * size + 2**23)
    terms = call(
        term_kernel,
        "term",
        info,
        [coeff, coeff_mate, left, left_mate, dense_own, dense_mate],
        [piece] * 8,
        16 * unit,
        20 * size + 2**21,
    )
    first = scatter(terms, "tcol", 4, 2)
    y = gather(first, "tcol", 4, 2)
    (y_sent,) = call(pack_kernel, "pack", info, y, [four], 0, 12 * size)
    y_mate = lax.ppermute(y_sent, ("trow", "tcol"), owners)
    own, mate = call(back_kernel, "back", info, [*y, left, left_mate], [pair_wide, pair], 16 * unit, 14 * size + 2**21)
    mate = swap(mate, "tcol", 1)
    (dense_sum,) = call(diag_back_kernel, "diag_back", info, [*y, dense], [eight_wide], 32 * unit, 24 * size + 2**22)
    terms = call(
        second_kernel,
        "second",
        info,
        [own, mate, right, dense_sum, y_mate, dense],
        [piece] * 8,
        48 * unit,
        30 * size + 3 * 2**20,
    )
    second = scatter(terms, "trow", 1, 4)
    return (first, second)


def solution(mesh):
    in_specs = (
        P(None, ("tcol", "trow")),
        P("trow", "tcol", None, None),
        P("trow", "tcol", None, None),
        P("tcol", None, None),
        P("trow", "tcol"),
    )
    out_specs = (P(None, ("trow", "tcol")), P(None, ("tcol", "trow")))
    return jax.shard_map(body, mesh=mesh, in_specs=in_specs, out_specs=out_specs, check_vma=False)
```

time: 123 us -> 104 us (0.85)
  starting transfers between devices: 57.4 us -> 44.4 us
  local copies, waits for them, and re-layouts: 8.93 us -> 5.97 us
  waiting for transfers between devices: 34.1 us -> 31.9 us
    ppermute x31, starting transfers between devices: 54.3 us -> 40.4 us  [swap(): return lax.ppermute(x, axis, [(i, i ^ bits) for i in range(size)])]
    dynamic_slice x2 -> x0, local copies, waits for them, and re-layouts: 5.12 us -> none  [the longest x1 2.8 us: body(): lax.dynamic_index_in_dim(left, 1 - core, 2, keepdims=False)]
    unnamed x52 -> x14, local copies, waits for them, and re-layouts: 3.17 us -> 5.89 us
    ppermute x31, waiting for transfers between devices: 34.1 us -> 31.9 us  [swap(): return lax.ppermute(x, axis, [(i, i ^ bits) for i in range(size)])]
    convert_element_type x4 -> x6, other arithmetic: 2.8 us -> 1 us  [add(): return total((v.astype(F32) for v in parts)).astype(BF16)]
    pallas_call x5 -> x8, Pallas kernels: 17 us -> 17.4 us  [call(): pl.pallas_call(kernel, name=name, out_shape=outs, in_specs=[SMEM] + [VMEM...]
  transfers between devices with their start and end apart: 33 -> 33, of which waited for: 18 -> 16; matrix products, arithmetic and copies ran while one was open for 3% -> 1% of each run, Pallas kernels for 5% -> 8%
where the time goes in v2:
time: 104 us; the launch traced here: 102 us
  starting transfers between devices  44.4 us (43%)
  waiting for transfers between devices  31.9 us (31%)
  Pallas kernels  17.4 us (17%)
  local copies, waits for them, and re-layouts  5.97 us (6%)
  other arithmetic  1.66 us (2%)
    ppermute x31, starting transfers between devices, swap(): return lax.ppermute(x, axis, [(i, i ^ bits) for i in range(size)])  40.4 us
    ppermute x31, waiting for transfers between devices, swap(): return lax.ppermute(x, axis, [(i, i ^ bits) for i in range(size)])  31.9 us
    pallas_call x8, Pallas kernels, call(): pl.pallas_call(kernel, name=name, out_shape=outs, in_specs=[SMEM] + [VMEM...  17.4 us
    unnamed x14, local copies, waits for them, and re-layouts  5.89 us
  transfers between devices with their start and end apart: 33, of which 16 were waited for; matrix products, arithmetic and copies ran while one was open for 1% of the time, Pallas kernels for 8%

profile of v2, /device:TPU:0, one launch (start us, length us, event | category | flops | bytes accessed | tf_op | source)
XLA Modules:
  0.0 102.2 jit_solution(9677248696686524444)
XLA Ops:
  0.7 1.7 %collective-permute-start = (bf16[256,256]{1,0:T(8,128)(2,1)}, bf16[256,256]{1,0:T(8,128)(2,1)S(1)}, u32[]{:S(2)}, u32[]{:S(2)}) collective-permute-start(bf16[256,256]{1,0:T(8,128)(2,1)} %refs_0_.5), channel_id=1, source_target_pairs={{0,64},{16,80},{32,96},{48,112},{64,0},{80,16},{96,32},{112,48},{1... | collective-permute-start | bytes 393224 | tf_op jit(solution)/shard_map/ppermute | solution.py:158
  2.4 4.0 %collective-permute-start.5 = (bf16[256,256]{1,0:T(8,128)(2,1)}, bf16[256,256]{1,0:T(8,128)(2,1)S(1)}, u32[]{:S(2)}, u32[]{:S(2)}) collective-permute-start(bf16[256,256]{1,0:T(8,128)(2,1)} %refs_0_.5), channel_id=1, source_target_pairs={{0,48},{16,32},{32,16},{48,0},{64,112},{80,96},{96,80},{112,64},{1... | collective-permute-start | bytes 393224 | tf_op jit(solution)/shard_map/ppermute | solution.py:158
  7.3 3.7 %collective-permute-start.6 = (bf16[256,256]{1,0:T(8,128)(2,1)S(1)}, bf16[256,256]{1,0:T(8,128)(2,1)S(1)}, u32[]{:S(2)}, u32[]{:S(2)}) collective-permute-start(bf16[256,256]{1,0:T(8,128)(2,1)S(1)} %collective-permute-done.refs_1_), channel_id=1, source_target_pairs={{0,48},{16,32},{32,16},{48,0},{64,112},{80,96},{96,80},{112,64},{1... | collective-permute-start | bytes 393224 | tf_op jit(solution)/shard_map/ppermute | solution.py:158
  11.0 2.0 %collective-permute-done.5.refs_6_ = bf16[256,256]{1,0:T(8,128)(2,1)S(1)} collective-permute-done((bf16[256,256]{1,0:T(8,128)(2,1)}, bf16[256,256]{1,0:T(8,128)(2,1)S(1)}, u32[]{:S(2)}, u32[]{:S(2)}) %collective-permute-start.5) | collective-permute-done | bytes 131104 | tf_op jit(solution)/shard_map/ppermute | solution.py:158
  15.8 3.7 %collective-permute-done.4.refs_5_ = bf16[256,256]{1,0:T(8,128)(2,1)S(1)} collective-permute-done((bf16[256,256]{1,0:T(8,128)(2,1)S(1)}, bf16[256,256]{1,0:T(8,128)(2,1)S(1)}, u32[]{:S(2)}, u32[]{:S(2)}) %collective-permute-start.4) | collective-permute-done | bytes 131104 | tf_op jit(solution)/shard_map/ppermute | solution.py:158
  19.5 3.4 %copy-done = bf16[1,2048,2048]{2,1,0:T(8,128)(2,1)S(1)} copy-done((bf16[1,2048,2048]{2,1,0:T(8,128)(2,1)S(1)}, bf16[1,2048,2048]{2,1,0:T(8,128)(2,1)}, u32[]{:S(2)}) %copy-start) | copy-done | bytes 8388632
  23.8 1.8 %diag_mate.1 = bf16[4,256,256]{2,1,0:T(8,128)(2,1)S(1)} custom-call(s32[8]{0:T(128)S(1)} %concatenate.3.info, bf16[256,256]{1,0:T(8,128)(2,1)S(1)} %copy-done.6, bf16[256,256]{1,0:T(8,128)(2,1)S(1)} %collective-permute-done.refs_1_, bf16[256,256]{1,0:T(8,128)(2,1)S(1)} %collective-permute-done.1.refs_2_, ...), custom_call_target="tpu_custom_call" | custom-call | flops 1073741824 | bytes 9961472 | tf_op jit(solution)/shard_map/diag_mate/pallas_call | solution.py:145
  25.6 2.1 %collective-permute-start.9 = (bf16[4,256,256]{2,1,0:T(8,128)(2,1)S(1)}, bf16[4,256,256]{2,1,0:T(8,128)(2,1)S(1)}, u32[]{:S(2)}, u32[]{:S(2)}) collective-permute-start(bf16[4,256,256]{2,1,0:T(8,128)(2,1)S(1)} %diag_mate.1), channel_id=1, source_target_pairs={{0,1},{1,0},{18,19},{19,18},{36,37},{37,36},{54,55},{55,54},{72,73... | collective-permute-start | bytes 1572872 | tf_op jit(solution)/shard_map/ppermute | solution.py:217
  27.7 1.6 %copy-done.3 = bf16[2,1,2048,256]{3,2,1,0:T(8,128)(2,1)S(1)} copy-done((bf16[2,1,2048,256]{3,2,1,0:T(8,128)(2,1)S(1)}, bf16[2,1,2048,256]{3,2,1,0:T(8,128)(2,1)}, u32[]{:S(2)}) %copy-start.3) | copy-done | bytes 2097176
  31.1 1.8 %diag_own.1.dense_own = bf16[4,256,256]{2,1,0:T(8,128)(2,1)S(1)} custom-call(s32[8]{0:T(128)S(1)} %concatenate.3.info, bf16[256,256]{1,0:T(8,128)(2,1)S(1)} %copy-done.6, bf16[256,256]{1,0:T(8,128)(2,1)S(1)} %collective-permute-done.refs_1_, bf16[256,256]{1,0:T(8,128)(2,1)S(1)} %collective-permute-done.1.refs_2_, ...), custom_call_target="tpu_custom_call" | custom-call | flops 1073741824 | bytes 9961472 | tf_op jit(solution)/shard_map/diag_own/pallas_call | solution.py:145
  33.0 3.4 %term.1 = (bf16[256,256]{1,0:T(8,128)(2,1)S(1)}, bf16[256,256]{1,0:T(8,128)(2,1)S(1)}, bf16[256,256]{1,0:T(8,128)(2,1)S(1)}, bf16[256,256]{1,0:T(8,128)(2,1)S(1)...) custom-call(s32[8]{0:T(128)S(1)} %concatenate.3.info, ...), custom_call_target="tpu_custom_call" | custom-call | flops 536870912 | bytes 4718592 | tf_op jit(solution)/shard_map/term/pallas_call | solution.py:145
  36.5 1.4 %collective-permute-start.10 = (bf16[256,256]{1,0:T(8,128)(2,1)S(1)}, bf16[256,256]{1,0:T(8,128)(2,1)S(1)}, u32[]{:S(2)}, u32[]{:S(2)}) collective-permute-start(bf16[256,256]{1,0:T(8,128)(2,1)S(1)} %get-tuple-element.21), channel_id=1, source_target_pairs={{0,4},{1,5},{2,6},{3,7},{4,0},{5,1},{6,2},{7,3},{8,12},{9,13},{10,... | collective-permute-start | bytes 393224 | tf_op jit(solution)/shard_map/ppermute | solution.py:158
  38.0 2.2 %collective-permute-start.11 = (bf16[256,256]{1,0:T(8,128)(2,1)S(1)}, bf16[256,256]{1,0:T(8,128)(2,1)S(1)}, u32[]{:S(2)}, u32[]{:S(2)}) collective-permute-start(bf16[256,256]{1,0:T(8,128)(2,1)S(1)} %get-tuple-element.22), channel_id=1, source_target_pairs={{0,12},{1,13},{2,14},{3,15},{4,8},{5,9},{6,10},{7,11},{8,4},{9,5},... | collective-permute-start | bytes 393224 | tf_op jit(solution)/shard_map/ppermute | solution.py:158
  41.4 2.0 %collective-permute-done.12 = bf16[256,256]{1,0:T(8,128)(2,1)S(1)} collective-permute-done((bf16[256,256]{1,0:T(8,128)(2,1)S(1)}, bf16[256,256]{1,0:T(8,128)(2,1)S(1)}, u32[]{:S(2)}, u32[]{:S(2)}) %collective-permute-start.12) | collective-permute-done | bytes 131104 | tf_op jit(solution)/shard_map/ppermute | solution.py:158
  45.7 2.6 %collective-permute-done.15 = bf16[256,256]{1,0:T(8,128)(2,1)S(1)} collective-permute-done((bf16[256,256]{1,0:T(8,128)(2,1)S(1)}, bf16[256,256]{1,0:T(8,128)(2,1)S(1)}, u32[]{:S(2)}, u32[]{:S(2)}) %collective-permute-start.15) | collective-permute-done | bytes 131104 | tf_op jit(solution)/shard_map/ppermute | solution.py:158
  48.3 3.8 %collective-permute-start.16 = (bf16[256,256]{1,0:T(8,128)(2,1)S(1)}, bf16[256,256]{1,0:T(8,128)(2,1)S(1)}, u32[]{:S(2)}, u32[]{:S(2)}) collective-permute-start(bf16[256,256]{1,0:T(8,128)(2,1)S(1)} %add_convert_fusion.4), channel_id=1, source_target_pairs={{0,2},{1,3},{2,0},{3,1},{4,6},{5,7},{6,4},{7,5},{8,10},{9,11},{10,... | collective-permute-start | bytes 393224 | tf_op jit(solution)/shard_map/ppermute | solution.py:158
  52.2 2.9 %collective-permute-done.16 = bf16[256,256]{1,0:T(8,128)(2,1)S(1)} collective-permute-done((bf16[256,256]{1,0:T(8,128)(2,1)S(1)}, bf16[256,256]{1,0:T(8,128)(2,1)S(1)}, u32[]{:S(2)}, u32[]{:S(2)}) %collective-permute-start.16) | collective-permute-done | bytes 131104 | tf_op jit(solution)/shard_map/ppermute | solution.py:158
  55.2 3.0 %collective-permute-start.20 = (bf16[256,256]{1,0:T(8,128)(2,1)S(1)}, bf16[256,256]{1,0:T(8,128)(2,1)S(1)}, u32[]{:S(2)}, u32[]{:S(2)}) collective-permute-start(bf16[256,256]{1,0:T(8,128)(2,1)S(1)} %add_convert_fusion.3.refs_0_), channel_id=1, source_target_pairs={{0,8},{1,9},{2,10},{3,11},{4,12},{5,13},{6,14},{7,15},{8,0},{9,1},... | collective-permute-start | bytes 393224 | tf_op jit(solution)/shard_map/ppermute | solution.py:158
  58.9 3.3 %collective-permute-start.22 = (bf16[256,256]{1,0:T(8,128)(2,1)S(1)}, bf16[256,256]{1,0:T(8,128)(2,1)S(1)}, u32[]{:S(2)}, u32[]{:S(2)}) collective-permute-start(bf16[256,256]{1,0:T(8,128)(2,1)S(1)} %add_convert_fusion.3.refs_0_), channel_id=1, source_target_pairs={{0,12},{1,13},{2,14},{3,15},{4,8},{5,9},{6,10},{7,11},{8,4},{9,5},... | collective-permute-start | bytes 393224 | tf_op jit(solution)/shard_map/ppermute | solution.py:158
  62.7 2.6 %collective-permute-start.21 = (bf16[256,256]{1,0:T(8,128)(2,1)S(1)}, bf16[256,256]{1,0:T(8,128)(2,1)S(1)}, u32[]{:S(2)}, u32[]{:S(2)}) collective-permute-start(bf16[256,256]{1,0:T(8,128)(2,1)S(1)} %collective-permute-done.20.refs_4_), channel_id=1, source_target_pairs={{0,2},{1,3},{2,0},{3,1},{4,6},{5,7},{6,4},{7,5},{8,10},{9,11},{10,... | collective-permute-start | bytes 393224 | tf_op jit(solution)/shard_map/ppermute | solution.py:158
  65.4 1.7 %collective-permute-start.23 = (bf16[256,256]{1,0:T(8,128)(2,1)S(1)}, bf16[256,256]{1,0:T(8,128)(2,1)S(1)}, u32[]{:S(2)}, u32[]{:S(2)}) collective-permute-start(bf16[256,256]{1,0:T(8,128)(2,1)S(1)} %collective-permute-done.17.refs_1_), channel_id=1, source_target_pairs={{0,12},{1,13},{2,14},{3,15},{4,8},{5,9},{6,10},{7,11},{8,4},{9,5},... | collective-permute-start | bytes 393224 | tf_op jit(solution)/shard_map/ppermute | solution.py:158
  67.2 2.0 %collective-permute-done.21.refs_5_ = bf16[256,256]{1,0:T(8,128)(2,1)S(1)} collective-permute-done((bf16[256,256]{1,0:T(8,128)(2,1)S(1)}, bf16[256,256]{1,0:T(8,128)(2,1)S(1)}, u32[]{:S(2)}, u32[]{:S(2)}) %collective-permute-start.21) | collective-permute-done | bytes 131104 | tf_op jit(solution)/shard_map/ppermute | solution.py:158
  69.2 2.3 %collective-permute-done.23.refs_7_ = bf16[256,256]{1,0:T(8,128)(2,1)S(1)} collective-permute-done((bf16[256,256]{1,0:T(8,128)(2,1)S(1)}, bf16[256,256]{1,0:T(8,128)(2,1)S(1)}, u32[]{:S(2)}, u32[]{:S(2)}) %collective-permute-start.23) | collective-permute-done | bytes 131104 | tf_op jit(solution)/shard_map/ppermute | solution.py:158
  72.7 1.9 %collective-permute-start.25 = (bf16[4,256,256]{2,1,0:T(8,128)(2,1)S(1)}, bf16[4,256,256]{2,1,0:T(8,128)(2,1)S(1)}, u32[]{:S(2)}, u32[]{:S(2)}) collective-permute-start(bf16[4,256,256]{2,1,0:T(8,128)(2,1)S(1)} %pack.1), channel_id=1, source_target_pairs={{0,1},{1,0},{18,19},{19,18},{36,37},{37,36},{54,55},{55,54},{72,73... | collective-permute-start | bytes 1572872 | tf_op jit(solution)/shard_map/ppermute | solution.py:231
  76.7 1.8 %diag_back.1.dense_sum = f32[8,256,256]{2,1,0:T(8,128)S(1)} custom-call(s32[8]{0:T(128)S(1)} %concatenate.3.info, bf16[256,256]{1,0:T(8,128)(2,1)S(1)} %add_convert_fusion.3.refs_0_, bf16[256,256]{1,0:T(8,128)(2,1)S(1)} %collective-permute-done.17.refs_1_, bf16[256,256]{1,0:T(8,128)(2,1)S(1)} %collective-permute-done.18.refs_2_, ...), custom_call_target="tpu_custom_call" | custom-call | flops 1073741824 | bytes 7340032 | tf_op jit(solution)/shard_map/diag_back/pallas_call | solution.py:145
  78.6 5.3 %second.1 = (bf16[256,256]{1,0:T(8,128)(2,1)S(1)}, bf16[256,256]{1,0:T(8,128)(2,1)S(1)}, bf16[256,256]{1,0:T(8,128)(2,1)S(1)}, bf16[256,256]{1,0:T(8,128)(2,1)S(...) custom-call(s32[8]{0:T(128)S(1)} %concatenate.3.info, ...), custom_call_target="tpu_custom_call" | custom-call | flops 1610612736 | bytes 7077888 | tf_op jit(solution)/shard_map/second/pallas_call | solution.py:145
  84.0 1.5 %collective-permute-start.27 = (bf16[256,256]{1,0:T(8,128)(2,1)S(1)}, bf16[256,256]{1,0:T(8,128)(2,1)S(1)}, u32[]{:S(2)}, u32[]{:S(2)}) collective-permute-start(bf16[256,256]{1,0:T(8,128)(2,1)S(1)} %get-tuple-element.32), channel_id=1, source_target_pairs={{0,48},{16,32},{32,16},{48,0},{64,112},{80,96},{96,80},{112,64},{1... | collective-permute-start | bytes 393224 | tf_op jit(solution)/shard_map/ppermute | solution.py:158
  86.0 2.6 %collective-permute-start.31 = (bf16[256,256]{1,0:T(8,128)(2,1)S(1)}, bf16[256,256]{1,0:T(8,128)(2,1)S(1)}, u32[]{:S(2)}, u32[]{:S(2)}) collective-permute-start(bf16[256,256]{1,0:T(8,128)(2,1)S(1)} %get-tuple-element.37), channel_id=1, source_target_pairs={{0,48},{16,32},{32,16},{48,0},{64,112},{80,96},{96,80},{112,64},{1... | collective-permute-start | bytes 393224 | tf_op jit(solution)/shard_map/ppermute | solution.py:158
  89.8 3.3 %collective-permute-done.30 = bf16[256,256]{1,0:T(8,128)(2,1)S(1)} collective-permute-done((bf16[256,256]{1,0:T(8,128)(2,1)S(1)}, bf16[256,256]{1,0:T(8,128)(2,1)S(1)}, u32[]{:S(2)}, u32[]{:S(2)}) %collective-permute-start.30) | collective-permute-done | bytes 131104 | tf_op jit(solution)/shard_map/ppermute | solution.py:158
  93.2 3.2 %collective-permute-done.31 = bf16[256,256]{1,0:T(8,128)(2,1)S(1)} collective-permute-done((bf16[256,256]{1,0:T(8,128)(2,1)S(1)}, bf16[256,256]{1,0:T(8,128)(2,1)S(1)}, u32[]{:S(2)}, u32[]{:S(2)}) %collective-permute-start.31) | collective-permute-done | bytes 131104 | tf_op jit(solution)/shard_map/ppermute | solution.py:158
  96.4 1.6 %collective-permute-start.32 = (bf16[256,256]{1,0:T(8,128)(2,1)S(1)}, bf16[256,256]{1,0:T(8,128)(2,1)S(1)}, u32[]{:S(2)}, u32[]{:S(2)}) collective-permute-start(bf16[256,256]{1,0:T(8,128)(2,1)S(1)} %add_convert_fusion.1), channel_id=1, source_target_pairs={{0,64},{16,80},{32,96},{48,112},{64,0},{80,16},{96,32},{112,48},{1... | collective-permute-start | bytes 393224 | tf_op jit(solution)/shard_map/ppermute | solution.py:158
  98.1 3.4 %collective-permute-done.32 = bf16[256,256]{1,0:T(8,128)(2,1)S(1)} collective-permute-done((bf16[256,256]{1,0:T(8,128)(2,1)S(1)}, bf16[256,256]{1,0:T(8,128)(2,1)S(1)}, u32[]{:S(2)}, u32[]{:S(2)}) %collective-permute-start.32) | collective-permute-done | bytes 131104 | tf_op jit(solution)/shard_map/ppermute | solution.py:158
  (64 shorter events, 17.5 us)
Async XLA Ops:
  0.6 32.4 %collective-permute-start.8 = (bf16[2,2048,256]{2,1,0:T(8,128)(2,1)}, bf16[2,2048,256]{2,1,0:T(8,128)(2,1)S(1)}, u32[]{:S(2)}, u32[]{:S(2)}) collective-permute-start(bf16[2,2048,256]{2,1,0:T(8,128)(2,1)} %bitcast.15), channel_id=1, source_target_pairs={{0,1},{1,0},{2,3},{3,2},{4,5},{5,4},{6,7},{7,6},{8,9},{9,8},{10,11... | collective-permute-start | bytes 6291464 | tf_op jit(solution)/shard_map/ppermute | solution.py:158
  0.7 6.6 %collective-permute-start = (bf16[256,256]{1,0:T(8,128)(2,1)}, bf16[256,256]{1,0:T(8,128)(2,1)S(1)}, u32[]{:S(2)}, u32[]{:S(2)}) collective-permute-start(bf16[256,256]{1,0:T(8,128)(2,1)} %refs_0_.5), channel_id=1, source_target_pairs={{0,64},{16,80},{32,96},{48,112},{64,0},{80,16},{96,32},{112,48},{1... | collective-permute-start | bytes 393224 | tf_op jit(solution)/shard_map/ppermute | solution.py:158
  2.4 10.6 %collective-permute-start.5 = (bf16[256,256]{1,0:T(8,128)(2,1)}, bf16[256,256]{1,0:T(8,128)(2,1)S(1)}, u32[]{:S(2)}, u32[]{:S(2)}) collective-permute-start(bf16[256,256]{1,0:T(8,128)(2,1)} %refs_0_.5), channel_id=1, source_target_pairs={{0,48},{16,32},{32,16},{48,0},{64,112},{80,96},{96,80},{112,64},{1... | collective-permute-start | bytes 393224 | tf_op jit(solution)/shard_map/ppermute | solution.py:158
  6.4 8.1 %collective-permute-start.3 = (bf16[256,256]{1,0:T(8,128)(2,1)}, bf16[256,256]{1,0:T(8,128)(2,1)S(1)}, u32[]{:S(2)}, u32[]{:S(2)}) collective-permute-start(bf16[256,256]{1,0:T(8,128)(2,1)} %refs_0_.5), channel_id=1, source_target_pairs={{0,32},{16,48},{32,0},{48,16},{64,96},{80,112},{96,64},{112,80},{1... | collective-permute-start | bytes 393224 | tf_op jit(solution)/shard_map/ppermute | solution.py:158
  6.4 9.4 %collective-permute-start.1 = (bf16[256,256]{1,0:T(8,128)(2,1)}, bf16[256,256]{1,0:T(8,128)(2,1)S(1)}, u32[]{:S(2)}, u32[]{:S(2)}) collective-permute-start(bf16[256,256]{1,0:T(8,128)(2,1)} %refs_0_.5), channel_id=1, source_target_pairs={{0,16},{16,0},{32,48},{48,32},{64,80},{80,64},{96,112},{112,96},{1... | collective-permute-start | bytes 393224 | tf_op jit(solution)/shard_map/ppermute | solution.py:158
  7.3 12.2 %collective-permute-start.6 = (bf16[256,256]{1,0:T(8,128)(2,1)S(1)}, bf16[256,256]{1,0:T(8,128)(2,1)S(1)}, u32[]{:S(2)}, u32[]{:S(2)}) collective-permute-start(bf16[256,256]{1,0:T(8,128)(2,1)S(1)} %collective-permute-done.refs_1_), channel_id=1, source_target_pairs={{0,48},{16,32},{32,16},{48,0},{64,112},{80,96},{96,80},{112,64},{1... | collective-permute-start | bytes 393224 | tf_op jit(solution)/shard_map/ppermute | solution.py:158
  13.0 6.5 %collective-permute-start.2 = (bf16[256,256]{1,0:T(8,128)(2,1)S(1)}, bf16[256,256]{1,0:T(8,128)(2,1)S(1)}, u32[]{:S(2)}, u32[]{:S(2)}) collective-permute-start(bf16[256,256]{1,0:T(8,128)(2,1)S(1)} %collective-permute-done.refs_1_), channel_id=1, source_target_pairs={{0,16},{16,0},{32,48},{48,32},{64,80},{80,64},{96,112},{112,96},{1... | collective-permute-start | bytes 393224 | tf_op jit(solution)/shard_map/ppermute | solution.py:158
  14.5 5.0 %collective-permute-start.4 = (bf16[256,256]{1,0:T(8,128)(2,1)S(1)}, bf16[256,256]{1,0:T(8,128)(2,1)S(1)}, u32[]{:S(2)}, u32[]{:S(2)}) collective-permute-start(bf16[256,256]{1,0:T(8,128)(2,1)S(1)} %collective-permute-done.3.refs_4_), channel_id=1, source_target_pairs={{0,64},{16,80},{32,96},{48,112},{64,0},{80,16},{96,32},{112,48},{1... | collective-permute-start | bytes 393224 | tf_op jit(solution)/shard_map/ppermute | solution.py:158
  25.6 7.4 %collective-permute-start.9 = (bf16[4,256,256]{2,1,0:T(8,128)(2,1)S(1)}, bf16[4,256,256]{2,1,0:T(8,128)(2,1)S(1)}, u32[]{:S(2)}, u32[]{:S(2)}) collective-permute-start(bf16[4,256,256]{2,1,0:T(8,128)(2,1)S(1)} %diag_mate.1), channel_id=1, source_target_pairs={{0,1},{1,0},{18,19},{19,18},{36,37},{37,36},{54,55},{55,54},{72,73... | collective-permute-start | bytes 1572872 | tf_op jit(solution)/shard_map/ppermute | solution.py:217
  36.4 7.0 %collective-permute-start.12 = (bf16[256,256]{1,0:T(8,128)(2,1)S(1)}, bf16[256,256]{1,0:T(8,128)(2,1)S(1)}, u32[]{:S(2)}, u32[]{:S(2)}) collective-permute-start(bf16[256,256]{1,0:T(8,128)(2,1)S(1)} %get-tuple-element.24), channel_id=1, source_target_pairs={{0,2},{1,3},{2,0},{3,1},{4,6},{5,7},{6,4},{7,5},{8,10},{9,11},{10,... | collective-permute-start | bytes 393224 | tf_op jit(solution)/shard_map/ppermute | solution.py:158
  36.5 15.6 %collective-permute-start.10 = (bf16[256,256]{1,0:T(8,128)(2,1)S(1)}, bf16[256,256]{1,0:T(8,128)(2,1)S(1)}, u32[]{:S(2)}, u32[]{:S(2)}) collective-permute-start(bf16[256,256]{1,0:T(8,128)(2,1)S(1)} %get-tuple-element.21), channel_id=1, source_target_pairs={{0,4},{1,5},{2,6},{3,7},{4,0},{5,1},{6,2},{7,3},{8,12},{9,13},{10,... | collective-permute-start | bytes 393224 | tf_op jit(solution)/shard_map/ppermute | solution.py:158
  38.0 14.2 %collective-permute-start.11 = (bf16[256,256]{1,0:T(8,128)(2,1)S(1)}, bf16[256,256]{1,0:T(8,128)(2,1)S(1)}, u32[]{:S(2)}, u32[]{:S(2)}) collective-permute-start(bf16[256,256]{1,0:T(8,128)(2,1)S(1)} %get-tuple-element.22), channel_id=1, source_target_pairs={{0,12},{1,13},{2,14},{3,15},{4,8},{5,9},{6,10},{7,11},{8,4},{9,5},... | collective-permute-start | bytes 393224 | tf_op jit(solution)/shard_map/ppermute | solution.py:158
  40.1 5.5 %collective-permute-start.14 = (bf16[256,256]{1,0:T(8,128)(2,1)S(1)}, bf16[256,256]{1,0:T(8,128)(2,1)S(1)}, u32[]{:S(2)}, u32[]{:S(2)}) collective-permute-start(bf16[256,256]{1,0:T(8,128)(2,1)S(1)} %get-tuple-element.26), channel_id=1, source_target_pairs={{0,4},{1,5},{2,6},{3,7},{4,0},{5,1},{6,2},{7,3},{8,12},{9,13},{10,... | collective-permute-start | bytes 393224 | tf_op jit(solution)/shard_map/ppermute | solution.py:158
  40.8 7.4 %collective-permute-start.15 = (bf16[256,256]{1,0:T(8,128)(2,1)S(1)}, bf16[256,256]{1,0:T(8,128)(2,1)S(1)}, u32[]{:S(2)}, u32[]{:S(2)}) collective-permute-start(bf16[256,256]{1,0:T(8,128)(2,1)S(1)} %get-tuple-element.27), channel_id=1, source_target_pairs={{0,12},{1,13},{2,14},{3,15},{4,8},{5,9},{6,10},{7,11},{8,4},{9,5},... | collective-permute-start | bytes 393224 | tf_op jit(solution)/shard_map/ppermute | solution.py:158
  43.5 8.7 %collective-permute-start.13 = (bf16[256,256]{1,0:T(8,128)(2,1)S(1)}, bf16[256,256]{1,0:T(8,128)(2,1)S(1)}, u32[]{:S(2)}, u32[]{:S(2)}) collective-permute-start(bf16[256,256]{1,0:T(8,128)(2,1)S(1)} %add_convert_fusion.5), channel_id=1, source_target_pairs={{0,8},{1,9},{2,10},{3,11},{4,12},{5,13},{6,14},{7,15},{8,0},{9,1},... | collective-permute-start | bytes 393224 | tf_op jit(solution)/shard_map/ppermute | solution.py:158
  48.3 6.8 %collective-permute-start.16 = (bf16[256,256]{1,0:T(8,128)(2,1)S(1)}, bf16[256,256]{1,0:T(8,128)(2,1)S(1)}, u32[]{:S(2)}, u32[]{:S(2)}) collective-permute-start(bf16[256,256]{1,0:T(8,128)(2,1)S(1)} %add_convert_fusion.4), channel_id=1, source_target_pairs={{0,2},{1,3},{2,0},{3,1},{4,6},{5,7},{6,4},{7,5},{8,10},{9,11},{10,... | collective-permute-start | bytes 393224 | tf_op jit(solution)/shard_map/ppermute | solution.py:158
  55.2 7.5 %collective-permute-start.20 = (bf16[256,256]{1,0:T(8,128)(2,1)S(1)}, bf16[256,256]{1,0:T(8,128)(2,1)S(1)}, u32[]{:S(2)}, u32[]{:S(2)}) collective-permute-start(bf16[256,256]{1,0:T(8,128)(2,1)S(1)} %add_convert_fusion.3.refs_0_), channel_id=1, source_target_pairs={{0,8},{1,9},{2,10},{3,11},{4,12},{5,13},{6,14},{7,15},{8,0},{9,1},... | collective-permute-start | bytes 393224 | tf_op jit(solution)/shard_map/ppermute | solution.py:158
  58.3 7.1 %collective-permute-start.17 = (bf16[256,256]{1,0:T(8,128)(2,1)S(1)}, bf16[256,256]{1,0:T(8,128)(2,1)S(1)}, u32[]{:S(2)}, u32[]{:S(2)}) collective-permute-start(bf16[256,256]{1,0:T(8,128)(2,1)S(1)} %add_convert_fusion.3.refs_0_), channel_id=1, source_target_pairs={{0,2},{1,3},{2,0},{3,1},{4,6},{5,7},{6,4},{7,5},{8,10},{9,11},{10,... | collective-permute-start | bytes 393224 | tf_op jit(solution)/shard_map/ppermute | solution.py:158
  58.9 8.1 %collective-permute-start.22 = (bf16[256,256]{1,0:T(8,128)(2,1)S(1)}, bf16[256,256]{1,0:T(8,128)(2,1)S(1)}, u32[]{:S(2)}, u32[]{:S(2)}) collective-permute-start(bf16[256,256]{1,0:T(8,128)(2,1)S(1)} %add_convert_fusion.3.refs_0_), channel_id=1, source_target_pairs={{0,12},{1,13},{2,14},{3,15},{4,8},{5,9},{6,10},{7,11},{8,4},{9,5},... | collective-permute-start | bytes 393224 | tf_op jit(solution)/shard_map/ppermute | solution.py:158
  62.2 5.0 %collective-permute-start.18 = (bf16[256,256]{1,0:T(8,128)(2,1)S(1)}, bf16[256,256]{1,0:T(8,128)(2,1)S(1)}, u32[]{:S(2)}, u32[]{:S(2)}) collective-permute-start(bf16[256,256]{1,0:T(8,128)(2,1)S(1)} %add_convert_fusion.3.refs_0_), channel_id=1, source_target_pairs={{0,4},{1,5},{2,6},{3,7},{4,0},{5,1},{6,2},{7,3},{8,12},{9,13},{10,... | collective-permute-start | bytes 393224 | tf_op jit(solution)/shard_map/ppermute | solution.py:158
  62.7 6.5 %collective-permute-start.21 = (bf16[256,256]{1,0:T(8,128)(2,1)S(1)}, bf16[256,256]{1,0:T(8,128)(2,1)S(1)}, u32[]{:S(2)}, u32[]{:S(2)}) collective-permute-start(bf16[256,256]{1,0:T(8,128)(2,1)S(1)} %collective-permute-done.20.refs_4_), channel_id=1, source_target_pairs={{0,2},{1,3},{2,0},{3,1},{4,6},{5,7},{6,4},{7,5},{8,10},{9,11},{10,... | collective-permute-start | bytes 393224 | tf_op jit(solution)/shard_map/ppermute | solution.py:158
  65.4 6.2 %collective-permute-start.23 = (bf16[256,256]{1,0:T(8,128)(2,1)S(1)}, bf16[256,256]{1,0:T(8,128)(2,1)S(1)}, u32[]{:S(2)}, u32[]{:S(2)}) collective-permute-start(bf16[256,256]{1,0:T(8,128)(2,1)S(1)} %collective-permute-done.17.refs_1_), channel_id=1, source_target_pairs={{0,12},{1,13},{2,14},{3,15},{4,8},{5,9},{6,10},{7,11},{8,4},{9,5},... | collective-permute-start | bytes 393224 | tf_op jit(solution)/shard_map/ppermute | solution.py:158
  67.0 5.0 %collective-permute-start.19 = (bf16[256,256]{1,0:T(8,128)(2,1)S(1)}, bf16[256,256]{1,0:T(8,128)(2,1)S(1)}, u32[]{:S(2)}, u32[]{:S(2)}) collective-permute-start(bf16[256,256]{1,0:T(8,128)(2,1)S(1)} %collective-permute-done.17.refs_1_), channel_id=1, source_target_pairs={{0,4},{1,5},{2,6},{3,7},{4,0},{5,1},{6,2},{7,3},{8,12},{9,13},{10,... | collective-permute-start | bytes 393224 | tf_op jit(solution)/shard_map/ppermute | solution.py:158
  72.7 5.8 %collective-permute-start.25 = (bf16[4,256,256]{2,1,0:T(8,128)(2,1)S(1)}, bf16[4,256,256]{2,1,0:T(8,128)(2,1)S(1)}, u32[]{:S(2)}, u32[]{:S(2)}) collective-permute-start(bf16[4,256,256]{2,1,0:T(8,128)(2,1)S(1)} %pack.1), channel_id=1, source_target_pairs={{0,1},{1,0},{18,19},{19,18},{36,37},{37,36},{54,55},{55,54},{72,73... | collective-permute-start | bytes 1572872 | tf_op jit(solution)/shard_map/ppermute | solution.py:231
  75.9 2.6 %collective-permute-start.24 = (bf16[2,256,256]{2,1,0:T(8,128)(2,1)S(1)}, bf16[2,256,256]{2,1,0:T(8,128)(2,1)S(1)}, u32[]{:S(2)}, u32[]{:S(2)}) collective-permute-start(bf16[2,256,256]{2,1,0:T(8,128)(2,1)S(1)} %get-tuple-element.29), channel_id=1, source_target_pairs={{0,1},{1,0},{2,3},{3,2},{4,5},{5,4},{6,7},{7,6},{8,9},{9,8},{10,11... | collective-permute-start | bytes 786440 | tf_op jit(solution)/shard_map/ppermute | solution.py:158
  83.8 5.5 %collective-permute-start.28 = (bf16[256,256]{1,0:T(8,128)(2,1)S(1)}, bf16[256,256]{1,0:T(8,128)(2,1)S(1)}, u32[]{:S(2)}, u32[]{:S(2)}) collective-permute-start(bf16[256,256]{1,0:T(8,128)(2,1)S(1)} %get-tuple-element.34), channel_id=1, source_target_pairs={{0,64},{16,80},{32,96},{48,112},{64,0},{80,16},{96,32},{112,48},{1... | collective-permute-start | bytes 393224 | tf_op jit(solution)/shard_map/ppermute | solution.py:158
  83.9 14.1 %collective-permute-start.26 = (bf16[256,256]{1,0:T(8,128)(2,1)S(1)}, bf16[256,256]{1,0:T(8,128)(2,1)S(1)}, u32[]{:S(2)}, u32[]{:S(2)}) collective-permute-start(bf16[256,256]{1,0:T(8,128)(2,1)S(1)} %get-tuple-element.31), channel_id=1, source_target_pairs={{0,16},{16,0},{32,48},{48,32},{64,80},{80,64},{96,112},{112,96},{1... | collective-permute-start | bytes 393224 | tf_op jit(solution)/shard_map/ppermute | solution.py:158
  84.0 14.0 %collective-permute-start.27 = (bf16[256,256]{1,0:T(8,128)(2,1)S(1)}, bf16[256,256]{1,0:T(8,128)(2,1)S(1)}, u32[]{:S(2)}, u32[]{:S(2)}) collective-permute-start(bf16[256,256]{1,0:T(8,128)(2,1)S(1)} %get-tuple-element.32), channel_id=1, source_target_pairs={{0,48},{16,32},{32,16},{48,0},{64,112},{80,96},{96,80},{112,64},{1... | collective-permute-start | bytes 393224 | tf_op jit(solution)/shard_map/ppermute | solution.py:158
  85.6 7.6 %collective-permute-start.30 = (bf16[256,256]{1,0:T(8,128)(2,1)S(1)}, bf16[256,256]{1,0:T(8,128)(2,1)S(1)}, u32[]{:S(2)}, u32[]{:S(2)}) collective-permute-start(bf16[256,256]{1,0:T(8,128)(2,1)S(1)} %get-tuple-element.36), channel_id=1, source_target_pairs={{0,16},{16,0},{32,48},{48,32},{64,80},{80,64},{96,112},{112,96},{1... | collective-permute-start | bytes 393224 | tf_op jit(solution)/shard_map/ppermute | solution.py:158
  86.0 10.3 %collective-permute-start.31 = (bf16[256,256]{1,0:T(8,128)(2,1)S(1)}, bf16[256,256]{1,0:T(8,128)(2,1)S(1)}, u32[]{:S(2)}, u32[]{:S(2)}) collective-permute-start(bf16[256,256]{1,0:T(8,128)(2,1)S(1)} %get-tuple-element.37), channel_id=1, source_target_pairs={{0,48},{16,32},{32,16},{48,0},{64,112},{80,96},{96,80},{112,64},{1... | collective-permute-start | bytes 393224 | tf_op jit(solution)/shard_map/ppermute | solution.py:158
  89.4 8.7 %collective-permute-start.29 = (bf16[256,256]{1,0:T(8,128)(2,1)S(1)}, bf16[256,256]{1,0:T(8,128)(2,1)S(1)}, u32[]{:S(2)}, u32[]{:S(2)}) collective-permute-start(bf16[256,256]{1,0:T(8,128)(2,1)S(1)} %add_convert_fusion.2), channel_id=1, source_target_pairs={{0,32},{16,48},{32,0},{48,16},{64,96},{80,112},{96,64},{112,80},{1... | collective-permute-start | bytes 393224 | tf_op jit(solution)/shard_map/ppermute | solution.py:158
  96.4 5.0 %collective-permute-start.32 = (bf16[256,256]{1,0:T(8,128)(2,1)S(1)}, bf16[256,256]{1,0:T(8,128)(2,1)S(1)}, u32[]{:S(2)}, u32[]{:S(2)}) collective-permute-start(bf16[256,256]{1,0:T(8,128)(2,1)S(1)} %add_convert_fusion.1), channel_id=1, source_target_pairs={{0,64},{16,80},{32,96},{48,112},{64,0},{80,16},{96,32},{112,48},{1... | collective-permute-start | bytes 393224 | tf_op jit(solution)/shard_map/ppermute | solution.py:158
  (8 other events, 42.2 us)

commit v3 on v2

v3 whole, which is shorter than its diff:
```python
import functools

import jax
import jax.numpy as jnp
from jax import lax
from jax.experimental import pallas as pl
from jax.experimental.pallas import tpu as pltpu
from jax.sharding import PartitionSpec as P

PIECE = 256
F32 = jnp.float32
BF16 = jnp.bfloat16
REL = [(d, x) for d in range(4) for x in range(2)]
FAR = [(1, 1), (3, 1), (2, 1)]
NEAR = [(1, 0), (3, 0), (2, 0), (0, 1), (0, 0)]
VMEM = pl.BlockSpec(memory_space=pltpu.VMEM)


def dot(a, b):
    return lax.dot_general(a, b, (((1,), (0,)), ((), ())), preferred_element_type=F32)


def dot_t(a, b):
    return lax.dot_general(a, b, (((1,), (1,)), ((), ())), preferred_element_type=F32)


def total(parts):
    return functools.reduce(lambda a, b: a + b, parts)


class Place:
    def __init__(self, buckets=None):
        trow = lax.axis_index("trow")
        tcol = lax.axis_index("tcol")
        self.x_lo, self.z = trow >> 2, trow & 3
        self.y, self.x_hi, self.core = tcol >> 2, (tcol >> 1) & 1, tcol & 1
        self.owner = trow == tcol >> 1
        if buckets is not None:
            self.ranks = [jnp.where(trow * 2 + t == tcol, 0, 16 << buckets[:, t : t + 1]) for t in range(2)]


def row_piece(info, rel):
    return (info.x_lo ^ rel[1]) * 4 + (info.z ^ rel[0])


def half_piece(info, rel):
    return (info.y ^ rel[0]) * 2 + (info.x_hi ^ rel[1])


def rows_of(piece):
    return pl.ds(pl.multiple_of(piece * PIECE, PIECE), PIECE)


def left_rows(info, piece):
    return rows_of((piece % 4) * 2 + info.core)


def masked(values, rank):
    columns = lax.broadcasted_iota(jnp.int32, values.shape, 1)
    return jnp.where(columns < rank, values, 0.0)


def coeff_kernel(buckets, *refs):
    info = Place(buckets)
    x, right, out = refs[:8], refs[8], refs[9]
    for t in range(2):
        acc = total(dot(x[n][...], right[t, rows_of(row_piece(info, rel)), :]) for n, rel in enumerate(REL))
        out[t] = masked(acc, info.ranks[t]).astype(BF16)


def diag_kernel(for_mate, *refs):
    info = Place()
    x, dense, out = refs[:8], refs[8], refs[9]
    parity = info.core ^ for_mate

    @pl.when(info.owner)
    def _():
        for q in range(4):
            rows = rows_of(2 * q + parity)
            acc = total(dot_t(x[n][...], dense[rows, rows_of(row_piece(info, rel))]) for n, rel in enumerate(REL))
            out[q] = acc.astype(out.dtype)


def term_kernel(rels, own, mate, left_own, left_mate, dense_own, dense_mate, *outs):
    info = Place()

    def low(piece):
        tile = piece // 4
        rows = left_rows(info, piece)
        return dot_t(own[tile], left_own[tile, rows, :]) + dot_t(mate[tile], left_mate[tile, rows, :])

    @pl.when(jnp.logical_not(info.owner))
    def _():
        for out, rel in zip(outs, rels):
            out[...] = low(half_piece(info, rel)).astype(BF16)

    @pl.when(info.owner)
    def _():
        for out, rel in zip(outs, rels):
            piece = half_piece(info, rel)
            extra = jnp.where(piece // 4 == info.core, dense_own[piece % 4], dense_mate[piece % 4])
            out[...] = (low(piece) + extra.astype(F32)).astype(BF16)


def pack_kernel(*refs):
    info = Place()
    y, out = refs[:8], refs[8]
    for n, rel in enumerate(REL):
        piece = half_piece(info, rel)

        @pl.when(jnp.logical_and(info.owner, piece // 4 != info.core))
        def _():
            out[piece % 4] = y[n][...]


def back_kernel(*refs):
    info = Place()
    y, left_own, left_mate, own, mate = refs[:8], refs[8], refs[9], refs[10], refs[11]
    for half in range(2):
        tile = (info.y // 2) ^ half
        for left, out in ((left_mate, mate), (left_own, own)):
            out[tile] = total(
                dot(y[n][...], left[tile, left_rows(info, half_piece(info, rel)), :])
                for n, rel in enumerate(REL)
                if rel[0] // 2 == half
            ).astype(out.dtype)


def diag_back_kernel(*refs):
    info = Place()
    y, dense, out = refs[:8], refs[8], refs[9]
    for half in range(2):

        @pl.when(jnp.logical_and(info.owner, (info.y // 2) ^ half == info.core))
        def _():
            for p in range(8):
                out[p] = total(
                    dot(y[n][...], dense[left_rows(info, half_piece(info, rel)), p * PIECE : (p + 1) * PIECE])
                    for n, rel in enumerate(REL)
                    if rel[0] // 2 == half
                )


def second_kernel(rels, buckets, own, mate, right, dense_sum, y_mate, dense, *outs):
    info = Place(buckets)
    coeff = [masked(own[t] + mate[t].astype(F32), info.ranks[t]).astype(BF16) for t in range(2)]

    def low(rows):
        return dot_t(coeff[0], right[0, rows, :]) + dot_t(coeff[1], right[1, rows, :])

    @pl.when(jnp.logical_not(info.owner))
    def _():
        for out, rel in zip(outs, rels):
            out[...] = low(rows_of(row_piece(info, rel))).astype(BF16)

    @pl.when(info.owner)
    def _():
        for out, rel in zip(outs, rels):
            piece = row_piece(info, rel)
            rows = rows_of(piece)
            rest = total(dot(y_mate[q], dense[rows_of(2 * q + 1 - info.core), rows]) for q in range(4))
            out[...] = (low(rows) + dense_sum[piece] + rest).astype(BF16)


def call(kernel, name, operands, outs, flops, moved, buckets=None):
    return pl.pallas_call(
        kernel,
        name=name,
        out_shape=outs,
        in_specs=[VMEM] * (len(operands) + (buckets is not None)),
        out_specs=[VMEM] * len(outs),
        compiler_params=pltpu.CompilerParams(vmem_limit_bytes=16 * 2**20),
        cost_estimate=pl.CostEstimate(flops=flops, bytes_accessed=moved, transcendentals=0),
    )(*([] if buckets is None else [buckets]), *operands)


def swap(x, axis, bits):
    size = lax.axis_size(axis)
    return lax.ppermute(x, axis, [(i, i ^ bits) for i in range(size)])


def gather(own, axis, ring, side, first=None):
    got = {(0, 0): own}
    got[(0, 1)] = swap(own, axis, side)
    if first is not None:
        got[(0, 1)], first = lax.optimization_barrier((got[(0, 1)], first))
    got[(2, 0)] = swap(own, axis, 2 * ring)
    got[(1, 0)] = swap(own, axis, ring)
    got[(3, 0)] = swap(own, axis, 3 * ring)
    got[(1, 1)] = swap(got[(0, 1)], axis, ring)
    got[(3, 1)] = swap(got[(0, 1)], axis, 3 * ring)
    got[(2, 1)] = swap(got[(2, 0)], axis, side)
    return [got[rel] for rel in REL], first


def add(*parts):
    return total(v.astype(F32) for v in parts).astype(BF16)


def scatter(pieces, axis, ring, side):
    piece = dict(zip(FAR + NEAR, pieces))
    far_1 = swap(piece[(1, 1)], axis, ring)
    far_3 = swap(piece[(3, 1)], axis, 3 * ring)
    far_2 = swap(piece[(2, 1)], axis, side)
    near_1 = swap(piece[(1, 0)], axis, ring)
    near_3 = swap(piece[(3, 0)], axis, 3 * ring)
    near_2 = swap(add(piece[(2, 0)], far_2), axis, 2 * ring)
    crossed = swap(add(piece[(0, 1)], far_1, far_3), axis, side)
    return add(piece[(0, 0)], near_1, near_3, near_2, crossed)


def body(signal, left_factors, right_factors, dense_diagonal, buckets):
    buckets = buckets.T
    right = right_factors[:, 0]
    left = left_factors[:, 0]
    dense = dense_diagonal[0]
    owners = [((b // 2) * 16 + b, (b // 2) * 16 + (b ^ 1)) for b in range(16)]

    count = signal.shape[0]
    unit = 2 * count * PIECE * PIECE
    size = count * PIECE * 2
    piece = jax.ShapeDtypeStruct((count, PIECE), BF16)
    pair = jax.ShapeDtypeStruct((2, count, PIECE), BF16)
    pair_wide = jax.ShapeDtypeStruct((2, count, PIECE), F32)
    four = jax.ShapeDtypeStruct((4, count, PIECE), BF16)
    eight_wide = jax.ShapeDtypeStruct((8, count, PIECE), F32)

    left_mate = swap(left, "tcol", 1)
    x, left_mate = gather(signal, "trow", 1, 4, left_mate)
    (coeff,) = call(coeff_kernel, "coeff", [*x, right], [pair], 16 * unit, 10 * size + 2**21, buckets)
    coeff_mate = swap(coeff, "tcol", 1)
    (dense_sent,) = call(functools.partial(diag_kernel, 1), "diag_mate", [*x, dense], [four], 32 * unit, 12 * size + 2**23)
    dense_mate = lax.ppermute(dense_sent, ("trow", "tcol"), owners)
    (dense_own,) = call(functools.partial(diag_kernel, 0), "diag_own", [*x, dense], [four], 32 * unit, 12 * size + 2**23)
    terms = []
    for rels in (FAR, NEAR):
        terms += call(
            functools.partial(term_kernel, rels),
            "term",
            [coeff, coeff_mate, left, left_mate, dense_own, dense_mate],
            [piece] * len(rels),
            2 * len(rels) * unit,
            2 * len(rels) * size + 2**21,
        )
    first = scatter(terms, "tcol", 4, 2)
    y, _ = gather(first, "tcol", 4, 2)
    (y_sent,) = call(pack_kernel, "pack", y, [four], 0, 12 * size)
    y_mate = lax.ppermute(y_sent, ("trow", "tcol"), owners)
    own, mate = call(back_kernel, "back", [*y, left, left_mate], [pair_wide, pair], 16 * unit, 14 * size + 2**21)
    mate = swap(mate, "tcol", 1)
    (dense_sum,) = call(diag_back_kernel, "diag_back", [*y, dense], [eight_wide], 32 * unit, 24 * size + 2**22)
    terms = []
    for rels in (FAR, NEAR):
        terms += call(
            functools.partial(second_kernel, rels),
            "second",
            [own, mate, right, dense_sum, y_mate, dense],
            [piece] * len(rels),
            6 * len(rels) * unit,
            4 * len(rels) * size + 3 * 2**20,
            buckets,
        )
    second = scatter(terms, "trow", 1, 4)
    return (first, second)


def solution(mesh):
    in_specs = (
        P(None, ("tcol", "trow")),
        P("trow", "tcol", None, None),
        P("trow", "tcol", None, None),
        P("tcol", None, None),
        P("trow", "tcol"),
    )
    out_specs = (P(None, ("trow", "tcol")), P(None, ("tcol", "trow")))
    return jax.shard_map(body, mesh=mesh, in_specs=in_specs, out_specs=out_specs, check_vma=False)
```

time: 104 us -> 83.6 us (0.80); the launches traced: 102 us -> 83.4 us
  Pallas kernels: 17.4 us -> 8.58 us
  waiting for transfers between devices: 31.9 us -> 23.6 us
    pallas_call x8 -> x10, Pallas kernels: 17.4 us -> 8.58 us  [call(): pl.pallas_call(kernel, name=name, out_shape=outs, in_specs=[VMEM] * (len(...]
    ppermute x31, waiting for transfers between devices: 31.9 us -> 23.6 us  [swap(): return lax.ppermute(x, axis, [(i, i ^ bits) for i in range(size)])]
    ppermute x31, starting transfers between devices: 40.4 us -> 39.2 us  [swap(): return lax.ppermute(x, axis, [(i, i ^ bits) for i in range(size)])]
    unnamed x14 -> x18, local copies, waits for them, and re-layouts: 5.89 us -> 5.9 us
  transfers between devices with their start and end apart: 33 -> 33, of which waited for: 16 -> 13; matrix products, arithmetic and copies ran while one was open for 1% -> 0% of each run, Pallas kernels for 8% -> 7%
where the time goes in v3:
time: 83.6 us; the launch traced here: 83.4 us
  starting transfers between devices  43.4 us (52%)
  waiting for transfers between devices  23.6 us (28%)
  Pallas kernels  8.58 us (10%)
  local copies, waits for them, and re-layouts  5.9 us (7%)
  other arithmetic  1 us (1%)
  between operations  0.89 us (1%)
    ppermute x31, starting transfers between devices, swap(): return lax.ppermute(x, axis, [(i, i ^ bits) for i in range(size)])  39.2 us
    ppermute x31, waiting for transfers between devices, swap(): return lax.ppermute(x, axis, [(i, i ^ bits) for i in range(size)])  23.6 us
    pallas_call x10, Pallas kernels, call(): pl.pallas_call(kernel, name=name, out_shape=outs, in_specs=[VMEM] * (len(...  8.58 us
    unnamed x18, local copies, waits for them, and re-layouts  5.9 us
    ppermute x1, starting transfers between devices, body(): dense_mate = lax.ppermute(dense_sent, ('trow', 'tcol'), owners)  2.18 us
    ppermute x1, starting transfers between devices, body(): y_mate = lax.ppermute(y_sent, ('trow', 'tcol'), owners)  2.1 us
  transfers between devices with their start and end apart: 33, of which 13 were waited for; matrix products, arithmetic and copies ran while one was open for 0% of the time, Pallas kernels for 7%

profile of v3, /device:TPU:0, one launch (start us, length us, event | category | flops | bytes accessed | tf_op | source)
XLA Modules:
  0.0 83.4 jit_solution(8511311276347165878)
XLA Ops:
  0.7 4.0 %collective-permute-start.4 = (bf16[256,256]{1,0:T(8,128)(2,1)}, bf16[256,256]{1,0:T(8,128)(2,1)S(1)}, u32[]{:S(2)}, u32[]{:S(2)}) collective-permute-start(bf16[256,256]{1,0:T(8,128)(2,1)} %refs_0_.5), channel_id=1, source_target_pairs={{0,32},{16,48},{32,0},{48,16},{64,96},{80,112},{96,64},{112,80},{1... | collective-permute-start | bytes 393224 | tf_op jit(solution)/shard_map/ppermute | solution.py:179
  4.8 1.5 %collective-permute-start = (bf16[256,256]{1,0:T(8,128)(2,1)}, bf16[256,256]{1,0:T(8,128)(2,1)S(1)}, u32[]{:S(2)}, u32[]{:S(2)}) collective-permute-start(bf16[256,256]{1,0:T(8,128)(2,1)} %refs_0_.5), channel_id=1, source_target_pairs={{0,64},{16,80},{32,96},{48,112},{64,0},{80,16},{96,32},{112,48},{1... | collective-permute-start | bytes 393224 | tf_op jit(solution)/shard_map/ppermute | solution.py:179
  7.3 1.8 %collective-permute-done.4.refs_4_ = bf16[256,256]{1,0:T(8,128)(2,1)S(1)} collective-permute-done((bf16[256,256]{1,0:T(8,128)(2,1)}, bf16[256,256]{1,0:T(8,128)(2,1)S(1)}, u32[]{:S(2)}, u32[]{:S(2)}) %collective-permute-start.4) | collective-permute-done | bytes 131104 | tf_op jit(solution)/shard_map/ppermute | solution.py:179
  9.0 1.5 %collective-permute-start.5 = (bf16[256,256]{1,0:T(8,128)(2,1)S(1)}, bf16[256,256]{1,0:T(8,128)(2,1)S(1)}, u32[]{:S(2)}, u32[]{:S(2)}) collective-permute-start(bf16[256,256]{1,0:T(8,128)(2,1)S(1)} %collective-permute-done.4.refs_4_), channel_id=1, source_target_pairs={{0,64},{16,80},{32,96},{48,112},{64,0},{80,16},{96,32},{112,48},{1... | collective-permute-start | bytes 393224 | tf_op jit(solution)/shard_map/ppermute | solution.py:179
  10.5 3.9 %collective-permute-start.7 = (bf16[256,256]{1,0:T(8,128)(2,1)S(1)}, bf16[256,256]{1,0:T(8,128)(2,1)S(1)}, u32[]{:S(2)}, u32[]{:S(2)}) collective-permute-start(bf16[256,256]{1,0:T(8,128)(2,1)S(1)} %collective-permute-done.refs_1_), channel_id=1, source_target_pairs={{0,48},{16,32},{32,16},{48,0},{64,112},{80,96},{96,80},{112,64},{1... | collective-permute-start | bytes 393224 | tf_op jit(solution)/shard_map/ppermute | solution.py:179
  14.5 2.9 %collective-permute-done.7.refs_7_ = bf16[256,256]{1,0:T(8,128)(2,1)S(1)} collective-permute-done((bf16[256,256]{1,0:T(8,128)(2,1)S(1)}, bf16[256,256]{1,0:T(8,128)(2,1)S(1)}, u32[]{:S(2)}, u32[]{:S(2)}) %collective-permute-start.7) | collective-permute-done | bytes 131104 | tf_op jit(solution)/shard_map/ppermute | solution.py:179
  17.4 2.0 %collective-permute-done.3.refs_3_ = bf16[256,256]{1,0:T(8,128)(2,1)S(1)} collective-permute-done((bf16[256,256]{1,0:T(8,128)(2,1)S(1)}, bf16[256,256]{1,0:T(8,128)(2,1)S(1)}, u32[]{:S(2)}, u32[]{:S(2)}) %collective-permute-start.3) | collective-permute-done | bytes 131104 | tf_op jit(solution)/shard_map/ppermute | solution.py:179
  19.5 3.4 %copy-done = bf16[1,2048,2048]{2,1,0:T(8,128)(2,1)S(1)} copy-done((bf16[1,2048,2048]{2,1,0:T(8,128)(2,1)S(1)}, bf16[1,2048,2048]{2,1,0:T(8,128)(2,1)}, u32[]{:S(2)}) %copy-start) | copy-done | bytes 8388632
  23.7 1.3 %diag_mate.1 = bf16[4,256,256]{2,1,0:T(8,128)(2,1)S(1)} custom-call(bf16[256,256]{1,0:T(8,128)(2,1)S(1)} %copy-done.6, bf16[256,256]{1,0:T(8,128)(2,1)S(1)} %collective-permute-done.refs_1_, bf16[256,256]{1,0:T(8,128)(2,1)S(1)} %collective-permute-done.2.refs_2_, bf16[256,256]{1,0:T(8,128)(2,1)S(1)} %collective-permute-done.3.refs_3_, ...), custom_call_target="tpu_custom_call" | custom-call | flops 1073741824 | bytes 9961472 | tf_op jit(solution)/shard_map/diag_mate/pallas_call | solution.py:166
  25.1 2.2 %collective-permute-start.9 = (bf16[4,256,256]{2,1,0:T(8,128)(2,1)S(1)}, bf16[4,256,256]{2,1,0:T(8,128)(2,1)S(1)}, u32[]{:S(2)}, u32[]{:S(2)}) collective-permute-start(bf16[4,256,256]{2,1,0:T(8,128)(2,1)S(1)} %diag_mate.1), channel_id=1, source_target_pairs={{0,1},{1,0},{18,19},{19,18},{36,37},{37,36},{54,55},{55,54},{72,73... | collective-permute-start | bytes 1572872 | tf_op jit(solution)/shard_map/ppermute | solution.py:233
  27.3 1.6 %copy-done.3 = bf16[2,1,2048,256]{3,2,1,0:T(8,128)(2,1)S(1)} copy-done((bf16[2,1,2048,256]{3,2,1,0:T(8,128)(2,1)S(1)}, bf16[2,1,2048,256]{3,2,1,0:T(8,128)(2,1)}, u32[]{:S(2)}) %copy-start.3) | copy-done | bytes 2097176
  30.2 1.3 %diag_own.1.dense_own = bf16[4,256,256]{2,1,0:T(8,128)(2,1)S(1)} custom-call(bf16[256,256]{1,0:T(8,128)(2,1)S(1)} %copy-done.7, bf16[256,256]{1,0:T(8,128)(2,1)S(1)} %collective-permute-done.refs_1_, bf16[256,256]{1,0:T(8,128)(2,1)S(1)} %collective-permute-done.2.refs_2_, bf16[256,256]{1,0:T(8,128)(2,1)S(1)} %collective-permute-done.3.refs_3_, ...), custom_call_target="tpu_custom_call" | custom-call | flops 1073741824 | bytes 9961472 | tf_op jit(solution)/shard_map/diag_own/pallas_call | solution.py:166
  32.3 1.6 %collective-permute-start.14 = (bf16[256,256]{1,0:T(8,128)(2,1)S(1)}, bf16[256,256]{1,0:T(8,128)(2,1)S(1)}, u32[]{:S(2)}, u32[]{:S(2)}) collective-permute-start(bf16[256,256]{1,0:T(8,128)(2,1)S(1)} %get-tuple-element.30), channel_id=1, source_target_pairs={{0,4},{1,5},{2,6},{3,7},{4,0},{5,1},{6,2},{7,3},{8,12},{9,13},{10,... | collective-permute-start | bytes 393224 | tf_op jit(solution)/shard_map/ppermute | solution.py:179
  33.9 2.2 %collective-permute-start.15 = (bf16[256,256]{1,0:T(8,128)(2,1)S(1)}, bf16[256,256]{1,0:T(8,128)(2,1)S(1)}, u32[]{:S(2)}, u32[]{:S(2)}) collective-permute-start(bf16[256,256]{1,0:T(8,128)(2,1)S(1)} %get-tuple-element.31), channel_id=1, source_target_pairs={{0,12},{1,13},{2,14},{3,15},{4,8},{5,9},{6,10},{7,11},{8,4},{9,5},... | collective-permute-start | bytes 393224 | tf_op jit(solution)/shard_map/ppermute | solution.py:179
  39.1 1.8 %collective-permute-start.13 = (bf16[256,256]{1,0:T(8,128)(2,1)S(1)}, bf16[256,256]{1,0:T(8,128)(2,1)S(1)}, u32[]{:S(2)}, u32[]{:S(2)}) collective-permute-start(bf16[256,256]{1,0:T(8,128)(2,1)S(1)} %add_convert_fusion.5), channel_id=1, source_target_pairs={{0,8},{1,9},{2,10},{3,11},{4,12},{5,13},{6,14},{7,15},{8,0},{9,1},... | collective-permute-start | bytes 393224 | tf_op jit(solution)/shard_map/ppermute | solution.py:179
  41.0 1.9 %collective-permute-start.16 = (bf16[256,256]{1,0:T(8,128)(2,1)S(1)}, bf16[256,256]{1,0:T(8,128)(2,1)S(1)}, u32[]{:S(2)}, u32[]{:S(2)}) collective-permute-start(bf16[256,256]{1,0:T(8,128)(2,1)S(1)} %add_convert_fusion.4), channel_id=1, source_target_pairs={{0,2},{1,3},{2,0},{3,1},{4,6},{5,7},{6,4},{7,5},{8,10},{9,11},{10,... | collective-permute-start | bytes 393224 | tf_op jit(solution)/shard_map/ppermute | solution.py:179
  42.9 3.5 %collective-permute-done.11 = bf16[256,256]{1,0:T(8,128)(2,1)S(1)} collective-permute-done((bf16[256,256]{1,0:T(8,128)(2,1)S(1)}, bf16[256,256]{1,0:T(8,128)(2,1)S(1)}, u32[]{:S(2)}, u32[]{:S(2)}) %collective-permute-start.11) | collective-permute-done | bytes 131104 | tf_op jit(solution)/shard_map/ppermute | solution.py:179
  47.6 2.0 %collective-permute-start.20 = (bf16[256,256]{1,0:T(8,128)(2,1)S(1)}, bf16[256,256]{1,0:T(8,128)(2,1)S(1)}, u32[]{:S(2)}, u32[]{:S(2)}) collective-permute-start(bf16[256,256]{1,0:T(8,128)(2,1)S(1)} %add_convert_fusion.3.refs_0_), channel_id=1, source_target_pairs={{0,8},{1,9},{2,10},{3,11},{4,12},{5,13},{6,14},{7,15},{8,0},{9,1},... | collective-permute-start | bytes 393224 | tf_op jit(solution)/shard_map/ppermute | solution.py:179
  49.6 1.7 %collective-permute-start.17 = (bf16[256,256]{1,0:T(8,128)(2,1)S(1)}, bf16[256,256]{1,0:T(8,128)(2,1)S(1)}, u32[]{:S(2)}, u32[]{:S(2)}) collective-permute-start(bf16[256,256]{1,0:T(8,128)(2,1)S(1)} %add_convert_fusion.3.refs_0_), channel_id=1, source_target_pairs={{0,2},{1,3},{2,0},{3,1},{4,6},{5,7},{6,4},{7,5},{8,10},{9,11},{10,... | collective-permute-start | bytes 393224 | tf_op jit(solution)/shard_map/ppermute | solution.py:179
  51.3 2.2 %collective-permute-start.22 = (bf16[256,256]{1,0:T(8,128)(2,1)S(1)}, bf16[256,256]{1,0:T(8,128)(2,1)S(1)}, u32[]{:S(2)}, u32[]{:S(2)}) collective-permute-start(bf16[256,256]{1,0:T(8,128)(2,1)S(1)} %add_convert_fusion.3.refs_0_), channel_id=1, source_target_pairs={{0,12},{1,13},{2,14},{3,15},{4,8},{5,9},{6,10},{7,11},{8,4},{9,5},... | collective-permute-start | bytes 393224 | tf_op jit(solution)/shard_map/ppermute | solution.py:179
  53.5 1.6 %collective-permute-done.20.refs_4_ = bf16[256,256]{1,0:T(8,128)(2,1)S(1)} collective-permute-done((bf16[256,256]{1,0:T(8,128)(2,1)S(1)}, bf16[256,256]{1,0:T(8,128)(2,1)S(1)}, u32[]{:S(2)}, u32[]{:S(2)}) %collective-permute-start.20) | collective-permute-done | bytes 131104 | tf_op jit(solution)/shard_map/ppermute | solution.py:179
  55.0 1.6 %collective-permute-start.21 = (bf16[256,256]{1,0:T(8,128)(2,1)S(1)}, bf16[256,256]{1,0:T(8,128)(2,1)S(1)}, u32[]{:S(2)}, u32[]{:S(2)}) collective-permute-start(bf16[256,256]{1,0:T(8,128)(2,1)S(1)} %collective-permute-done.20.refs_4_), channel_id=1, source_target_pairs={{0,2},{1,3},{2,0},{3,1},{4,6},{5,7},{6,4},{7,5},{8,10},{9,11},{10,... | collective-permute-start | bytes 393224 | tf_op jit(solution)/shard_map/ppermute | solution.py:179
  57.4 1.3 %collective-permute-start.23 = (bf16[256,256]{1,0:T(8,128)(2,1)S(1)}, bf16[256,256]{1,0:T(8,128)(2,1)S(1)}, u32[]{:S(2)}, u32[]{:S(2)}) collective-permute-start(bf16[256,256]{1,0:T(8,128)(2,1)S(1)} %collective-permute-done.17.refs_1_), channel_id=1, source_target_pairs={{0,12},{1,13},{2,14},{3,15},{4,8},{5,9},{6,10},{7,11},{8,4},{9,5},... | collective-permute-start | bytes 393224 | tf_op jit(solution)/shard_map/ppermute | solution.py:179
  58.8 2.7 %collective-permute-done.21.refs_5_ = bf16[256,256]{1,0:T(8,128)(2,1)S(1)} collective-permute-done((bf16[256,256]{1,0:T(8,128)(2,1)S(1)}, bf16[256,256]{1,0:T(8,128)(2,1)S(1)}, u32[]{:S(2)}, u32[]{:S(2)}) %collective-permute-start.21) | collective-permute-done | bytes 131104 | tf_op jit(solution)/shard_map/ppermute | solution.py:179
  61.5 2.1 %collective-permute-done.23.refs_7_ = bf16[256,256]{1,0:T(8,128)(2,1)S(1)} collective-permute-done((bf16[256,256]{1,0:T(8,128)(2,1)S(1)}, bf16[256,256]{1,0:T(8,128)(2,1)S(1)}, u32[]{:S(2)}, u32[]{:S(2)}) %collective-permute-start.23) | collective-permute-done | bytes 131104 | tf_op jit(solution)/shard_map/ppermute | solution.py:179
  63.8 2.1 %collective-permute-start.25 = (bf16[4,256,256]{2,1,0:T(8,128)(2,1)S(1)}, bf16[4,256,256]{2,1,0:T(8,128)(2,1)S(1)}, u32[]{:S(2)}, u32[]{:S(2)}) collective-permute-start(bf16[4,256,256]{2,1,0:T(8,128)(2,1)S(1)} %pack.1), channel_id=1, source_target_pairs={{0,1},{1,0},{18,19},{19,18},{36,37},{37,36},{54,55},{55,54},{72,73... | collective-permute-start | bytes 1572872 | tf_op jit(solution)/shard_map/ppermute | solution.py:248
  67.2 1.3 %diag_back.1.dense_sum = f32[8,256,256]{2,1,0:T(8,128)S(1)} custom-call(bf16[256,256]{1,0:T(8,128)(2,1)S(1)} %add_convert_fusion.3.refs_0_, bf16[256,256]{1,0:T(8,128)(2,1)S(1)} %collective-permute-done.17.refs_1_, bf16[256,256]{1,0:T(8,128)(2,1)S(1)} %collective-permute-done.18.refs_2_, bf16[256,256]{1,0:T(8,128)(2,1)S(1)} %collective-permute-done.19.refs_3_, ...), custom_call_target="tpu_custom_call" | custom-call | flops 1073741824 | bytes 7340032 | tf_op jit(solution)/shard_map/diag_back/pallas_call | solution.py:166
  71.5 1.3 %second.2 = (bf16[256,256]{1,0:T(8,128)(2,1)S(1)}, bf16[256,256]{1,0:T(8,128)(2,1)S(1)}, bf16[256,256]{1,0:T(8,128)(2,1)S(1)}, bf16[256,256]{1,0:T(8,128)(2,1)S(1)}, bf16[256,256]{1,0:T(8,128)(2,1)S(1)}) custom-call(s32[1,2]{1,0:T(1,128)S(1)} %bitcast.18, f32[2,256,256]{2,1,0:T(8,128)S(1)} %get-tuple-element.32.own, ...), custom_call_target="tpu_custom_call" | custom-call | flops 1006632960 | bytes 5767168 | tf_op jit(solution)/shard_map/second/pallas_call | solution.py:166
  73.6 1.7 %collective-permute-start.27 = (bf16[256,256]{1,0:T(8,128)(2,1)S(1)}, bf16[256,256]{1,0:T(8,128)(2,1)S(1)}, u32[]{:S(2)}, u32[]{:S(2)}) collective-permute-start(bf16[256,256]{1,0:T(8,128)(2,1)S(1)} %get-tuple-element.36), channel_id=1, source_target_pairs={{0,48},{16,32},{32,16},{48,0},{64,112},{80,96},{96,80},{112,64},{1... | collective-permute-start | bytes 393224 | tf_op jit(solution)/shard_map/ppermute | solution.py:179
  75.4 1.8 %collective-permute-start.29 = (bf16[256,256]{1,0:T(8,128)(2,1)S(1)}, bf16[256,256]{1,0:T(8,128)(2,1)S(1)}, u32[]{:S(2)}, u32[]{:S(2)}) collective-permute-start(bf16[256,256]{1,0:T(8,128)(2,1)S(1)} %add_convert_fusion.2), channel_id=1, source_target_pairs={{0,32},{16,48},{32,0},{48,16},{64,96},{80,112},{96,64},{112,80},{1... | collective-permute-start | bytes 393224 | tf_op jit(solution)/shard_map/ppermute | solution.py:179
  77.2 1.7 %collective-permute-start.32 = (bf16[256,256]{1,0:T(8,128)(2,1)S(1)}, bf16[256,256]{1,0:T(8,128)(2,1)S(1)}, u32[]{:S(2)}, u32[]{:S(2)}) collective-permute-start(bf16[256,256]{1,0:T(8,128)(2,1)S(1)} %add_convert_fusion.1), channel_id=1, source_target_pairs={{0,64},{16,80},{32,96},{48,112},{64,0},{80,16},{96,32},{112,48},{1... | collective-permute-start | bytes 393224 | tf_op jit(solution)/shard_map/ppermute | solution.py:179
  79.0 3.6 %collective-permute-done.27 = bf16[256,256]{1,0:T(8,128)(2,1)S(1)} collective-permute-done((bf16[256,256]{1,0:T(8,128)(2,1)S(1)}, bf16[256,256]{1,0:T(8,128)(2,1)S(1)}, u32[]{:S(2)}, u32[]{:S(2)}) %collective-permute-start.27) | collective-permute-done | bytes 131104 | tf_op jit(solution)/shard_map/ppermute | solution.py:179
  (68 shorter events, 15.6 us)
Async XLA Ops:
  0.6 9.9 %collective-permute-start.1 = (bf16[2,2048,256]{2,1,0:T(8,128)(2,1)}, bf16[2,2048,256]{2,1,0:T(8,128)(2,1)S(1)}, u32[]{:S(2)}, u32[]{:S(2)}) collective-permute-start(bf16[2,2048,256]{2,1,0:T(8,128)(2,1)} %bitcast.9), channel_id=1, source_target_pairs={{0,1},{1,0},{2,3},{3,2},{4,5},{5,4},{6,7},{7,6},{8,9},{9,8},{10,11... | collective-permute-start | bytes 6291464 | tf_op jit(solution)/shard_map/ppermute | solution.py:179
  0.7 8.3 %collective-permute-start.4 = (bf16[256,256]{1,0:T(8,128)(2,1)}, bf16[256,256]{1,0:T(8,128)(2,1)S(1)}, u32[]{:S(2)}, u32[]{:S(2)}) collective-permute-start(bf16[256,256]{1,0:T(8,128)(2,1)} %refs_0_.5), channel_id=1, source_target_pairs={{0,32},{16,48},{32,0},{48,16},{64,96},{80,112},{96,64},{112,80},{1... | collective-permute-start | bytes 393224 | tf_op jit(solution)/shard_map/ppermute | solution.py:179
  4.8 5.8 %collective-permute-start = (bf16[256,256]{1,0:T(8,128)(2,1)}, bf16[256,256]{1,0:T(8,128)(2,1)S(1)}, u32[]{:S(2)}, u32[]{:S(2)}) collective-permute-start(bf16[256,256]{1,0:T(8,128)(2,1)} %refs_0_.5), channel_id=1, source_target_pairs={{0,64},{16,80},{32,96},{48,112},{64,0},{80,16},{96,32},{112,48},{1... | collective-permute-start | bytes 393224 | tf_op jit(solution)/shard_map/ppermute | solution.py:179
  6.3 8.2 %collective-permute-start.6 = (bf16[256,256]{1,0:T(8,128)(2,1)}, bf16[256,256]{1,0:T(8,128)(2,1)S(1)}, u32[]{:S(2)}, u32[]{:S(2)}) collective-permute-start(bf16[256,256]{1,0:T(8,128)(2,1)} %refs_0_.5), channel_id=1, source_target_pairs={{0,48},{16,32},{32,16},{48,0},{64,112},{80,96},{96,80},{112,64},{1... | collective-permute-start | bytes 393224 | tf_op jit(solution)/shard_map/ppermute | solution.py:179
  7.0 7.5 %collective-permute-start.2 = (bf16[256,256]{1,0:T(8,128)(2,1)}, bf16[256,256]{1,0:T(8,128)(2,1)S(1)}, u32[]{:S(2)}, u32[]{:S(2)}) collective-permute-start(bf16[256,256]{1,0:T(8,128)(2,1)} %refs_0_.5), channel_id=1, source_target_pairs={{0,16},{16,0},{32,48},{48,32},{64,80},{80,64},{96,112},{112,96},{1... | collective-permute-start | bytes 393224 | tf_op jit(solution)/shard_map/ppermute | solution.py:179
  9.0 5.5 %collective-permute-start.5 = (bf16[256,256]{1,0:T(8,128)(2,1)S(1)}, bf16[256,256]{1,0:T(8,128)(2,1)S(1)}, u32[]{:S(2)}, u32[]{:S(2)}) collective-permute-start(bf16[256,256]{1,0:T(8,128)(2,1)S(1)} %collective-permute-done.4.refs_4_), channel_id=1, source_target_pairs={{0,64},{16,80},{32,96},{48,112},{64,0},{80,16},{96,32},{112,48},{1... | collective-permute-start | bytes 393224 | tf_op jit(solution)/shard_map/ppermute | solution.py:179
  10.5 6.9 %collective-permute-start.7 = (bf16[256,256]{1,0:T(8,128)(2,1)S(1)}, bf16[256,256]{1,0:T(8,128)(2,1)S(1)}, u32[]{:S(2)}, u32[]{:S(2)}) collective-permute-start(bf16[256,256]{1,0:T(8,128)(2,1)S(1)} %collective-permute-done.refs_1_), channel_id=1, source_target_pairs={{0,48},{16,32},{32,16},{48,0},{64,112},{80,96},{96,80},{112,64},{1... | collective-permute-start | bytes 393224 | tf_op jit(solution)/shard_map/ppermute | solution.py:179
  14.5 5.0 %collective-permute-start.3 = (bf16[256,256]{1,0:T(8,128)(2,1)S(1)}, bf16[256,256]{1,0:T(8,128)(2,1)S(1)}, u32[]{:S(2)}, u32[]{:S(2)}) collective-permute-start(bf16[256,256]{1,0:T(8,128)(2,1)S(1)} %collective-permute-done.refs_1_), channel_id=1, source_target_pairs={{0,16},{16,0},{32,48},{48,32},{64,80},{80,64},{96,112},{112,96},{1... | collective-permute-start | bytes 393224 | tf_op jit(solution)/shard_map/ppermute | solution.py:179
  25.1 6.4 %collective-permute-start.9 = (bf16[4,256,256]{2,1,0:T(8,128)(2,1)S(1)}, bf16[4,256,256]{2,1,0:T(8,128)(2,1)S(1)}, u32[]{:S(2)}, u32[]{:S(2)}) collective-permute-start(bf16[4,256,256]{2,1,0:T(8,128)(2,1)S(1)} %diag_mate.1), channel_id=1, source_target_pairs={{0,1},{1,0},{18,19},{19,18},{36,37},{37,36},{54,55},{55,54},{72,73... | collective-permute-start | bytes 1572872 | tf_op jit(solution)/shard_map/ppermute | solution.py:233
  29.6 1.9 %collective-permute-start.8 = (bf16[2,256,256]{2,1,0:T(8,128)(2,1)S(1)}, bf16[2,256,256]{2,1,0:T(8,128)(2,1)S(1)}, u32[]{:S(2)}, u32[]{:S(2)}) collective-permute-start(bf16[2,256,256]{2,1,0:T(8,128)(2,1)S(1)} %coeff.1.own), channel_id=1, source_target_pairs={{0,1},{1,0},{2,3},{3,2},{4,5},{5,4},{6,7},{7,6},{8,9},{9,8},{10,11... | collective-permute-start | bytes 786440 | tf_op jit(solution)/shard_map/ppermute | solution.py:179
  31.9 7.2 %collective-permute-start.12 = (bf16[256,256]{1,0:T(8,128)(2,1)S(1)}, bf16[256,256]{1,0:T(8,128)(2,1)S(1)}, u32[]{:S(2)}, u32[]{:S(2)}) collective-permute-start(bf16[256,256]{1,0:T(8,128)(2,1)S(1)} %get-tuple-element.28), channel_id=1, source_target_pairs={{0,2},{1,3},{2,0},{3,1},{4,6},{5,7},{6,4},{7,5},{8,10},{9,11},{10,... | collective-permute-start | bytes 393224 | tf_op jit(solution)/shard_map/ppermute | solution.py:179
  32.3 8.6 %collective-permute-start.14 = (bf16[256,256]{1,0:T(8,128)(2,1)S(1)}, bf16[256,256]{1,0:T(8,128)(2,1)S(1)}, u32[]{:S(2)}, u32[]{:S(2)}) collective-permute-start(bf16[256,256]{1,0:T(8,128)(2,1)S(1)} %get-tuple-element.30), channel_id=1, source_target_pairs={{0,4},{1,5},{2,6},{3,7},{4,0},{5,1},{6,2},{7,3},{8,12},{9,13},{10,... | collective-permute-start | bytes 393224 | tf_op jit(solution)/shard_map/ppermute | solution.py:179
  33.9 7.0 %collective-permute-start.15 = (bf16[256,256]{1,0:T(8,128)(2,1)S(1)}, bf16[256,256]{1,0:T(8,128)(2,1)S(1)}, u32[]{:S(2)}, u32[]{:S(2)}) collective-permute-start(bf16[256,256]{1,0:T(8,128)(2,1)S(1)} %get-tuple-element.31), channel_id=1, source_target_pairs={{0,12},{1,13},{2,14},{3,15},{4,8},{5,9},{6,10},{7,11},{8,4},{9,5},... | collective-permute-start | bytes 393224 | tf_op jit(solution)/shard_map/ppermute | solution.py:179
  36.6 6.3 %collective-permute-start.10 = (bf16[256,256]{1,0:T(8,128)(2,1)S(1)}, bf16[256,256]{1,0:T(8,128)(2,1)S(1)}, u32[]{:S(2)}, u32[]{:S(2)}) collective-permute-start(bf16[256,256]{1,0:T(8,128)(2,1)S(1)} %get-tuple-element.25), channel_id=1, source_target_pairs={{0,4},{1,5},{2,6},{3,7},{4,0},{5,1},{6,2},{7,3},{8,12},{9,13},{10,... | collective-permute-start | bytes 393224 | tf_op jit(solution)/shard_map/ppermute | solution.py:179
  37.4 9.0 %collective-permute-start.11 = (bf16[256,256]{1,0:T(8,128)(2,1)S(1)}, bf16[256,256]{1,0:T(8,128)(2,1)S(1)}, u32[]{:S(2)}, u32[]{:S(2)}) collective-permute-start(bf16[256,256]{1,0:T(8,128)(2,1)S(1)} %get-tuple-element.26), channel_id=1, source_target_pairs={{0,12},{1,13},{2,14},{3,15},{4,8},{5,9},{6,10},{7,11},{8,4},{9,5},... | collective-permute-start | bytes 393224 | tf_op jit(solution)/shard_map/ppermute | solution.py:179
  39.1 7.2 %collective-permute-start.13 = (bf16[256,256]{1,0:T(8,128)(2,1)S(1)}, bf16[256,256]{1,0:T(8,128)(2,1)S(1)}, u32[]{:S(2)}, u32[]{:S(2)}) collective-permute-start(bf16[256,256]{1,0:T(8,128)(2,1)S(1)} %add_convert_fusion.5), channel_id=1, source_target_pairs={{0,8},{1,9},{2,10},{3,11},{4,12},{5,13},{6,14},{7,15},{8,0},{9,1},... | collective-permute-start | bytes 393224 | tf_op jit(solution)/shard_map/ppermute | solution.py:179
  41.0 6.6 %collective-permute-start.16 = (bf16[256,256]{1,0:T(8,128)(2,1)S(1)}, bf16[256,256]{1,0:T(8,128)(2,1)S(1)}, u32[]{:S(2)}, u32[]{:S(2)}) collective-permute-start(bf16[256,256]{1,0:T(8,128)(2,1)S(1)} %add_convert_fusion.4), channel_id=1, source_target_pairs={{0,2},{1,3},{2,0},{3,1},{4,6},{5,7},{6,4},{7,5},{8,10},{9,11},{10,... | collective-permute-start | bytes 393224 | tf_op jit(solution)/shard_map/ppermute | solution.py:179
  47.6 7.4 %collective-permute-start.20 = (bf16[256,256]{1,0:T(8,128)(2,1)S(1)}, bf16[256,256]{1,0:T(8,128)(2,1)S(1)}, u32[]{:S(2)}, u32[]{:S(2)}) collective-permute-start(bf16[256,256]{1,0:T(8,128)(2,1)S(1)} %add_convert_fusion.3.refs_0_), channel_id=1, source_target_pairs={{0,8},{1,9},{2,10},{3,11},{4,12},{5,13},{6,14},{7,15},{8,0},{9,1},... | collective-permute-start | bytes 393224 | tf_op jit(solution)/shard_map/ppermute | solution.py:179
  49.6 7.8 %collective-permute-start.17 = (bf16[256,256]{1,0:T(8,128)(2,1)S(1)}, bf16[256,256]{1,0:T(8,128)(2,1)S(1)}, u32[]{:S(2)}, u32[]{:S(2)}) collective-permute-start(bf16[256,256]{1,0:T(8,128)(2,1)S(1)} %add_convert_fusion.3.refs_0_), channel_id=1, source_target_pairs={{0,2},{1,3},{2,0},{3,1},{4,6},{5,7},{6,4},{7,5},{8,10},{9,11},{10,... | collective-permute-start | bytes 393224 | tf_op jit(solution)/shard_map/ppermute | solution.py:179
  51.3 7.5 %collective-permute-start.22 = (bf16[256,256]{1,0:T(8,128)(2,1)S(1)}, bf16[256,256]{1,0:T(8,128)(2,1)S(1)}, u32[]{:S(2)}, u32[]{:S(2)}) collective-permute-start(bf16[256,256]{1,0:T(8,128)(2,1)S(1)} %add_convert_fusion.3.refs_0_), channel_id=1, source_target_pairs={{0,12},{1,13},{2,14},{3,15},{4,8},{5,9},{6,10},{7,11},{8,4},{9,5},... | collective-permute-start | bytes 393224 | tf_op jit(solution)/shard_map/ppermute | solution.py:179
  53.5 5.3 %collective-permute-start.18 = (bf16[256,256]{1,0:T(8,128)(2,1)S(1)}, bf16[256,256]{1,0:T(8,128)(2,1)S(1)}, u32[]{:S(2)}, u32[]{:S(2)}) collective-permute-start(bf16[256,256]{1,0:T(8,128)(2,1)S(1)} %add_convert_fusion.3.refs_0_), channel_id=1, source_target_pairs={{0,4},{1,5},{2,6},{3,7},{4,0},{5,1},{6,2},{7,3},{8,12},{9,13},{10,... | collective-permute-start | bytes 393224 | tf_op jit(solution)/shard_map/ppermute | solution.py:179
  55.0 6.5 %collective-permute-start.21 = (bf16[256,256]{1,0:T(8,128)(2,1)S(1)}, bf16[256,256]{1,0:T(8,128)(2,1)S(1)}, u32[]{:S(2)}, u32[]{:S(2)}) collective-permute-start(bf16[256,256]{1,0:T(8,128)(2,1)S(1)} %collective-permute-done.20.refs_4_), channel_id=1, source_target_pairs={{0,2},{1,3},{2,0},{3,1},{4,6},{5,7},{6,4},{7,5},{8,10},{9,11},{10,... | collective-permute-start | bytes 393224 | tf_op jit(solution)/shard_map/ppermute | solution.py:179
  57.4 6.2 %collective-permute-start.23 = (bf16[256,256]{1,0:T(8,128)(2,1)S(1)}, bf16[256,256]{1,0:T(8,128)(2,1)S(1)}, u32[]{:S(2)}, u32[]{:S(2)}) collective-permute-start(bf16[256,256]{1,0:T(8,128)(2,1)S(1)} %collective-permute-done.17.refs_1_), channel_id=1, source_target_pairs={{0,12},{1,13},{2,14},{3,15},{4,8},{5,9},{6,10},{7,11},{8,4},{9,5},... | collective-permute-start | bytes 393224 | tf_op jit(solution)/shard_map/ppermute | solution.py:179
  58.8 5.0 %collective-permute-start.19 = (bf16[256,256]{1,0:T(8,128)(2,1)S(1)}, bf16[256,256]{1,0:T(8,128)(2,1)S(1)}, u32[]{:S(2)}, u32[]{:S(2)}) collective-permute-start(bf16[256,256]{1,0:T(8,128)(2,1)S(1)} %collective-permute-done.17.refs_1_), channel_id=1, source_target_pairs={{0,4},{1,5},{2,6},{3,7},{4,0},{5,1},{6,2},{7,3},{8,12},{9,13},{10,... | collective-permute-start | bytes 393224 | tf_op jit(solution)/shard_map/ppermute | solution.py:179
  63.8 4.7 %collective-permute-start.25 = (bf16[4,256,256]{2,1,0:T(8,128)(2,1)S(1)}, bf16[4,256,256]{2,1,0:T(8,128)(2,1)S(1)}, u32[]{:S(2)}, u32[]{:S(2)}) collective-permute-start(bf16[4,256,256]{2,1,0:T(8,128)(2,1)S(1)} %pack.1), channel_id=1, source_target_pairs={{0,1},{1,0},{18,19},{19,18},{36,37},{37,36},{54,55},{55,54},{72,73... | collective-permute-start | bytes 1572872 | tf_op jit(solution)/shard_map/ppermute | solution.py:248
  69.5 5.8 %collective-permute-start.28 = (bf16[256,256]{1,0:T(8,128)(2,1)S(1)}, bf16[256,256]{1,0:T(8,128)(2,1)S(1)}, u32[]{:S(2)}, u32[]{:S(2)}) collective-permute-start(bf16[256,256]{1,0:T(8,128)(2,1)S(1)} %get-tuple-element.38), channel_id=1, source_target_pairs={{0,64},{16,80},{32,96},{48,112},{64,0},{80,16},{96,32},{112,48},{1... | collective-permute-start | bytes 393224 | tf_op jit(solution)/shard_map/ppermute | solution.py:179
  69.9 7.2 %collective-permute-start.30 = (bf16[256,256]{1,0:T(8,128)(2,1)S(1)}, bf16[256,256]{1,0:T(8,128)(2,1)S(1)}, u32[]{:S(2)}, u32[]{:S(2)}) collective-permute-start(bf16[256,256]{1,0:T(8,128)(2,1)S(1)} %get-tuple-element.40), channel_id=1, source_target_pairs={{0,16},{16,0},{32,48},{48,32},{64,80},{80,64},{96,112},{112,96},{1... | collective-permute-start | bytes 393224 | tf_op jit(solution)/shard_map/ppermute | solution.py:179
  70.3 6.8 %collective-permute-start.31 = (bf16[256,256]{1,0:T(8,128)(2,1)S(1)}, bf16[256,256]{1,0:T(8,128)(2,1)S(1)}, u32[]{:S(2)}, u32[]{:S(2)}) collective-permute-start(bf16[256,256]{1,0:T(8,128)(2,1)S(1)} %get-tuple-element.41), channel_id=1, source_target_pairs={{0,48},{16,32},{32,16},{48,0},{64,112},{80,96},{96,80},{112,64},{1... | collective-permute-start | bytes 393224 | tf_op jit(solution)/shard_map/ppermute | solution.py:179
  72.8 6.2 %collective-permute-start.26 = (bf16[256,256]{1,0:T(8,128)(2,1)S(1)}, bf16[256,256]{1,0:T(8,128)(2,1)S(1)}, u32[]{:S(2)}, u32[]{:S(2)}) collective-permute-start(bf16[256,256]{1,0:T(8,128)(2,1)S(1)} %get-tuple-element.35), channel_id=1, source_target_pairs={{0,16},{16,0},{32,48},{48,32},{64,80},{80,64},{96,112},{112,96},{1... | collective-permute-start | bytes 393224 | tf_op jit(solution)/shard_map/ppermute | solution.py:179
  73.6 9.0 %collective-permute-start.27 = (bf16[256,256]{1,0:T(8,128)(2,1)S(1)}, bf16[256,256]{1,0:T(8,128)(2,1)S(1)}, u32[]{:S(2)}, u32[]{:S(2)}) collective-permute-start(bf16[256,256]{1,0:T(8,128)(2,1)S(1)} %get-tuple-element.36), channel_id=1, source_target_pairs={{0,48},{16,32},{32,16},{48,0},{64,112},{80,96},{96,80},{112,64},{1... | collective-permute-start | bytes 393224 | tf_op jit(solution)/shard_map/ppermute | solution.py:179
  75.4 7.3 %collective-permute-start.29 = (bf16[256,256]{1,0:T(8,128)(2,1)S(1)}, bf16[256,256]{1,0:T(8,128)(2,1)S(1)}, u32[]{:S(2)}, u32[]{:S(2)}) collective-permute-start(bf16[256,256]{1,0:T(8,128)(2,1)S(1)} %add_convert_fusion.2), channel_id=1, source_target_pairs={{0,32},{16,48},{32,0},{48,16},{64,96},{80,112},{96,64},{112,80},{1... | collective-permute-start | bytes 393224 | tf_op jit(solution)/shard_map/ppermute | solution.py:179
  77.2 5.5 %collective-permute-start.32 = (bf16[256,256]{1,0:T(8,128)(2,1)S(1)}, bf16[256,256]{1,0:T(8,128)(2,1)S(1)}, u32[]{:S(2)}, u32[]{:S(2)}) collective-permute-start(bf16[256,256]{1,0:T(8,128)(2,1)S(1)} %add_convert_fusion.1), channel_id=1, source_target_pairs={{0,64},{16,80},{32,96},{48,112},{64,0},{80,16},{96,32},{112,48},{1... | collective-permute-start | bytes 393224 | tf_op jit(solution)/shard_map/ppermute | solution.py:179
  (10 other events, 44.6 us)

commit v4 on v3

--- a/solution.py
+++ b/solution.py
@@ -160,6 +160,39 @@
             rows = rows_of(piece)
             rest = total(dot(y_mate[q], dense[rows_of(2 * q + 1 - info.core), rows]) for q in range(4))
             out[...] = (low(rows) + dense_sum[piece] + rest).astype(BF16)
+
+
+def load_kernel(right, signal, dense, right_out, signal_out, dense_out, sems):
+    copies = [
+        pltpu.make_async_copy(right, right_out, sems.at[0]),
+        pltpu.make_async_copy(signal, signal_out, sems.at[1]),
+    ]
+    for copy in copies:
+        copy.start()
+
+    @pl.when(Place().owner)
+    def _():
+        blocks = [pltpu.make_async_copy(dense.at[rows_of(p), :], dense_out.at[rows_of(p), :], sems.at[2 + p]) for p in range(8)]
+        for block in blocks:
+            block.start()
+        for block in blocks:
+            block.wait()
+
+    for copy in copies:
+        copy.wait()
+
+
+def load(*arrays):
+    return pl.pallas_call(
+        load_kernel,
+        name="load",
+        out_shape=[pltpu.VMEM(v.shape, v.dtype) for v in arrays],
+        in_specs=[pl.BlockSpec(memory_space=pltpu.HBM)] * len(arrays),
+        out_specs=[VMEM] * len(arrays),
+        scratch_shapes=[pltpu.SemaphoreType.DMA((10,))],
+        compiler_params=pltpu.CompilerParams(vmem_limit_bytes=16 * 2**20),
+        cost_estimate=pl.CostEstimate(flops=0, bytes_accessed=20 * 2**20, transcendentals=0),
+    )(*(pltpu.with_memory_space_constraint(v, pltpu.HBM) for v in arrays))
 
 
 def call(kernel, name, operands, outs, flops, moved, buckets=None):
@@ -179,18 +212,20 @@
     return lax.ppermute(x, axis, [(i, i ^ bits) for i in range(size)])
 
 
-def gather(own, axis, ring, side, first=None):
+def gather(own, axis, ring, side, first=None, loaded=()):
     got = {(0, 0): own}
     got[(0, 1)] = swap(own, axis, side)
     if first is not None:
         got[(0, 1)], first = lax.optimization_barrier((got[(0, 1)], first))
     got[(2, 0)] = swap(own, axis, 2 * ring)
+    if first is not None:
+        got[(2, 0)], *loaded = lax.optimization_barrier((got[(2, 0)], *loaded))
     got[(1, 0)] = swap(own, axis, ring)
     got[(3, 0)] = swap(own, axis, 3 * ring)
     got[(1, 1)] = swap(got[(0, 1)], axis, ring)
     got[(3, 1)] = swap(got[(0, 1)], axis, 3 * ring)
     got[(2, 1)] = swap(got[(2, 0)], axis, side)
-    return [got[rel] for rel in REL], first
+    return [got[rel] for rel in REL], first, loaded
 
 
 def add(*parts):
@@ -226,7 +261,8 @@
     eight_wide = jax.ShapeDtypeStruct((8, count, PIECE), F32)
 
     left_mate = swap(left, "tcol", 1)
-    x, left_mate = gather(signal, "trow", 1, 4, left_mate)
+    x, left_mate, loaded = gather(signal, "trow", 1, 4, left_mate, load(right, signal, dense))
+    right, x[0], dense = loaded
     (coeff,) = call(coeff_kernel, "coeff", [*x, right], [pair], 16 * unit, 10 * size + 2**21, buckets)
     coeff_mate = swap(coeff, "tcol", 1)
     (dense_sent,) = call(functools.partial(diag_kernel, 1), "diag_mate", [*x, dense], [four], 32 * unit, 12 * size + 2**23)
@@ -243,7 +279,7 @@
             2 * len(rels) * size + 2**21,
         )
     first = scatter(terms, "tcol", 4, 2)
-    y, _ = gather(first, "tcol", 4, 2)
+    y, _, _ = gather(first, "tcol", 4, 2)
     (y_sent,) = call(pack_kernel, "pack", y, [four], 0, 12 * size)
     y_mate = lax.ppermute(y_sent, ("trow", "tcol"), owners)
     own, mate = call(back_kernel, "back", [*y, left, left_mate], [pair_wide, pair], 16 * unit, 14 * size + 2**21)

time: 83.6 us -> 77.4 us (0.926)
  local copies, waits for them, and re-layouts: 5.9 us -> 0.02 us
  Pallas kernels: 8.58 us -> 12.7 us
  waiting for transfers between devices: 23.6 us -> 20.6 us
  starting transfers between devices: 43.4 us -> 42 us
    unnamed x18 -> x6, local copies, waits for them, and re-layouts: 5.9 us -> 0.02 us
    pallas_call x0 -> x1, Pallas kernels: none -> 4.12 us  [load(): pl.pallas_call(load_kernel, name='load', out_shape=[pltpu.VMEM(v.shape, v...]
    ppermute x31, waiting for transfers between devices: 23.6 us -> 20.6 us  [swap(): return lax.ppermute(x, axis, [(i, i ^ bits) for i in range(size)])]
    ppermute x31, starting transfers between devices: 39.2 us -> 38 us  [swap(): return lax.ppermute(x, axis, [(i, i ^ bits) for i in range(size)])]
  transfers between devices with their start and end apart: 33 -> 33, of which waited for: 13 -> 14; matrix products, arithmetic and copies ran while one was open for 0% -> 0% of each run, Pallas kernels for 7% -> 13%
where the time goes in v4:
time: 77.4 us; the launch traced here: 77.2 us
  starting transfers between devices  42 us (54%)
  waiting for transfers between devices  20.6 us (27%)
  Pallas kernels  12.7 us (16%)
  other arithmetic  1 us (1%)
  between operations  0.9 us (1%)
    ppermute x31, starting transfers between devices, swap(): return lax.ppermute(x, axis, [(i, i ^ bits) for i in range(size)])  38 us
    ppermute x31, waiting for transfers between devices, swap(): return lax.ppermute(x, axis, [(i, i ^ bits) for i in range(size)])  20.6 us
    pallas_call x10, Pallas kernels, call(): pl.pallas_call(kernel, name=name, out_shape=outs, in_specs=[VMEM] * (len(...  8.56 us
    pallas_call x1, Pallas kernels, load(): pl.pallas_call(load_kernel, name='load', out_shape=[pltpu.VMEM(v.shape, v...  4.12 us
    ppermute x1, starting transfers between devices, body(): y_mate = lax.ppermute(y_sent, ('trow', 'tcol'), owners)  2.1 us
    ppermute x1, starting transfers between devices, body(): dense_mate = lax.ppermute(dense_sent, ('trow', 'tcol'), owners)  1.92 us
  transfers between devices with their start and end apart: 33, of which 14 were waited for; matrix products, arithmetic and copies ran while one was open for 0% of the time, Pallas kernels for 13%

profile of v4, /device:TPU:0, one launch (start us, length us, event | category | flops | bytes accessed | tf_op | source)
XLA Modules:
  0.0 77.2 jit_solution(9881402490450502690)
XLA Ops:
  0.7 4.0 %collective-permute-start = (bf16[256,256]{1,0:T(8,128)(2,1)}, bf16[256,256]{1,0:T(8,128)(2,1)S(1)}, u32[]{:S(2)}, u32[]{:S(2)}) collective-permute-start(bf16[256,256]{1,0:T(8,128)(2,1)} %signal.1), channel_id=1, source_target_pairs={{0,32},{16,48},{32,0},{48,16},{64,96},{80,112},{96,64},{112,80},{1... | collective-permute-start | bytes 393224 | tf_op jit(solution)/shard_map/ppermute | solution.py:212
  4.8 1.5 %collective-permute-start.1 = (bf16[256,256]{1,0:T(8,128)(2,1)}, bf16[256,256]{1,0:T(8,128)(2,1)S(1)}, u32[]{:S(2)}, u32[]{:S(2)}) collective-permute-start(bf16[256,256]{1,0:T(8,128)(2,1)} %signal.1), channel_id=1, source_target_pairs={{0,64},{16,80},{32,96},{48,112},{64,0},{80,16},{96,32},{112,48},{1... | collective-permute-start | bytes 393224 | tf_op jit(solution)/shard_map/ppermute | solution.py:212
  7.3 4.1 %load.1 = (bf16[2,2048,256]{2,1,0:T(8,128)(2,1)S(1)}, bf16[256,256]{1,0:T(8,128)(2,1)S(1)}, bf16[2048,2048]{1,0:T(8,128)(2,1)S(1)}) custom-call(bf16[2,2048,256]{2,1,0:T(8,128)(2,1)} %bitcast.12, bf16[256,256]{1,0:T(8,128)(2,1)} %signal.1, bf16[2048,2048]{1,0:T(8,128)(2,1)} %bitcast.11), custom_call_target="tpu_custom_call" | custom-call | bytes 20971520 | tf_op jit(solution)/shard_map/load/pallas_call | solution.py:186
  11.5 2.9 %collective-permute-start.7 = (bf16[256,256]{1,0:T(8,128)(2,1)S(1)}, bf16[256,256]{1,0:T(8,128)(2,1)S(1)}, u32[]{:S(2)}, u32[]{:S(2)}) collective-permute-start(bf16[256,256]{1,0:T(8,128)(2,1)S(1)} %collective-permute-done.1.refs_1_), channel_id=1, source_target_pairs={{0,48},{16,32},{32,16},{48,0},{64,112},{80,96},{96,80},{112,64},{1... | collective-permute-start | bytes 393224 | tf_op jit(solution)/shard_map/ppermute | solution.py:212
  14.5 2.0 %collective-permute-done.5.refs_5_ = bf16[256,256]{1,0:T(8,128)(2,1)S(1)} collective-permute-done((bf16[256,256]{1,0:T(8,128)(2,1)S(1)}, bf16[256,256]{1,0:T(8,128)(2,1)S(1)}, u32[]{:S(2)}, u32[]{:S(2)}) %collective-permute-start.5) | collective-permute-done | bytes 131104 | tf_op jit(solution)/shard_map/ppermute | solution.py:212
  16.5 1.3 %collective-permute-done.7.refs_7_ = bf16[256,256]{1,0:T(8,128)(2,1)S(1)} collective-permute-done((bf16[256,256]{1,0:T(8,128)(2,1)S(1)}, bf16[256,256]{1,0:T(8,128)(2,1)S(1)}, u32[]{:S(2)}, u32[]{:S(2)}) %collective-permute-start.7) | collective-permute-done | bytes 131104 | tf_op jit(solution)/shard_map/ppermute | solution.py:212
  17.8 1.6 %collective-permute-done.4.refs_3_ = bf16[256,256]{1,0:T(8,128)(2,1)S(1)} collective-permute-done((bf16[256,256]{1,0:T(8,128)(2,1)S(1)}, bf16[256,256]{1,0:T(8,128)(2,1)S(1)}, u32[]{:S(2)}, u32[]{:S(2)}) %collective-permute-start.4) | collective-permute-done | bytes 131104 | tf_op jit(solution)/shard_map/ppermute | solution.py:212
  19.5 1.3 %diag_mate.1 = bf16[4,256,256]{2,1,0:T(8,128)(2,1)S(1)} custom-call(bf16[256,256]{1,0:T(8,128)(2,1)S(1)} %get-tuple-element.32.refs_0_, bf16[256,256]{1,0:T(8,128)(2,1)S(1)} %collective-permute-done.1.refs_1_, bf16[256,256]{1,0:T(8,128)(2,1)S(1)} %collective-permute-done.3.refs_2_, bf16[256,256]{1,0:T(8,128)(2,1)S(1)} %collective-permute-done.4.refs_3_, ...), custom_call_target="tpu_custom_call" | custom-call | flops 1073741824 | bytes 9961472 | tf_op jit(solution)/shard_map/diag_mate/pallas_call | solution.py:199
  20.8 1.9 %collective-permute-start.9 = (bf16[4,256,256]{2,1,0:T(8,128)(2,1)S(1)}, bf16[4,256,256]{2,1,0:T(8,128)(2,1)S(1)}, u32[]{:S(2)}, u32[]{:S(2)}) collective-permute-start(bf16[4,256,256]{2,1,0:T(8,128)(2,1)S(1)} %diag_mate.1), channel_id=1, source_target_pairs={{0,1},{1,0},{18,19},{19,18},{36,37},{37,36},{54,55},{55,54},{72,73... | collective-permute-start | bytes 1572872 | tf_op jit(solution)/shard_map/ppermute | solution.py:269
  24.0 1.3 %diag_own.1.dense_own = bf16[4,256,256]{2,1,0:T(8,128)(2,1)S(1)} custom-call(bf16[256,256]{1,0:T(8,128)(2,1)S(1)} %get-tuple-element.32.refs_0_, bf16[256,256]{1,0:T(8,128)(2,1)S(1)} %collective-permute-done.1.refs_1_, bf16[256,256]{1,0:T(8,128)(2,1)S(1)} %collective-permute-done.3.refs_2_, bf16[256,256]{1,0:T(8,128)(2,1)S(1)} %collective-permute-done.4.refs_3_, ...), custom_call_target="tpu_custom_call" | custom-call | flops 1073741824 | bytes 9961472 | tf_op jit(solution)/shard_map/diag_own/pallas_call | solution.py:199
  25.9 1.5 %collective-permute-start.14 = (bf16[256,256]{1,0:T(8,128)(2,1)S(1)}, bf16[256,256]{1,0:T(8,128)(2,1)S(1)}, u32[]{:S(2)}, u32[]{:S(2)}) collective-permute-start(bf16[256,256]{1,0:T(8,128)(2,1)S(1)} %get-tuple-element.44), channel_id=1, source_target_pairs={{0,4},{1,5},{2,6},{3,7},{4,0},{5,1},{6,2},{7,3},{8,12},{9,13},{10,... | collective-permute-start | bytes 393224 | tf_op jit(solution)/shard_map/ppermute | solution.py:212
  27.3 2.2 %collective-permute-start.15 = (bf16[256,256]{1,0:T(8,128)(2,1)S(1)}, bf16[256,256]{1,0:T(8,128)(2,1)S(1)}, u32[]{:S(2)}, u32[]{:S(2)}) collective-permute-start(bf16[256,256]{1,0:T(8,128)(2,1)S(1)} %get-tuple-element.45), channel_id=1, source_target_pairs={{0,12},{1,13},{2,14},{3,15},{4,8},{5,9},{6,10},{7,11},{8,4},{9,5},... | collective-permute-start | bytes 393224 | tf_op jit(solution)/shard_map/ppermute | solution.py:212
  30.1 1.3 %collective-permute-start.10 = (bf16[256,256]{1,0:T(8,128)(2,1)S(1)}, bf16[256,256]{1,0:T(8,128)(2,1)S(1)}, u32[]{:S(2)}, u32[]{:S(2)}) collective-permute-start(bf16[256,256]{1,0:T(8,128)(2,1)S(1)} %get-tuple-element.39), channel_id=1, source_target_pairs={{0,4},{1,5},{2,6},{3,7},{4,0},{5,1},{6,2},{7,3},{8,12},{9,13},{10,... | collective-permute-start | bytes 393224 | tf_op jit(solution)/shard_map/ppermute | solution.py:212
  31.9 1.0 %collective-permute-done.12 = bf16[256,256]{1,0:T(8,128)(2,1)S(1)} collective-permute-done((bf16[256,256]{1,0:T(8,128)(2,1)S(1)}, bf16[256,256]{1,0:T(8,128)(2,1)S(1)}, u32[]{:S(2)}, u32[]{:S(2)}) %collective-permute-start.12) | collective-permute-done | bytes 131104 | tf_op jit(solution)/shard_map/ppermute | solution.py:212
  33.0 1.4 %collective-permute-start.13 = (bf16[256,256]{1,0:T(8,128)(2,1)S(1)}, bf16[256,256]{1,0:T(8,128)(2,1)S(1)}, u32[]{:S(2)}, u32[]{:S(2)}) collective-permute-start(bf16[256,256]{1,0:T(8,128)(2,1)S(1)} %add_convert_fusion.5), channel_id=1, source_target_pairs={{0,8},{1,9},{2,10},{3,11},{4,12},{5,13},{6,14},{7,15},{8,0},{9,1},... | collective-permute-start | bytes 393224 | tf_op jit(solution)/shard_map/ppermute | solution.py:212
  34.4 2.3 %collective-permute-start.16 = (bf16[256,256]{1,0:T(8,128)(2,1)S(1)}, bf16[256,256]{1,0:T(8,128)(2,1)S(1)}, u32[]{:S(2)}, u32[]{:S(2)}) collective-permute-start(bf16[256,256]{1,0:T(8,128)(2,1)S(1)} %add_convert_fusion.4), channel_id=1, source_target_pairs={{0,2},{1,3},{2,0},{3,1},{4,6},{5,7},{6,4},{7,5},{8,10},{9,11},{10,... | collective-permute-start | bytes 393224 | tf_op jit(solution)/shard_map/ppermute | solution.py:212
  36.7 3.5 %collective-permute-done.11 = bf16[256,256]{1,0:T(8,128)(2,1)S(1)} collective-permute-done((bf16[256,256]{1,0:T(8,128)(2,1)S(1)}, bf16[256,256]{1,0:T(8,128)(2,1)S(1)}, u32[]{:S(2)}, u32[]{:S(2)}) %collective-permute-start.11) | collective-permute-done | bytes 131104 | tf_op jit(solution)/shard_map/ppermute | solution.py:212
  41.1 2.8 %collective-permute-start.20 = (bf16[256,256]{1,0:T(8,128)(2,1)S(1)}, bf16[256,256]{1,0:T(8,128)(2,1)S(1)}, u32[]{:S(2)}, u32[]{:S(2)}) collective-permute-start(bf16[256,256]{1,0:T(8,128)(2,1)S(1)} %add_convert_fusion.3.refs_0_), channel_id=1, source_target_pairs={{0,8},{1,9},{2,10},{3,11},{4,12},{5,13},{6,14},{7,15},{8,0},{9,1},... | collective-permute-start | bytes 393224 | tf_op jit(solution)/shard_map/ppermute | solution.py:212
  43.9 1.2 %collective-permute-start.17 = (bf16[256,256]{1,0:T(8,128)(2,1)S(1)}, bf16[256,256]{1,0:T(8,128)(2,1)S(1)}, u32[]{:S(2)}, u32[]{:S(2)}) collective-permute-start(bf16[256,256]{1,0:T(8,128)(2,1)S(1)} %add_convert_fusion.3.refs_0_), channel_id=1, source_target_pairs={{0,2},{1,3},{2,0},{3,1},{4,6},{5,7},{6,4},{7,5},{8,10},{9,11},{10,... | collective-permute-start | bytes 393224 | tf_op jit(solution)/shard_map/ppermute | solution.py:212
  45.1 2.2 %collective-permute-start.22 = (bf16[256,256]{1,0:T(8,128)(2,1)S(1)}, bf16[256,256]{1,0:T(8,128)(2,1)S(1)}, u32[]{:S(2)}, u32[]{:S(2)}) collective-permute-start(bf16[256,256]{1,0:T(8,128)(2,1)S(1)} %add_convert_fusion.3.refs_0_), channel_id=1, source_target_pairs={{0,12},{1,13},{2,14},{3,15},{4,8},{5,9},{6,10},{7,11},{8,4},{9,5},... | collective-permute-start | bytes 393224 | tf_op jit(solution)/shard_map/ppermute | solution.py:212
  48.1 2.4 %collective-permute-start.21 = (bf16[256,256]{1,0:T(8,128)(2,1)S(1)}, bf16[256,256]{1,0:T(8,128)(2,1)S(1)}, u32[]{:S(2)}, u32[]{:S(2)}) collective-permute-start(bf16[256,256]{1,0:T(8,128)(2,1)S(1)} %collective-permute-done.20.refs_4_), channel_id=1, source_target_pairs={{0,2},{1,3},{2,0},{3,1},{4,6},{5,7},{6,4},{7,5},{8,10},{9,11},{10,... | collective-permute-start | bytes 393224 | tf_op jit(solution)/shard_map/ppermute | solution.py:212
  51.0 1.3 %collective-permute-start.23 = (bf16[256,256]{1,0:T(8,128)(2,1)S(1)}, bf16[256,256]{1,0:T(8,128)(2,1)S(1)}, u32[]{:S(2)}, u32[]{:S(2)}) collective-permute-start(bf16[256,256]{1,0:T(8,128)(2,1)S(1)} %collective-permute-done.17.refs_1_), channel_id=1, source_target_pairs={{0,12},{1,13},{2,14},{3,15},{4,8},{5,9},{6,10},{7,11},{8,4},{9,5},... | collective-permute-start | bytes 393224 | tf_op jit(solution)/shard_map/ppermute | solution.py:212
  52.5 2.1 %collective-permute-done.21.refs_5_ = bf16[256,256]{1,0:T(8,128)(2,1)S(1)} collective-permute-done((bf16[256,256]{1,0:T(8,128)(2,1)S(1)}, bf16[256,256]{1,0:T(8,128)(2,1)S(1)}, u32[]{:S(2)}, u32[]{:S(2)}) %collective-permute-start.21) | collective-permute-done | bytes 131104 | tf_op jit(solution)/shard_map/ppermute | solution.py:212
  54.6 2.6 %collective-permute-done.23.refs_7_ = bf16[256,256]{1,0:T(8,128)(2,1)S(1)} collective-permute-done((bf16[256,256]{1,0:T(8,128)(2,1)S(1)}, bf16[256,256]{1,0:T(8,128)(2,1)S(1)}, u32[]{:S(2)}, u32[]{:S(2)}) %collective-permute-start.23) | collective-permute-done | bytes 131104 | tf_op jit(solution)/shard_map/ppermute | solution.py:212
  57.4 2.1 %collective-permute-start.25 = (bf16[4,256,256]{2,1,0:T(8,128)(2,1)S(1)}, bf16[4,256,256]{2,1,0:T(8,128)(2,1)S(1)}, u32[]{:S(2)}, u32[]{:S(2)}) collective-permute-start(bf16[4,256,256]{2,1,0:T(8,128)(2,1)S(1)} %pack.1), channel_id=1, source_target_pairs={{0,1},{1,0},{18,19},{19,18},{36,37},{37,36},{54,55},{55,54},{72,73... | collective-permute-start | bytes 1572872 | tf_op jit(solution)/shard_map/ppermute | solution.py:284
  60.8 1.3 %diag_back.1.dense_sum = f32[8,256,256]{2,1,0:T(8,128)S(1)} custom-call(bf16[256,256]{1,0:T(8,128)(2,1)S(1)} %add_convert_fusion.3.refs_0_, bf16[256,256]{1,0:T(8,128)(2,1)S(1)} %collective-permute-done.17.refs_1_, bf16[256,256]{1,0:T(8,128)(2,1)S(1)} %collective-permute-done.18.refs_2_, bf16[256,256]{1,0:T(8,128)(2,1)S(1)} %collective-permute-done.19.refs_3_, ...), custom_call_target="tpu_custom_call" | custom-call | flops 1073741824 | bytes 7340032 | tf_op jit(solution)/shard_map/diag_back/pallas_call | solution.py:199
  64.2 1.2 %collective-permute-start.31 = (bf16[256,256]{1,0:T(8,128)(2,1)S(1)}, bf16[256,256]{1,0:T(8,128)(2,1)S(1)}, u32[]{:S(2)}, u32[]{:S(2)}) collective-permute-start(bf16[256,256]{1,0:T(8,128)(2,1)S(1)} %get-tuple-element.55), channel_id=1, source_target_pairs={{0,48},{16,32},{32,16},{48,0},{64,112},{80,96},{96,80},{112,64},{1... | collective-permute-start | bytes 393224 | tf_op jit(solution)/shard_map/ppermute | solution.py:212
  65.3 1.3 %second.2 = (bf16[256,256]{1,0:T(8,128)(2,1)S(1)}, bf16[256,256]{1,0:T(8,128)(2,1)S(1)}, bf16[256,256]{1,0:T(8,128)(2,1)S(1)}, bf16[256,256]{1,0:T(8,128)(2,1)S(1)}, bf16[256,256]{1,0:T(8,128)(2,1)S(1)}) custom-call(s32[1,2]{1,0:T(1,128)S(1)} %bitcast.10, f32[2,256,256]{2,1,0:T(8,128)S(1)} %get-tuple-element.46.own, ...), custom_call_target="tpu_custom_call" | custom-call | flops 1006632960 | bytes 5767168 | tf_op jit(solution)/shard_map/second/pallas_call | solution.py:199
  67.5 1.7 %collective-permute-start.27 = (bf16[256,256]{1,0:T(8,128)(2,1)S(1)}, bf16[256,256]{1,0:T(8,128)(2,1)S(1)}, u32[]{:S(2)}, u32[]{:S(2)}) collective-permute-start(bf16[256,256]{1,0:T(8,128)(2,1)S(1)} %get-tuple-element.50), channel_id=1, source_target_pairs={{0,48},{16,32},{32,16},{48,0},{64,112},{80,96},{96,80},{112,64},{1... | collective-permute-start | bytes 393224 | tf_op jit(solution)/shard_map/ppermute | solution.py:212
  69.2 1.7 %collective-permute-start.29 = (bf16[256,256]{1,0:T(8,128)(2,1)S(1)}, bf16[256,256]{1,0:T(8,128)(2,1)S(1)}, u32[]{:S(2)}, u32[]{:S(2)}) collective-permute-start(bf16[256,256]{1,0:T(8,128)(2,1)S(1)} %add_convert_fusion.2), channel_id=1, source_target_pairs={{0,32},{16,48},{32,0},{48,16},{64,96},{80,112},{96,64},{112,80},{1... | collective-permute-start | bytes 393224 | tf_op jit(solution)/shard_map/ppermute | solution.py:212
  71.0 1.4 %collective-permute-start.32 = (bf16[256,256]{1,0:T(8,128)(2,1)S(1)}, bf16[256,256]{1,0:T(8,128)(2,1)S(1)}, u32[]{:S(2)}, u32[]{:S(2)}) collective-permute-start(bf16[256,256]{1,0:T(8,128)(2,1)S(1)} %add_convert_fusion.1), channel_id=1, source_target_pairs={{0,64},{16,80},{32,96},{48,112},{64,0},{80,16},{96,32},{112,48},{1... | collective-permute-start | bytes 393224 | tf_op jit(solution)/shard_map/ppermute | solution.py:212
  72.8 3.7 %collective-permute-done.27 = bf16[256,256]{1,0:T(8,128)(2,1)S(1)} collective-permute-done((bf16[256,256]{1,0:T(8,128)(2,1)S(1)}, bf16[256,256]{1,0:T(8,128)(2,1)S(1)}, u32[]{:S(2)}, u32[]{:S(2)}) %collective-permute-start.27) | collective-permute-done | bytes 131104 | tf_op jit(solution)/shard_map/ppermute | solution.py:212
  (57 shorter events, 12.1 us)
Async XLA Ops:
  0.6 10.9 %collective-permute-start.2 = (bf16[2,2048,256]{2,1,0:T(8,128)(2,1)}, bf16[2,2048,256]{2,1,0:T(8,128)(2,1)S(1)}, u32[]{:S(2)}, u32[]{:S(2)}) collective-permute-start(bf16[2,2048,256]{2,1,0:T(8,128)(2,1)} %bitcast.4), channel_id=1, source_target_pairs={{0,1},{1,0},{2,3},{3,2},{4,5},{5,4},{6,7},{7,6},{8,9},{9,8},{10,11... | collective-permute-start | bytes 6291464 | tf_op jit(solution)/shard_map/ppermute | solution.py:212
  0.7 10.7 %collective-permute-start = (bf16[256,256]{1,0:T(8,128)(2,1)}, bf16[256,256]{1,0:T(8,128)(2,1)S(1)}, u32[]{:S(2)}, u32[]{:S(2)}) collective-permute-start(bf16[256,256]{1,0:T(8,128)(2,1)} %signal.1), channel_id=1, source_target_pairs={{0,32},{16,48},{32,0},{48,16},{64,96},{80,112},{96,64},{112,80},{1... | collective-permute-start | bytes 393224 | tf_op jit(solution)/shard_map/ppermute | solution.py:212
  4.8 6.8 %collective-permute-start.1 = (bf16[256,256]{1,0:T(8,128)(2,1)}, bf16[256,256]{1,0:T(8,128)(2,1)S(1)}, u32[]{:S(2)}, u32[]{:S(2)}) collective-permute-start(bf16[256,256]{1,0:T(8,128)(2,1)} %signal.1), channel_id=1, source_target_pairs={{0,64},{16,80},{32,96},{48,112},{64,0},{80,16},{96,32},{112,48},{1... | collective-permute-start | bytes 393224 | tf_op jit(solution)/shard_map/ppermute | solution.py:212
  6.3 8.2 %collective-permute-start.6 = (bf16[256,256]{1,0:T(8,128)(2,1)}, bf16[256,256]{1,0:T(8,128)(2,1)S(1)}, u32[]{:S(2)}, u32[]{:S(2)}) collective-permute-start(bf16[256,256]{1,0:T(8,128)(2,1)} %signal.1), channel_id=1, source_target_pairs={{0,48},{16,32},{32,16},{48,0},{64,112},{80,96},{96,80},{112,64},{1... | collective-permute-start | bytes 393224 | tf_op jit(solution)/shard_map/ppermute | solution.py:212
  7.0 7.5 %collective-permute-start.3 = (bf16[256,256]{1,0:T(8,128)(2,1)}, bf16[256,256]{1,0:T(8,128)(2,1)S(1)}, u32[]{:S(2)}, u32[]{:S(2)}) collective-permute-start(bf16[256,256]{1,0:T(8,128)(2,1)} %signal.1), channel_id=1, source_target_pairs={{0,16},{16,0},{32,48},{48,32},{64,80},{80,64},{96,112},{112,96},{1... | collective-permute-start | bytes 393224 | tf_op jit(solution)/shard_map/ppermute | solution.py:212
  11.4 5.1 %collective-permute-start.5 = (bf16[256,256]{1,0:T(8,128)(2,1)S(1)}, bf16[256,256]{1,0:T(8,128)(2,1)S(1)}, u32[]{:S(2)}, u32[]{:S(2)}) collective-permute-start(bf16[256,256]{1,0:T(8,128)(2,1)S(1)} %collective-permute-done.refs_4_), channel_id=1, source_target_pairs={{0,64},{16,80},{32,96},{48,112},{64,0},{80,16},{96,32},{112,48},{1... | collective-permute-start | bytes 393224 | tf_op jit(solution)/shard_map/ppermute | solution.py:212
  11.5 6.3 %collective-permute-start.7 = (bf16[256,256]{1,0:T(8,128)(2,1)S(1)}, bf16[256,256]{1,0:T(8,128)(2,1)S(1)}, u32[]{:S(2)}, u32[]{:S(2)}) collective-permute-start(bf16[256,256]{1,0:T(8,128)(2,1)S(1)} %collective-permute-done.1.refs_1_), channel_id=1, source_target_pairs={{0,48},{16,32},{32,16},{48,0},{64,112},{80,96},{96,80},{112,64},{1... | collective-permute-start | bytes 393224 | tf_op jit(solution)/shard_map/ppermute | solution.py:212
  14.5 5.0 %collective-permute-start.4 = (bf16[256,256]{1,0:T(8,128)(2,1)S(1)}, bf16[256,256]{1,0:T(8,128)(2,1)S(1)}, u32[]{:S(2)}, u32[]{:S(2)}) collective-permute-start(bf16[256,256]{1,0:T(8,128)(2,1)S(1)} %collective-permute-done.1.refs_1_), channel_id=1, source_target_pairs={{0,16},{16,0},{32,48},{48,32},{64,80},{80,64},{96,112},{112,96},{1... | collective-permute-start | bytes 393224 | tf_op jit(solution)/shard_map/ppermute | solution.py:212
  20.8 4.6 %collective-permute-start.9 = (bf16[4,256,256]{2,1,0:T(8,128)(2,1)S(1)}, bf16[4,256,256]{2,1,0:T(8,128)(2,1)S(1)}, u32[]{:S(2)}, u32[]{:S(2)}) collective-permute-start(bf16[4,256,256]{2,1,0:T(8,128)(2,1)S(1)} %diag_mate.1), channel_id=1, source_target_pairs={{0,1},{1,0},{18,19},{19,18},{36,37},{37,36},{54,55},{55,54},{72,73... | collective-permute-start | bytes 1572872 | tf_op jit(solution)/shard_map/ppermute | solution.py:269
  23.4 1.9 %collective-permute-start.8 = (bf16[2,256,256]{2,1,0:T(8,128)(2,1)S(1)}, bf16[2,256,256]{2,1,0:T(8,128)(2,1)S(1)}, u32[]{:S(2)}, u32[]{:S(2)}) collective-permute-start(bf16[2,256,256]{2,1,0:T(8,128)(2,1)S(1)} %coeff.1.own), channel_id=1, source_target_pairs={{0,1},{1,0},{2,3},{3,2},{4,5},{5,4},{6,7},{7,6},{8,9},{9,8},{10,11... | collective-permute-start | bytes 786440 | tf_op jit(solution)/shard_map/ppermute | solution.py:212
  25.8 7.2 %collective-permute-start.12 = (bf16[256,256]{1,0:T(8,128)(2,1)S(1)}, bf16[256,256]{1,0:T(8,128)(2,1)S(1)}, u32[]{:S(2)}, u32[]{:S(2)}) collective-permute-start(bf16[256,256]{1,0:T(8,128)(2,1)S(1)} %get-tuple-element.42), channel_id=1, source_target_pairs={{0,2},{1,3},{2,0},{3,1},{4,6},{5,7},{6,4},{7,5},{8,10},{9,11},{10,... | collective-permute-start | bytes 393224 | tf_op jit(solution)/shard_map/ppermute | solution.py:212
  25.9 8.5 %collective-permute-start.14 = (bf16[256,256]{1,0:T(8,128)(2,1)S(1)}, bf16[256,256]{1,0:T(8,128)(2,1)S(1)}, u32[]{:S(2)}, u32[]{:S(2)}) collective-permute-start(bf16[256,256]{1,0:T(8,128)(2,1)S(1)} %get-tuple-element.44), channel_id=1, source_target_pairs={{0,4},{1,5},{2,6},{3,7},{4,0},{5,1},{6,2},{7,3},{8,12},{9,13},{10,... | collective-permute-start | bytes 393224 | tf_op jit(solution)/shard_map/ppermute | solution.py:212
  27.3 7.0 %collective-permute-start.15 = (bf16[256,256]{1,0:T(8,128)(2,1)S(1)}, bf16[256,256]{1,0:T(8,128)(2,1)S(1)}, u32[]{:S(2)}, u32[]{:S(2)}) collective-permute-start(bf16[256,256]{1,0:T(8,128)(2,1)S(1)} %get-tuple-element.45), channel_id=1, source_target_pairs={{0,12},{1,13},{2,14},{3,15},{4,8},{5,9},{6,10},{7,11},{8,4},{9,5},... | collective-permute-start | bytes 393224 | tf_op jit(solution)/shard_map/ppermute | solution.py:212
  30.1 6.7 %collective-permute-start.10 = (bf16[256,256]{1,0:T(8,128)(2,1)S(1)}, bf16[256,256]{1,0:T(8,128)(2,1)S(1)}, u32[]{:S(2)}, u32[]{:S(2)}) collective-permute-start(bf16[256,256]{1,0:T(8,128)(2,1)S(1)} %get-tuple-element.39), channel_id=1, source_target_pairs={{0,4},{1,5},{2,6},{3,7},{4,0},{5,1},{6,2},{7,3},{8,12},{9,13},{10,... | collective-permute-start | bytes 393224 | tf_op jit(solution)/shard_map/ppermute | solution.py:212
  31.3 9.0 %collective-permute-start.11 = (bf16[256,256]{1,0:T(8,128)(2,1)S(1)}, bf16[256,256]{1,0:T(8,128)(2,1)S(1)}, u32[]{:S(2)}, u32[]{:S(2)}) collective-permute-start(bf16[256,256]{1,0:T(8,128)(2,1)S(1)} %get-tuple-element.40), channel_id=1, source_target_pairs={{0,12},{1,13},{2,14},{3,15},{4,8},{5,9},{6,10},{7,11},{8,4},{9,5},... | collective-permute-start | bytes 393224 | tf_op jit(solution)/shard_map/ppermute | solution.py:212
  33.0 7.3 %collective-permute-start.13 = (bf16[256,256]{1,0:T(8,128)(2,1)S(1)}, bf16[256,256]{1,0:T(8,128)(2,1)S(1)}, u32[]{:S(2)}, u32[]{:S(2)}) collective-permute-start(bf16[256,256]{1,0:T(8,128)(2,1)S(1)} %add_convert_fusion.5), channel_id=1, source_target_pairs={{0,8},{1,9},{2,10},{3,11},{4,12},{5,13},{6,14},{7,15},{8,0},{9,1},... | collective-permute-start | bytes 393224 | tf_op jit(solution)/shard_map/ppermute | solution.py:212
  34.4 6.6 %collective-permute-start.16 = (bf16[256,256]{1,0:T(8,128)(2,1)S(1)}, bf16[256,256]{1,0:T(8,128)(2,1)S(1)}, u32[]{:S(2)}, u32[]{:S(2)}) collective-permute-start(bf16[256,256]{1,0:T(8,128)(2,1)S(1)} %add_convert_fusion.4), channel_id=1, source_target_pairs={{0,2},{1,3},{2,0},{3,1},{4,6},{5,7},{6,4},{7,5},{8,10},{9,11},{10,... | collective-permute-start | bytes 393224 | tf_op jit(solution)/shard_map/ppermute | solution.py:212
  41.1 7.0 %collective-permute-start.20 = (bf16[256,256]{1,0:T(8,128)(2,1)S(1)}, bf16[256,256]{1,0:T(8,128)(2,1)S(1)}, u32[]{:S(2)}, u32[]{:S(2)}) collective-permute-start(bf16[256,256]{1,0:T(8,128)(2,1)S(1)} %add_convert_fusion.3.refs_0_), channel_id=1, source_target_pairs={{0,8},{1,9},{2,10},{3,11},{4,12},{5,13},{6,14},{7,15},{8,0},{9,1},... | collective-permute-start | bytes 393224 | tf_op jit(solution)/shard_map/ppermute | solution.py:212
  43.9 7.1 %collective-permute-start.17 = (bf16[256,256]{1,0:T(8,128)(2,1)S(1)}, bf16[256,256]{1,0:T(8,128)(2,1)S(1)}, u32[]{:S(2)}, u32[]{:S(2)}) collective-permute-start(bf16[256,256]{1,0:T(8,128)(2,1)S(1)} %add_convert_fusion.3.refs_0_), channel_id=1, source_target_pairs={{0,2},{1,3},{2,0},{3,1},{4,6},{5,7},{6,4},{7,5},{8,10},{9,11},{10,... | collective-permute-start | bytes 393224 | tf_op jit(solution)/shard_map/ppermute | solution.py:212
  45.1 7.2 %collective-permute-start.22 = (bf16[256,256]{1,0:T(8,128)(2,1)S(1)}, bf16[256,256]{1,0:T(8,128)(2,1)S(1)}, u32[]{:S(2)}, u32[]{:S(2)}) collective-permute-start(bf16[256,256]{1,0:T(8,128)(2,1)S(1)} %add_convert_fusion.3.refs_0_), channel_id=1, source_target_pairs={{0,12},{1,13},{2,14},{3,15},{4,8},{5,9},{6,10},{7,11},{8,4},{9,5},... | collective-permute-start | bytes 393224 | tf_op jit(solution)/shard_map/ppermute | solution.py:212
  47.3 5.2 %collective-permute-start.18 = (bf16[256,256]{1,0:T(8,128)(2,1)S(1)}, bf16[256,256]{1,0:T(8,128)(2,1)S(1)}, u32[]{:S(2)}, u32[]{:S(2)}) collective-permute-start(bf16[256,256]{1,0:T(8,128)(2,1)S(1)} %add_convert_fusion.3.refs_0_), channel_id=1, source_target_pairs={{0,4},{1,5},{2,6},{3,7},{4,0},{5,1},{6,2},{7,3},{8,12},{9,13},{10,... | collective-permute-start | bytes 393224 | tf_op jit(solution)/shard_map/ppermute | solution.py:212
  48.1 6.5 %collective-permute-start.21 = (bf16[256,256]{1,0:T(8,128)(2,1)S(1)}, bf16[256,256]{1,0:T(8,128)(2,1)S(1)}, u32[]{:S(2)}, u32[]{:S(2)}) collective-permute-start(bf16[256,256]{1,0:T(8,128)(2,1)S(1)} %collective-permute-done.20.refs_4_), channel_id=1, source_target_pairs={{0,2},{1,3},{2,0},{3,1},{4,6},{5,7},{6,4},{7,5},{8,10},{9,11},{10,... | collective-permute-start | bytes 393224 | tf_op jit(solution)/shard_map/ppermute | solution.py:212
  51.0 6.2 %collective-permute-start.23 = (bf16[256,256]{1,0:T(8,128)(2,1)S(1)}, bf16[256,256]{1,0:T(8,128)(2,1)S(1)}, u32[]{:S(2)}, u32[]{:S(2)}) collective-permute-start(bf16[256,256]{1,0:T(8,128)(2,1)S(1)} %collective-permute-done.17.refs_1_), channel_id=1, source_target_pairs={{0,12},{1,13},{2,14},{3,15},{4,8},{5,9},{6,10},{7,11},{8,4},{9,5},... | collective-permute-start | bytes 393224 | tf_op jit(solution)/shard_map/ppermute | solution.py:212
  52.3 5.0 %collective-permute-start.19 = (bf16[256,256]{1,0:T(8,128)(2,1)S(1)}, bf16[256,256]{1,0:T(8,128)(2,1)S(1)}, u32[]{:S(2)}, u32[]{:S(2)}) collective-permute-start(bf16[256,256]{1,0:T(8,128)(2,1)S(1)} %collective-permute-done.17.refs_1_), channel_id=1, source_target_pairs={{0,4},{1,5},{2,6},{3,7},{4,0},{5,1},{6,2},{7,3},{8,12},{9,13},{10,... | collective-permute-start | bytes 393224 | tf_op jit(solution)/shard_map/ppermute | solution.py:212
  57.4 4.7 %collective-permute-start.25 = (bf16[4,256,256]{2,1,0:T(8,128)(2,1)S(1)}, bf16[4,256,256]{2,1,0:T(8,128)(2,1)S(1)}, u32[]{:S(2)}, u32[]{:S(2)}) collective-permute-start(bf16[4,256,256]{2,1,0:T(8,128)(2,1)S(1)} %pack.1), channel_id=1, source_target_pairs={{0,1},{1,0},{18,19},{19,18},{36,37},{37,36},{54,55},{55,54},{72,73... | collective-permute-start | bytes 1572872 | tf_op jit(solution)/shard_map/ppermute | solution.py:284
  63.0 6.2 %collective-permute-start.28 = (bf16[256,256]{1,0:T(8,128)(2,1)S(1)}, bf16[256,256]{1,0:T(8,128)(2,1)S(1)}, u32[]{:S(2)}, u32[]{:S(2)}) collective-permute-start(bf16[256,256]{1,0:T(8,128)(2,1)S(1)} %get-tuple-element.52), channel_id=1, source_target_pairs={{0,64},{16,80},{32,96},{48,112},{64,0},{80,16},{96,32},{112,48},{1... | collective-permute-start | bytes 393224 | tf_op jit(solution)/shard_map/ppermute | solution.py:212
  63.8 7.2 %collective-permute-start.30 = (bf16[256,256]{1,0:T(8,128)(2,1)S(1)}, bf16[256,256]{1,0:T(8,128)(2,1)S(1)}, u32[]{:S(2)}, u32[]{:S(2)}) collective-permute-start(bf16[256,256]{1,0:T(8,128)(2,1)S(1)} %get-tuple-element.54), channel_id=1, source_target_pairs={{0,16},{16,0},{32,48},{48,32},{64,80},{80,64},{96,112},{112,96},{1... | collective-permute-start | bytes 393224 | tf_op jit(solution)/shard_map/ppermute | solution.py:212
  64.2 6.8 %collective-permute-start.31 = (bf16[256,256]{1,0:T(8,128)(2,1)S(1)}, bf16[256,256]{1,0:T(8,128)(2,1)S(1)}, u32[]{:S(2)}, u32[]{:S(2)}) collective-permute-start(bf16[256,256]{1,0:T(8,128)(2,1)S(1)} %get-tuple-element.55), channel_id=1, source_target_pairs={{0,48},{16,32},{32,16},{48,0},{64,112},{80,96},{96,80},{112,64},{1... | collective-permute-start | bytes 393224 | tf_op jit(solution)/shard_map/ppermute | solution.py:212
  66.7 6.1 %collective-permute-start.26 = (bf16[256,256]{1,0:T(8,128)(2,1)S(1)}, bf16[256,256]{1,0:T(8,128)(2,1)S(1)}, u32[]{:S(2)}, u32[]{:S(2)}) collective-permute-start(bf16[256,256]{1,0:T(8,128)(2,1)S(1)} %get-tuple-element.49), channel_id=1, source_target_pairs={{0,16},{16,0},{32,48},{48,32},{64,80},{80,64},{96,112},{112,96},{1... | collective-permute-start | bytes 393224 | tf_op jit(solution)/shard_map/ppermute | solution.py:212
  67.5 9.0 %collective-permute-start.27 = (bf16[256,256]{1,0:T(8,128)(2,1)S(1)}, bf16[256,256]{1,0:T(8,128)(2,1)S(1)}, u32[]{:S(2)}, u32[]{:S(2)}) collective-permute-start(bf16[256,256]{1,0:T(8,128)(2,1)S(1)} %get-tuple-element.50), channel_id=1, source_target_pairs={{0,48},{16,32},{32,16},{48,0},{64,112},{80,96},{96,80},{112,64},{1... | collective-permute-start | bytes 393224 | tf_op jit(solution)/shard_map/ppermute | solution.py:212
  69.2 7.2 %collective-permute-start.29 = (bf16[256,256]{1,0:T(8,128)(2,1)S(1)}, bf16[256,256]{1,0:T(8,128)(2,1)S(1)}, u32[]{:S(2)}, u32[]{:S(2)}) collective-permute-start(bf16[256,256]{1,0:T(8,128)(2,1)S(1)} %add_convert_fusion.2), channel_id=1, source_target_pairs={{0,32},{16,48},{32,0},{48,16},{64,96},{80,112},{96,64},{112,80},{1... | collective-permute-start | bytes 393224 | tf_op jit(solution)/shard_map/ppermute | solution.py:212
  71.0 5.5 %collective-permute-start.32 = (bf16[256,256]{1,0:T(8,128)(2,1)S(1)}, bf16[256,256]{1,0:T(8,128)(2,1)S(1)}, u32[]{:S(2)}, u32[]{:S(2)}) collective-permute-start(bf16[256,256]{1,0:T(8,128)(2,1)S(1)} %add_convert_fusion.1), channel_id=1, source_target_pairs={{0,64},{16,80},{32,96},{48,112},{64,0},{80,16},{96,32},{112,48},{1... | collective-permute-start | bytes 393224 | tf_op jit(solution)/shard_map/ppermute | solution.py:212
  (4 other events, 34.8 us)

commit v5 on v4

--- a/solution.py
+++ b/solution.py
@@ -249,7 +249,6 @@
     right = right_factors[:, 0]
     left = left_factors[:, 0]
     dense = dense_diagonal[0]
-    owners = [((b // 2) * 16 + b, (b // 2) * 16 + (b ^ 1)) for b in range(16)]
 
     count = signal.shape[0]
     unit = 2 * count * PIECE * PIECE
@@ -266,7 +265,7 @@
     (coeff,) = call(coeff_kernel, "coeff", [*x, right], [pair], 16 * unit, 10 * size + 2**21, buckets)
     coeff_mate = swap(coeff, "tcol", 1)
     (dense_sent,) = call(functools.partial(diag_kernel, 1), "diag_mate", [*x, dense], [four], 32 * unit, 12 * size + 2**23)
-    dense_mate = lax.ppermute(dense_sent, ("trow", "tcol"), owners)
+    dense_mate = swap(dense_sent, "tcol", 1)
     (dense_own,) = call(functools.partial(diag_kernel, 0), "diag_own", [*x, dense], [four], 32 * unit, 12 * size + 2**23)
     terms = []
     for rels in (FAR, NEAR):
@@ -281,7 +280,7 @@
     first = scatter(terms, "tcol", 4, 2)
     y, _, _ = gather(first, "tcol", 4, 2)
     (y_sent,) = call(pack_kernel, "pack", y, [four], 0, 12 * size)
-    y_mate = lax.ppermute(y_sent, ("trow", "tcol"), owners)
+    y_mate = swap(y_sent, "tcol", 1)
     own, mate = call(back_kernel, "back", [*y, left, left_mate], [pair_wide, pair], 16 * unit, 14 * size + 2**21)
     mate = swap(mate, "tcol", 1)
     (dense_sum,) = call(diag_back_kernel, "diag_back", [*y, dense], [eight_wide], 32 * unit, 24 * size + 2**22)

time: 77.4 us -> 74.7 us (0.965)
  starting transfers between devices: 42 us -> 39.3 us
    ppermute x2 -> x0, starting transfers between devices: 4.02 us -> none  [the longest x1 2.1 us: body(): y_mate = lax.ppermute(y_sent, ('trow', 'tcol'), owners)]
    ppermute x31 -> x33, starting transfers between devices: 38 us -> 39.3 us  [swap(): return lax.ppermute(x, axis, [(i, i ^ bits) for i in range(size)])]
    ppermute x31 -> x33, waiting for transfers between devices: 20.6 us -> 20.7 us  [swap(): return lax.ppermute(x, axis, [(i, i ^ bits) for i in range(size)])]
  transfers between devices with their start and end apart: 33 -> 33, of which waited for: 14 -> 13; matrix products, arithmetic and copies ran while one was open for 0% -> 0% of each run, Pallas kernels for 13% -> 13%
where the time goes in v5:
time: 74.7 us; the launch traced here: 74.6 us
  starting transfers between devices  39.3 us (53%)
  waiting for transfers between devices  20.7 us (28%)
  Pallas kernels  12.7 us (17%)
  other arithmetic  1 us (1%)
  between operations  0.9 us (1%)
    ppermute x33, starting transfers between devices, swap(): return lax.ppermute(x, axis, [(i, i ^ bits) for i in range(size)])  39.3 us
    ppermute x33, waiting for transfers between devices, swap(): return lax.ppermute(x, axis, [(i, i ^ bits) for i in range(size)])  20.7 us
    pallas_call x10, Pallas kernels, call(): pl.pallas_call(kernel, name=name, out_shape=outs, in_specs=[VMEM] * (len(...  8.57 us
    pallas_call x1, Pallas kernels, load(): pl.pallas_call(load_kernel, name='load', out_shape=[pltpu.VMEM(v.shape, v...  4.12 us
  transfers between devices with their start and end apart: 33, of which 13 were waited for; matrix products, arithmetic and copies ran while one was open for 0% of the time, Pallas kernels for 13%

profile of v5, /device:TPU:0, one launch (start us, length us, event | category | flops | bytes accessed | tf_op | source)
XLA Modules:
  0.0 74.6 jit_solution(9773592458992886845)
XLA Ops:
  0.7 4.0 %collective-permute-start = (bf16[256,256]{1,0:T(8,128)(2,1)}, bf16[256,256]{1,0:T(8,128)(2,1)S(1)}, u32[]{:S(2)}, u32[]{:S(2)}) collective-permute-start(bf16[256,256]{1,0:T(8,128)(2,1)} %signal.1), channel_id=1, source_target_pairs={{0,32},{16,48},{32,0},{48,16},{64,96},{80,112},{96,64},{112,80},{1... | collective-permute-start | bytes 393224 | tf_op jit(solution)/shard_map/ppermute | solution.py:212
  4.8 1.5 %collective-permute-start.1 = (bf16[256,256]{1,0:T(8,128)(2,1)}, bf16[256,256]{1,0:T(8,128)(2,1)S(1)}, u32[]{:S(2)}, u32[]{:S(2)}) collective-permute-start(bf16[256,256]{1,0:T(8,128)(2,1)} %signal.1), channel_id=1, source_target_pairs={{0,64},{16,80},{32,96},{48,112},{64,0},{80,16},{96,32},{112,48},{1... | collective-permute-start | bytes 393224 | tf_op jit(solution)/shard_map/ppermute | solution.py:212
  7.3 4.1 %load.1 = (bf16[2,2048,256]{2,1,0:T(8,128)(2,1)S(1)}, bf16[256,256]{1,0:T(8,128)(2,1)S(1)}, bf16[2048,2048]{1,0:T(8,128)(2,1)S(1)}) custom-call(bf16[2,2048,256]{2,1,0:T(8,128)(2,1)} %bitcast.12, bf16[256,256]{1,0:T(8,128)(2,1)} %signal.1, bf16[2048,2048]{1,0:T(8,128)(2,1)} %bitcast.11), custom_call_target="tpu_custom_call" | custom-call | bytes 20971520 | tf_op jit(solution)/shard_map/load/pallas_call | solution.py:186
  11.5 2.9 %collective-permute-start.7 = (bf16[256,256]{1,0:T(8,128)(2,1)S(1)}, bf16[256,256]{1,0:T(8,128)(2,1)S(1)}, u32[]{:S(2)}, u32[]{:S(2)}) collective-permute-start(bf16[256,256]{1,0:T(8,128)(2,1)S(1)} %collective-permute-done.1.refs_1_), channel_id=1, source_target_pairs={{0,48},{16,32},{32,16},{48,0},{64,112},{80,96},{96,80},{112,64},{1... | collective-permute-start | bytes 393224 | tf_op jit(solution)/shard_map/ppermute | solution.py:212
  14.5 2.0 %collective-permute-done.5.refs_5_ = bf16[256,256]{1,0:T(8,128)(2,1)S(1)} collective-permute-done((bf16[256,256]{1,0:T(8,128)(2,1)S(1)}, bf16[256,256]{1,0:T(8,128)(2,1)S(1)}, u32[]{:S(2)}, u32[]{:S(2)}) %collective-permute-start.5) | collective-permute-done | bytes 131104 | tf_op jit(solution)/shard_map/ppermute | solution.py:212
  16.5 1.3 %collective-permute-done.7.refs_7_ = bf16[256,256]{1,0:T(8,128)(2,1)S(1)} collective-permute-done((bf16[256,256]{1,0:T(8,128)(2,1)S(1)}, bf16[256,256]{1,0:T(8,128)(2,1)S(1)}, u32[]{:S(2)}, u32[]{:S(2)}) %collective-permute-start.7) | collective-permute-done | bytes 131104 | tf_op jit(solution)/shard_map/ppermute | solution.py:212
  17.8 1.6 %collective-permute-done.4.refs_3_ = bf16[256,256]{1,0:T(8,128)(2,1)S(1)} collective-permute-done((bf16[256,256]{1,0:T(8,128)(2,1)S(1)}, bf16[256,256]{1,0:T(8,128)(2,1)S(1)}, u32[]{:S(2)}, u32[]{:S(2)}) %collective-permute-start.4) | collective-permute-done | bytes 131104 | tf_op jit(solution)/shard_map/ppermute | solution.py:212
  19.5 1.3 %diag_mate.1 = bf16[4,256,256]{2,1,0:T(8,128)(2,1)S(1)} custom-call(bf16[256,256]{1,0:T(8,128)(2,1)S(1)} %get-tuple-element.32.refs_0_, bf16[256,256]{1,0:T(8,128)(2,1)S(1)} %collective-permute-done.1.refs_1_, bf16[256,256]{1,0:T(8,128)(2,1)S(1)} %collective-permute-done.3.refs_2_, bf16[256,256]{1,0:T(8,128)(2,1)S(1)} %collective-permute-done.4.refs_3_, ...), custom_call_target="tpu_custom_call" | custom-call | flops 1073741824 | bytes 9961472 | tf_op jit(solution)/shard_map/diag_mate/pallas_call | solution.py:199
  22.1 1.3 %diag_own.1.dense_own = bf16[4,256,256]{2,1,0:T(8,128)(2,1)S(1)} custom-call(bf16[256,256]{1,0:T(8,128)(2,1)S(1)} %get-tuple-element.32.refs_0_, bf16[256,256]{1,0:T(8,128)(2,1)S(1)} %collective-permute-done.1.refs_1_, bf16[256,256]{1,0:T(8,128)(2,1)S(1)} %collective-permute-done.3.refs_2_, bf16[256,256]{1,0:T(8,128)(2,1)S(1)} %collective-permute-done.4.refs_3_, ...), custom_call_target="tpu_custom_call" | custom-call | flops 1073741824 | bytes 9961472 | tf_op jit(solution)/shard_map/diag_own/pallas_call | solution.py:199
  23.9 1.3 %collective-permute-start.12 = (bf16[256,256]{1,0:T(8,128)(2,1)S(1)}, bf16[256,256]{1,0:T(8,128)(2,1)S(1)}, u32[]{:S(2)}, u32[]{:S(2)}) collective-permute-start(bf16[256,256]{1,0:T(8,128)(2,1)S(1)} %get-tuple-element.42), channel_id=1, source_target_pairs={{0,2},{1,3},{2,0},{3,1},{4,6},{5,7},{6,4},{7,5},{8,10},{9,11},{10,... | collective-permute-start | bytes 393224 | tf_op jit(solution)/shard_map/ppermute | solution.py:212
  25.2 1.6 %collective-permute-start.14 = (bf16[256,256]{1,0:T(8,128)(2,1)S(1)}, bf16[256,256]{1,0:T(8,128)(2,1)S(1)}, u32[]{:S(2)}, u32[]{:S(2)}) collective-permute-start(bf16[256,256]{1,0:T(8,128)(2,1)S(1)} %get-tuple-element.44), channel_id=1, source_target_pairs={{0,4},{1,5},{2,6},{3,7},{4,0},{5,1},{6,2},{7,3},{8,12},{9,13},{10,... | collective-permute-start | bytes 393224 | tf_op jit(solution)/shard_map/ppermute | solution.py:212
  26.8 2.2 %collective-permute-start.15 = (bf16[256,256]{1,0:T(8,128)(2,1)S(1)}, bf16[256,256]{1,0:T(8,128)(2,1)S(1)}, u32[]{:S(2)}, u32[]{:S(2)}) collective-permute-start(bf16[256,256]{1,0:T(8,128)(2,1)S(1)} %get-tuple-element.45), channel_id=1, source_target_pairs={{0,12},{1,13},{2,14},{3,15},{4,8},{5,9},{6,10},{7,11},{8,4},{9,5},... | collective-permute-start | bytes 393224 | tf_op jit(solution)/shard_map/ppermute | solution.py:212
  29.5 1.3 %collective-permute-start.10 = (bf16[256,256]{1,0:T(8,128)(2,1)S(1)}, bf16[256,256]{1,0:T(8,128)(2,1)S(1)}, u32[]{:S(2)}, u32[]{:S(2)}) collective-permute-start(bf16[256,256]{1,0:T(8,128)(2,1)S(1)} %get-tuple-element.39), channel_id=1, source_target_pairs={{0,4},{1,5},{2,6},{3,7},{4,0},{5,1},{6,2},{7,3},{8,12},{9,13},{10,... | collective-permute-start | bytes 393224 | tf_op jit(solution)/shard_map/ppermute | solution.py:212
  31.4 2.4 %collective-permute-start.13 = (bf16[256,256]{1,0:T(8,128)(2,1)S(1)}, bf16[256,256]{1,0:T(8,128)(2,1)S(1)}, u32[]{:S(2)}, u32[]{:S(2)}) collective-permute-start(bf16[256,256]{1,0:T(8,128)(2,1)S(1)} %add_convert_fusion.5), channel_id=1, source_target_pairs={{0,8},{1,9},{2,10},{3,11},{4,12},{5,13},{6,14},{7,15},{8,0},{9,1},... | collective-permute-start | bytes 393224 | tf_op jit(solution)/shard_map/ppermute | solution.py:212
  33.8 2.1 %collective-permute-start.16 = (bf16[256,256]{1,0:T(8,128)(2,1)S(1)}, bf16[256,256]{1,0:T(8,128)(2,1)S(1)}, u32[]{:S(2)}, u32[]{:S(2)}) collective-permute-start(bf16[256,256]{1,0:T(8,128)(2,1)S(1)} %add_convert_fusion.4), channel_id=1, source_target_pairs={{0,2},{1,3},{2,0},{3,1},{4,6},{5,7},{6,4},{7,5},{8,10},{9,11},{10,... | collective-permute-start | bytes 393224 | tf_op jit(solution)/shard_map/ppermute | solution.py:212
  35.9 3.8 %collective-permute-done.11 = bf16[256,256]{1,0:T(8,128)(2,1)S(1)} collective-permute-done((bf16[256,256]{1,0:T(8,128)(2,1)S(1)}, bf16[256,256]{1,0:T(8,128)(2,1)S(1)}, u32[]{:S(2)}, u32[]{:S(2)}) %collective-permute-start.11) | collective-permute-done | bytes 131104 | tf_op jit(solution)/shard_map/ppermute | solution.py:212
  40.5 2.8 %collective-permute-start.20 = (bf16[256,256]{1,0:T(8,128)(2,1)S(1)}, bf16[256,256]{1,0:T(8,128)(2,1)S(1)}, u32[]{:S(2)}, u32[]{:S(2)}) collective-permute-start(bf16[256,256]{1,0:T(8,128)(2,1)S(1)} %add_convert_fusion.3.refs_0_), channel_id=1, source_target_pairs={{0,8},{1,9},{2,10},{3,11},{4,12},{5,13},{6,14},{7,15},{8,0},{9,1},... | collective-permute-start | bytes 393224 | tf_op jit(solution)/shard_map/ppermute | solution.py:212
  43.5 2.9 %collective-permute-start.22 = (bf16[256,256]{1,0:T(8,128)(2,1)S(1)}, bf16[256,256]{1,0:T(8,128)(2,1)S(1)}, u32[]{:S(2)}, u32[]{:S(2)}) collective-permute-start(bf16[256,256]{1,0:T(8,128)(2,1)S(1)} %add_convert_fusion.3.refs_0_), channel_id=1, source_target_pairs={{0,12},{1,13},{2,14},{3,15},{4,8},{5,9},{6,10},{7,11},{8,4},{9,5},... | collective-permute-start | bytes 393224 | tf_op jit(solution)/shard_map/ppermute | solution.py:212
  46.4 1.7 %collective-permute-done.20.refs_4_ = bf16[256,256]{1,0:T(8,128)(2,1)S(1)} collective-permute-done((bf16[256,256]{1,0:T(8,128)(2,1)S(1)}, bf16[256,256]{1,0:T(8,128)(2,1)S(1)}, u32[]{:S(2)}, u32[]{:S(2)}) %collective-permute-start.20) | collective-permute-done | bytes 131104 | tf_op jit(solution)/shard_map/ppermute | solution.py:212
  48.1 2.1 %collective-permute-start.21 = (bf16[256,256]{1,0:T(8,128)(2,1)S(1)}, bf16[256,256]{1,0:T(8,128)(2,1)S(1)}, u32[]{:S(2)}, u32[]{:S(2)}) collective-permute-start(bf16[256,256]{1,0:T(8,128)(2,1)S(1)} %collective-permute-done.20.refs_4_), channel_id=1, source_target_pairs={{0,2},{1,3},{2,0},{3,1},{4,6},{5,7},{6,4},{7,5},{8,10},{9,11},{10,... | collective-permute-start | bytes 393224 | tf_op jit(solution)/shard_map/ppermute | solution.py:212
  50.9 1.2 %collective-permute-start.23 = (bf16[256,256]{1,0:T(8,128)(2,1)S(1)}, bf16[256,256]{1,0:T(8,128)(2,1)S(1)}, u32[]{:S(2)}, u32[]{:S(2)}) collective-permute-start(bf16[256,256]{1,0:T(8,128)(2,1)S(1)} %collective-permute-done.17.refs_1_), channel_id=1, source_target_pairs={{0,12},{1,13},{2,14},{3,15},{4,8},{5,9},{6,10},{7,11},{8,4},{9,5},... | collective-permute-start | bytes 393224 | tf_op jit(solution)/shard_map/ppermute | solution.py:212
  52.2 2.4 %collective-permute-done.21.refs_5_ = bf16[256,256]{1,0:T(8,128)(2,1)S(1)} collective-permute-done((bf16[256,256]{1,0:T(8,128)(2,1)S(1)}, bf16[256,256]{1,0:T(8,128)(2,1)S(1)}, u32[]{:S(2)}, u32[]{:S(2)}) %collective-permute-start.21) | collective-permute-done | bytes 131104 | tf_op jit(solution)/shard_map/ppermute | solution.py:212
  54.6 2.5 %collective-permute-done.23.refs_7_ = bf16[256,256]{1,0:T(8,128)(2,1)S(1)} collective-permute-done((bf16[256,256]{1,0:T(8,128)(2,1)S(1)}, bf16[256,256]{1,0:T(8,128)(2,1)S(1)}, u32[]{:S(2)}, u32[]{:S(2)}) %collective-permute-start.23) | collective-permute-done | bytes 131104 | tf_op jit(solution)/shard_map/ppermute | solution.py:212
  58.7 1.3 %diag_back.1.dense_sum = f32[8,256,256]{2,1,0:T(8,128)S(1)} custom-call(bf16[256,256]{1,0:T(8,128)(2,1)S(1)} %add_convert_fusion.3.refs_0_, bf16[256,256]{1,0:T(8,128)(2,1)S(1)} %collective-permute-done.17.refs_1_, bf16[256,256]{1,0:T(8,128)(2,1)S(1)} %collective-permute-done.18.refs_2_, bf16[256,256]{1,0:T(8,128)(2,1)S(1)} %collective-permute-done.19.refs_3_, ...), custom_call_target="tpu_custom_call" | custom-call | flops 1073741824 | bytes 7340032 | tf_op jit(solution)/shard_map/diag_back/pallas_call | solution.py:199
  60.1 0.9 %second.3 = (bf16[256,256]{1,0:T(8,128)(2,1)S(1)}, bf16[256,256]{1,0:T(8,128)(2,1)S(1)}, bf16[256,256]{1,0:T(8,128)(2,1)S(1)}) custom-call(s32[1,2]{1,0:T(1,128)S(1)} %bitcast.9, f32[2,256,256]{2,1,0:T(8,128)S(1)} %get-tuple-element.46.own, bf16[2,256,256]{2,1,0:T(8,128)(2,1)S(1)} %collective-permute-done.24.mate, ...), custom_call_target="tpu_custom_call" | custom-call | flops 603979776 | bytes 4718592 | tf_op jit(solution)/shard_map/second/pallas_call | solution.py:199
  61.2 1.5 %collective-permute-start.31 = (bf16[256,256]{1,0:T(8,128)(2,1)S(1)}, bf16[256,256]{1,0:T(8,128)(2,1)S(1)}, u32[]{:S(2)}, u32[]{:S(2)}) collective-permute-start(bf16[256,256]{1,0:T(8,128)(2,1)S(1)} %get-tuple-element.55), channel_id=1, source_target_pairs={{0,48},{16,32},{32,16},{48,0},{64,112},{80,96},{96,80},{112,64},{1... | collective-permute-start | bytes 393224 | tf_op jit(solution)/shard_map/ppermute | solution.py:212
  62.7 1.3 %second.2 = (bf16[256,256]{1,0:T(8,128)(2,1)S(1)}, bf16[256,256]{1,0:T(8,128)(2,1)S(1)}, bf16[256,256]{1,0:T(8,128)(2,1)S(1)}, bf16[256,256]{1,0:T(8,128)(2,1)S(1)}, bf16[256,256]{1,0:T(8,128)(2,1)S(1)}) custom-call(s32[1,2]{1,0:T(1,128)S(1)} %bitcast.10, f32[2,256,256]{2,1,0:T(8,128)S(1)} %get-tuple-element.46.own, ...), custom_call_target="tpu_custom_call" | custom-call | flops 1006632960 | bytes 5767168 | tf_op jit(solution)/shard_map/second/pallas_call | solution.py:199
  64.0 0.8 %collective-permute-start.26 = (bf16[256,256]{1,0:T(8,128)(2,1)S(1)}, bf16[256,256]{1,0:T(8,128)(2,1)S(1)}, u32[]{:S(2)}, u32[]{:S(2)}) collective-permute-start(bf16[256,256]{1,0:T(8,128)(2,1)S(1)} %get-tuple-element.49), channel_id=1, source_target_pairs={{0,16},{16,0},{32,48},{48,32},{64,80},{80,64},{96,112},{112,96},{1... | collective-permute-start | bytes 393224 | tf_op jit(solution)/shard_map/ppermute | solution.py:212
  64.9 1.7 %collective-permute-start.27 = (bf16[256,256]{1,0:T(8,128)(2,1)S(1)}, bf16[256,256]{1,0:T(8,128)(2,1)S(1)}, u32[]{:S(2)}, u32[]{:S(2)}) collective-permute-start(bf16[256,256]{1,0:T(8,128)(2,1)S(1)} %get-tuple-element.50), channel_id=1, source_target_pairs={{0,48},{16,32},{32,16},{48,0},{64,112},{80,96},{96,80},{112,64},{1... | collective-permute-start | bytes 393224 | tf_op jit(solution)/shard_map/ppermute | solution.py:212
  66.7 1.6 %collective-permute-start.29 = (bf16[256,256]{1,0:T(8,128)(2,1)S(1)}, bf16[256,256]{1,0:T(8,128)(2,1)S(1)}, u32[]{:S(2)}, u32[]{:S(2)}) collective-permute-start(bf16[256,256]{1,0:T(8,128)(2,1)S(1)} %add_convert_fusion.2), channel_id=1, source_target_pairs={{0,32},{16,48},{32,0},{48,16},{64,96},{80,112},{96,64},{112,80},{1... | collective-permute-start | bytes 393224 | tf_op jit(solution)/shard_map/ppermute | solution.py:212
  68.4 1.8 %collective-permute-start.32 = (bf16[256,256]{1,0:T(8,128)(2,1)S(1)}, bf16[256,256]{1,0:T(8,128)(2,1)S(1)}, u32[]{:S(2)}, u32[]{:S(2)}) collective-permute-start(bf16[256,256]{1,0:T(8,128)(2,1)S(1)} %add_convert_fusion.1), channel_id=1, source_target_pairs={{0,64},{16,80},{32,96},{48,112},{64,0},{80,16},{96,32},{112,48},{1... | collective-permute-start | bytes 393224 | tf_op jit(solution)/shard_map/ppermute | solution.py:212
  70.3 3.5 %collective-permute-done.27 = bf16[256,256]{1,0:T(8,128)(2,1)S(1)} collective-permute-done((bf16[256,256]{1,0:T(8,128)(2,1)S(1)}, bf16[256,256]{1,0:T(8,128)(2,1)S(1)}, u32[]{:S(2)}, u32[]{:S(2)}) %collective-permute-start.27) | collective-permute-done | bytes 131104 | tf_op jit(solution)/shard_map/ppermute | solution.py:212
  (57 shorter events, 8.9 us)
Async XLA Ops:
  0.6 10.9 %collective-permute-start.2 = (bf16[2,2048,256]{2,1,0:T(8,128)(2,1)}, bf16[2,2048,256]{2,1,0:T(8,128)(2,1)S(1)}, u32[]{:S(2)}, u32[]{:S(2)}) collective-permute-start(bf16[2,2048,256]{2,1,0:T(8,128)(2,1)} %bitcast.4), channel_id=1, source_target_pairs={{0,1},{1,0},{2,3},{3,2},{4,5},{5,4},{6,7},{7,6},{8,9},{9,8},{10,11... | collective-permute-start | bytes 6291464 | tf_op jit(solution)/shard_map/ppermute | solution.py:212
  0.7 10.7 %collective-permute-start = (bf16[256,256]{1,0:T(8,128)(2,1)}, bf16[256,256]{1,0:T(8,128)(2,1)S(1)}, u32[]{:S(2)}, u32[]{:S(2)}) collective-permute-start(bf16[256,256]{1,0:T(8,128)(2,1)} %signal.1), channel_id=1, source_target_pairs={{0,32},{16,48},{32,0},{48,16},{64,96},{80,112},{96,64},{112,80},{1... | collective-permute-start | bytes 393224 | tf_op jit(solution)/shard_map/ppermute | solution.py:212
  4.8 6.8 %collective-permute-start.1 = (bf16[256,256]{1,0:T(8,128)(2,1)}, bf16[256,256]{1,0:T(8,128)(2,1)S(1)}, u32[]{:S(2)}, u32[]{:S(2)}) collective-permute-start(bf16[256,256]{1,0:T(8,128)(2,1)} %signal.1), channel_id=1, source_target_pairs={{0,64},{16,80},{32,96},{48,112},{64,0},{80,16},{96,32},{112,48},{1... | collective-permute-start | bytes 393224 | tf_op jit(solution)/shard_map/ppermute | solution.py:212
  6.3 8.2 %collective-permute-start.6 = (bf16[256,256]{1,0:T(8,128)(2,1)}, bf16[256,256]{1,0:T(8,128)(2,1)S(1)}, u32[]{:S(2)}, u32[]{:S(2)}) collective-permute-start(bf16[256,256]{1,0:T(8,128)(2,1)} %signal.1), channel_id=1, source_target_pairs={{0,48},{16,32},{32,16},{48,0},{64,112},{80,96},{96,80},{112,64},{1... | collective-permute-start | bytes 393224 | tf_op jit(solution)/shard_map/ppermute | solution.py:212
  7.0 7.5 %collective-permute-start.3 = (bf16[256,256]{1,0:T(8,128)(2,1)}, bf16[256,256]{1,0:T(8,128)(2,1)S(1)}, u32[]{:S(2)}, u32[]{:S(2)}) collective-permute-start(bf16[256,256]{1,0:T(8,128)(2,1)} %signal.1), channel_id=1, source_target_pairs={{0,16},{16,0},{32,48},{48,32},{64,80},{80,64},{96,112},{112,96},{1... | collective-permute-start | bytes 393224 | tf_op jit(solution)/shard_map/ppermute | solution.py:212
  11.4 5.1 %collective-permute-start.5 = (bf16[256,256]{1,0:T(8,128)(2,1)S(1)}, bf16[256,256]{1,0:T(8,128)(2,1)S(1)}, u32[]{:S(2)}, u32[]{:S(2)}) collective-permute-start(bf16[256,256]{1,0:T(8,128)(2,1)S(1)} %collective-permute-done.refs_4_), channel_id=1, source_target_pairs={{0,64},{16,80},{32,96},{48,112},{64,0},{80,16},{96,32},{112,48},{1... | collective-permute-start | bytes 393224 | tf_op jit(solution)/shard_map/ppermute | solution.py:212
  11.5 6.3 %collective-permute-start.7 = (bf16[256,256]{1,0:T(8,128)(2,1)S(1)}, bf16[256,256]{1,0:T(8,128)(2,1)S(1)}, u32[]{:S(2)}, u32[]{:S(2)}) collective-permute-start(bf16[256,256]{1,0:T(8,128)(2,1)S(1)} %collective-permute-done.1.refs_1_), channel_id=1, source_target_pairs={{0,48},{16,32},{32,16},{48,0},{64,112},{80,96},{96,80},{112,64},{1... | collective-permute-start | bytes 393224 | tf_op jit(solution)/shard_map/ppermute | solution.py:212
  14.5 5.0 %collective-permute-start.4 = (bf16[256,256]{1,0:T(8,128)(2,1)S(1)}, bf16[256,256]{1,0:T(8,128)(2,1)S(1)}, u32[]{:S(2)}, u32[]{:S(2)}) collective-permute-start(bf16[256,256]{1,0:T(8,128)(2,1)S(1)} %collective-permute-done.1.refs_1_), channel_id=1, source_target_pairs={{0,16},{16,0},{32,48},{48,32},{64,80},{80,64},{96,112},{112,96},{1... | collective-permute-start | bytes 393224 | tf_op jit(solution)/shard_map/ppermute | solution.py:212
  20.8 2.7 %collective-permute-start.9 = (bf16[4,256,256]{2,1,0:T(8,128)(2,1)S(1)}, bf16[4,256,256]{2,1,0:T(8,128)(2,1)S(1)}, u32[]{:S(2)}, u32[]{:S(2)}) collective-permute-start(bf16[4,256,256]{2,1,0:T(8,128)(2,1)S(1)} %diag_mate.1), channel_id=1, source_target_pairs={{0,1},{1,0},{2,3},{3,2},{4,5},{5,4},{6,7},{7,6},{8,9},{9,8},{10,11... | collective-permute-start | bytes 1572872 | tf_op jit(solution)/shard_map/ppermute | solution.py:212
  21.6 1.9 %collective-permute-start.8 = (bf16[2,256,256]{2,1,0:T(8,128)(2,1)S(1)}, bf16[2,256,256]{2,1,0:T(8,128)(2,1)S(1)}, u32[]{:S(2)}, u32[]{:S(2)}) collective-permute-start(bf16[2,256,256]{2,1,0:T(8,128)(2,1)S(1)} %coeff.1.own), channel_id=1, source_target_pairs={{0,1},{1,0},{2,3},{3,2},{4,5},{5,4},{6,7},{7,6},{8,9},{9,8},{10,11... | collective-permute-start | bytes 786440 | tf_op jit(solution)/shard_map/ppermute | solution.py:212
  23.9 7.4 %collective-permute-start.12 = (bf16[256,256]{1,0:T(8,128)(2,1)S(1)}, bf16[256,256]{1,0:T(8,128)(2,1)S(1)}, u32[]{:S(2)}, u32[]{:S(2)}) collective-permute-start(bf16[256,256]{1,0:T(8,128)(2,1)S(1)} %get-tuple-element.42), channel_id=1, source_target_pairs={{0,2},{1,3},{2,0},{3,1},{4,6},{5,7},{6,4},{7,5},{8,10},{9,11},{10,... | collective-permute-start | bytes 393224 | tf_op jit(solution)/shard_map/ppermute | solution.py:212
  25.2 8.6 %collective-permute-start.14 = (bf16[256,256]{1,0:T(8,128)(2,1)S(1)}, bf16[256,256]{1,0:T(8,128)(2,1)S(1)}, u32[]{:S(2)}, u32[]{:S(2)}) collective-permute-start(bf16[256,256]{1,0:T(8,128)(2,1)S(1)} %get-tuple-element.44), channel_id=1, source_target_pairs={{0,4},{1,5},{2,6},{3,7},{4,0},{5,1},{6,2},{7,3},{8,12},{9,13},{10,... | collective-permute-start | bytes 393224 | tf_op jit(solution)/shard_map/ppermute | solution.py:212
  26.8 7.0 %collective-permute-start.15 = (bf16[256,256]{1,0:T(8,128)(2,1)S(1)}, bf16[256,256]{1,0:T(8,128)(2,1)S(1)}, u32[]{:S(2)}, u32[]{:S(2)}) collective-permute-start(bf16[256,256]{1,0:T(8,128)(2,1)S(1)} %get-tuple-element.45), channel_id=1, source_target_pairs={{0,12},{1,13},{2,14},{3,15},{4,8},{5,9},{6,10},{7,11},{8,4},{9,5},... | collective-permute-start | bytes 393224 | tf_op jit(solution)/shard_map/ppermute | solution.py:212
  29.5 6.4 %collective-permute-start.10 = (bf16[256,256]{1,0:T(8,128)(2,1)S(1)}, bf16[256,256]{1,0:T(8,128)(2,1)S(1)}, u32[]{:S(2)}, u32[]{:S(2)}) collective-permute-start(bf16[256,256]{1,0:T(8,128)(2,1)S(1)} %get-tuple-element.39), channel_id=1, source_target_pairs={{0,4},{1,5},{2,6},{3,7},{4,0},{5,1},{6,2},{7,3},{8,12},{9,13},{10,... | collective-permute-start | bytes 393224 | tf_op jit(solution)/shard_map/ppermute | solution.py:212
  30.7 9.0 %collective-permute-start.11 = (bf16[256,256]{1,0:T(8,128)(2,1)S(1)}, bf16[256,256]{1,0:T(8,128)(2,1)S(1)}, u32[]{:S(2)}, u32[]{:S(2)}) collective-permute-start(bf16[256,256]{1,0:T(8,128)(2,1)S(1)} %get-tuple-element.40), channel_id=1, source_target_pairs={{0,12},{1,13},{2,14},{3,15},{4,8},{5,9},{6,10},{7,11},{8,4},{9,5},... | collective-permute-start | bytes 393224 | tf_op jit(solution)/shard_map/ppermute | solution.py:212
  31.4 8.3 %collective-permute-start.13 = (bf16[256,256]{1,0:T(8,128)(2,1)S(1)}, bf16[256,256]{1,0:T(8,128)(2,1)S(1)}, u32[]{:S(2)}, u32[]{:S(2)}) collective-permute-start(bf16[256,256]{1,0:T(8,128)(2,1)S(1)} %add_convert_fusion.5), channel_id=1, source_target_pairs={{0,8},{1,9},{2,10},{3,11},{4,12},{5,13},{6,14},{7,15},{8,0},{9,1},... | collective-permute-start | bytes 393224 | tf_op jit(solution)/shard_map/ppermute | solution.py:212
  33.8 6.6 %collective-permute-start.16 = (bf16[256,256]{1,0:T(8,128)(2,1)S(1)}, bf16[256,256]{1,0:T(8,128)(2,1)S(1)}, u32[]{:S(2)}, u32[]{:S(2)}) collective-permute-start(bf16[256,256]{1,0:T(8,128)(2,1)S(1)} %add_convert_fusion.4), channel_id=1, source_target_pairs={{0,2},{1,3},{2,0},{3,1},{4,6},{5,7},{6,4},{7,5},{8,10},{9,11},{10,... | collective-permute-start | bytes 393224 | tf_op jit(solution)/shard_map/ppermute | solution.py:212
  40.5 7.6 %collective-permute-start.20 = (bf16[256,256]{1,0:T(8,128)(2,1)S(1)}, bf16[256,256]{1,0:T(8,128)(2,1)S(1)}, u32[]{:S(2)}, u32[]{:S(2)}) collective-permute-start(bf16[256,256]{1,0:T(8,128)(2,1)S(1)} %add_convert_fusion.3.refs_0_), channel_id=1, source_target_pairs={{0,8},{1,9},{2,10},{3,11},{4,12},{5,13},{6,14},{7,15},{8,0},{9,1},... | collective-permute-start | bytes 393224 | tf_op jit(solution)/shard_map/ppermute | solution.py:212
  43.3 7.6 %collective-permute-start.17 = (bf16[256,256]{1,0:T(8,128)(2,1)S(1)}, bf16[256,256]{1,0:T(8,128)(2,1)S(1)}, u32[]{:S(2)}, u32[]{:S(2)}) collective-permute-start(bf16[256,256]{1,0:T(8,128)(2,1)S(1)} %add_convert_fusion.3.refs_0_), channel_id=1, source_target_pairs={{0,2},{1,3},{2,0},{3,1},{4,6},{5,7},{6,4},{7,5},{8,10},{9,11},{10,... | collective-permute-start | bytes 393224 | tf_op jit(solution)/shard_map/ppermute | solution.py:212
  43.5 8.7 %collective-permute-start.22 = (bf16[256,256]{1,0:T(8,128)(2,1)S(1)}, bf16[256,256]{1,0:T(8,128)(2,1)S(1)}, u32[]{:S(2)}, u32[]{:S(2)}) collective-permute-start(bf16[256,256]{1,0:T(8,128)(2,1)S(1)} %add_convert_fusion.3.refs_0_), channel_id=1, source_target_pairs={{0,12},{1,13},{2,14},{3,15},{4,8},{5,9},{6,10},{7,11},{8,4},{9,5},... | collective-permute-start | bytes 393224 | tf_op jit(solution)/shard_map/ppermute | solution.py:212
  46.4 5.8 %collective-permute-start.18 = (bf16[256,256]{1,0:T(8,128)(2,1)S(1)}, bf16[256,256]{1,0:T(8,128)(2,1)S(1)}, u32[]{:S(2)}, u32[]{:S(2)}) collective-permute-start(bf16[256,256]{1,0:T(8,128)(2,1)S(1)} %add_convert_fusion.3.refs_0_), channel_id=1, source_target_pairs={{0,4},{1,5},{2,6},{3,7},{4,0},{5,1},{6,2},{7,3},{8,12},{9,13},{10,... | collective-permute-start | bytes 393224 | tf_op jit(solution)/shard_map/ppermute | solution.py:212
  48.1 6.5 %collective-permute-start.21 = (bf16[256,256]{1,0:T(8,128)(2,1)S(1)}, bf16[256,256]{1,0:T(8,128)(2,1)S(1)}, u32[]{:S(2)}, u32[]{:S(2)}) collective-permute-start(bf16[256,256]{1,0:T(8,128)(2,1)S(1)} %collective-permute-done.20.refs_4_), channel_id=1, source_target_pairs={{0,2},{1,3},{2,0},{3,1},{4,6},{5,7},{6,4},{7,5},{8,10},{9,11},{10,... | collective-permute-start | bytes 393224 | tf_op jit(solution)/shard_map/ppermute | solution.py:212
  50.9 6.2 %collective-permute-start.23 = (bf16[256,256]{1,0:T(8,128)(2,1)S(1)}, bf16[256,256]{1,0:T(8,128)(2,1)S(1)}, u32[]{:S(2)}, u32[]{:S(2)}) collective-permute-start(bf16[256,256]{1,0:T(8,128)(2,1)S(1)} %collective-permute-done.17.refs_1_), channel_id=1, source_target_pairs={{0,12},{1,13},{2,14},{3,15},{4,8},{5,9},{6,10},{7,11},{8,4},{9,5},... | collective-permute-start | bytes 393224 | tf_op jit(solution)/shard_map/ppermute | solution.py:212
  52.1 5.0 %collective-permute-start.19 = (bf16[256,256]{1,0:T(8,128)(2,1)S(1)}, bf16[256,256]{1,0:T(8,128)(2,1)S(1)}, u32[]{:S(2)}, u32[]{:S(2)}) collective-permute-start(bf16[256,256]{1,0:T(8,128)(2,1)S(1)} %collective-permute-done.17.refs_1_), channel_id=1, source_target_pairs={{0,4},{1,5},{2,6},{3,7},{4,0},{5,1},{6,2},{7,3},{8,12},{9,13},{10,... | collective-permute-start | bytes 393224 | tf_op jit(solution)/shard_map/ppermute | solution.py:212
  57.2 2.9 %collective-permute-start.25 = (bf16[4,256,256]{2,1,0:T(8,128)(2,1)S(1)}, bf16[4,256,256]{2,1,0:T(8,128)(2,1)S(1)}, u32[]{:S(2)}, u32[]{:S(2)}) collective-permute-start(bf16[4,256,256]{2,1,0:T(8,128)(2,1)S(1)} %pack.1), channel_id=1, source_target_pairs={{0,1},{1,0},{2,3},{3,2},{4,5},{5,4},{6,7},{7,6},{8,9},{9,8},{10,11... | collective-permute-start | bytes 1572872 | tf_op jit(solution)/shard_map/ppermute | solution.py:212
  61.0 5.7 %collective-permute-start.28 = (bf16[256,256]{1,0:T(8,128)(2,1)S(1)}, bf16[256,256]{1,0:T(8,128)(2,1)S(1)}, u32[]{:S(2)}, u32[]{:S(2)}) collective-permute-start(bf16[256,256]{1,0:T(8,128)(2,1)S(1)} %get-tuple-element.52), channel_id=1, source_target_pairs={{0,64},{16,80},{32,96},{48,112},{64,0},{80,16},{96,32},{112,48},{1... | collective-permute-start | bytes 393224 | tf_op jit(solution)/shard_map/ppermute | solution.py:212
  61.1 7.3 %collective-permute-start.30 = (bf16[256,256]{1,0:T(8,128)(2,1)S(1)}, bf16[256,256]{1,0:T(8,128)(2,1)S(1)}, u32[]{:S(2)}, u32[]{:S(2)}) collective-permute-start(bf16[256,256]{1,0:T(8,128)(2,1)S(1)} %get-tuple-element.54), channel_id=1, source_target_pairs={{0,16},{16,0},{32,48},{48,32},{64,80},{80,64},{96,112},{112,96},{1... | collective-permute-start | bytes 393224 | tf_op jit(solution)/shard_map/ppermute | solution.py:212
  61.2 7.2 %collective-permute-start.31 = (bf16[256,256]{1,0:T(8,128)(2,1)S(1)}, bf16[256,256]{1,0:T(8,128)(2,1)S(1)}, u32[]{:S(2)}, u32[]{:S(2)}) collective-permute-start(bf16[256,256]{1,0:T(8,128)(2,1)S(1)} %get-tuple-element.55), channel_id=1, source_target_pairs={{0,48},{16,32},{32,16},{48,0},{64,112},{80,96},{96,80},{112,64},{1... | collective-permute-start | bytes 393224 | tf_op jit(solution)/shard_map/ppermute | solution.py:212
  64.0 6.3 %collective-permute-start.26 = (bf16[256,256]{1,0:T(8,128)(2,1)S(1)}, bf16[256,256]{1,0:T(8,128)(2,1)S(1)}, u32[]{:S(2)}, u32[]{:S(2)}) collective-permute-start(bf16[256,256]{1,0:T(8,128)(2,1)S(1)} %get-tuple-element.49), channel_id=1, source_target_pairs={{0,16},{16,0},{32,48},{48,32},{64,80},{80,64},{96,112},{112,96},{1... | collective-permute-start | bytes 393224 | tf_op jit(solution)/shard_map/ppermute | solution.py:212
  64.9 9.0 %collective-permute-start.27 = (bf16[256,256]{1,0:T(8,128)(2,1)S(1)}, bf16[256,256]{1,0:T(8,128)(2,1)S(1)}, u32[]{:S(2)}, u32[]{:S(2)}) collective-permute-start(bf16[256,256]{1,0:T(8,128)(2,1)S(1)} %get-tuple-element.50), channel_id=1, source_target_pairs={{0,48},{16,32},{32,16},{48,0},{64,112},{80,96},{96,80},{112,64},{1... | collective-permute-start | bytes 393224 | tf_op jit(solution)/shard_map/ppermute | solution.py:212
  66.7 7.1 %collective-permute-start.29 = (bf16[256,256]{1,0:T(8,128)(2,1)S(1)}, bf16[256,256]{1,0:T(8,128)(2,1)S(1)}, u32[]{:S(2)}, u32[]{:S(2)}) collective-permute-start(bf16[256,256]{1,0:T(8,128)(2,1)S(1)} %add_convert_fusion.2), channel_id=1, source_target_pairs={{0,32},{16,48},{32,0},{48,16},{64,96},{80,112},{96,64},{112,80},{1... | collective-permute-start | bytes 393224 | tf_op jit(solution)/shard_map/ppermute | solution.py:212
  68.4 5.4 %collective-permute-start.32 = (bf16[256,256]{1,0:T(8,128)(2,1)S(1)}, bf16[256,256]{1,0:T(8,128)(2,1)S(1)}, u32[]{:S(2)}, u32[]{:S(2)}) collective-permute-start(bf16[256,256]{1,0:T(8,128)(2,1)S(1)} %add_convert_fusion.1), channel_id=1, source_target_pairs={{0,64},{16,80},{32,96},{48,112},{64,0},{80,16},{96,32},{112,48},{1... | collective-permute-start | bytes 393224 | tf_op jit(solution)/shard_map/ppermute | solution.py:212
  (4 other events, 31.4 us)

commit v6 on v5

--- a/solution.py
+++ b/solution.py
@@ -162,24 +162,14 @@
             out[...] = (low(rows) + dense_sum[piece] + rest).astype(BF16)
 
 
-def load_kernel(right, signal, dense, right_out, signal_out, dense_out, sems):
-    copies = [
-        pltpu.make_async_copy(right, right_out, sems.at[0]),
-        pltpu.make_async_copy(signal, signal_out, sems.at[1]),
-    ]
-    for copy in copies:
-        copy.start()
-
+def load_kernel(dense, dense_out, sems):
     @pl.when(Place().owner)
     def _():
-        blocks = [pltpu.make_async_copy(dense.at[rows_of(p), :], dense_out.at[rows_of(p), :], sems.at[2 + p]) for p in range(8)]
+        blocks = [pltpu.make_async_copy(dense.at[rows_of(p), :], dense_out.at[rows_of(p), :], sems.at[p]) for p in range(8)]
         for block in blocks:
             block.start()
         for block in blocks:
             block.wait()
-
-    for copy in copies:
-        copy.wait()
 
 
 def load(*arrays):
@@ -215,11 +205,9 @@
 def gather(own, axis, ring, side, first=None, loaded=()):
     got = {(0, 0): own}
     got[(0, 1)] = swap(own, axis, side)
-    if first is not None:
-        got[(0, 1)], first = lax.optimization_barrier((got[(0, 1)], first))
     got[(2, 0)] = swap(own, axis, 2 * ring)
     if first is not None:
-        got[(2, 0)], *loaded = lax.optimization_barrier((got[(2, 0)], *loaded))
+        got[(2, 0)], first, *loaded = lax.optimization_barrier((got[(2, 0)], first, *loaded))
     got[(1, 0)] = swap(own, axis, ring)
     got[(3, 0)] = swap(own, axis, 3 * ring)
     got[(1, 1)] = swap(got[(0, 1)], axis, ring)
@@ -260,8 +248,8 @@
     eight_wide = jax.ShapeDtypeStruct((8, count, PIECE), F32)
 
     left_mate = swap(left, "tcol", 1)
-    x, left_mate, loaded = gather(signal, "trow", 1, 4, left_mate, load(right, signal, dense))
-    right, x[0], dense = loaded
+    x, left_mate, loaded = gather(signal, "trow", 1, 4, left_mate, load(dense))
+    (dense,) = loaded
     (coeff,) = call(coeff_kernel, "coeff", [*x, right], [pair], 16 * unit, 10 * size + 2**21, buckets)
     coeff_mate = swap(coeff, "tcol", 1)
     (dense_sent,) = call(functools.partial(diag_kernel, 1), "diag_mate", [*x, dense], [four], 32 * unit, 12 * size + 2**23)

time: 74.7 us -> 74.4 us (level)
  waiting for transfers between devices: 20.7 us -> 21.7 us
  starting transfers between devices: 39.3 us -> 38.5 us
    ppermute x33, waiting for transfers between devices: 20.7 us -> 21.7 us  [swap(): return lax.ppermute(x, axis, [(i, i ^ bits) for i in range(size)])]
    ppermute x33, starting transfers between devices: 39.3 us -> 38.5 us  [swap(): return lax.ppermute(x, axis, [(i, i ^ bits) for i in range(size)])]
where the time goes in v6:
time: 74.4 us; the launch traced here: 74.3 us
  starting transfers between devices  38.5 us (52%)
  waiting for transfers between devices  21.7 us (29%)
  Pallas kernels  12.1 us (16%)
  other arithmetic  0.99 us (1%)
  between operations  0.9 us (1%)
    ppermute x33, starting transfers between devices, swap(): return lax.ppermute(x, axis, [(i, i ^ bits) for i in range(size)])  38.5 us
    ppermute x33, waiting for transfers between devices, swap(): return lax.ppermute(x, axis, [(i, i ^ bits) for i in range(size)])  21.7 us
    pallas_call x10, Pallas kernels, call(): pl.pallas_call(kernel, name=name, out_shape=outs, in_specs=[VMEM] * (len(...  8.62 us
    pallas_call x1, Pallas kernels, load(): pl.pallas_call(load_kernel, name='load', out_shape=[pltpu.VMEM(v.shape, v...  3.52 us
  transfers between devices with their start and end apart: 33, of which 13 were waited for; matrix products, arithmetic and copies ran while one was open for 0% of the time, Pallas kernels for 13%

profile of v6, /device:TPU:0, one launch (start us, length us, event | category | flops | bytes accessed | tf_op | source)
XLA Modules:
  0.0 74.3 jit_solution(11225507161304708469)
XLA Ops:
  0.7 1.7 %collective-permute-start = (bf16[256,256]{1,0:T(8,128)(2,1)}, bf16[256,256]{1,0:T(8,128)(2,1)S(1)}, u32[]{:S(2)}, u32[]{:S(2)}) collective-permute-start(bf16[256,256]{1,0:T(8,128)(2,1)} %refs_0_.5), channel_id=1, source_target_pairs={{0,64},{16,80},{32,96},{48,112},{64,0},{80,16},{96,32},{112,48},{1... | collective-permute-start | bytes 393224 | tf_op jit(solution)/shard_map/ppermute | solution.py:202
  2.4 3.9 %collective-permute-start.3 = (bf16[256,256]{1,0:T(8,128)(2,1)}, bf16[256,256]{1,0:T(8,128)(2,1)S(1)}, u32[]{:S(2)}, u32[]{:S(2)}) collective-permute-start(bf16[256,256]{1,0:T(8,128)(2,1)} %refs_0_.5), channel_id=1, source_target_pairs={{0,32},{16,48},{32,0},{48,16},{64,96},{80,112},{96,64},{112,80},{1... | collective-permute-start | bytes 393224 | tf_op jit(solution)/shard_map/ppermute | solution.py:202
  7.3 3.5 %load.1.refs_8_.dense = bf16[2048,2048]{1,0:T(8,128)(2,1)S(1)} custom-call(bf16[2048,2048]{1,0:T(8,128)(2,1)} %bitcast.14), custom_call_target="tpu_custom_call" | custom-call | bytes 20971520 | tf_op jit(solution)/shard_map/load/pallas_call | solution.py:176
  13.1 1.3 %collective-permute-done.1.refs_2_ = bf16[256,256]{1,0:T(8,128)(2,1)S(1)} collective-permute-done((bf16[256,256]{1,0:T(8,128)(2,1)}, bf16[256,256]{1,0:T(8,128)(2,1)S(1)}, u32[]{:S(2)}, u32[]{:S(2)}) %collective-permute-start.1) | collective-permute-done | bytes 131104 | tf_op jit(solution)/shard_map/ppermute | solution.py:202
  14.5 2.7 %collective-permute-done.7.refs_7_ = bf16[256,256]{1,0:T(8,128)(2,1)S(1)} collective-permute-done((bf16[256,256]{1,0:T(8,128)(2,1)S(1)}, bf16[256,256]{1,0:T(8,128)(2,1)S(1)}, u32[]{:S(2)}, u32[]{:S(2)}) %collective-permute-start.7) | collective-permute-done | bytes 131104 | tf_op jit(solution)/shard_map/ppermute | solution.py:202
  17.1 1.3 %diag_mate.1 = bf16[4,256,256]{2,1,0:T(8,128)(2,1)S(1)} custom-call(bf16[256,256]{1,0:T(8,128)(2,1)S(1)} %copy-done.3, bf16[256,256]{1,0:T(8,128)(2,1)S(1)} %collective-permute-done.refs_1_, bf16[256,256]{1,0:T(8,128)(2,1)S(1)} %collective-permute-done.1.refs_2_, bf16[256,256]{1,0:T(8,128)(2,1)S(1)} %collective-permute-done.2.refs_3_, ...), custom_call_target="tpu_custom_call" | custom-call | flops 1073741824 | bytes 9961472 | tf_op jit(solution)/shard_map/diag_mate/pallas_call | solution.py:189
  19.9 1.3 %diag_own.1.dense_own = bf16[4,256,256]{2,1,0:T(8,128)(2,1)S(1)} custom-call(bf16[256,256]{1,0:T(8,128)(2,1)S(1)} %copy-done.3, bf16[256,256]{1,0:T(8,128)(2,1)S(1)} %collective-permute-done.refs_1_, bf16[256,256]{1,0:T(8,128)(2,1)S(1)} %collective-permute-done.1.refs_2_, bf16[256,256]{1,0:T(8,128)(2,1)S(1)} %collective-permute-done.2.refs_3_, ...), custom_call_target="tpu_custom_call" | custom-call | flops 1073741824 | bytes 9961472 | tf_op jit(solution)/shard_map/diag_own/pallas_call | solution.py:189
  21.6 1.8 %collective-permute-start.12 = (bf16[256,256]{1,0:T(8,128)(2,1)S(1)}, bf16[256,256]{1,0:T(8,128)(2,1)S(1)}, u32[]{:S(2)}, u32[]{:S(2)}) collective-permute-start(bf16[256,256]{1,0:T(8,128)(2,1)S(1)} %get-tuple-element.30), channel_id=1, source_target_pairs={{0,2},{1,3},{2,0},{3,1},{4,6},{5,7},{6,4},{7,5},{8,10},{9,11},{10,... | collective-permute-start | bytes 393224 | tf_op jit(solution)/shard_map/ppermute | solution.py:202
  23.5 2.5 %collective-permute-start.14 = (bf16[256,256]{1,0:T(8,128)(2,1)S(1)}, bf16[256,256]{1,0:T(8,128)(2,1)S(1)}, u32[]{:S(2)}, u32[]{:S(2)}) collective-permute-start(bf16[256,256]{1,0:T(8,128)(2,1)S(1)} %get-tuple-element.32), channel_id=1, source_target_pairs={{0,4},{1,5},{2,6},{3,7},{4,0},{5,1},{6,2},{7,3},{8,12},{9,13},{10,... | collective-permute-start | bytes 393224 | tf_op jit(solution)/shard_map/ppermute | solution.py:202
  27.0 1.3 %collective-permute-start.10 = (bf16[256,256]{1,0:T(8,128)(2,1)S(1)}, bf16[256,256]{1,0:T(8,128)(2,1)S(1)}, u32[]{:S(2)}, u32[]{:S(2)}) collective-permute-start(bf16[256,256]{1,0:T(8,128)(2,1)S(1)} %get-tuple-element.27), channel_id=1, source_target_pairs={{0,4},{1,5},{2,6},{3,7},{4,0},{5,1},{6,2},{7,3},{8,12},{9,13},{10,... | collective-permute-start | bytes 393224 | tf_op jit(solution)/shard_map/ppermute | solution.py:202
  28.2 1.7 %collective-permute-start.11 = (bf16[256,256]{1,0:T(8,128)(2,1)S(1)}, bf16[256,256]{1,0:T(8,128)(2,1)S(1)}, u32[]{:S(2)}, u32[]{:S(2)}) collective-permute-start(bf16[256,256]{1,0:T(8,128)(2,1)S(1)} %get-tuple-element.28), channel_id=1, source_target_pairs={{0,12},{1,13},{2,14},{3,15},{4,8},{5,9},{6,10},{7,11},{8,4},{9,5},... | collective-permute-start | bytes 393224 | tf_op jit(solution)/shard_map/ppermute | solution.py:202
  29.9 1.5 %collective-permute-start.13 = (bf16[256,256]{1,0:T(8,128)(2,1)S(1)}, bf16[256,256]{1,0:T(8,128)(2,1)S(1)}, u32[]{:S(2)}, u32[]{:S(2)}) collective-permute-start(bf16[256,256]{1,0:T(8,128)(2,1)S(1)} %add_convert_fusion.5), channel_id=1, source_target_pairs={{0,8},{1,9},{2,10},{3,11},{4,12},{5,13},{6,14},{7,15},{8,0},{9,1},... | collective-permute-start | bytes 393224 | tf_op jit(solution)/shard_map/ppermute | solution.py:202
  31.4 2.0 %collective-permute-done.15 = bf16[256,256]{1,0:T(8,128)(2,1)S(1)} collective-permute-done((bf16[256,256]{1,0:T(8,128)(2,1)S(1)}, bf16[256,256]{1,0:T(8,128)(2,1)S(1)}, u32[]{:S(2)}, u32[]{:S(2)}) %collective-permute-start.15) | collective-permute-done | bytes 131104 | tf_op jit(solution)/shard_map/ppermute | solution.py:202
  33.5 2.2 %collective-permute-start.16 = (bf16[256,256]{1,0:T(8,128)(2,1)S(1)}, bf16[256,256]{1,0:T(8,128)(2,1)S(1)}, u32[]{:S(2)}, u32[]{:S(2)}) collective-permute-start(bf16[256,256]{1,0:T(8,128)(2,1)S(1)} %add_convert_fusion.4), channel_id=1, source_target_pairs={{0,2},{1,3},{2,0},{3,1},{4,6},{5,7},{6,4},{7,5},{8,10},{9,11},{10,... | collective-permute-start | bytes 393224 | tf_op jit(solution)/shard_map/ppermute | solution.py:202
  35.6 2.3 %collective-permute-done.11 = bf16[256,256]{1,0:T(8,128)(2,1)S(1)} collective-permute-done((bf16[256,256]{1,0:T(8,128)(2,1)S(1)}, bf16[256,256]{1,0:T(8,128)(2,1)S(1)}, u32[]{:S(2)}, u32[]{:S(2)}) %collective-permute-start.11) | collective-permute-done | bytes 131104 | tf_op jit(solution)/shard_map/ppermute | solution.py:202
  38.0 2.1 %collective-permute-done.16 = bf16[256,256]{1,0:T(8,128)(2,1)S(1)} collective-permute-done((bf16[256,256]{1,0:T(8,128)(2,1)S(1)}, bf16[256,256]{1,0:T(8,128)(2,1)S(1)}, u32[]{:S(2)}, u32[]{:S(2)}) %collective-permute-start.16) | collective-permute-done | bytes 131104 | tf_op jit(solution)/shard_map/ppermute | solution.py:202
  40.3 2.0 %collective-permute-start.17 = (bf16[256,256]{1,0:T(8,128)(2,1)S(1)}, bf16[256,256]{1,0:T(8,128)(2,1)S(1)}, u32[]{:S(2)}, u32[]{:S(2)}) collective-permute-start(bf16[256,256]{1,0:T(8,128)(2,1)S(1)} %add_convert_fusion.3.refs_0_), channel_id=1, source_target_pairs={{0,2},{1,3},{2,0},{3,1},{4,6},{5,7},{6,4},{7,5},{8,10},{9,11},{10,... | collective-permute-start | bytes 393224 | tf_op jit(solution)/shard_map/ppermute | solution.py:202
  42.4 1.5 %collective-permute-start.22 = (bf16[256,256]{1,0:T(8,128)(2,1)S(1)}, bf16[256,256]{1,0:T(8,128)(2,1)S(1)}, u32[]{:S(2)}, u32[]{:S(2)}) collective-permute-start(bf16[256,256]{1,0:T(8,128)(2,1)S(1)} %add_convert_fusion.3.refs_0_), channel_id=1, source_target_pairs={{0,12},{1,13},{2,14},{3,15},{4,8},{5,9},{6,10},{7,11},{8,4},{9,5},... | collective-permute-start | bytes 393224 | tf_op jit(solution)/shard_map/ppermute | solution.py:202
  43.9 1.9 %collective-permute-start.18 = (bf16[256,256]{1,0:T(8,128)(2,1)S(1)}, bf16[256,256]{1,0:T(8,128)(2,1)S(1)}, u32[]{:S(2)}, u32[]{:S(2)}) collective-permute-start(bf16[256,256]{1,0:T(8,128)(2,1)S(1)} %add_convert_fusion.3.refs_0_), channel_id=1, source_target_pairs={{0,4},{1,5},{2,6},{3,7},{4,0},{5,1},{6,2},{7,3},{8,12},{9,13},{10,... | collective-permute-start | bytes 393224 | tf_op jit(solution)/shard_map/ppermute | solution.py:202
  45.8 1.7 %collective-permute-done.20.refs_4_ = bf16[256,256]{1,0:T(8,128)(2,1)S(1)} collective-permute-done((bf16[256,256]{1,0:T(8,128)(2,1)S(1)}, bf16[256,256]{1,0:T(8,128)(2,1)S(1)}, u32[]{:S(2)}, u32[]{:S(2)}) %collective-permute-start.20) | collective-permute-done | bytes 131104 | tf_op jit(solution)/shard_map/ppermute | solution.py:202
  47.4 1.5 %collective-permute-start.21 = (bf16[256,256]{1,0:T(8,128)(2,1)S(1)}, bf16[256,256]{1,0:T(8,128)(2,1)S(1)}, u32[]{:S(2)}, u32[]{:S(2)}) collective-permute-start(bf16[256,256]{1,0:T(8,128)(2,1)S(1)} %collective-permute-done.20.refs_4_), channel_id=1, source_target_pairs={{0,2},{1,3},{2,0},{3,1},{4,6},{5,7},{6,4},{7,5},{8,10},{9,11},{10,... | collective-permute-start | bytes 393224 | tf_op jit(solution)/shard_map/ppermute | solution.py:202
  48.9 1.7 %collective-permute-start.23 = (bf16[256,256]{1,0:T(8,128)(2,1)S(1)}, bf16[256,256]{1,0:T(8,128)(2,1)S(1)}, u32[]{:S(2)}, u32[]{:S(2)}) collective-permute-start(bf16[256,256]{1,0:T(8,128)(2,1)S(1)} %collective-permute-done.17.refs_1_), channel_id=1, source_target_pairs={{0,12},{1,13},{2,14},{3,15},{4,8},{5,9},{6,10},{7,11},{8,4},{9,5},... | collective-permute-start | bytes 393224 | tf_op jit(solution)/shard_map/ppermute | solution.py:202
  50.7 3.3 %collective-permute-done.21.refs_5_ = bf16[256,256]{1,0:T(8,128)(2,1)S(1)} collective-permute-done((bf16[256,256]{1,0:T(8,128)(2,1)S(1)}, bf16[256,256]{1,0:T(8,128)(2,1)S(1)}, u32[]{:S(2)}, u32[]{:S(2)}) %collective-permute-start.21) | collective-permute-done | bytes 131104 | tf_op jit(solution)/shard_map/ppermute | solution.py:202
  53.9 1.2 %collective-permute-done.23.refs_7_ = bf16[256,256]{1,0:T(8,128)(2,1)S(1)} collective-permute-done((bf16[256,256]{1,0:T(8,128)(2,1)S(1)}, bf16[256,256]{1,0:T(8,128)(2,1)S(1)}, u32[]{:S(2)}, u32[]{:S(2)}) %collective-permute-start.23) | collective-permute-done | bytes 131104 | tf_op jit(solution)/shard_map/ppermute | solution.py:202
  57.3 1.3 %diag_back.1.dense_sum = f32[8,256,256]{2,1,0:T(8,128)S(1)} custom-call(bf16[256,256]{1,0:T(8,128)(2,1)S(1)} %add_convert_fusion.3.refs_0_, bf16[256,256]{1,0:T(8,128)(2,1)S(1)} %collective-permute-done.17.refs_1_, bf16[256,256]{1,0:T(8,128)(2,1)S(1)} %collective-permute-done.18.refs_2_, bf16[256,256]{1,0:T(8,128)(2,1)S(1)} %collective-permute-done.19.refs_3_, ...), custom_call_target="tpu_custom_call" | custom-call | flops 1073741824 | bytes 7340032 | tf_op jit(solution)/shard_map/diag_back/pallas_call | solution.py:189
  59.7 1.4 %collective-permute-start.30 = (bf16[256,256]{1,0:T(8,128)(2,1)S(1)}, bf16[256,256]{1,0:T(8,128)(2,1)S(1)}, u32[]{:S(2)}, u32[]{:S(2)}) collective-permute-start(bf16[256,256]{1,0:T(8,128)(2,1)S(1)} %get-tuple-element.42), channel_id=1, source_target_pairs={{0,16},{16,0},{32,48},{48,32},{64,80},{80,64},{96,112},{112,96},{1... | collective-permute-start | bytes 393224 | tf_op jit(solution)/shard_map/ppermute | solution.py:202
  61.1 1.6 %collective-permute-start.31 = (bf16[256,256]{1,0:T(8,128)(2,1)S(1)}, bf16[256,256]{1,0:T(8,128)(2,1)S(1)}, u32[]{:S(2)}, u32[]{:S(2)}) collective-permute-start(bf16[256,256]{1,0:T(8,128)(2,1)S(1)} %get-tuple-element.43), channel_id=1, source_target_pairs={{0,48},{16,32},{32,16},{48,0},{64,112},{80,96},{96,80},{112,64},{1... | collective-permute-start | bytes 393224 | tf_op jit(solution)/shard_map/ppermute | solution.py:202
  62.8 1.3 %second.2 = (bf16[256,256]{1,0:T(8,128)(2,1)S(1)}, bf16[256,256]{1,0:T(8,128)(2,1)S(1)}, bf16[256,256]{1,0:T(8,128)(2,1)S(1)}, bf16[256,256]{1,0:T(8,128)(2,1)S(1)}, bf16[256,256]{1,0:T(8,128)(2,1)S(1)}) custom-call(s32[1,2]{1,0:T(1,128)S(1)} %bitcast.13, f32[2,256,256]{2,1,0:T(8,128)S(1)} %get-tuple-element.34.own, ...), custom_call_target="tpu_custom_call" | custom-call | flops 1006632960 | bytes 5767168 | tf_op jit(solution)/shard_map/second/pallas_call | solution.py:189
  64.2 1.0 %collective-permute-start.27 = (bf16[256,256]{1,0:T(8,128)(2,1)S(1)}, bf16[256,256]{1,0:T(8,128)(2,1)S(1)}, u32[]{:S(2)}, u32[]{:S(2)}) collective-permute-start(bf16[256,256]{1,0:T(8,128)(2,1)S(1)} %get-tuple-element.38), channel_id=1, source_target_pairs={{0,48},{16,32},{32,16},{48,0},{64,112},{80,96},{96,80},{112,64},{1... | collective-permute-start | bytes 393224 | tf_op jit(solution)/shard_map/ppermute | solution.py:202
  65.2 3.2 %collective-permute-start.29 = (bf16[256,256]{1,0:T(8,128)(2,1)S(1)}, bf16[256,256]{1,0:T(8,128)(2,1)S(1)}, u32[]{:S(2)}, u32[]{:S(2)}) collective-permute-start(bf16[256,256]{1,0:T(8,128)(2,1)S(1)} %add_convert_fusion.2), channel_id=1, source_target_pairs={{0,32},{16,48},{32,0},{48,16},{64,96},{80,112},{96,64},{112,80},{1... | collective-permute-start | bytes 393224 | tf_op jit(solution)/shard_map/ppermute | solution.py:202
  68.5 1.0 %collective-permute-start.32 = (bf16[256,256]{1,0:T(8,128)(2,1)S(1)}, bf16[256,256]{1,0:T(8,128)(2,1)S(1)}, u32[]{:S(2)}, u32[]{:S(2)}) collective-permute-start(bf16[256,256]{1,0:T(8,128)(2,1)S(1)} %add_convert_fusion.1), channel_id=1, source_target_pairs={{0,64},{16,80},{32,96},{48,112},{64,0},{80,16},{96,32},{112,48},{1... | collective-permute-start | bytes 393224 | tf_op jit(solution)/shard_map/ppermute | solution.py:202
  70.1 3.1 %collective-permute-done.27 = bf16[256,256]{1,0:T(8,128)(2,1)S(1)} collective-permute-done((bf16[256,256]{1,0:T(8,128)(2,1)S(1)}, bf16[256,256]{1,0:T(8,128)(2,1)S(1)}, u32[]{:S(2)}, u32[]{:S(2)}) %collective-permute-start.27) | collective-permute-done | bytes 131104 | tf_op jit(solution)/shard_map/ppermute | solution.py:202
  (61 shorter events, 11.7 us)
Async XLA Ops:
  0.6 11.3 %collective-permute-start.4 = (bf16[2,2048,256]{2,1,0:T(8,128)(2,1)}, bf16[2,2048,256]{2,1,0:T(8,128)(2,1)S(1)}, u32[]{:S(2)}, u32[]{:S(2)}) collective-permute-start(bf16[2,2048,256]{2,1,0:T(8,128)(2,1)} %bitcast.4), channel_id=1, source_target_pairs={{0,1},{1,0},{2,3},{3,2},{4,5},{5,4},{6,7},{7,6},{8,9},{9,8},{10,11... | collective-permute-start | bytes 6291464 | tf_op jit(solution)/shard_map/ppermute | solution.py:202
  0.7 10.1 %collective-permute-start = (bf16[256,256]{1,0:T(8,128)(2,1)}, bf16[256,256]{1,0:T(8,128)(2,1)S(1)}, u32[]{:S(2)}, u32[]{:S(2)}) collective-permute-start(bf16[256,256]{1,0:T(8,128)(2,1)} %refs_0_.5), channel_id=1, source_target_pairs={{0,64},{16,80},{32,96},{48,112},{64,0},{80,16},{96,32},{112,48},{1... | collective-permute-start | bytes 393224 | tf_op jit(solution)/shard_map/ppermute | solution.py:202
  2.4 8.6 %collective-permute-start.3 = (bf16[256,256]{1,0:T(8,128)(2,1)}, bf16[256,256]{1,0:T(8,128)(2,1)S(1)}, u32[]{:S(2)}, u32[]{:S(2)}) collective-permute-start(bf16[256,256]{1,0:T(8,128)(2,1)} %refs_0_.5), channel_id=1, source_target_pairs={{0,32},{16,48},{32,0},{48,16},{64,96},{80,112},{96,64},{112,80},{1... | collective-permute-start | bytes 393224 | tf_op jit(solution)/shard_map/ppermute | solution.py:202
  6.3 6.9 %collective-permute-start.6 = (bf16[256,256]{1,0:T(8,128)(2,1)}, bf16[256,256]{1,0:T(8,128)(2,1)S(1)}, u32[]{:S(2)}, u32[]{:S(2)}) collective-permute-start(bf16[256,256]{1,0:T(8,128)(2,1)} %refs_0_.5), channel_id=1, source_target_pairs={{0,48},{16,32},{32,16},{48,0},{64,112},{80,96},{96,80},{112,64},{1... | collective-permute-start | bytes 393224 | tf_op jit(solution)/shard_map/ppermute | solution.py:202
  7.0 7.5 %collective-permute-start.1 = (bf16[256,256]{1,0:T(8,128)(2,1)}, bf16[256,256]{1,0:T(8,128)(2,1)S(1)}, u32[]{:S(2)}, u32[]{:S(2)}) collective-permute-start(bf16[256,256]{1,0:T(8,128)(2,1)} %refs_0_.5), channel_id=1, source_target_pairs={{0,16},{16,0},{32,48},{48,32},{64,80},{80,64},{96,112},{112,96},{1... | collective-permute-start | bytes 393224 | tf_op jit(solution)/shard_map/ppermute | solution.py:202
  10.8 6.3 %collective-permute-start.7 = (bf16[256,256]{1,0:T(8,128)(2,1)S(1)}, bf16[256,256]{1,0:T(8,128)(2,1)S(1)}, u32[]{:S(2)}, u32[]{:S(2)}) collective-permute-start(bf16[256,256]{1,0:T(8,128)(2,1)S(1)} %collective-permute-done.refs_1_), channel_id=1, source_target_pairs={{0,48},{16,32},{32,16},{48,0},{64,112},{80,96},{96,80},{112,64},{1... | collective-permute-start | bytes 393224 | tf_op jit(solution)/shard_map/ppermute | solution.py:202
  11.0 6.2 %collective-permute-start.2 = (bf16[256,256]{1,0:T(8,128)(2,1)S(1)}, bf16[256,256]{1,0:T(8,128)(2,1)S(1)}, u32[]{:S(2)}, u32[]{:S(2)}) collective-permute-start(bf16[256,256]{1,0:T(8,128)(2,1)S(1)} %collective-permute-done.refs_1_), channel_id=1, source_target_pairs={{0,16},{16,0},{32,48},{48,32},{64,80},{80,64},{96,112},{112,96},{1... | collective-permute-start | bytes 393224 | tf_op jit(solution)/shard_map/ppermute | solution.py:202
  11.9 5.2 %collective-permute-start.5 = (bf16[256,256]{1,0:T(8,128)(2,1)S(1)}, bf16[256,256]{1,0:T(8,128)(2,1)S(1)}, u32[]{:S(2)}, u32[]{:S(2)}) collective-permute-start(bf16[256,256]{1,0:T(8,128)(2,1)S(1)} %collective-permute-done.3.refs_4_), channel_id=1, source_target_pairs={{0,64},{16,80},{32,96},{48,112},{64,0},{80,16},{96,32},{112,48},{1... | collective-permute-start | bytes 393224 | tf_op jit(solution)/shard_map/ppermute | solution.py:202
  18.5 2.7 %collective-permute-start.9 = (bf16[4,256,256]{2,1,0:T(8,128)(2,1)S(1)}, bf16[4,256,256]{2,1,0:T(8,128)(2,1)S(1)}, u32[]{:S(2)}, u32[]{:S(2)}) collective-permute-start(bf16[4,256,256]{2,1,0:T(8,128)(2,1)S(1)} %diag_mate.1), channel_id=1, source_target_pairs={{0,1},{1,0},{2,3},{3,2},{4,5},{5,4},{6,7},{7,6},{8,9},{9,8},{10,11... | collective-permute-start | bytes 1572872 | tf_op jit(solution)/shard_map/ppermute | solution.py:202
  19.3 1.8 %collective-permute-start.8 = (bf16[2,256,256]{2,1,0:T(8,128)(2,1)S(1)}, bf16[2,256,256]{2,1,0:T(8,128)(2,1)S(1)}, u32[]{:S(2)}, u32[]{:S(2)}) collective-permute-start(bf16[2,256,256]{2,1,0:T(8,128)(2,1)S(1)} %coeff.1.own), channel_id=1, source_target_pairs={{0,1},{1,0},{2,3},{3,2},{4,5},{5,4},{6,7},{7,6},{8,9},{9,8},{10,11... | collective-permute-start | bytes 786440 | tf_op jit(solution)/shard_map/ppermute | solution.py:202
  21.6 8.3 %collective-permute-start.12 = (bf16[256,256]{1,0:T(8,128)(2,1)S(1)}, bf16[256,256]{1,0:T(8,128)(2,1)S(1)}, u32[]{:S(2)}, u32[]{:S(2)}) collective-permute-start(bf16[256,256]{1,0:T(8,128)(2,1)S(1)} %get-tuple-element.30), channel_id=1, source_target_pairs={{0,2},{1,3},{2,0},{3,1},{4,6},{5,7},{6,4},{7,5},{8,10},{9,11},{10,... | collective-permute-start | bytes 393224 | tf_op jit(solution)/shard_map/ppermute | solution.py:202
  23.5 7.9 %collective-permute-start.14 = (bf16[256,256]{1,0:T(8,128)(2,1)S(1)}, bf16[256,256]{1,0:T(8,128)(2,1)S(1)}, u32[]{:S(2)}, u32[]{:S(2)}) collective-permute-start(bf16[256,256]{1,0:T(8,128)(2,1)S(1)} %get-tuple-element.32), channel_id=1, source_target_pairs={{0,4},{1,5},{2,6},{3,7},{4,0},{5,1},{6,2},{7,3},{8,12},{9,13},{10,... | collective-permute-start | bytes 393224 | tf_op jit(solution)/shard_map/ppermute | solution.py:202
  25.9 7.5 %collective-permute-start.15 = (bf16[256,256]{1,0:T(8,128)(2,1)S(1)}, bf16[256,256]{1,0:T(8,128)(2,1)S(1)}, u32[]{:S(2)}, u32[]{:S(2)}) collective-permute-start(bf16[256,256]{1,0:T(8,128)(2,1)S(1)} %get-tuple-element.33), channel_id=1, source_target_pairs={{0,12},{1,13},{2,14},{3,15},{4,8},{5,9},{6,10},{7,11},{8,4},{9,5},... | collective-permute-start | bytes 393224 | tf_op jit(solution)/shard_map/ppermute | solution.py:202
  27.0 8.7 %collective-permute-start.10 = (bf16[256,256]{1,0:T(8,128)(2,1)S(1)}, bf16[256,256]{1,0:T(8,128)(2,1)S(1)}, u32[]{:S(2)}, u32[]{:S(2)}) collective-permute-start(bf16[256,256]{1,0:T(8,128)(2,1)S(1)} %get-tuple-element.27), channel_id=1, source_target_pairs={{0,4},{1,5},{2,6},{3,7},{4,0},{5,1},{6,2},{7,3},{8,12},{9,13},{10,... | collective-permute-start | bytes 393224 | tf_op jit(solution)/shard_map/ppermute | solution.py:202
  28.2 9.7 %collective-permute-start.11 = (bf16[256,256]{1,0:T(8,128)(2,1)S(1)}, bf16[256,256]{1,0:T(8,128)(2,1)S(1)}, u32[]{:S(2)}, u32[]{:S(2)}) collective-permute-start(bf16[256,256]{1,0:T(8,128)(2,1)S(1)} %get-tuple-element.28), channel_id=1, source_target_pairs={{0,12},{1,13},{2,14},{3,15},{4,8},{5,9},{6,10},{7,11},{8,4},{9,5},... | collective-permute-start | bytes 393224 | tf_op jit(solution)/shard_map/ppermute | solution.py:202
  29.9 8.0 %collective-permute-start.13 = (bf16[256,256]{1,0:T(8,128)(2,1)S(1)}, bf16[256,256]{1,0:T(8,128)(2,1)S(1)}, u32[]{:S(2)}, u32[]{:S(2)}) collective-permute-start(bf16[256,256]{1,0:T(8,128)(2,1)S(1)} %add_convert_fusion.5), channel_id=1, source_target_pairs={{0,8},{1,9},{2,10},{3,11},{4,12},{5,13},{6,14},{7,15},{8,0},{9,1},... | collective-permute-start | bytes 393224 | tf_op jit(solution)/shard_map/ppermute | solution.py:202
  33.5 6.6 %collective-permute-start.16 = (bf16[256,256]{1,0:T(8,128)(2,1)S(1)}, bf16[256,256]{1,0:T(8,128)(2,1)S(1)}, u32[]{:S(2)}, u32[]{:S(2)}) collective-permute-start(bf16[256,256]{1,0:T(8,128)(2,1)S(1)} %add_convert_fusion.4), channel_id=1, source_target_pairs={{0,2},{1,3},{2,0},{3,1},{4,6},{5,7},{6,4},{7,5},{8,10},{9,11},{10,... | collective-permute-start | bytes 393224 | tf_op jit(solution)/shard_map/ppermute | solution.py:202
  40.1 7.3 %collective-permute-start.20 = (bf16[256,256]{1,0:T(8,128)(2,1)S(1)}, bf16[256,256]{1,0:T(8,128)(2,1)S(1)}, u32[]{:S(2)}, u32[]{:S(2)}) collective-permute-start(bf16[256,256]{1,0:T(8,128)(2,1)S(1)} %add_convert_fusion.3.refs_0_), channel_id=1, source_target_pairs={{0,8},{1,9},{2,10},{3,11},{4,12},{5,13},{6,14},{7,15},{8,0},{9,1},... | collective-permute-start | bytes 393224 | tf_op jit(solution)/shard_map/ppermute | solution.py:202
  40.3 8.6 %collective-permute-start.17 = (bf16[256,256]{1,0:T(8,128)(2,1)S(1)}, bf16[256,256]{1,0:T(8,128)(2,1)S(1)}, u32[]{:S(2)}, u32[]{:S(2)}) collective-permute-start(bf16[256,256]{1,0:T(8,128)(2,1)S(1)} %add_convert_fusion.3.refs_0_), channel_id=1, source_target_pairs={{0,2},{1,3},{2,0},{3,1},{4,6},{5,7},{6,4},{7,5},{8,10},{9,11},{10,... | collective-permute-start | bytes 393224 | tf_op jit(solution)/shard_map/ppermute | solution.py:202
  42.4 8.3 %collective-permute-start.22 = (bf16[256,256]{1,0:T(8,128)(2,1)S(1)}, bf16[256,256]{1,0:T(8,128)(2,1)S(1)}, u32[]{:S(2)}, u32[]{:S(2)}) collective-permute-start(bf16[256,256]{1,0:T(8,128)(2,1)S(1)} %add_convert_fusion.3.refs_0_), channel_id=1, source_target_pairs={{0,12},{1,13},{2,14},{3,15},{4,8},{5,9},{6,10},{7,11},{8,4},{9,5},... | collective-permute-start | bytes 393224 | tf_op jit(solution)/shard_map/ppermute | solution.py:202
  43.9 6.8 %collective-permute-start.18 = (bf16[256,256]{1,0:T(8,128)(2,1)S(1)}, bf16[256,256]{1,0:T(8,128)(2,1)S(1)}, u32[]{:S(2)}, u32[]{:S(2)}) collective-permute-start(bf16[256,256]{1,0:T(8,128)(2,1)S(1)} %add_convert_fusion.3.refs_0_), channel_id=1, source_target_pairs={{0,4},{1,5},{2,6},{3,7},{4,0},{5,1},{6,2},{7,3},{8,12},{9,13},{10,... | collective-permute-start | bytes 393224 | tf_op jit(solution)/shard_map/ppermute | solution.py:202
  47.4 6.5 %collective-permute-start.21 = (bf16[256,256]{1,0:T(8,128)(2,1)S(1)}, bf16[256,256]{1,0:T(8,128)(2,1)S(1)}, u32[]{:S(2)}, u32[]{:S(2)}) collective-permute-start(bf16[256,256]{1,0:T(8,128)(2,1)S(1)} %collective-permute-done.20.refs_4_), channel_id=1, source_target_pairs={{0,2},{1,3},{2,0},{3,1},{4,6},{5,7},{6,4},{7,5},{8,10},{9,11},{10,... | collective-permute-start | bytes 393224 | tf_op jit(solution)/shard_map/ppermute | solution.py:202
  48.9 6.2 %collective-permute-start.23 = (bf16[256,256]{1,0:T(8,128)(2,1)S(1)}, bf16[256,256]{1,0:T(8,128)(2,1)S(1)}, u32[]{:S(2)}, u32[]{:S(2)}) collective-permute-start(bf16[256,256]{1,0:T(8,128)(2,1)S(1)} %collective-permute-done.17.refs_1_), channel_id=1, source_target_pairs={{0,12},{1,13},{2,14},{3,15},{4,8},{5,9},{6,10},{7,11},{8,4},{9,5},... | collective-permute-start | bytes 393224 | tf_op jit(solution)/shard_map/ppermute | solution.py:202
  50.6 5.0 %collective-permute-start.19 = (bf16[256,256]{1,0:T(8,128)(2,1)S(1)}, bf16[256,256]{1,0:T(8,128)(2,1)S(1)}, u32[]{:S(2)}, u32[]{:S(2)}) collective-permute-start(bf16[256,256]{1,0:T(8,128)(2,1)S(1)} %collective-permute-done.17.refs_1_), channel_id=1, source_target_pairs={{0,4},{1,5},{2,6},{3,7},{4,0},{5,1},{6,2},{7,3},{8,12},{9,13},{10,... | collective-permute-start | bytes 393224 | tf_op jit(solution)/shard_map/ppermute | solution.py:202
  55.7 2.9 %collective-permute-start.25 = (bf16[4,256,256]{2,1,0:T(8,128)(2,1)S(1)}, bf16[4,256,256]{2,1,0:T(8,128)(2,1)S(1)}, u32[]{:S(2)}, u32[]{:S(2)}) collective-permute-start(bf16[4,256,256]{2,1,0:T(8,128)(2,1)S(1)} %pack.1), channel_id=1, source_target_pairs={{0,1},{1,0},{2,3},{3,2},{4,5},{5,4},{6,7},{7,6},{8,9},{9,8},{10,11... | collective-permute-start | bytes 1572872 | tf_op jit(solution)/shard_map/ppermute | solution.py:202
  59.5 5.7 %collective-permute-start.28 = (bf16[256,256]{1,0:T(8,128)(2,1)S(1)}, bf16[256,256]{1,0:T(8,128)(2,1)S(1)}, u32[]{:S(2)}, u32[]{:S(2)}) collective-permute-start(bf16[256,256]{1,0:T(8,128)(2,1)S(1)} %get-tuple-element.40), channel_id=1, source_target_pairs={{0,64},{16,80},{32,96},{48,112},{64,0},{80,16},{96,32},{112,48},{1... | collective-permute-start | bytes 393224 | tf_op jit(solution)/shard_map/ppermute | solution.py:202
  59.7 8.7 %collective-permute-start.30 = (bf16[256,256]{1,0:T(8,128)(2,1)S(1)}, bf16[256,256]{1,0:T(8,128)(2,1)S(1)}, u32[]{:S(2)}, u32[]{:S(2)}) collective-permute-start(bf16[256,256]{1,0:T(8,128)(2,1)S(1)} %get-tuple-element.42), channel_id=1, source_target_pairs={{0,16},{16,0},{32,48},{48,32},{64,80},{80,64},{96,112},{112,96},{1... | collective-permute-start | bytes 393224 | tf_op jit(solution)/shard_map/ppermute | solution.py:202
  61.1 7.3 %collective-permute-start.31 = (bf16[256,256]{1,0:T(8,128)(2,1)S(1)}, bf16[256,256]{1,0:T(8,128)(2,1)S(1)}, u32[]{:S(2)}, u32[]{:S(2)}) collective-permute-start(bf16[256,256]{1,0:T(8,128)(2,1)S(1)} %get-tuple-element.43), channel_id=1, source_target_pairs={{0,48},{16,32},{32,16},{48,0},{64,112},{80,96},{96,80},{112,64},{1... | collective-permute-start | bytes 393224 | tf_op jit(solution)/shard_map/ppermute | solution.py:202
  64.1 6.0 %collective-permute-start.26 = (bf16[256,256]{1,0:T(8,128)(2,1)S(1)}, bf16[256,256]{1,0:T(8,128)(2,1)S(1)}, u32[]{:S(2)}, u32[]{:S(2)}) collective-permute-start(bf16[256,256]{1,0:T(8,128)(2,1)S(1)} %get-tuple-element.37), channel_id=1, source_target_pairs={{0,16},{16,0},{32,48},{48,32},{64,80},{80,64},{96,112},{112,96},{1... | collective-permute-start | bytes 393224 | tf_op jit(solution)/shard_map/ppermute | solution.py:202
  64.2 9.0 %collective-permute-start.27 = (bf16[256,256]{1,0:T(8,128)(2,1)S(1)}, bf16[256,256]{1,0:T(8,128)(2,1)S(1)}, u32[]{:S(2)}, u32[]{:S(2)}) collective-permute-start(bf16[256,256]{1,0:T(8,128)(2,1)S(1)} %get-tuple-element.38), channel_id=1, source_target_pairs={{0,48},{16,32},{32,16},{48,0},{64,112},{80,96},{96,80},{112,64},{1... | collective-permute-start | bytes 393224 | tf_op jit(solution)/shard_map/ppermute | solution.py:202
  65.2 8.0 %collective-permute-start.29 = (bf16[256,256]{1,0:T(8,128)(2,1)S(1)}, bf16[256,256]{1,0:T(8,128)(2,1)S(1)}, u32[]{:S(2)}, u32[]{:S(2)}) collective-permute-start(bf16[256,256]{1,0:T(8,128)(2,1)S(1)} %add_convert_fusion.2), channel_id=1, source_target_pairs={{0,32},{16,48},{32,0},{48,16},{64,96},{80,112},{96,64},{112,80},{1... | collective-permute-start | bytes 393224 | tf_op jit(solution)/shard_map/ppermute | solution.py:202
  68.5 5.0 %collective-permute-start.32 = (bf16[256,256]{1,0:T(8,128)(2,1)S(1)}, bf16[256,256]{1,0:T(8,128)(2,1)S(1)}, u32[]{:S(2)}, u32[]{:S(2)}) collective-permute-start(bf16[256,256]{1,0:T(8,128)(2,1)S(1)} %add_convert_fusion.1), channel_id=1, source_target_pairs={{0,64},{16,80},{32,96},{48,112},{64,0},{80,16},{96,32},{112,48},{1... | collective-permute-start | bytes 393224 | tf_op jit(solution)/shard_map/ppermute | solution.py:202
  (6 other events, 46.2 us)

commit v7 on v6

--- a/solution.py
+++ b/solution.py
@@ -13,6 +13,7 @@
 REL = [(d, x) for d in range(4) for x in range(2)]
 FAR = [(1, 1), (3, 1), (2, 1)]
 NEAR = [(1, 0), (3, 0), (2, 0), (0, 1), (0, 0)]
+GROUPS_D = [[(1, 1), (3, 1), (2, 1)], [(2, 0), (0, 1)], [(1, 0), (3, 0), (0, 0)]]
 VMEM = pl.BlockSpec(memory_space=pltpu.VMEM)
 
 
@@ -220,8 +221,8 @@
     return total(v.astype(F32) for v in parts).astype(BF16)
 
 
-def scatter(pieces, axis, ring, side):
-    piece = dict(zip(FAR + NEAR, pieces))
+def scatter(pieces, axis, ring, side, order=FAR + NEAR):
+    piece = dict(zip(order, pieces))
     far_1 = swap(piece[(1, 1)], axis, ring)
     far_3 = swap(piece[(3, 1)], axis, 3 * ring)
     far_2 = swap(piece[(2, 1)], axis, side)
@@ -273,7 +274,7 @@
     mate = swap(mate, "tcol", 1)
     (dense_sum,) = call(diag_back_kernel, "diag_back", [*y, dense], [eight_wide], 32 * unit, 24 * size + 2**22)
     terms = []
-    for rels in (FAR, NEAR):
+    for rels in GROUPS_D:
         terms += call(
             functools.partial(second_kernel, rels),
             "second",
@@ -283,7 +284,7 @@
             4 * len(rels) * size + 3 * 2**20,
             buckets,
         )
-    second = scatter(terms, "trow", 1, 4)
+    second = scatter(terms, "trow", 1, 4, sum(GROUPS_D, []))
     return (first, second)
 
 

time: 74.4 us -> 74.4 us (level)
    pallas_call x10 -> x11, Pallas kernels: 8.62 us -> 8.87 us  [call(): pl.pallas_call(kernel, name=name, out_shape=outs, in_specs=[VMEM] * (len(...]
  transfers between devices with their start and end apart: 33 -> 33, of which waited for: 13 -> 12; matrix products, arithmetic and copies ran while one was open for 0% -> 0% of each run, Pallas kernels for 13% -> 13%
where the time goes in v7:
time: 74.4 us; the launch traced here: 74.3 us
  starting transfers between devices  38.4 us (52%)
  waiting for transfers between devices  21.6 us (29%)
  Pallas kernels  12.4 us (17%)
  other arithmetic  1.01 us (1%)
  between operations  0.91 us (1%)
    ppermute x33, starting transfers between devices, swap(): return lax.ppermute(x, axis, [(i, i ^ bits) for i in range(size)])  38.4 us
    ppermute x33, waiting for transfers between devices, swap(): return lax.ppermute(x, axis, [(i, i ^ bits) for i in range(size)])  21.6 us
    pallas_call x11, Pallas kernels, call(): pl.pallas_call(kernel, name=name, out_shape=outs, in_specs=[VMEM] * (len(...  8.87 us
    pallas_call x1, Pallas kernels, load(): pl.pallas_call(load_kernel, name='load', out_shape=[pltpu.VMEM(v.shape, v...  3.52 us
  transfers between devices with their start and end apart: 33, of which 12 were waited for; matrix products, arithmetic and copies ran while one was open for 0% of the time, Pallas kernels for 13%

profile of v7, /device:TPU:0, one launch (start us, length us, event | category | flops | bytes accessed | tf_op | source)
XLA Modules:
  0.0 74.3 jit_solution(7660315716455176293)
XLA Ops:
  0.7 1.7 %collective-permute-start = (bf16[256,256]{1,0:T(8,128)(2,1)}, bf16[256,256]{1,0:T(8,128)(2,1)S(1)}, u32[]{:S(2)}, u32[]{:S(2)}) collective-permute-start(bf16[256,256]{1,0:T(8,128)(2,1)} %refs_0_.5), channel_id=1, source_target_pairs={{0,64},{16,80},{32,96},{48,112},{64,0},{80,16},{96,32},{112,48},{1... | collective-permute-start | bytes 393224 | tf_op jit(solution)/shard_map/ppermute | solution.py:203
  2.4 3.9 %collective-permute-start.3 = (bf16[256,256]{1,0:T(8,128)(2,1)}, bf16[256,256]{1,0:T(8,128)(2,1)S(1)}, u32[]{:S(2)}, u32[]{:S(2)}) collective-permute-start(bf16[256,256]{1,0:T(8,128)(2,1)} %refs_0_.5), channel_id=1, source_target_pairs={{0,32},{16,48},{32,0},{48,16},{64,96},{80,112},{96,64},{112,80},{1... | collective-permute-start | bytes 393224 | tf_op jit(solution)/shard_map/ppermute | solution.py:203
  7.3 3.5 %load.1.refs_8_.dense = bf16[2048,2048]{1,0:T(8,128)(2,1)S(1)} custom-call(bf16[2048,2048]{1,0:T(8,128)(2,1)} %bitcast.16), custom_call_target="tpu_custom_call" | custom-call | bytes 20971520 | tf_op jit(solution)/shard_map/load/pallas_call | solution.py:177
  11.0 1.0 %collective-permute-start.2 = (bf16[256,256]{1,0:T(8,128)(2,1)S(1)}, bf16[256,256]{1,0:T(8,128)(2,1)S(1)}, u32[]{:S(2)}, u32[]{:S(2)}) collective-permute-start(bf16[256,256]{1,0:T(8,128)(2,1)S(1)} %collective-permute-done.refs_1_), channel_id=1, source_target_pairs={{0,16},{16,0},{32,48},{48,32},{64,80},{80,64},{96,112},{112,96},{1... | collective-permute-start | bytes 393224 | tf_op jit(solution)/shard_map/ppermute | solution.py:203
  13.1 1.3 %collective-permute-done.1.refs_2_ = bf16[256,256]{1,0:T(8,128)(2,1)S(1)} collective-permute-done((bf16[256,256]{1,0:T(8,128)(2,1)}, bf16[256,256]{1,0:T(8,128)(2,1)S(1)}, u32[]{:S(2)}, u32[]{:S(2)}) %collective-permute-start.1) | collective-permute-done | bytes 131104 | tf_op jit(solution)/shard_map/ppermute | solution.py:203
  14.5 2.7 %collective-permute-done.7.refs_7_ = bf16[256,256]{1,0:T(8,128)(2,1)S(1)} collective-permute-done((bf16[256,256]{1,0:T(8,128)(2,1)S(1)}, bf16[256,256]{1,0:T(8,128)(2,1)S(1)}, u32[]{:S(2)}, u32[]{:S(2)}) %collective-permute-start.7) | collective-permute-done | bytes 131104 | tf_op jit(solution)/shard_map/ppermute | solution.py:203
  17.1 1.3 %diag_mate.1 = bf16[4,256,256]{2,1,0:T(8,128)(2,1)S(1)} custom-call(bf16[256,256]{1,0:T(8,128)(2,1)S(1)} %copy-done.3, bf16[256,256]{1,0:T(8,128)(2,1)S(1)} %collective-permute-done.refs_1_, bf16[256,256]{1,0:T(8,128)(2,1)S(1)} %collective-permute-done.1.refs_2_, bf16[256,256]{1,0:T(8,128)(2,1)S(1)} %collective-permute-done.2.refs_3_, ...), custom_call_target="tpu_custom_call" | custom-call | flops 1073741824 | bytes 9961472 | tf_op jit(solution)/shard_map/diag_mate/pallas_call | solution.py:190
  19.9 1.3 %diag_own.1.dense_own = bf16[4,256,256]{2,1,0:T(8,128)(2,1)S(1)} custom-call(bf16[256,256]{1,0:T(8,128)(2,1)S(1)} %copy-done.3, bf16[256,256]{1,0:T(8,128)(2,1)S(1)} %collective-permute-done.refs_1_, bf16[256,256]{1,0:T(8,128)(2,1)S(1)} %collective-permute-done.1.refs_2_, bf16[256,256]{1,0:T(8,128)(2,1)S(1)} %collective-permute-done.2.refs_3_, ...), custom_call_target="tpu_custom_call" | custom-call | flops 1073741824 | bytes 9961472 | tf_op jit(solution)/shard_map/diag_own/pallas_call | solution.py:190
  21.6 1.8 %collective-permute-start.12 = (bf16[256,256]{1,0:T(8,128)(2,1)S(1)}, bf16[256,256]{1,0:T(8,128)(2,1)S(1)}, u32[]{:S(2)}, u32[]{:S(2)}) collective-permute-start(bf16[256,256]{1,0:T(8,128)(2,1)S(1)} %get-tuple-element.30), channel_id=1, source_target_pairs={{0,2},{1,3},{2,0},{3,1},{4,6},{5,7},{6,4},{7,5},{8,10},{9,11},{10,... | collective-permute-start | bytes 393224 | tf_op jit(solution)/shard_map/ppermute | solution.py:203
  23.5 2.5 %collective-permute-start.14 = (bf16[256,256]{1,0:T(8,128)(2,1)S(1)}, bf16[256,256]{1,0:T(8,128)(2,1)S(1)}, u32[]{:S(2)}, u32[]{:S(2)}) collective-permute-start(bf16[256,256]{1,0:T(8,128)(2,1)S(1)} %get-tuple-element.32), channel_id=1, source_target_pairs={{0,4},{1,5},{2,6},{3,7},{4,0},{5,1},{6,2},{7,3},{8,12},{9,13},{10,... | collective-permute-start | bytes 393224 | tf_op jit(solution)/shard_map/ppermute | solution.py:203
  27.0 1.3 %collective-permute-start.10 = (bf16[256,256]{1,0:T(8,128)(2,1)S(1)}, bf16[256,256]{1,0:T(8,128)(2,1)S(1)}, u32[]{:S(2)}, u32[]{:S(2)}) collective-permute-start(bf16[256,256]{1,0:T(8,128)(2,1)S(1)} %get-tuple-element.27), channel_id=1, source_target_pairs={{0,4},{1,5},{2,6},{3,7},{4,0},{5,1},{6,2},{7,3},{8,12},{9,13},{10,... | collective-permute-start | bytes 393224 | tf_op jit(solution)/shard_map/ppermute | solution.py:203
  28.2 1.7 %collective-permute-start.11 = (bf16[256,256]{1,0:T(8,128)(2,1)S(1)}, bf16[256,256]{1,0:T(8,128)(2,1)S(1)}, u32[]{:S(2)}, u32[]{:S(2)}) collective-permute-start(bf16[256,256]{1,0:T(8,128)(2,1)S(1)} %get-tuple-element.28), channel_id=1, source_target_pairs={{0,12},{1,13},{2,14},{3,15},{4,8},{5,9},{6,10},{7,11},{8,4},{9,5},... | collective-permute-start | bytes 393224 | tf_op jit(solution)/shard_map/ppermute | solution.py:203
  29.9 1.5 %collective-permute-start.13 = (bf16[256,256]{1,0:T(8,128)(2,1)S(1)}, bf16[256,256]{1,0:T(8,128)(2,1)S(1)}, u32[]{:S(2)}, u32[]{:S(2)}) collective-permute-start(bf16[256,256]{1,0:T(8,128)(2,1)S(1)} %add_convert_fusion.5), channel_id=1, source_target_pairs={{0,8},{1,9},{2,10},{3,11},{4,12},{5,13},{6,14},{7,15},{8,0},{9,1},... | collective-permute-start | bytes 393224 | tf_op jit(solution)/shard_map/ppermute | solution.py:203
  31.4 2.0 %collective-permute-done.15 = bf16[256,256]{1,0:T(8,128)(2,1)S(1)} collective-permute-done((bf16[256,256]{1,0:T(8,128)(2,1)S(1)}, bf16[256,256]{1,0:T(8,128)(2,1)S(1)}, u32[]{:S(2)}, u32[]{:S(2)}) %collective-permute-start.15) | collective-permute-done | bytes 131104 | tf_op jit(solution)/shard_map/ppermute | solution.py:203
  33.5 2.2 %collective-permute-start.16 = (bf16[256,256]{1,0:T(8,128)(2,1)S(1)}, bf16[256,256]{1,0:T(8,128)(2,1)S(1)}, u32[]{:S(2)}, u32[]{:S(2)}) collective-permute-start(bf16[256,256]{1,0:T(8,128)(2,1)S(1)} %add_convert_fusion.4), channel_id=1, source_target_pairs={{0,2},{1,3},{2,0},{3,1},{4,6},{5,7},{6,4},{7,5},{8,10},{9,11},{10,... | collective-permute-start | bytes 393224 | tf_op jit(solution)/shard_map/ppermute | solution.py:203
  35.6 2.3 %collective-permute-done.11 = bf16[256,256]{1,0:T(8,128)(2,1)S(1)} collective-permute-done((bf16[256,256]{1,0:T(8,128)(2,1)S(1)}, bf16[256,256]{1,0:T(8,128)(2,1)S(1)}, u32[]{:S(2)}, u32[]{:S(2)}) %collective-permute-start.11) | collective-permute-done | bytes 131104 | tf_op jit(solution)/shard_map/ppermute | solution.py:203
  38.0 2.1 %collective-permute-done.16 = bf16[256,256]{1,0:T(8,128)(2,1)S(1)} collective-permute-done((bf16[256,256]{1,0:T(8,128)(2,1)S(1)}, bf16[256,256]{1,0:T(8,128)(2,1)S(1)}, u32[]{:S(2)}, u32[]{:S(2)}) %collective-permute-start.16) | collective-permute-done | bytes 131104 | tf_op jit(solution)/shard_map/ppermute | solution.py:203
  40.4 2.0 %collective-permute-start.17 = (bf16[256,256]{1,0:T(8,128)(2,1)S(1)}, bf16[256,256]{1,0:T(8,128)(2,1)S(1)}, u32[]{:S(2)}, u32[]{:S(2)}) collective-permute-start(bf16[256,256]{1,0:T(8,128)(2,1)S(1)} %add_convert_fusion.3.refs_0_), channel_id=1, source_target_pairs={{0,2},{1,3},{2,0},{3,1},{4,6},{5,7},{6,4},{7,5},{8,10},{9,11},{10,... | collective-permute-start | bytes 393224 | tf_op jit(solution)/shard_map/ppermute | solution.py:203
  42.4 1.5 %collective-permute-start.22 = (bf16[256,256]{1,0:T(8,128)(2,1)S(1)}, bf16[256,256]{1,0:T(8,128)(2,1)S(1)}, u32[]{:S(2)}, u32[]{:S(2)}) collective-permute-start(bf16[256,256]{1,0:T(8,128)(2,1)S(1)} %add_convert_fusion.3.refs_0_), channel_id=1, source_target_pairs={{0,12},{1,13},{2,14},{3,15},{4,8},{5,9},{6,10},{7,11},{8,4},{9,5},... | collective-permute-start | bytes 393224 | tf_op jit(solution)/shard_map/ppermute | solution.py:203
  43.9 1.9 %collective-permute-start.18 = (bf16[256,256]{1,0:T(8,128)(2,1)S(1)}, bf16[256,256]{1,0:T(8,128)(2,1)S(1)}, u32[]{:S(2)}, u32[]{:S(2)}) collective-permute-start(bf16[256,256]{1,0:T(8,128)(2,1)S(1)} %add_convert_fusion.3.refs_0_), channel_id=1, source_target_pairs={{0,4},{1,5},{2,6},{3,7},{4,0},{5,1},{6,2},{7,3},{8,12},{9,13},{10,... | collective-permute-start | bytes 393224 | tf_op jit(solution)/shard_map/ppermute | solution.py:203
  45.8 1.7 %collective-permute-done.20.refs_4_ = bf16[256,256]{1,0:T(8,128)(2,1)S(1)} collective-permute-done((bf16[256,256]{1,0:T(8,128)(2,1)S(1)}, bf16[256,256]{1,0:T(8,128)(2,1)S(1)}, u32[]{:S(2)}, u32[]{:S(2)}) %collective-permute-start.20) | collective-permute-done | bytes 131104 | tf_op jit(solution)/shard_map/ppermute | solution.py:203
  47.5 1.5 %collective-permute-start.21 = (bf16[256,256]{1,0:T(8,128)(2,1)S(1)}, bf16[256,256]{1,0:T(8,128)(2,1)S(1)}, u32[]{:S(2)}, u32[]{:S(2)}) collective-permute-start(bf16[256,256]{1,0:T(8,128)(2,1)S(1)} %collective-permute-done.20.refs_4_), channel_id=1, source_target_pairs={{0,2},{1,3},{2,0},{3,1},{4,6},{5,7},{6,4},{7,5},{8,10},{9,11},{10,... | collective-permute-start | bytes 393224 | tf_op jit(solution)/shard_map/ppermute | solution.py:203
  49.0 1.7 %collective-permute-start.23 = (bf16[256,256]{1,0:T(8,128)(2,1)S(1)}, bf16[256,256]{1,0:T(8,128)(2,1)S(1)}, u32[]{:S(2)}, u32[]{:S(2)}) collective-permute-start(bf16[256,256]{1,0:T(8,128)(2,1)S(1)} %collective-permute-done.17.refs_1_), channel_id=1, source_target_pairs={{0,12},{1,13},{2,14},{3,15},{4,8},{5,9},{6,10},{7,11},{8,4},{9,5},... | collective-permute-start | bytes 393224 | tf_op jit(solution)/shard_map/ppermute | solution.py:203
  50.7 3.3 %collective-permute-done.21.refs_5_ = bf16[256,256]{1,0:T(8,128)(2,1)S(1)} collective-permute-done((bf16[256,256]{1,0:T(8,128)(2,1)S(1)}, bf16[256,256]{1,0:T(8,128)(2,1)S(1)}, u32[]{:S(2)}, u32[]{:S(2)}) %collective-permute-start.21) | collective-permute-done | bytes 131104 | tf_op jit(solution)/shard_map/ppermute | solution.py:203
  53.9 1.2 %collective-permute-done.23.refs_7_ = bf16[256,256]{1,0:T(8,128)(2,1)S(1)} collective-permute-done((bf16[256,256]{1,0:T(8,128)(2,1)S(1)}, bf16[256,256]{1,0:T(8,128)(2,1)S(1)}, u32[]{:S(2)}, u32[]{:S(2)}) %collective-permute-start.23) | collective-permute-done | bytes 131104 | tf_op jit(solution)/shard_map/ppermute | solution.py:203
  57.3 1.3 %diag_back.1.dense_sum = f32[8,256,256]{2,1,0:T(8,128)S(1)} custom-call(bf16[256,256]{1,0:T(8,128)(2,1)S(1)} %add_convert_fusion.3.refs_0_, bf16[256,256]{1,0:T(8,128)(2,1)S(1)} %collective-permute-done.17.refs_1_, bf16[256,256]{1,0:T(8,128)(2,1)S(1)} %collective-permute-done.18.refs_2_, bf16[256,256]{1,0:T(8,128)(2,1)S(1)} %collective-permute-done.19.refs_3_, ...), custom_call_target="tpu_custom_call" | custom-call | flops 1073741824 | bytes 7340032 | tf_op jit(solution)/shard_map/diag_back/pallas_call | solution.py:190
  59.7 1.4 %collective-permute-start.30 = (bf16[256,256]{1,0:T(8,128)(2,1)S(1)}, bf16[256,256]{1,0:T(8,128)(2,1)S(1)}, u32[]{:S(2)}, u32[]{:S(2)}) collective-permute-start(bf16[256,256]{1,0:T(8,128)(2,1)S(1)} %get-tuple-element.42), channel_id=1, source_target_pairs={{0,16},{16,0},{32,48},{48,32},{64,80},{80,64},{96,112},{112,96},{1... | collective-permute-start | bytes 393224 | tf_op jit(solution)/shard_map/ppermute | solution.py:203
  61.1 1.6 %collective-permute-start.31 = (bf16[256,256]{1,0:T(8,128)(2,1)S(1)}, bf16[256,256]{1,0:T(8,128)(2,1)S(1)}, u32[]{:S(2)}, u32[]{:S(2)}) collective-permute-start(bf16[256,256]{1,0:T(8,128)(2,1)S(1)} %get-tuple-element.43), channel_id=1, source_target_pairs={{0,48},{16,32},{32,16},{48,0},{64,112},{80,96},{96,80},{112,64},{1... | collective-permute-start | bytes 393224 | tf_op jit(solution)/shard_map/ppermute | solution.py:203
  64.0 1.0 %collective-permute-start.27 = (bf16[256,256]{1,0:T(8,128)(2,1)S(1)}, bf16[256,256]{1,0:T(8,128)(2,1)S(1)}, u32[]{:S(2)}, u32[]{:S(2)}) collective-permute-start(bf16[256,256]{1,0:T(8,128)(2,1)S(1)} %get-tuple-element.38), channel_id=1, source_target_pairs={{0,48},{16,32},{32,16},{48,0},{64,112},{80,96},{96,80},{112,64},{1... | collective-permute-start | bytes 393224 | tf_op jit(solution)/shard_map/ppermute | solution.py:203
  65.8 2.6 %collective-permute-start.29 = (bf16[256,256]{1,0:T(8,128)(2,1)S(1)}, bf16[256,256]{1,0:T(8,128)(2,1)S(1)}, u32[]{:S(2)}, u32[]{:S(2)}) collective-permute-start(bf16[256,256]{1,0:T(8,128)(2,1)S(1)} %add_convert_fusion.2), channel_id=1, source_target_pairs={{0,32},{16,48},{32,0},{48,16},{64,96},{80,112},{96,64},{112,80},{1... | collective-permute-start | bytes 393224 | tf_op jit(solution)/shard_map/ppermute | solution.py:203
  68.5 1.2 %collective-permute-start.32 = (bf16[256,256]{1,0:T(8,128)(2,1)S(1)}, bf16[256,256]{1,0:T(8,128)(2,1)S(1)}, u32[]{:S(2)}, u32[]{:S(2)}) collective-permute-start(bf16[256,256]{1,0:T(8,128)(2,1)S(1)} %add_convert_fusion.1), channel_id=1, source_target_pairs={{0,64},{16,80},{32,96},{48,112},{64,0},{80,16},{96,32},{112,48},{1... | collective-permute-start | bytes 393224 | tf_op jit(solution)/shard_map/ppermute | solution.py:203
  69.6 3.5 %collective-permute-done.27 = bf16[256,256]{1,0:T(8,128)(2,1)S(1)} collective-permute-done((bf16[256,256]{1,0:T(8,128)(2,1)S(1)}, bf16[256,256]{1,0:T(8,128)(2,1)S(1)}, u32[]{:S(2)}, u32[]{:S(2)}) %collective-permute-start.27) | collective-permute-done | bytes 131104 | tf_op jit(solution)/shard_map/ppermute | solution.py:203
  (62 shorter events, 12.1 us)
Async XLA Ops:
  0.6 11.3 %collective-permute-start.4 = (bf16[2,2048,256]{2,1,0:T(8,128)(2,1)}, bf16[2,2048,256]{2,1,0:T(8,128)(2,1)S(1)}, u32[]{:S(2)}, u32[]{:S(2)}) collective-permute-start(bf16[2,2048,256]{2,1,0:T(8,128)(2,1)} %bitcast.8), channel_id=1, source_target_pairs={{0,1},{1,0},{2,3},{3,2},{4,5},{5,4},{6,7},{7,6},{8,9},{9,8},{10,11... | collective-permute-start | bytes 6291464 | tf_op jit(solution)/shard_map/ppermute | solution.py:203
  0.7 10.1 %collective-permute-start = (bf16[256,256]{1,0:T(8,128)(2,1)}, bf16[256,256]{1,0:T(8,128)(2,1)S(1)}, u32[]{:S(2)}, u32[]{:S(2)}) collective-permute-start(bf16[256,256]{1,0:T(8,128)(2,1)} %refs_0_.5), channel_id=1, source_target_pairs={{0,64},{16,80},{32,96},{48,112},{64,0},{80,16},{96,32},{112,48},{1... | collective-permute-start | bytes 393224 | tf_op jit(solution)/shard_map/ppermute | solution.py:203
  2.4 8.6 %collective-permute-start.3 = (bf16[256,256]{1,0:T(8,128)(2,1)}, bf16[256,256]{1,0:T(8,128)(2,1)S(1)}, u32[]{:S(2)}, u32[]{:S(2)}) collective-permute-start(bf16[256,256]{1,0:T(8,128)(2,1)} %refs_0_.5), channel_id=1, source_target_pairs={{0,32},{16,48},{32,0},{48,16},{64,96},{80,112},{96,64},{112,80},{1... | collective-permute-start | bytes 393224 | tf_op jit(solution)/shard_map/ppermute | solution.py:203
  6.3 6.9 %collective-permute-start.6 = (bf16[256,256]{1,0:T(8,128)(2,1)}, bf16[256,256]{1,0:T(8,128)(2,1)S(1)}, u32[]{:S(2)}, u32[]{:S(2)}) collective-permute-start(bf16[256,256]{1,0:T(8,128)(2,1)} %refs_0_.5), channel_id=1, source_target_pairs={{0,48},{16,32},{32,16},{48,0},{64,112},{80,96},{96,80},{112,64},{1... | collective-permute-start | bytes 393224 | tf_op jit(solution)/shard_map/ppermute | solution.py:203
  7.0 7.5 %collective-permute-start.1 = (bf16[256,256]{1,0:T(8,128)(2,1)}, bf16[256,256]{1,0:T(8,128)(2,1)S(1)}, u32[]{:S(2)}, u32[]{:S(2)}) collective-permute-start(bf16[256,256]{1,0:T(8,128)(2,1)} %refs_0_.5), channel_id=1, source_target_pairs={{0,16},{16,0},{32,48},{48,32},{64,80},{80,64},{96,112},{112,96},{1... | collective-permute-start | bytes 393224 | tf_op jit(solution)/shard_map/ppermute | solution.py:203
  10.8 6.3 %collective-permute-start.7 = (bf16[256,256]{1,0:T(8,128)(2,1)S(1)}, bf16[256,256]{1,0:T(8,128)(2,1)S(1)}, u32[]{:S(2)}, u32[]{:S(2)}) collective-permute-start(bf16[256,256]{1,0:T(8,128)(2,1)S(1)} %collective-permute-done.refs_1_), channel_id=1, source_target_pairs={{0,48},{16,32},{32,16},{48,0},{64,112},{80,96},{96,80},{112,64},{1... | collective-permute-start | bytes 393224 | tf_op jit(solution)/shard_map/ppermute | solution.py:203
  11.0 6.2 %collective-permute-start.2 = (bf16[256,256]{1,0:T(8,128)(2,1)S(1)}, bf16[256,256]{1,0:T(8,128)(2,1)S(1)}, u32[]{:S(2)}, u32[]{:S(2)}) collective-permute-start(bf16[256,256]{1,0:T(8,128)(2,1)S(1)} %collective-permute-done.refs_1_), channel_id=1, source_target_pairs={{0,16},{16,0},{32,48},{48,32},{64,80},{80,64},{96,112},{112,96},{1... | collective-permute-start | bytes 393224 | tf_op jit(solution)/shard_map/ppermute | solution.py:203
  11.9 5.2 %collective-permute-start.5 = (bf16[256,256]{1,0:T(8,128)(2,1)S(1)}, bf16[256,256]{1,0:T(8,128)(2,1)S(1)}, u32[]{:S(2)}, u32[]{:S(2)}) collective-permute-start(bf16[256,256]{1,0:T(8,128)(2,1)S(1)} %collective-permute-done.3.refs_4_), channel_id=1, source_target_pairs={{0,64},{16,80},{32,96},{48,112},{64,0},{80,16},{96,32},{112,48},{1... | collective-permute-start | bytes 393224 | tf_op jit(solution)/shard_map/ppermute | solution.py:203
  18.5 2.7 %collective-permute-start.9 = (bf16[4,256,256]{2,1,0:T(8,128)(2,1)S(1)}, bf16[4,256,256]{2,1,0:T(8,128)(2,1)S(1)}, u32[]{:S(2)}, u32[]{:S(2)}) collective-permute-start(bf16[4,256,256]{2,1,0:T(8,128)(2,1)S(1)} %diag_mate.1), channel_id=1, source_target_pairs={{0,1},{1,0},{2,3},{3,2},{4,5},{5,4},{6,7},{7,6},{8,9},{9,8},{10,11... | collective-permute-start | bytes 1572872 | tf_op jit(solution)/shard_map/ppermute | solution.py:203
  19.3 1.8 %collective-permute-start.8 = (bf16[2,256,256]{2,1,0:T(8,128)(2,1)S(1)}, bf16[2,256,256]{2,1,0:T(8,128)(2,1)S(1)}, u32[]{:S(2)}, u32[]{:S(2)}) collective-permute-start(bf16[2,256,256]{2,1,0:T(8,128)(2,1)S(1)} %coeff.1.own), channel_id=1, source_target_pairs={{0,1},{1,0},{2,3},{3,2},{4,5},{5,4},{6,7},{7,6},{8,9},{9,8},{10,11... | collective-permute-start | bytes 786440 | tf_op jit(solution)/shard_map/ppermute | solution.py:203
  21.6 8.3 %collective-permute-start.12 = (bf16[256,256]{1,0:T(8,128)(2,1)S(1)}, bf16[256,256]{1,0:T(8,128)(2,1)S(1)}, u32[]{:S(2)}, u32[]{:S(2)}) collective-permute-start(bf16[256,256]{1,0:T(8,128)(2,1)S(1)} %get-tuple-element.30), channel_id=1, source_target_pairs={{0,2},{1,3},{2,0},{3,1},{4,6},{5,7},{6,4},{7,5},{8,10},{9,11},{10,... | collective-permute-start | bytes 393224 | tf_op jit(solution)/shard_map/ppermute | solution.py:203
  23.5 7.9 %collective-permute-start.14 = (bf16[256,256]{1,0:T(8,128)(2,1)S(1)}, bf16[256,256]{1,0:T(8,128)(2,1)S(1)}, u32[]{:S(2)}, u32[]{:S(2)}) collective-permute-start(bf16[256,256]{1,0:T(8,128)(2,1)S(1)} %get-tuple-element.32), channel_id=1, source_target_pairs={{0,4},{1,5},{2,6},{3,7},{4,0},{5,1},{6,2},{7,3},{8,12},{9,13},{10,... | collective-permute-start | bytes 393224 | tf_op jit(solution)/shard_map/ppermute | solution.py:203
  25.9 7.5 %collective-permute-start.15 = (bf16[256,256]{1,0:T(8,128)(2,1)S(1)}, bf16[256,256]{1,0:T(8,128)(2,1)S(1)}, u32[]{:S(2)}, u32[]{:S(2)}) collective-permute-start(bf16[256,256]{1,0:T(8,128)(2,1)S(1)} %get-tuple-element.33), channel_id=1, source_target_pairs={{0,12},{1,13},{2,14},{3,15},{4,8},{5,9},{6,10},{7,11},{8,4},{9,5},... | collective-permute-start | bytes 393224 | tf_op jit(solution)/shard_map/ppermute | solution.py:203
  27.0 8.7 %collective-permute-start.10 = (bf16[256,256]{1,0:T(8,128)(2,1)S(1)}, bf16[256,256]{1,0:T(8,128)(2,1)S(1)}, u32[]{:S(2)}, u32[]{:S(2)}) collective-permute-start(bf16[256,256]{1,0:T(8,128)(2,1)S(1)} %get-tuple-element.27), channel_id=1, source_target_pairs={{0,4},{1,5},{2,6},{3,7},{4,0},{5,1},{6,2},{7,3},{8,12},{9,13},{10,... | collective-permute-start | bytes 393224 | tf_op jit(solution)/shard_map/ppermute | solution.py:203
  28.2 9.7 %collective-permute-start.11 = (bf16[256,256]{1,0:T(8,128)(2,1)S(1)}, bf16[256,256]{1,0:T(8,128)(2,1)S(1)}, u32[]{:S(2)}, u32[]{:S(2)}) collective-permute-start(bf16[256,256]{1,0:T(8,128)(2,1)S(1)} %get-tuple-element.28), channel_id=1, source_target_pairs={{0,12},{1,13},{2,14},{3,15},{4,8},{5,9},{6,10},{7,11},{8,4},{9,5},... | collective-permute-start | bytes 393224 | tf_op jit(solution)/shard_map/ppermute | solution.py:203
  29.9 8.0 %collective-permute-start.13 = (bf16[256,256]{1,0:T(8,128)(2,1)S(1)}, bf16[256,256]{1,0:T(8,128)(2,1)S(1)}, u32[]{:S(2)}, u32[]{:S(2)}) collective-permute-start(bf16[256,256]{1,0:T(8,128)(2,1)S(1)} %add_convert_fusion.5), channel_id=1, source_target_pairs={{0,8},{1,9},{2,10},{3,11},{4,12},{5,13},{6,14},{7,15},{8,0},{9,1},... | collective-permute-start | bytes 393224 | tf_op jit(solution)/shard_map/ppermute | solution.py:203
  33.5 6.6 %collective-permute-start.16 = (bf16[256,256]{1,0:T(8,128)(2,1)S(1)}, bf16[256,256]{1,0:T(8,128)(2,1)S(1)}, u32[]{:S(2)}, u32[]{:S(2)}) collective-permute-start(bf16[256,256]{1,0:T(8,128)(2,1)S(1)} %add_convert_fusion.4), channel_id=1, source_target_pairs={{0,2},{1,3},{2,0},{3,1},{4,6},{5,7},{6,4},{7,5},{8,10},{9,11},{10,... | collective-permute-start | bytes 393224 | tf_op jit(solution)/shard_map/ppermute | solution.py:203
  40.1 7.3 %collective-permute-start.20 = (bf16[256,256]{1,0:T(8,128)(2,1)S(1)}, bf16[256,256]{1,0:T(8,128)(2,1)S(1)}, u32[]{:S(2)}, u32[]{:S(2)}) collective-permute-start(bf16[256,256]{1,0:T(8,128)(2,1)S(1)} %add_convert_fusion.3.refs_0_), channel_id=1, source_target_pairs={{0,8},{1,9},{2,10},{3,11},{4,12},{5,13},{6,14},{7,15},{8,0},{9,1},... | collective-permute-start | bytes 393224 | tf_op jit(solution)/shard_map/ppermute | solution.py:203
  40.4 8.6 %collective-permute-start.17 = (bf16[256,256]{1,0:T(8,128)(2,1)S(1)}, bf16[256,256]{1,0:T(8,128)(2,1)S(1)}, u32[]{:S(2)}, u32[]{:S(2)}) collective-permute-start(bf16[256,256]{1,0:T(8,128)(2,1)S(1)} %add_convert_fusion.3.refs_0_), channel_id=1, source_target_pairs={{0,2},{1,3},{2,0},{3,1},{4,6},{5,7},{6,4},{7,5},{8,10},{9,11},{10,... | collective-permute-start | bytes 393224 | tf_op jit(solution)/shard_map/ppermute | solution.py:203
  42.4 8.3 %collective-permute-start.22 = (bf16[256,256]{1,0:T(8,128)(2,1)S(1)}, bf16[256,256]{1,0:T(8,128)(2,1)S(1)}, u32[]{:S(2)}, u32[]{:S(2)}) collective-permute-start(bf16[256,256]{1,0:T(8,128)(2,1)S(1)} %add_convert_fusion.3.refs_0_), channel_id=1, source_target_pairs={{0,12},{1,13},{2,14},{3,15},{4,8},{5,9},{6,10},{7,11},{8,4},{9,5},... | collective-permute-start | bytes 393224 | tf_op jit(solution)/shard_map/ppermute | solution.py:203
  43.9 6.8 %collective-permute-start.18 = (bf16[256,256]{1,0:T(8,128)(2,1)S(1)}, bf16[256,256]{1,0:T(8,128)(2,1)S(1)}, u32[]{:S(2)}, u32[]{:S(2)}) collective-permute-start(bf16[256,256]{1,0:T(8,128)(2,1)S(1)} %add_convert_fusion.3.refs_0_), channel_id=1, source_target_pairs={{0,4},{1,5},{2,6},{3,7},{4,0},{5,1},{6,2},{7,3},{8,12},{9,13},{10,... | collective-permute-start | bytes 393224 | tf_op jit(solution)/shard_map/ppermute | solution.py:203
  47.5 6.5 %collective-permute-start.21 = (bf16[256,256]{1,0:T(8,128)(2,1)S(1)}, bf16[256,256]{1,0:T(8,128)(2,1)S(1)}, u32[]{:S(2)}, u32[]{:S(2)}) collective-permute-start(bf16[256,256]{1,0:T(8,128)(2,1)S(1)} %collective-permute-done.20.refs_4_), channel_id=1, source_target_pairs={{0,2},{1,3},{2,0},{3,1},{4,6},{5,7},{6,4},{7,5},{8,10},{9,11},{10,... | collective-permute-start | bytes 393224 | tf_op jit(solution)/shard_map/ppermute | solution.py:203
  49.0 6.2 %collective-permute-start.23 = (bf16[256,256]{1,0:T(8,128)(2,1)S(1)}, bf16[256,256]{1,0:T(8,128)(2,1)S(1)}, u32[]{:S(2)}, u32[]{:S(2)}) collective-permute-start(bf16[256,256]{1,0:T(8,128)(2,1)S(1)} %collective-permute-done.17.refs_1_), channel_id=1, source_target_pairs={{0,12},{1,13},{2,14},{3,15},{4,8},{5,9},{6,10},{7,11},{8,4},{9,5},... | collective-permute-start | bytes 393224 | tf_op jit(solution)/shard_map/ppermute | solution.py:203
  50.7 5.0 %collective-permute-start.19 = (bf16[256,256]{1,0:T(8,128)(2,1)S(1)}, bf16[256,256]{1,0:T(8,128)(2,1)S(1)}, u32[]{:S(2)}, u32[]{:S(2)}) collective-permute-start(bf16[256,256]{1,0:T(8,128)(2,1)S(1)} %collective-permute-done.17.refs_1_), channel_id=1, source_target_pairs={{0,4},{1,5},{2,6},{3,7},{4,0},{5,1},{6,2},{7,3},{8,12},{9,13},{10,... | collective-permute-start | bytes 393224 | tf_op jit(solution)/shard_map/ppermute | solution.py:203
  55.7 2.9 %collective-permute-start.25 = (bf16[4,256,256]{2,1,0:T(8,128)(2,1)S(1)}, bf16[4,256,256]{2,1,0:T(8,128)(2,1)S(1)}, u32[]{:S(2)}, u32[]{:S(2)}) collective-permute-start(bf16[4,256,256]{2,1,0:T(8,128)(2,1)S(1)} %pack.1), channel_id=1, source_target_pairs={{0,1},{1,0},{2,3},{3,2},{4,5},{5,4},{6,7},{7,6},{8,9},{9,8},{10,11... | collective-permute-start | bytes 1572872 | tf_op jit(solution)/shard_map/ppermute | solution.py:203
  59.5 6.3 %collective-permute-start.28 = (bf16[256,256]{1,0:T(8,128)(2,1)S(1)}, bf16[256,256]{1,0:T(8,128)(2,1)S(1)}, u32[]{:S(2)}, u32[]{:S(2)}) collective-permute-start(bf16[256,256]{1,0:T(8,128)(2,1)S(1)} %get-tuple-element.40), channel_id=1, source_target_pairs={{0,64},{16,80},{32,96},{48,112},{64,0},{80,16},{96,32},{112,48},{1... | collective-permute-start | bytes 393224 | tf_op jit(solution)/shard_map/ppermute | solution.py:203
  59.7 8.7 %collective-permute-start.30 = (bf16[256,256]{1,0:T(8,128)(2,1)S(1)}, bf16[256,256]{1,0:T(8,128)(2,1)S(1)}, u32[]{:S(2)}, u32[]{:S(2)}) collective-permute-start(bf16[256,256]{1,0:T(8,128)(2,1)S(1)} %get-tuple-element.42), channel_id=1, source_target_pairs={{0,16},{16,0},{32,48},{48,32},{64,80},{80,64},{96,112},{112,96},{1... | collective-permute-start | bytes 393224 | tf_op jit(solution)/shard_map/ppermute | solution.py:203
  61.1 7.3 %collective-permute-start.31 = (bf16[256,256]{1,0:T(8,128)(2,1)S(1)}, bf16[256,256]{1,0:T(8,128)(2,1)S(1)}, u32[]{:S(2)}, u32[]{:S(2)}) collective-permute-start(bf16[256,256]{1,0:T(8,128)(2,1)S(1)} %get-tuple-element.43), channel_id=1, source_target_pairs={{0,48},{16,32},{32,16},{48,0},{64,112},{80,96},{96,80},{112,64},{1... | collective-permute-start | bytes 393224 | tf_op jit(solution)/shard_map/ppermute | solution.py:203
  63.7 5.9 %collective-permute-start.26 = (bf16[256,256]{1,0:T(8,128)(2,1)S(1)}, bf16[256,256]{1,0:T(8,128)(2,1)S(1)}, u32[]{:S(2)}, u32[]{:S(2)}) collective-permute-start(bf16[256,256]{1,0:T(8,128)(2,1)S(1)} %get-tuple-element.37), channel_id=1, source_target_pairs={{0,16},{16,0},{32,48},{48,32},{64,80},{80,64},{96,112},{112,96},{1... | collective-permute-start | bytes 393224 | tf_op jit(solution)/shard_map/ppermute | solution.py:203
  64.0 9.1 %collective-permute-start.27 = (bf16[256,256]{1,0:T(8,128)(2,1)S(1)}, bf16[256,256]{1,0:T(8,128)(2,1)S(1)}, u32[]{:S(2)}, u32[]{:S(2)}) collective-permute-start(bf16[256,256]{1,0:T(8,128)(2,1)S(1)} %get-tuple-element.38), channel_id=1, source_target_pairs={{0,48},{16,32},{32,16},{48,0},{64,112},{80,96},{96,80},{112,64},{1... | collective-permute-start | bytes 393224 | tf_op jit(solution)/shard_map/ppermute | solution.py:203
  65.8 7.4 %collective-permute-start.29 = (bf16[256,256]{1,0:T(8,128)(2,1)S(1)}, bf16[256,256]{1,0:T(8,128)(2,1)S(1)}, u32[]{:S(2)}, u32[]{:S(2)}) collective-permute-start(bf16[256,256]{1,0:T(8,128)(2,1)S(1)} %add_convert_fusion.2), channel_id=1, source_target_pairs={{0,32},{16,48},{32,0},{48,16},{64,96},{80,112},{96,64},{112,80},{1... | collective-permute-start | bytes 393224 | tf_op jit(solution)/shard_map/ppermute | solution.py:203
  68.5 5.0 %collective-permute-start.32 = (bf16[256,256]{1,0:T(8,128)(2,1)S(1)}, bf16[256,256]{1,0:T(8,128)(2,1)S(1)}, u32[]{:S(2)}, u32[]{:S(2)}) collective-permute-start(bf16[256,256]{1,0:T(8,128)(2,1)S(1)} %add_convert_fusion.1), channel_id=1, source_target_pairs={{0,64},{16,80},{32,96},{48,112},{64,0},{80,16},{96,32},{112,48},{1... | collective-permute-start | bytes 393224 | tf_op jit(solution)/shard_map/ppermute | solution.py:203
  (6 other events, 46.2 us)

commit v8 on v7

--- a/solution.py
+++ b/solution.py
@@ -208,7 +208,7 @@
     got[(0, 1)] = swap(own, axis, side)
     got[(2, 0)] = swap(own, axis, 2 * ring)
     if first is not None:
-        got[(2, 0)], first, *loaded = lax.optimization_barrier((got[(2, 0)], first, *loaded))
+        got[(2, 0)], first = lax.optimization_barrier((got[(2, 0)], first))
     got[(1, 0)] = swap(own, axis, ring)
     got[(3, 0)] = swap(own, axis, 3 * ring)
     got[(1, 1)] = swap(got[(0, 1)], axis, ring)
@@ -249,8 +249,9 @@
     eight_wide = jax.ShapeDtypeStruct((8, count, PIECE), F32)
 
     left_mate = swap(left, "tcol", 1)
-    x, left_mate, loaded = gather(signal, "trow", 1, 4, left_mate, load(dense))
-    (dense,) = loaded
+    x, left_mate, _ = gather(signal, "trow", 1, 4, left_mate)
+    x[6], dense = lax.optimization_barrier((x[6], dense))
+    (dense,) = load(dense)
     (coeff,) = call(coeff_kernel, "coeff", [*x, right], [pair], 16 * unit, 10 * size + 2**21, buckets)
     coeff_mate = swap(coeff, "tcol", 1)
     (dense_sent,) = call(functools.partial(diag_kernel, 1), "diag_mate", [*x, dense], [four], 32 * unit, 12 * size + 2**23)

time: 74.4 us -> 74.4 us (level)
  waiting for transfers between devices: 21.6 us -> 18.6 us
  starting transfers between devices: 38.4 us -> 41.3 us
    ppermute x33, waiting for transfers between devices: 21.6 us -> 18.6 us  [swap(): return lax.ppermute(x, axis, [(i, i ^ bits) for i in range(size)])]
    ppermute x33, starting transfers between devices: 38.4 us -> 41.3 us  [swap(): return lax.ppermute(x, axis, [(i, i ^ bits) for i in range(size)])]
  transfers between devices with their start and end apart: 33 -> 33, of which waited for: 12 -> 11; matrix products, arithmetic and copies ran while one was open for 0% -> 0% of each run, Pallas kernels for 13% -> 13%
where the time goes in v8:
time: 74.4 us; the launch traced here: 74.3 us
  starting transfers between devices  41.3 us (56%)
  waiting for transfers between devices  18.6 us (25%)
  Pallas kernels  12.4 us (17%)
  other arithmetic  1.01 us (1%)
  between operations  0.92 us (1%)
    ppermute x33, starting transfers between devices, swap(): return lax.ppermute(x, axis, [(i, i ^ bits) for i in range(size)])  41.3 us
    ppermute x33, waiting for transfers between devices, swap(): return lax.ppermute(x, axis, [(i, i ^ bits) for i in range(size)])  18.6 us
    pallas_call x11, Pallas kernels, call(): pl.pallas_call(kernel, name=name, out_shape=outs, in_specs=[VMEM] * (len(...  8.86 us
    pallas_call x1, Pallas kernels, load(): pl.pallas_call(load_kernel, name='load', out_shape=[pltpu.VMEM(v.shape, v...  3.52 us
  transfers between devices with their start and end apart: 33, of which 11 were waited for; matrix products, arithmetic and copies ran while one was open for 0% of the time, Pallas kernels for 13%

profile of v8, /device:TPU:0, one launch (start us, length us, event | category | flops | bytes accessed | tf_op | source)
XLA Modules:
  0.0 74.3 jit_solution(9424629442559225528)
XLA Ops:
  0.7 1.7 %collective-permute-start = (bf16[256,256]{1,0:T(8,128)(2,1)}, bf16[256,256]{1,0:T(8,128)(2,1)S(1)}, u32[]{:S(2)}, u32[]{:S(2)}) collective-permute-start(bf16[256,256]{1,0:T(8,128)(2,1)} %refs_0_.5), channel_id=1, source_target_pairs={{0,64},{16,80},{32,96},{48,112},{64,0},{80,16},{96,32},{112,48},{1... | collective-permute-start | bytes 393224 | tf_op jit(solution)/shard_map/ppermute | solution.py:203
  2.4 3.9 %collective-permute-start.3 = (bf16[256,256]{1,0:T(8,128)(2,1)}, bf16[256,256]{1,0:T(8,128)(2,1)S(1)}, u32[]{:S(2)}, u32[]{:S(2)}) collective-permute-start(bf16[256,256]{1,0:T(8,128)(2,1)} %refs_0_.5), channel_id=1, source_target_pairs={{0,32},{16,48},{32,0},{48,16},{64,96},{80,112},{96,64},{112,80},{1... | collective-permute-start | bytes 393224 | tf_op jit(solution)/shard_map/ppermute | solution.py:203
  7.3 3.7 %collective-permute-start.7 = (bf16[256,256]{1,0:T(8,128)(2,1)S(1)}, bf16[256,256]{1,0:T(8,128)(2,1)S(1)}, u32[]{:S(2)}, u32[]{:S(2)}) collective-permute-start(bf16[256,256]{1,0:T(8,128)(2,1)S(1)} %collective-permute-done.refs_1_), channel_id=1, source_target_pairs={{0,48},{16,32},{32,16},{48,0},{64,112},{80,96},{96,80},{112,64},{1... | collective-permute-start | bytes 393224 | tf_op jit(solution)/shard_map/ppermute | solution.py:203
  11.0 1.0 %collective-permute-start.2 = (bf16[256,256]{1,0:T(8,128)(2,1)S(1)}, bf16[256,256]{1,0:T(8,128)(2,1)S(1)}, u32[]{:S(2)}, u32[]{:S(2)}) collective-permute-start(bf16[256,256]{1,0:T(8,128)(2,1)S(1)} %collective-permute-done.refs_1_), channel_id=1, source_target_pairs={{0,16},{16,0},{32,48},{48,32},{64,80},{80,64},{96,112},{112,96},{1... | collective-permute-start | bytes 393224 | tf_op jit(solution)/shard_map/ppermute | solution.py:203
  12.6 1.5 %collective-permute-done.6.refs_6_ = bf16[256,256]{1,0:T(8,128)(2,1)S(1)} collective-permute-done((bf16[256,256]{1,0:T(8,128)(2,1)}, bf16[256,256]{1,0:T(8,128)(2,1)S(1)}, u32[]{:S(2)}, u32[]{:S(2)}) %collective-permute-start.6) | collective-permute-done | bytes 131104 | tf_op jit(solution)/shard_map/ppermute | solution.py:203
  14.1 3.5 %load.1.refs_8_.dense = bf16[2048,2048]{1,0:T(8,128)(2,1)S(1)} custom-call(bf16[2048,2048]{1,0:T(8,128)(2,1)} %bitcast.16), custom_call_target="tpu_custom_call" | custom-call | bytes 20971520 | tf_op jit(solution)/shard_map/load/pallas_call | solution.py:177
  17.7 1.3 %diag_mate.1 = bf16[4,256,256]{2,1,0:T(8,128)(2,1)S(1)} custom-call(bf16[256,256]{1,0:T(8,128)(2,1)S(1)} %copy-done.3, bf16[256,256]{1,0:T(8,128)(2,1)S(1)} %collective-permute-done.refs_1_, bf16[256,256]{1,0:T(8,128)(2,1)S(1)} %collective-permute-done.1.refs_2_, bf16[256,256]{1,0:T(8,128)(2,1)S(1)} %collective-permute-done.2.refs_3_, ...), custom_call_target="tpu_custom_call" | custom-call | flops 1073741824 | bytes 9961472 | tf_op jit(solution)/shard_map/diag_mate/pallas_call | solution.py:190
  20.4 1.3 %diag_own.1.dense_own = bf16[4,256,256]{2,1,0:T(8,128)(2,1)S(1)} custom-call(bf16[256,256]{1,0:T(8,128)(2,1)S(1)} %copy-done.3, bf16[256,256]{1,0:T(8,128)(2,1)S(1)} %collective-permute-done.refs_1_, bf16[256,256]{1,0:T(8,128)(2,1)S(1)} %collective-permute-done.1.refs_2_, bf16[256,256]{1,0:T(8,128)(2,1)S(1)} %collective-permute-done.2.refs_3_, ...), custom_call_target="tpu_custom_call" | custom-call | flops 1073741824 | bytes 9961472 | tf_op jit(solution)/shard_map/diag_own/pallas_call | solution.py:190
  22.6 1.6 %collective-permute-start.14 = (bf16[256,256]{1,0:T(8,128)(2,1)S(1)}, bf16[256,256]{1,0:T(8,128)(2,1)S(1)}, u32[]{:S(2)}, u32[]{:S(2)}) collective-permute-start(bf16[256,256]{1,0:T(8,128)(2,1)S(1)} %get-tuple-element.34), channel_id=1, source_target_pairs={{0,4},{1,5},{2,6},{3,7},{4,0},{5,1},{6,2},{7,3},{8,12},{9,13},{10,... | collective-permute-start | bytes 393224 | tf_op jit(solution)/shard_map/ppermute | solution.py:203
  24.2 2.2 %collective-permute-start.15 = (bf16[256,256]{1,0:T(8,128)(2,1)S(1)}, bf16[256,256]{1,0:T(8,128)(2,1)S(1)}, u32[]{:S(2)}, u32[]{:S(2)}) collective-permute-start(bf16[256,256]{1,0:T(8,128)(2,1)S(1)} %get-tuple-element.35), channel_id=1, source_target_pairs={{0,12},{1,13},{2,14},{3,15},{4,8},{5,9},{6,10},{7,11},{8,4},{9,5},... | collective-permute-start | bytes 393224 | tf_op jit(solution)/shard_map/ppermute | solution.py:203
  27.0 0.8 %collective-permute-start.10 = (bf16[256,256]{1,0:T(8,128)(2,1)S(1)}, bf16[256,256]{1,0:T(8,128)(2,1)S(1)}, u32[]{:S(2)}, u32[]{:S(2)}) collective-permute-start(bf16[256,256]{1,0:T(8,128)(2,1)S(1)} %get-tuple-element.29), channel_id=1, source_target_pairs={{0,4},{1,5},{2,6},{3,7},{4,0},{5,1},{6,2},{7,3},{8,12},{9,13},{10,... | collective-permute-start | bytes 393224 | tf_op jit(solution)/shard_map/ppermute | solution.py:203
  28.3 1.0 %collective-permute-done.12 = bf16[256,256]{1,0:T(8,128)(2,1)S(1)} collective-permute-done((bf16[256,256]{1,0:T(8,128)(2,1)S(1)}, bf16[256,256]{1,0:T(8,128)(2,1)S(1)}, u32[]{:S(2)}, u32[]{:S(2)}) %collective-permute-start.12) | collective-permute-done | bytes 131104 | tf_op jit(solution)/shard_map/ppermute | solution.py:203
  29.4 1.9 %collective-permute-start.13 = (bf16[256,256]{1,0:T(8,128)(2,1)S(1)}, bf16[256,256]{1,0:T(8,128)(2,1)S(1)}, u32[]{:S(2)}, u32[]{:S(2)}) collective-permute-start(bf16[256,256]{1,0:T(8,128)(2,1)S(1)} %add_convert_fusion.5), channel_id=1, source_target_pairs={{0,8},{1,9},{2,10},{3,11},{4,12},{5,13},{6,14},{7,15},{8,0},{9,1},... | collective-permute-start | bytes 393224 | tf_op jit(solution)/shard_map/ppermute | solution.py:203
  31.3 2.0 %collective-permute-start.16 = (bf16[256,256]{1,0:T(8,128)(2,1)S(1)}, bf16[256,256]{1,0:T(8,128)(2,1)S(1)}, u32[]{:S(2)}, u32[]{:S(2)}) collective-permute-start(bf16[256,256]{1,0:T(8,128)(2,1)S(1)} %add_convert_fusion.4), channel_id=1, source_target_pairs={{0,2},{1,3},{2,0},{3,1},{4,6},{5,7},{6,4},{7,5},{8,10},{9,11},{10,... | collective-permute-start | bytes 393224 | tf_op jit(solution)/shard_map/ppermute | solution.py:203
  33.4 3.3 %collective-permute-done.11 = bf16[256,256]{1,0:T(8,128)(2,1)S(1)} collective-permute-done((bf16[256,256]{1,0:T(8,128)(2,1)S(1)}, bf16[256,256]{1,0:T(8,128)(2,1)S(1)}, u32[]{:S(2)}, u32[]{:S(2)}) %collective-permute-start.11) | collective-permute-done | bytes 131104 | tf_op jit(solution)/shard_map/ppermute | solution.py:203
  36.7 1.2 %collective-permute-done.16 = bf16[256,256]{1,0:T(8,128)(2,1)S(1)} collective-permute-done((bf16[256,256]{1,0:T(8,128)(2,1)S(1)}, bf16[256,256]{1,0:T(8,128)(2,1)S(1)}, u32[]{:S(2)}, u32[]{:S(2)}) %collective-permute-start.16) | collective-permute-done | bytes 131104 | tf_op jit(solution)/shard_map/ppermute | solution.py:203
  38.0 2.1 %collective-permute-start.20 = (bf16[256,256]{1,0:T(8,128)(2,1)S(1)}, bf16[256,256]{1,0:T(8,128)(2,1)S(1)}, u32[]{:S(2)}, u32[]{:S(2)}) collective-permute-start(bf16[256,256]{1,0:T(8,128)(2,1)S(1)} %add_convert_fusion.3.refs_0_), channel_id=1, source_target_pairs={{0,8},{1,9},{2,10},{3,11},{4,12},{5,13},{6,14},{7,15},{8,0},{9,1},... | collective-permute-start | bytes 393224 | tf_op jit(solution)/shard_map/ppermute | solution.py:203
  40.1 1.4 %collective-permute-start.17 = (bf16[256,256]{1,0:T(8,128)(2,1)S(1)}, bf16[256,256]{1,0:T(8,128)(2,1)S(1)}, u32[]{:S(2)}, u32[]{:S(2)}) collective-permute-start(bf16[256,256]{1,0:T(8,128)(2,1)S(1)} %add_convert_fusion.3.refs_0_), channel_id=1, source_target_pairs={{0,2},{1,3},{2,0},{3,1},{4,6},{5,7},{6,4},{7,5},{8,10},{9,11},{10,... | collective-permute-start | bytes 393224 | tf_op jit(solution)/shard_map/ppermute | solution.py:203
  41.5 1.9 %collective-permute-start.22 = (bf16[256,256]{1,0:T(8,128)(2,1)S(1)}, bf16[256,256]{1,0:T(8,128)(2,1)S(1)}, u32[]{:S(2)}, u32[]{:S(2)}) collective-permute-start(bf16[256,256]{1,0:T(8,128)(2,1)S(1)} %add_convert_fusion.3.refs_0_), channel_id=1, source_target_pairs={{0,12},{1,13},{2,14},{3,15},{4,8},{5,9},{6,10},{7,11},{8,4},{9,5},... | collective-permute-start | bytes 393224 | tf_op jit(solution)/shard_map/ppermute | solution.py:203
  43.5 2.0 %collective-permute-done.20.refs_4_ = bf16[256,256]{1,0:T(8,128)(2,1)S(1)} collective-permute-done((bf16[256,256]{1,0:T(8,128)(2,1)S(1)}, bf16[256,256]{1,0:T(8,128)(2,1)S(1)}, u32[]{:S(2)}, u32[]{:S(2)}) %collective-permute-start.20) | collective-permute-done | bytes 131104 | tf_op jit(solution)/shard_map/ppermute | solution.py:203
  45.5 1.9 %collective-permute-start.21 = (bf16[256,256]{1,0:T(8,128)(2,1)S(1)}, bf16[256,256]{1,0:T(8,128)(2,1)S(1)}, u32[]{:S(2)}, u32[]{:S(2)}) collective-permute-start(bf16[256,256]{1,0:T(8,128)(2,1)S(1)} %collective-permute-done.20.refs_4_), channel_id=1, source_target_pairs={{0,2},{1,3},{2,0},{3,1},{4,6},{5,7},{6,4},{7,5},{8,10},{9,11},{10,... | collective-permute-start | bytes 393224 | tf_op jit(solution)/shard_map/ppermute | solution.py:203
  47.8 0.9 %collective-permute-start.23 = (bf16[256,256]{1,0:T(8,128)(2,1)S(1)}, bf16[256,256]{1,0:T(8,128)(2,1)S(1)}, u32[]{:S(2)}, u32[]{:S(2)}) collective-permute-start(bf16[256,256]{1,0:T(8,128)(2,1)S(1)} %collective-permute-done.17.refs_1_), channel_id=1, source_target_pairs={{0,12},{1,13},{2,14},{3,15},{4,8},{5,9},{6,10},{7,11},{8,4},{9,5},... | collective-permute-start | bytes 393224 | tf_op jit(solution)/shard_map/ppermute | solution.py:203
  49.7 2.3 %collective-permute-done.21.refs_5_ = bf16[256,256]{1,0:T(8,128)(2,1)S(1)} collective-permute-done((bf16[256,256]{1,0:T(8,128)(2,1)S(1)}, bf16[256,256]{1,0:T(8,128)(2,1)S(1)}, u32[]{:S(2)}, u32[]{:S(2)}) %collective-permute-start.21) | collective-permute-done | bytes 131104 | tf_op jit(solution)/shard_map/ppermute | solution.py:203
  52.0 2.0 %collective-permute-done.23.refs_7_ = bf16[256,256]{1,0:T(8,128)(2,1)S(1)} collective-permute-done((bf16[256,256]{1,0:T(8,128)(2,1)S(1)}, bf16[256,256]{1,0:T(8,128)(2,1)S(1)}, u32[]{:S(2)}, u32[]{:S(2)}) %collective-permute-start.23) | collective-permute-done | bytes 131104 | tf_op jit(solution)/shard_map/ppermute | solution.py:203
  55.7 1.3 %diag_back.1.dense_sum = f32[8,256,256]{2,1,0:T(8,128)S(1)} custom-call(bf16[256,256]{1,0:T(8,128)(2,1)S(1)} %add_convert_fusion.3.refs_0_, bf16[256,256]{1,0:T(8,128)(2,1)S(1)} %collective-permute-done.17.refs_1_, bf16[256,256]{1,0:T(8,128)(2,1)S(1)} %collective-permute-done.18.refs_2_, bf16[256,256]{1,0:T(8,128)(2,1)S(1)} %collective-permute-done.19.refs_3_, ...), custom_call_target="tpu_custom_call" | custom-call | flops 1073741824 | bytes 7340032 | tf_op jit(solution)/shard_map/diag_back/pallas_call | solution.py:190
  57.0 0.9 %second.5 = (bf16[256,256]{1,0:T(8,128)(2,1)S(1)}, bf16[256,256]{1,0:T(8,128)(2,1)S(1)}, bf16[256,256]{1,0:T(8,128)(2,1)S(1)}) custom-call(s32[1,2]{1,0:T(1,128)S(1)} %bitcast.13, f32[2,256,256]{2,1,0:T(8,128)S(1)} %get-tuple-element.36.own, bf16[2,256,256]{2,1,0:T(8,128)(2,1)S(1)} %collective-permute-done.24.mate, bf16[2,2048,256]{2,1,0:T(8,128)(2,1)S(1)} %bitcast.5, ...), custom_call_target="tpu_custom_call" | custom-call | flops 603979776 | bytes 4718592 | tf_op jit(solution)/shard_map/second/pallas_call | solution.py:190
  57.9 1.4 %collective-permute-start.28 = (bf16[256,256]{1,0:T(8,128)(2,1)S(1)}, bf16[256,256]{1,0:T(8,128)(2,1)S(1)}, u32[]{:S(2)}, u32[]{:S(2)}) collective-permute-start(bf16[256,256]{1,0:T(8,128)(2,1)S(1)} %get-tuple-element.42), channel_id=1, source_target_pairs={{0,64},{16,80},{32,96},{48,112},{64,0},{80,16},{96,32},{112,48},{1... | collective-permute-start | bytes 393224 | tf_op jit(solution)/shard_map/ppermute | solution.py:203
  59.3 1.5 %collective-permute-start.30 = (bf16[256,256]{1,0:T(8,128)(2,1)S(1)}, bf16[256,256]{1,0:T(8,128)(2,1)S(1)}, u32[]{:S(2)}, u32[]{:S(2)}) collective-permute-start(bf16[256,256]{1,0:T(8,128)(2,1)S(1)} %get-tuple-element.44), channel_id=1, source_target_pairs={{0,16},{16,0},{32,48},{48,32},{64,80},{80,64},{96,112},{112,96},{1... | collective-permute-start | bytes 393224 | tf_op jit(solution)/shard_map/ppermute | solution.py:203
  60.8 2.0 %collective-permute-start.31 = (bf16[256,256]{1,0:T(8,128)(2,1)S(1)}, bf16[256,256]{1,0:T(8,128)(2,1)S(1)}, u32[]{:S(2)}, u32[]{:S(2)}) collective-permute-start(bf16[256,256]{1,0:T(8,128)(2,1)S(1)} %get-tuple-element.45), channel_id=1, source_target_pairs={{0,48},{16,32},{32,16},{48,0},{64,112},{80,96},{96,80},{112,64},{1... | collective-permute-start | bytes 393224 | tf_op jit(solution)/shard_map/ppermute | solution.py:203
  62.8 0.9 %second.3 = (bf16[256,256]{1,0:T(8,128)(2,1)S(1)}, bf16[256,256]{1,0:T(8,128)(2,1)S(1)}, bf16[256,256]{1,0:T(8,128)(2,1)S(1)}) custom-call(s32[1,2]{1,0:T(1,128)S(1)} %bitcast.14, f32[2,256,256]{2,1,0:T(8,128)S(1)} %get-tuple-element.36.own, bf16[2,256,256]{2,1,0:T(8,128)(2,1)S(1)} %collective-permute-done.24.mate, bf16[2,2048,256]{2,1,0:T(8,128)(2,1)S(1)} %bitcast.6, ...), custom_call_target="tpu_custom_call" | custom-call | flops 603979776 | bytes 4718592 | tf_op jit(solution)/shard_map/second/pallas_call | solution.py:190
  65.7 2.7 %collective-permute-start.29 = (bf16[256,256]{1,0:T(8,128)(2,1)S(1)}, bf16[256,256]{1,0:T(8,128)(2,1)S(1)}, u32[]{:S(2)}, u32[]{:S(2)}) collective-permute-start(bf16[256,256]{1,0:T(8,128)(2,1)S(1)} %add_convert_fusion.2), channel_id=1, source_target_pairs={{0,32},{16,48},{32,0},{48,16},{64,96},{80,112},{96,64},{112,80},{1... | collective-permute-start | bytes 393224 | tf_op jit(solution)/shard_map/ppermute | solution.py:203
  69.2 4.2 %collective-permute-done.27 = bf16[256,256]{1,0:T(8,128)(2,1)S(1)} collective-permute-done((bf16[256,256]{1,0:T(8,128)(2,1)S(1)}, bf16[256,256]{1,0:T(8,128)(2,1)S(1)}, u32[]{:S(2)}, u32[]{:S(2)}) %collective-permute-start.27) | collective-permute-done | bytes 131104 | tf_op jit(solution)/shard_map/ppermute | solution.py:203
  (62 shorter events, 12.2 us)
Async XLA Ops:
  0.6 11.3 %collective-permute-start.4 = (bf16[2,2048,256]{2,1,0:T(8,128)(2,1)}, bf16[2,2048,256]{2,1,0:T(8,128)(2,1)S(1)}, u32[]{:S(2)}, u32[]{:S(2)}) collective-permute-start(bf16[2,2048,256]{2,1,0:T(8,128)(2,1)} %bitcast.8), channel_id=1, source_target_pairs={{0,1},{1,0},{2,3},{3,2},{4,5},{5,4},{6,7},{7,6},{8,9},{9,8},{10,11... | collective-permute-start | bytes 6291464 | tf_op jit(solution)/shard_map/ppermute | solution.py:203
  0.7 6.6 %collective-permute-start = (bf16[256,256]{1,0:T(8,128)(2,1)}, bf16[256,256]{1,0:T(8,128)(2,1)S(1)}, u32[]{:S(2)}, u32[]{:S(2)}) collective-permute-start(bf16[256,256]{1,0:T(8,128)(2,1)} %refs_0_.5), channel_id=1, source_target_pairs={{0,64},{16,80},{32,96},{48,112},{64,0},{80,16},{96,32},{112,48},{1... | collective-permute-start | bytes 393224 | tf_op jit(solution)/shard_map/ppermute | solution.py:203
  2.4 8.6 %collective-permute-start.3 = (bf16[256,256]{1,0:T(8,128)(2,1)}, bf16[256,256]{1,0:T(8,128)(2,1)S(1)}, u32[]{:S(2)}, u32[]{:S(2)}) collective-permute-start(bf16[256,256]{1,0:T(8,128)(2,1)} %refs_0_.5), channel_id=1, source_target_pairs={{0,32},{16,48},{32,0},{48,16},{64,96},{80,112},{96,64},{112,80},{1... | collective-permute-start | bytes 393224 | tf_op jit(solution)/shard_map/ppermute | solution.py:203
  6.3 7.8 %collective-permute-start.6 = (bf16[256,256]{1,0:T(8,128)(2,1)}, bf16[256,256]{1,0:T(8,128)(2,1)S(1)}, u32[]{:S(2)}, u32[]{:S(2)}) collective-permute-start(bf16[256,256]{1,0:T(8,128)(2,1)} %refs_0_.5), channel_id=1, source_target_pairs={{0,48},{16,32},{32,16},{48,0},{64,112},{80,96},{96,80},{112,64},{1... | collective-permute-start | bytes 393224 | tf_op jit(solution)/shard_map/ppermute | solution.py:203
  7.0 10.6 %collective-permute-start.1 = (bf16[256,256]{1,0:T(8,128)(2,1)}, bf16[256,256]{1,0:T(8,128)(2,1)S(1)}, u32[]{:S(2)}, u32[]{:S(2)}) collective-permute-start(bf16[256,256]{1,0:T(8,128)(2,1)} %refs_0_.5), channel_id=1, source_target_pairs={{0,16},{16,0},{32,48},{48,32},{64,80},{80,64},{96,112},{112,96},{1... | collective-permute-start | bytes 393224 | tf_op jit(solution)/shard_map/ppermute | solution.py:203
  7.3 10.3 %collective-permute-start.7 = (bf16[256,256]{1,0:T(8,128)(2,1)S(1)}, bf16[256,256]{1,0:T(8,128)(2,1)S(1)}, u32[]{:S(2)}, u32[]{:S(2)}) collective-permute-start(bf16[256,256]{1,0:T(8,128)(2,1)S(1)} %collective-permute-done.refs_1_), channel_id=1, source_target_pairs={{0,48},{16,32},{32,16},{48,0},{64,112},{80,96},{96,80},{112,64},{1... | collective-permute-start | bytes 393224 | tf_op jit(solution)/shard_map/ppermute | solution.py:203
  11.0 6.7 %collective-permute-start.2 = (bf16[256,256]{1,0:T(8,128)(2,1)S(1)}, bf16[256,256]{1,0:T(8,128)(2,1)S(1)}, u32[]{:S(2)}, u32[]{:S(2)}) collective-permute-start(bf16[256,256]{1,0:T(8,128)(2,1)S(1)} %collective-permute-done.refs_1_), channel_id=1, source_target_pairs={{0,16},{16,0},{32,48},{48,32},{64,80},{80,64},{96,112},{112,96},{1... | collective-permute-start | bytes 393224 | tf_op jit(solution)/shard_map/ppermute | solution.py:203
  11.9 5.7 %collective-permute-start.5 = (bf16[256,256]{1,0:T(8,128)(2,1)S(1)}, bf16[256,256]{1,0:T(8,128)(2,1)S(1)}, u32[]{:S(2)}, u32[]{:S(2)}) collective-permute-start(bf16[256,256]{1,0:T(8,128)(2,1)S(1)} %collective-permute-done.3.refs_4_), channel_id=1, source_target_pairs={{0,64},{16,80},{32,96},{48,112},{64,0},{80,16},{96,32},{112,48},{1... | collective-permute-start | bytes 393224 | tf_op jit(solution)/shard_map/ppermute | solution.py:203
  19.0 2.7 %collective-permute-start.9 = (bf16[4,256,256]{2,1,0:T(8,128)(2,1)S(1)}, bf16[4,256,256]{2,1,0:T(8,128)(2,1)S(1)}, u32[]{:S(2)}, u32[]{:S(2)}) collective-permute-start(bf16[4,256,256]{2,1,0:T(8,128)(2,1)S(1)} %diag_mate.1), channel_id=1, source_target_pairs={{0,1},{1,0},{2,3},{3,2},{4,5},{5,4},{6,7},{7,6},{8,9},{9,8},{10,11... | collective-permute-start | bytes 1572872 | tf_op jit(solution)/shard_map/ppermute | solution.py:203
  22.2 7.2 %collective-permute-start.12 = (bf16[256,256]{1,0:T(8,128)(2,1)S(1)}, bf16[256,256]{1,0:T(8,128)(2,1)S(1)}, u32[]{:S(2)}, u32[]{:S(2)}) collective-permute-start(bf16[256,256]{1,0:T(8,128)(2,1)S(1)} %get-tuple-element.32), channel_id=1, source_target_pairs={{0,2},{1,3},{2,0},{3,1},{4,6},{5,7},{6,4},{7,5},{8,10},{9,11},{10,... | collective-permute-start | bytes 393224 | tf_op jit(solution)/shard_map/ppermute | solution.py:203
  22.6 8.6 %collective-permute-start.14 = (bf16[256,256]{1,0:T(8,128)(2,1)S(1)}, bf16[256,256]{1,0:T(8,128)(2,1)S(1)}, u32[]{:S(2)}, u32[]{:S(2)}) collective-permute-start(bf16[256,256]{1,0:T(8,128)(2,1)S(1)} %get-tuple-element.34), channel_id=1, source_target_pairs={{0,4},{1,5},{2,6},{3,7},{4,0},{5,1},{6,2},{7,3},{8,12},{9,13},{10,... | collective-permute-start | bytes 393224 | tf_op jit(solution)/shard_map/ppermute | solution.py:203
  24.2 7.0 %collective-permute-start.15 = (bf16[256,256]{1,0:T(8,128)(2,1)S(1)}, bf16[256,256]{1,0:T(8,128)(2,1)S(1)}, u32[]{:S(2)}, u32[]{:S(2)}) collective-permute-start(bf16[256,256]{1,0:T(8,128)(2,1)S(1)} %get-tuple-element.35), channel_id=1, source_target_pairs={{0,12},{1,13},{2,14},{3,15},{4,8},{5,9},{6,10},{7,11},{8,4},{9,5},... | collective-permute-start | bytes 393224 | tf_op jit(solution)/shard_map/ppermute | solution.py:203
  27.0 6.4 %collective-permute-start.10 = (bf16[256,256]{1,0:T(8,128)(2,1)S(1)}, bf16[256,256]{1,0:T(8,128)(2,1)S(1)}, u32[]{:S(2)}, u32[]{:S(2)}) collective-permute-start(bf16[256,256]{1,0:T(8,128)(2,1)S(1)} %get-tuple-element.29), channel_id=1, source_target_pairs={{0,4},{1,5},{2,6},{3,7},{4,0},{5,1},{6,2},{7,3},{8,12},{9,13},{10,... | collective-permute-start | bytes 393224 | tf_op jit(solution)/shard_map/ppermute | solution.py:203
  27.7 9.0 %collective-permute-start.11 = (bf16[256,256]{1,0:T(8,128)(2,1)S(1)}, bf16[256,256]{1,0:T(8,128)(2,1)S(1)}, u32[]{:S(2)}, u32[]{:S(2)}) collective-permute-start(bf16[256,256]{1,0:T(8,128)(2,1)S(1)} %get-tuple-element.30), channel_id=1, source_target_pairs={{0,12},{1,13},{2,14},{3,15},{4,8},{5,9},{6,10},{7,11},{8,4},{9,5},... | collective-permute-start | bytes 393224 | tf_op jit(solution)/shard_map/ppermute | solution.py:203
  29.4 7.3 %collective-permute-start.13 = (bf16[256,256]{1,0:T(8,128)(2,1)S(1)}, bf16[256,256]{1,0:T(8,128)(2,1)S(1)}, u32[]{:S(2)}, u32[]{:S(2)}) collective-permute-start(bf16[256,256]{1,0:T(8,128)(2,1)S(1)} %add_convert_fusion.5), channel_id=1, source_target_pairs={{0,8},{1,9},{2,10},{3,11},{4,12},{5,13},{6,14},{7,15},{8,0},{9,1},... | collective-permute-start | bytes 393224 | tf_op jit(solution)/shard_map/ppermute | solution.py:203
  31.3 6.6 %collective-permute-start.16 = (bf16[256,256]{1,0:T(8,128)(2,1)S(1)}, bf16[256,256]{1,0:T(8,128)(2,1)S(1)}, u32[]{:S(2)}, u32[]{:S(2)}) collective-permute-start(bf16[256,256]{1,0:T(8,128)(2,1)S(1)} %add_convert_fusion.4), channel_id=1, source_target_pairs={{0,2},{1,3},{2,0},{3,1},{4,6},{5,7},{6,4},{7,5},{8,10},{9,11},{10,... | collective-permute-start | bytes 393224 | tf_op jit(solution)/shard_map/ppermute | solution.py:203
  38.0 7.5 %collective-permute-start.20 = (bf16[256,256]{1,0:T(8,128)(2,1)S(1)}, bf16[256,256]{1,0:T(8,128)(2,1)S(1)}, u32[]{:S(2)}, u32[]{:S(2)}) collective-permute-start(bf16[256,256]{1,0:T(8,128)(2,1)S(1)} %add_convert_fusion.3.refs_0_), channel_id=1, source_target_pairs={{0,8},{1,9},{2,10},{3,11},{4,12},{5,13},{6,14},{7,15},{8,0},{9,1},... | collective-permute-start | bytes 393224 | tf_op jit(solution)/shard_map/ppermute | solution.py:203
  40.1 7.7 %collective-permute-start.17 = (bf16[256,256]{1,0:T(8,128)(2,1)S(1)}, bf16[256,256]{1,0:T(8,128)(2,1)S(1)}, u32[]{:S(2)}, u32[]{:S(2)}) collective-permute-start(bf16[256,256]{1,0:T(8,128)(2,1)S(1)} %add_convert_fusion.3.refs_0_), channel_id=1, source_target_pairs={{0,2},{1,3},{2,0},{3,1},{4,6},{5,7},{6,4},{7,5},{8,10},{9,11},{10,... | collective-permute-start | bytes 393224 | tf_op jit(solution)/shard_map/ppermute | solution.py:203
  41.5 7.8 %collective-permute-start.22 = (bf16[256,256]{1,0:T(8,128)(2,1)S(1)}, bf16[256,256]{1,0:T(8,128)(2,1)S(1)}, u32[]{:S(2)}, u32[]{:S(2)}) collective-permute-start(bf16[256,256]{1,0:T(8,128)(2,1)S(1)} %add_convert_fusion.3.refs_0_), channel_id=1, source_target_pairs={{0,12},{1,13},{2,14},{3,15},{4,8},{5,9},{6,10},{7,11},{8,4},{9,5},... | collective-permute-start | bytes 393224 | tf_op jit(solution)/shard_map/ppermute | solution.py:203
  43.4 6.2 %collective-permute-start.18 = (bf16[256,256]{1,0:T(8,128)(2,1)S(1)}, bf16[256,256]{1,0:T(8,128)(2,1)S(1)}, u32[]{:S(2)}, u32[]{:S(2)}) collective-permute-start(bf16[256,256]{1,0:T(8,128)(2,1)S(1)} %add_convert_fusion.3.refs_0_), channel_id=1, source_target_pairs={{0,4},{1,5},{2,6},{3,7},{4,0},{5,1},{6,2},{7,3},{8,12},{9,13},{10,... | collective-permute-start | bytes 393224 | tf_op jit(solution)/shard_map/ppermute | solution.py:203
  45.5 6.5 %collective-permute-start.21 = (bf16[256,256]{1,0:T(8,128)(2,1)S(1)}, bf16[256,256]{1,0:T(8,128)(2,1)S(1)}, u32[]{:S(2)}, u32[]{:S(2)}) collective-permute-start(bf16[256,256]{1,0:T(8,128)(2,1)S(1)} %collective-permute-done.20.refs_4_), channel_id=1, source_target_pairs={{0,2},{1,3},{2,0},{3,1},{4,6},{5,7},{6,4},{7,5},{8,10},{9,11},{10,... | collective-permute-start | bytes 393224 | tf_op jit(solution)/shard_map/ppermute | solution.py:203
  47.8 6.2 %collective-permute-start.23 = (bf16[256,256]{1,0:T(8,128)(2,1)S(1)}, bf16[256,256]{1,0:T(8,128)(2,1)S(1)}, u32[]{:S(2)}, u32[]{:S(2)}) collective-permute-start(bf16[256,256]{1,0:T(8,128)(2,1)S(1)} %collective-permute-done.17.refs_1_), channel_id=1, source_target_pairs={{0,12},{1,13},{2,14},{3,15},{4,8},{5,9},{6,10},{7,11},{8,4},{9,5},... | collective-permute-start | bytes 393224 | tf_op jit(solution)/shard_map/ppermute | solution.py:203
  48.7 5.3 %collective-permute-start.19 = (bf16[256,256]{1,0:T(8,128)(2,1)S(1)}, bf16[256,256]{1,0:T(8,128)(2,1)S(1)}, u32[]{:S(2)}, u32[]{:S(2)}) collective-permute-start(bf16[256,256]{1,0:T(8,128)(2,1)S(1)} %collective-permute-done.17.refs_1_), channel_id=1, source_target_pairs={{0,4},{1,5},{2,6},{3,7},{4,0},{5,1},{6,2},{7,3},{8,12},{9,13},{10,... | collective-permute-start | bytes 393224 | tf_op jit(solution)/shard_map/ppermute | solution.py:203
  54.1 2.9 %collective-permute-start.25 = (bf16[4,256,256]{2,1,0:T(8,128)(2,1)S(1)}, bf16[4,256,256]{2,1,0:T(8,128)(2,1)S(1)}, u32[]{:S(2)}, u32[]{:S(2)}) collective-permute-start(bf16[4,256,256]{2,1,0:T(8,128)(2,1)S(1)} %pack.1), channel_id=1, source_target_pairs={{0,1},{1,0},{2,3},{3,2},{4,5},{5,4},{6,7},{7,6},{8,9},{9,8},{10,11... | collective-permute-start | bytes 1572872 | tf_op jit(solution)/shard_map/ppermute | solution.py:203
  55.1 1.8 %collective-permute-start.24 = (bf16[2,256,256]{2,1,0:T(8,128)(2,1)S(1)}, bf16[2,256,256]{2,1,0:T(8,128)(2,1)S(1)}, u32[]{:S(2)}, u32[]{:S(2)}) collective-permute-start(bf16[2,256,256]{2,1,0:T(8,128)(2,1)S(1)} %get-tuple-element.37), channel_id=1, source_target_pairs={{0,1},{1,0},{2,3},{3,2},{4,5},{5,4},{6,7},{7,6},{8,9},{9,8},{10,11... | collective-permute-start | bytes 786440 | tf_op jit(solution)/shard_map/ppermute | solution.py:203
  57.9 7.7 %collective-permute-start.28 = (bf16[256,256]{1,0:T(8,128)(2,1)S(1)}, bf16[256,256]{1,0:T(8,128)(2,1)S(1)}, u32[]{:S(2)}, u32[]{:S(2)}) collective-permute-start(bf16[256,256]{1,0:T(8,128)(2,1)S(1)} %get-tuple-element.42), channel_id=1, source_target_pairs={{0,64},{16,80},{32,96},{48,112},{64,0},{80,16},{96,32},{112,48},{1... | collective-permute-start | bytes 393224 | tf_op jit(solution)/shard_map/ppermute | solution.py:203
  59.3 9.1 %collective-permute-start.30 = (bf16[256,256]{1,0:T(8,128)(2,1)S(1)}, bf16[256,256]{1,0:T(8,128)(2,1)S(1)}, u32[]{:S(2)}, u32[]{:S(2)}) collective-permute-start(bf16[256,256]{1,0:T(8,128)(2,1)S(1)} %get-tuple-element.44), channel_id=1, source_target_pairs={{0,16},{16,0},{32,48},{48,32},{64,80},{80,64},{96,112},{112,96},{1... | collective-permute-start | bytes 393224 | tf_op jit(solution)/shard_map/ppermute | solution.py:203
  60.8 7.7 %collective-permute-start.31 = (bf16[256,256]{1,0:T(8,128)(2,1)S(1)}, bf16[256,256]{1,0:T(8,128)(2,1)S(1)}, u32[]{:S(2)}, u32[]{:S(2)}) collective-permute-start(bf16[256,256]{1,0:T(8,128)(2,1)S(1)} %get-tuple-element.45), channel_id=1, source_target_pairs={{0,48},{16,32},{32,16},{48,0},{64,112},{80,96},{96,80},{112,64},{1... | collective-permute-start | bytes 393224 | tf_op jit(solution)/shard_map/ppermute | solution.py:203
  63.7 5.5 %collective-permute-start.26 = (bf16[256,256]{1,0:T(8,128)(2,1)S(1)}, bf16[256,256]{1,0:T(8,128)(2,1)S(1)}, u32[]{:S(2)}, u32[]{:S(2)}) collective-permute-start(bf16[256,256]{1,0:T(8,128)(2,1)S(1)} %get-tuple-element.39), channel_id=1, source_target_pairs={{0,16},{16,0},{32,48},{48,32},{64,80},{80,64},{96,112},{112,96},{1... | collective-permute-start | bytes 393224 | tf_op jit(solution)/shard_map/ppermute | solution.py:203
  64.3 9.0 %collective-permute-start.27 = (bf16[256,256]{1,0:T(8,128)(2,1)S(1)}, bf16[256,256]{1,0:T(8,128)(2,1)S(1)}, u32[]{:S(2)}, u32[]{:S(2)}) collective-permute-start(bf16[256,256]{1,0:T(8,128)(2,1)S(1)} %get-tuple-element.40), channel_id=1, source_target_pairs={{0,48},{16,32},{32,16},{48,0},{64,112},{80,96},{96,80},{112,64},{1... | collective-permute-start | bytes 393224 | tf_op jit(solution)/shard_map/ppermute | solution.py:203
  65.7 7.6 %collective-permute-start.29 = (bf16[256,256]{1,0:T(8,128)(2,1)S(1)}, bf16[256,256]{1,0:T(8,128)(2,1)S(1)}, u32[]{:S(2)}, u32[]{:S(2)}) collective-permute-start(bf16[256,256]{1,0:T(8,128)(2,1)S(1)} %add_convert_fusion.2), channel_id=1, source_target_pairs={{0,32},{16,48},{32,0},{48,16},{64,96},{80,112},{96,64},{112,80},{1... | collective-permute-start | bytes 393224 | tf_op jit(solution)/shard_map/ppermute | solution.py:203
  68.5 5.0 %collective-permute-start.32 = (bf16[256,256]{1,0:T(8,128)(2,1)S(1)}, bf16[256,256]{1,0:T(8,128)(2,1)S(1)}, u32[]{:S(2)}, u32[]{:S(2)}) collective-permute-start(bf16[256,256]{1,0:T(8,128)(2,1)S(1)} %add_convert_fusion.1), channel_id=1, source_target_pairs={{0,64},{16,80},{32,96},{48,112},{64,0},{80,16},{96,32},{112,48},{1... | collective-permute-start | bytes 393224 | tf_op jit(solution)/shard_map/ppermute | solution.py:203
  (6 other events, 28.1 us)

commit v9 on v7

--- a/solution.py
+++ b/solution.py
@@ -14,6 +14,7 @@
 FAR = [(1, 1), (3, 1), (2, 1)]
 NEAR = [(1, 0), (3, 0), (2, 0), (0, 1), (0, 0)]
 GROUPS_D = [[(1, 1), (3, 1), (2, 1)], [(2, 0), (0, 1)], [(1, 0), (3, 0), (0, 0)]]
+GROUPS_B = [[(1, 1), (3, 1), (2, 1)], [(2, 0)], [(0, 1), (1, 0), (3, 0), (0, 0)]]
 VMEM = pl.BlockSpec(memory_space=pltpu.VMEM)
 
 
@@ -257,7 +258,7 @@
     dense_mate = swap(dense_sent, "tcol", 1)
     (dense_own,) = call(functools.partial(diag_kernel, 0), "diag_own", [*x, dense], [four], 32 * unit, 12 * size + 2**23)
     terms = []
-    for rels in (FAR, NEAR):
+    for rels in GROUPS_B:
         terms += call(
             functools.partial(term_kernel, rels),
             "term",
@@ -266,7 +267,7 @@
             2 * len(rels) * unit,
             2 * len(rels) * size + 2**21,
         )
-    first = scatter(terms, "tcol", 4, 2)
+    first = scatter(terms, "tcol", 4, 2, sum(GROUPS_B, []))
     y, _, _ = gather(first, "tcol", 4, 2)
     (y_sent,) = call(pack_kernel, "pack", y, [four], 0, 12 * size)
     y_mate = swap(y_sent, "tcol", 1)

time: 74.4 us -> 74.4 us (level)
    pallas_call x11 -> x12, Pallas kernels: 8.87 us -> 9.06 us  [call(): pl.pallas_call(kernel, name=name, out_shape=outs, in_specs=[VMEM] * (len(...]
where the time goes in v9:
time: 74.4 us; the launch traced here: 74.3 us
  starting transfers between devices  37.9 us (51%)
  waiting for transfers between devices  21.8 us (29%)
  Pallas kernels  12.6 us (17%)
  other arithmetic  1 us (1%)
  between operations  0.92 us (1%)
    ppermute x33, starting transfers between devices, swap(): return lax.ppermute(x, axis, [(i, i ^ bits) for i in range(size)])  37.9 us
    ppermute x33, waiting for transfers between devices, swap(): return lax.ppermute(x, axis, [(i, i ^ bits) for i in range(size)])  21.8 us
    pallas_call x12, Pallas kernels, call(): pl.pallas_call(kernel, name=name, out_shape=outs, in_specs=[VMEM] * (len(...  9.06 us
    pallas_call x1, Pallas kernels, load(): pl.pallas_call(load_kernel, name='load', out_shape=[pltpu.VMEM(v.shape, v...  3.52 us
  transfers between devices with their start and end apart: 33, of which 12 were waited for; matrix products, arithmetic and copies ran while one was open for 0% of the time, Pallas kernels for 13%

profile of v9, /device:TPU:0, one launch (start us, length us, event | category | flops | bytes accessed | tf_op | source)
XLA Modules:
  0.0 74.3 jit_solution(10302753926342011505)
XLA Ops:
  0.7 1.7 %collective-permute-start = (bf16[256,256]{1,0:T(8,128)(2,1)}, bf16[256,256]{1,0:T(8,128)(2,1)S(1)}, u32[]{:S(2)}, u32[]{:S(2)}) collective-permute-start(bf16[256,256]{1,0:T(8,128)(2,1)} %refs_0_.5), channel_id=1, source_target_pairs={{0,64},{16,80},{32,96},{48,112},{64,0},{80,16},{96,32},{112,48},{1... | collective-permute-start | bytes 393224 | tf_op jit(solution)/shard_map/ppermute | solution.py:204
  2.4 3.9 %collective-permute-start.3 = (bf16[256,256]{1,0:T(8,128)(2,1)}, bf16[256,256]{1,0:T(8,128)(2,1)S(1)}, u32[]{:S(2)}, u32[]{:S(2)}) collective-permute-start(bf16[256,256]{1,0:T(8,128)(2,1)} %refs_0_.5), channel_id=1, source_target_pairs={{0,32},{16,48},{32,0},{48,16},{64,96},{80,112},{96,64},{112,80},{1... | collective-permute-start | bytes 393224 | tf_op jit(solution)/shard_map/ppermute | solution.py:204
  7.3 3.5 %load.1.refs_8_.dense = bf16[2048,2048]{1,0:T(8,128)(2,1)S(1)} custom-call(bf16[2048,2048]{1,0:T(8,128)(2,1)} %bitcast.17), custom_call_target="tpu_custom_call" | custom-call | bytes 20971520 | tf_op jit(solution)/shard_map/load/pallas_call | solution.py:178
  11.0 1.0 %collective-permute-start.2 = (bf16[256,256]{1,0:T(8,128)(2,1)S(1)}, bf16[256,256]{1,0:T(8,128)(2,1)S(1)}, u32[]{:S(2)}, u32[]{:S(2)}) collective-permute-start(bf16[256,256]{1,0:T(8,128)(2,1)S(1)} %collective-permute-done.refs_1_), channel_id=1, source_target_pairs={{0,16},{16,0},{32,48},{48,32},{64,80},{80,64},{96,112},{112,96},{1... | collective-permute-start | bytes 393224 | tf_op jit(solution)/shard_map/ppermute | solution.py:204
  13.1 1.3 %collective-permute-done.1.refs_2_ = bf16[256,256]{1,0:T(8,128)(2,1)S(1)} collective-permute-done((bf16[256,256]{1,0:T(8,128)(2,1)}, bf16[256,256]{1,0:T(8,128)(2,1)S(1)}, u32[]{:S(2)}, u32[]{:S(2)}) %collective-permute-start.1) | collective-permute-done | bytes 131104 | tf_op jit(solution)/shard_map/ppermute | solution.py:204
  14.5 2.7 %collective-permute-done.7.refs_7_ = bf16[256,256]{1,0:T(8,128)(2,1)S(1)} collective-permute-done((bf16[256,256]{1,0:T(8,128)(2,1)S(1)}, bf16[256,256]{1,0:T(8,128)(2,1)S(1)}, u32[]{:S(2)}, u32[]{:S(2)}) %collective-permute-start.7) | collective-permute-done | bytes 131104 | tf_op jit(solution)/shard_map/ppermute | solution.py:204
  17.1 1.3 %diag_mate.1 = bf16[4,256,256]{2,1,0:T(8,128)(2,1)S(1)} custom-call(bf16[256,256]{1,0:T(8,128)(2,1)S(1)} %copy-done.3, bf16[256,256]{1,0:T(8,128)(2,1)S(1)} %collective-permute-done.refs_1_, bf16[256,256]{1,0:T(8,128)(2,1)S(1)} %collective-permute-done.1.refs_2_, bf16[256,256]{1,0:T(8,128)(2,1)S(1)} %collective-permute-done.2.refs_3_, ...), custom_call_target="tpu_custom_call" | custom-call | flops 1073741824 | bytes 9961472 | tf_op jit(solution)/shard_map/diag_mate/pallas_call | solution.py:191
  19.9 1.3 %diag_own.1.dense_own = bf16[4,256,256]{2,1,0:T(8,128)(2,1)S(1)} custom-call(bf16[256,256]{1,0:T(8,128)(2,1)S(1)} %copy-done.3, bf16[256,256]{1,0:T(8,128)(2,1)S(1)} %collective-permute-done.refs_1_, bf16[256,256]{1,0:T(8,128)(2,1)S(1)} %collective-permute-done.1.refs_2_, bf16[256,256]{1,0:T(8,128)(2,1)S(1)} %collective-permute-done.2.refs_3_, ...), custom_call_target="tpu_custom_call" | custom-call | flops 1073741824 | bytes 9961472 | tf_op jit(solution)/shard_map/diag_own/pallas_call | solution.py:191
  21.6 1.8 %collective-permute-start.12 = (bf16[256,256]{1,0:T(8,128)(2,1)S(1)}, bf16[256,256]{1,0:T(8,128)(2,1)S(1)}, u32[]{:S(2)}, u32[]{:S(2)}) collective-permute-start(bf16[256,256]{1,0:T(8,128)(2,1)S(1)} %get-tuple-element.28), channel_id=1, source_target_pairs={{0,2},{1,3},{2,0},{3,1},{4,6},{5,7},{6,4},{7,5},{8,10},{9,11},{10,... | collective-permute-start | bytes 393224 | tf_op jit(solution)/shard_map/ppermute | solution.py:204
  23.5 2.5 %collective-permute-start.14 = (bf16[256,256]{1,0:T(8,128)(2,1)S(1)}, bf16[256,256]{1,0:T(8,128)(2,1)S(1)}, u32[]{:S(2)}, u32[]{:S(2)}) collective-permute-start(bf16[256,256]{1,0:T(8,128)(2,1)S(1)} %get-tuple-element.30), channel_id=1, source_target_pairs={{0,4},{1,5},{2,6},{3,7},{4,0},{5,1},{6,2},{7,3},{8,12},{9,13},{10,... | collective-permute-start | bytes 393224 | tf_op jit(solution)/shard_map/ppermute | solution.py:204
  26.9 1.3 %collective-permute-start.10 = (bf16[256,256]{1,0:T(8,128)(2,1)S(1)}, bf16[256,256]{1,0:T(8,128)(2,1)S(1)}, u32[]{:S(2)}, u32[]{:S(2)}) collective-permute-start(bf16[256,256]{1,0:T(8,128)(2,1)S(1)} %get-tuple-element.26), channel_id=1, source_target_pairs={{0,4},{1,5},{2,6},{3,7},{4,0},{5,1},{6,2},{7,3},{8,12},{9,13},{10,... | collective-permute-start | bytes 393224 | tf_op jit(solution)/shard_map/ppermute | solution.py:204
  28.2 1.7 %collective-permute-start.11 = (bf16[256,256]{1,0:T(8,128)(2,1)S(1)}, bf16[256,256]{1,0:T(8,128)(2,1)S(1)}, u32[]{:S(2)}, u32[]{:S(2)}) collective-permute-start(bf16[256,256]{1,0:T(8,128)(2,1)S(1)} %get-tuple-element.27), channel_id=1, source_target_pairs={{0,12},{1,13},{2,14},{3,15},{4,8},{5,9},{6,10},{7,11},{8,4},{9,5},... | collective-permute-start | bytes 393224 | tf_op jit(solution)/shard_map/ppermute | solution.py:204
  30.1 1.5 %collective-permute-start.13 = (bf16[256,256]{1,0:T(8,128)(2,1)S(1)}, bf16[256,256]{1,0:T(8,128)(2,1)S(1)}, u32[]{:S(2)}, u32[]{:S(2)}) collective-permute-start(bf16[256,256]{1,0:T(8,128)(2,1)S(1)} %add_convert_fusion.5), channel_id=1, source_target_pairs={{0,8},{1,9},{2,10},{3,11},{4,12},{5,13},{6,14},{7,15},{8,0},{9,1},... | collective-permute-start | bytes 393224 | tf_op jit(solution)/shard_map/ppermute | solution.py:204
  31.6 1.9 %collective-permute-done.15 = bf16[256,256]{1,0:T(8,128)(2,1)S(1)} collective-permute-done((bf16[256,256]{1,0:T(8,128)(2,1)S(1)}, bf16[256,256]{1,0:T(8,128)(2,1)S(1)}, u32[]{:S(2)}, u32[]{:S(2)}) %collective-permute-start.15) | collective-permute-done | bytes 131104 | tf_op jit(solution)/shard_map/ppermute | solution.py:204
  33.5 1.9 %collective-permute-start.16 = (bf16[256,256]{1,0:T(8,128)(2,1)S(1)}, bf16[256,256]{1,0:T(8,128)(2,1)S(1)}, u32[]{:S(2)}, u32[]{:S(2)}) collective-permute-start(bf16[256,256]{1,0:T(8,128)(2,1)S(1)} %add_convert_fusion.4), channel_id=1, source_target_pairs={{0,2},{1,3},{2,0},{3,1},{4,6},{5,7},{6,4},{7,5},{8,10},{9,11},{10,... | collective-permute-start | bytes 393224 | tf_op jit(solution)/shard_map/ppermute | solution.py:204
  35.4 2.6 %collective-permute-done.11 = bf16[256,256]{1,0:T(8,128)(2,1)S(1)} collective-permute-done((bf16[256,256]{1,0:T(8,128)(2,1)S(1)}, bf16[256,256]{1,0:T(8,128)(2,1)S(1)}, u32[]{:S(2)}, u32[]{:S(2)}) %collective-permute-start.11) | collective-permute-done | bytes 131104 | tf_op jit(solution)/shard_map/ppermute | solution.py:204
  38.0 2.1 %collective-permute-done.16 = bf16[256,256]{1,0:T(8,128)(2,1)S(1)} collective-permute-done((bf16[256,256]{1,0:T(8,128)(2,1)S(1)}, bf16[256,256]{1,0:T(8,128)(2,1)S(1)}, u32[]{:S(2)}, u32[]{:S(2)}) %collective-permute-start.16) | collective-permute-done | bytes 131104 | tf_op jit(solution)/shard_map/ppermute | solution.py:204
  40.6 1.7 %collective-permute-start.17 = (bf16[256,256]{1,0:T(8,128)(2,1)S(1)}, bf16[256,256]{1,0:T(8,128)(2,1)S(1)}, u32[]{:S(2)}, u32[]{:S(2)}) collective-permute-start(bf16[256,256]{1,0:T(8,128)(2,1)S(1)} %add_convert_fusion.3.refs_0_), channel_id=1, source_target_pairs={{0,2},{1,3},{2,0},{3,1},{4,6},{5,7},{6,4},{7,5},{8,10},{9,11},{10,... | collective-permute-start | bytes 393224 | tf_op jit(solution)/shard_map/ppermute | solution.py:204
  42.3 1.6 %collective-permute-start.22 = (bf16[256,256]{1,0:T(8,128)(2,1)S(1)}, bf16[256,256]{1,0:T(8,128)(2,1)S(1)}, u32[]{:S(2)}, u32[]{:S(2)}) collective-permute-start(bf16[256,256]{1,0:T(8,128)(2,1)S(1)} %add_convert_fusion.3.refs_0_), channel_id=1, source_target_pairs={{0,12},{1,13},{2,14},{3,15},{4,8},{5,9},{6,10},{7,11},{8,4},{9,5},... | collective-permute-start | bytes 393224 | tf_op jit(solution)/shard_map/ppermute | solution.py:204
  43.9 1.7 %collective-permute-start.18 = (bf16[256,256]{1,0:T(8,128)(2,1)S(1)}, bf16[256,256]{1,0:T(8,128)(2,1)S(1)}, u32[]{:S(2)}, u32[]{:S(2)}) collective-permute-start(bf16[256,256]{1,0:T(8,128)(2,1)S(1)} %add_convert_fusion.3.refs_0_), channel_id=1, source_target_pairs={{0,4},{1,5},{2,6},{3,7},{4,0},{5,1},{6,2},{7,3},{8,12},{9,13},{10,... | collective-permute-start | bytes 393224 | tf_op jit(solution)/shard_map/ppermute | solution.py:204
  45.5 2.2 %collective-permute-done.20.refs_4_ = bf16[256,256]{1,0:T(8,128)(2,1)S(1)} collective-permute-done((bf16[256,256]{1,0:T(8,128)(2,1)S(1)}, bf16[256,256]{1,0:T(8,128)(2,1)S(1)}, u32[]{:S(2)}, u32[]{:S(2)}) %collective-permute-start.20) | collective-permute-done | bytes 131104 | tf_op jit(solution)/shard_map/ppermute | solution.py:204
  47.7 1.4 %collective-permute-start.21 = (bf16[256,256]{1,0:T(8,128)(2,1)S(1)}, bf16[256,256]{1,0:T(8,128)(2,1)S(1)}, u32[]{:S(2)}, u32[]{:S(2)}) collective-permute-start(bf16[256,256]{1,0:T(8,128)(2,1)S(1)} %collective-permute-done.20.refs_4_), channel_id=1, source_target_pairs={{0,2},{1,3},{2,0},{3,1},{4,6},{5,7},{6,4},{7,5},{8,10},{9,11},{10,... | collective-permute-start | bytes 393224 | tf_op jit(solution)/shard_map/ppermute | solution.py:204
  49.2 1.5 %collective-permute-start.23 = (bf16[256,256]{1,0:T(8,128)(2,1)S(1)}, bf16[256,256]{1,0:T(8,128)(2,1)S(1)}, u32[]{:S(2)}, u32[]{:S(2)}) collective-permute-start(bf16[256,256]{1,0:T(8,128)(2,1)S(1)} %collective-permute-done.17.refs_1_), channel_id=1, source_target_pairs={{0,12},{1,13},{2,14},{3,15},{4,8},{5,9},{6,10},{7,11},{8,4},{9,5},... | collective-permute-start | bytes 393224 | tf_op jit(solution)/shard_map/ppermute | solution.py:204
  50.8 3.4 %collective-permute-done.21.refs_5_ = bf16[256,256]{1,0:T(8,128)(2,1)S(1)} collective-permute-done((bf16[256,256]{1,0:T(8,128)(2,1)S(1)}, bf16[256,256]{1,0:T(8,128)(2,1)S(1)}, u32[]{:S(2)}, u32[]{:S(2)}) %collective-permute-start.21) | collective-permute-done | bytes 131104 | tf_op jit(solution)/shard_map/ppermute | solution.py:204
  54.2 1.1 %collective-permute-done.23.refs_7_ = bf16[256,256]{1,0:T(8,128)(2,1)S(1)} collective-permute-done((bf16[256,256]{1,0:T(8,128)(2,1)S(1)}, bf16[256,256]{1,0:T(8,128)(2,1)S(1)}, u32[]{:S(2)}, u32[]{:S(2)}) %collective-permute-start.23) | collective-permute-done | bytes 131104 | tf_op jit(solution)/shard_map/ppermute | solution.py:204
  57.3 1.3 %diag_back.1.dense_sum = f32[8,256,256]{2,1,0:T(8,128)S(1)} custom-call(bf16[256,256]{1,0:T(8,128)(2,1)S(1)} %add_convert_fusion.3.refs_0_, bf16[256,256]{1,0:T(8,128)(2,1)S(1)} %collective-permute-done.17.refs_1_, bf16[256,256]{1,0:T(8,128)(2,1)S(1)} %collective-permute-done.18.refs_2_, bf16[256,256]{1,0:T(8,128)(2,1)S(1)} %collective-permute-done.19.refs_3_, ...), custom_call_target="tpu_custom_call" | custom-call | flops 1073741824 | bytes 7340032 | tf_op jit(solution)/shard_map/diag_back/pallas_call | solution.py:191
  59.7 1.6 %collective-permute-start.30 = (bf16[256,256]{1,0:T(8,128)(2,1)S(1)}, bf16[256,256]{1,0:T(8,128)(2,1)S(1)}, u32[]{:S(2)}, u32[]{:S(2)}) collective-permute-start(bf16[256,256]{1,0:T(8,128)(2,1)S(1)} %get-tuple-element.40), channel_id=1, source_target_pairs={{0,16},{16,0},{32,48},{48,32},{64,80},{80,64},{96,112},{112,96},{1... | collective-permute-start | bytes 393224 | tf_op jit(solution)/shard_map/ppermute | solution.py:204
  61.3 1.5 %collective-permute-start.31 = (bf16[256,256]{1,0:T(8,128)(2,1)S(1)}, bf16[256,256]{1,0:T(8,128)(2,1)S(1)}, u32[]{:S(2)}, u32[]{:S(2)}) collective-permute-start(bf16[256,256]{1,0:T(8,128)(2,1)S(1)} %get-tuple-element.41), channel_id=1, source_target_pairs={{0,48},{16,32},{32,16},{48,0},{64,112},{80,96},{96,80},{112,64},{1... | collective-permute-start | bytes 393224 | tf_op jit(solution)/shard_map/ppermute | solution.py:204
  64.2 1.0 %collective-permute-start.27 = (bf16[256,256]{1,0:T(8,128)(2,1)S(1)}, bf16[256,256]{1,0:T(8,128)(2,1)S(1)}, u32[]{:S(2)}, u32[]{:S(2)}) collective-permute-start(bf16[256,256]{1,0:T(8,128)(2,1)S(1)} %get-tuple-element.36), channel_id=1, source_target_pairs={{0,48},{16,32},{32,16},{48,0},{64,112},{80,96},{96,80},{112,64},{1... | collective-permute-start | bytes 393224 | tf_op jit(solution)/shard_map/ppermute | solution.py:204
  65.9 2.5 %collective-permute-start.29 = (bf16[256,256]{1,0:T(8,128)(2,1)S(1)}, bf16[256,256]{1,0:T(8,128)(2,1)S(1)}, u32[]{:S(2)}, u32[]{:S(2)}) collective-permute-start(bf16[256,256]{1,0:T(8,128)(2,1)S(1)} %add_convert_fusion.2), channel_id=1, source_target_pairs={{0,32},{16,48},{32,0},{48,16},{64,96},{80,112},{96,64},{112,80},{1... | collective-permute-start | bytes 393224 | tf_op jit(solution)/shard_map/ppermute | solution.py:204
  68.5 1.3 %collective-permute-start.32 = (bf16[256,256]{1,0:T(8,128)(2,1)S(1)}, bf16[256,256]{1,0:T(8,128)(2,1)S(1)}, u32[]{:S(2)}, u32[]{:S(2)}) collective-permute-start(bf16[256,256]{1,0:T(8,128)(2,1)S(1)} %add_convert_fusion.1), channel_id=1, source_target_pairs={{0,64},{16,80},{32,96},{48,112},{64,0},{80,16},{96,32},{112,48},{1... | collective-permute-start | bytes 393224 | tf_op jit(solution)/shard_map/ppermute | solution.py:204
  69.8 3.5 %collective-permute-done.27 = bf16[256,256]{1,0:T(8,128)(2,1)S(1)} collective-permute-done((bf16[256,256]{1,0:T(8,128)(2,1)S(1)}, bf16[256,256]{1,0:T(8,128)(2,1)S(1)}, u32[]{:S(2)}, u32[]{:S(2)}) %collective-permute-start.27) | collective-permute-done | bytes 131104 | tf_op jit(solution)/shard_map/ppermute | solution.py:204
  (63 shorter events, 12.4 us)
Async XLA Ops:
  0.6 11.3 %collective-permute-start.4 = (bf16[2,2048,256]{2,1,0:T(8,128)(2,1)}, bf16[2,2048,256]{2,1,0:T(8,128)(2,1)S(1)}, u32[]{:S(2)}, u32[]{:S(2)}) collective-permute-start(bf16[2,2048,256]{2,1,0:T(8,128)(2,1)} %bitcast.4), channel_id=1, source_target_pairs={{0,1},{1,0},{2,3},{3,2},{4,5},{5,4},{6,7},{7,6},{8,9},{9,8},{10,11... | collective-permute-start | bytes 6291464 | tf_op jit(solution)/shard_map/ppermute | solution.py:204
  0.7 10.1 %collective-permute-start = (bf16[256,256]{1,0:T(8,128)(2,1)}, bf16[256,256]{1,0:T(8,128)(2,1)S(1)}, u32[]{:S(2)}, u32[]{:S(2)}) collective-permute-start(bf16[256,256]{1,0:T(8,128)(2,1)} %refs_0_.5), channel_id=1, source_target_pairs={{0,64},{16,80},{32,96},{48,112},{64,0},{80,16},{96,32},{112,48},{1... | collective-permute-start | bytes 393224 | tf_op jit(solution)/shard_map/ppermute | solution.py:204
  2.4 8.6 %collective-permute-start.3 = (bf16[256,256]{1,0:T(8,128)(2,1)}, bf16[256,256]{1,0:T(8,128)(2,1)S(1)}, u32[]{:S(2)}, u32[]{:S(2)}) collective-permute-start(bf16[256,256]{1,0:T(8,128)(2,1)} %refs_0_.5), channel_id=1, source_target_pairs={{0,32},{16,48},{32,0},{48,16},{64,96},{80,112},{96,64},{112,80},{1... | collective-permute-start | bytes 393224 | tf_op jit(solution)/shard_map/ppermute | solution.py:204
  6.3 6.9 %collective-permute-start.6 = (bf16[256,256]{1,0:T(8,128)(2,1)}, bf16[256,256]{1,0:T(8,128)(2,1)S(1)}, u32[]{:S(2)}, u32[]{:S(2)}) collective-permute-start(bf16[256,256]{1,0:T(8,128)(2,1)} %refs_0_.5), channel_id=1, source_target_pairs={{0,48},{16,32},{32,16},{48,0},{64,112},{80,96},{96,80},{112,64},{1... | collective-permute-start | bytes 393224 | tf_op jit(solution)/shard_map/ppermute | solution.py:204
  7.0 7.5 %collective-permute-start.1 = (bf16[256,256]{1,0:T(8,128)(2,1)}, bf16[256,256]{1,0:T(8,128)(2,1)S(1)}, u32[]{:S(2)}, u32[]{:S(2)}) collective-permute-start(bf16[256,256]{1,0:T(8,128)(2,1)} %refs_0_.5), channel_id=1, source_target_pairs={{0,16},{16,0},{32,48},{48,32},{64,80},{80,64},{96,112},{112,96},{1... | collective-permute-start | bytes 393224 | tf_op jit(solution)/shard_map/ppermute | solution.py:204
  10.8 6.3 %collective-permute-start.7 = (bf16[256,256]{1,0:T(8,128)(2,1)S(1)}, bf16[256,256]{1,0:T(8,128)(2,1)S(1)}, u32[]{:S(2)}, u32[]{:S(2)}) collective-permute-start(bf16[256,256]{1,0:T(8,128)(2,1)S(1)} %collective-permute-done.refs_1_), channel_id=1, source_target_pairs={{0,48},{16,32},{32,16},{48,0},{64,112},{80,96},{96,80},{112,64},{1... | collective-permute-start | bytes 393224 | tf_op jit(solution)/shard_map/ppermute | solution.py:204
  11.0 6.2 %collective-permute-start.2 = (bf16[256,256]{1,0:T(8,128)(2,1)S(1)}, bf16[256,256]{1,0:T(8,128)(2,1)S(1)}, u32[]{:S(2)}, u32[]{:S(2)}) collective-permute-start(bf16[256,256]{1,0:T(8,128)(2,1)S(1)} %collective-permute-done.refs_1_), channel_id=1, source_target_pairs={{0,16},{16,0},{32,48},{48,32},{64,80},{80,64},{96,112},{112,96},{1... | collective-permute-start | bytes 393224 | tf_op jit(solution)/shard_map/ppermute | solution.py:204
  11.9 5.2 %collective-permute-start.5 = (bf16[256,256]{1,0:T(8,128)(2,1)S(1)}, bf16[256,256]{1,0:T(8,128)(2,1)S(1)}, u32[]{:S(2)}, u32[]{:S(2)}) collective-permute-start(bf16[256,256]{1,0:T(8,128)(2,1)S(1)} %collective-permute-done.3.refs_4_), channel_id=1, source_target_pairs={{0,64},{16,80},{32,96},{48,112},{64,0},{80,16},{96,32},{112,48},{1... | collective-permute-start | bytes 393224 | tf_op jit(solution)/shard_map/ppermute | solution.py:204
  18.5 2.7 %collective-permute-start.9 = (bf16[4,256,256]{2,1,0:T(8,128)(2,1)S(1)}, bf16[4,256,256]{2,1,0:T(8,128)(2,1)S(1)}, u32[]{:S(2)}, u32[]{:S(2)}) collective-permute-start(bf16[4,256,256]{2,1,0:T(8,128)(2,1)S(1)} %diag_mate.1), channel_id=1, source_target_pairs={{0,1},{1,0},{2,3},{3,2},{4,5},{5,4},{6,7},{7,6},{8,9},{9,8},{10,11... | collective-permute-start | bytes 1572872 | tf_op jit(solution)/shard_map/ppermute | solution.py:204
  19.3 1.8 %collective-permute-start.8 = (bf16[2,256,256]{2,1,0:T(8,128)(2,1)S(1)}, bf16[2,256,256]{2,1,0:T(8,128)(2,1)S(1)}, u32[]{:S(2)}, u32[]{:S(2)}) collective-permute-start(bf16[2,256,256]{2,1,0:T(8,128)(2,1)S(1)} %coeff.1.own), channel_id=1, source_target_pairs={{0,1},{1,0},{2,3},{3,2},{4,5},{5,4},{6,7},{7,6},{8,9},{9,8},{10,11... | collective-permute-start | bytes 786440 | tf_op jit(solution)/shard_map/ppermute | solution.py:204
  21.6 8.5 %collective-permute-start.12 = (bf16[256,256]{1,0:T(8,128)(2,1)S(1)}, bf16[256,256]{1,0:T(8,128)(2,1)S(1)}, u32[]{:S(2)}, u32[]{:S(2)}) collective-permute-start(bf16[256,256]{1,0:T(8,128)(2,1)S(1)} %get-tuple-element.28), channel_id=1, source_target_pairs={{0,2},{1,3},{2,0},{3,1},{4,6},{5,7},{6,4},{7,5},{8,10},{9,11},{10,... | collective-permute-start | bytes 393224 | tf_op jit(solution)/shard_map/ppermute | solution.py:204
  23.5 8.1 %collective-permute-start.14 = (bf16[256,256]{1,0:T(8,128)(2,1)S(1)}, bf16[256,256]{1,0:T(8,128)(2,1)S(1)}, u32[]{:S(2)}, u32[]{:S(2)}) collective-permute-start(bf16[256,256]{1,0:T(8,128)(2,1)S(1)} %get-tuple-element.30), channel_id=1, source_target_pairs={{0,4},{1,5},{2,6},{3,7},{4,0},{5,1},{6,2},{7,3},{8,12},{9,13},{10,... | collective-permute-start | bytes 393224 | tf_op jit(solution)/shard_map/ppermute | solution.py:204
  25.9 7.5 %collective-permute-start.15 = (bf16[256,256]{1,0:T(8,128)(2,1)S(1)}, bf16[256,256]{1,0:T(8,128)(2,1)S(1)}, u32[]{:S(2)}, u32[]{:S(2)}) collective-permute-start(bf16[256,256]{1,0:T(8,128)(2,1)S(1)} %get-tuple-element.31), channel_id=1, source_target_pairs={{0,12},{1,13},{2,14},{3,15},{4,8},{5,9},{6,10},{7,11},{8,4},{9,5},... | collective-permute-start | bytes 393224 | tf_op jit(solution)/shard_map/ppermute | solution.py:204
  26.9 8.5 %collective-permute-start.10 = (bf16[256,256]{1,0:T(8,128)(2,1)S(1)}, bf16[256,256]{1,0:T(8,128)(2,1)S(1)}, u32[]{:S(2)}, u32[]{:S(2)}) collective-permute-start(bf16[256,256]{1,0:T(8,128)(2,1)S(1)} %get-tuple-element.26), channel_id=1, source_target_pairs={{0,4},{1,5},{2,6},{3,7},{4,0},{5,1},{6,2},{7,3},{8,12},{9,13},{10,... | collective-permute-start | bytes 393224 | tf_op jit(solution)/shard_map/ppermute | solution.py:204
  28.2 9.8 %collective-permute-start.11 = (bf16[256,256]{1,0:T(8,128)(2,1)S(1)}, bf16[256,256]{1,0:T(8,128)(2,1)S(1)}, u32[]{:S(2)}, u32[]{:S(2)}) collective-permute-start(bf16[256,256]{1,0:T(8,128)(2,1)S(1)} %get-tuple-element.27), channel_id=1, source_target_pairs={{0,12},{1,13},{2,14},{3,15},{4,8},{5,9},{6,10},{7,11},{8,4},{9,5},... | collective-permute-start | bytes 393224 | tf_op jit(solution)/shard_map/ppermute | solution.py:204
  30.1 7.8 %collective-permute-start.13 = (bf16[256,256]{1,0:T(8,128)(2,1)S(1)}, bf16[256,256]{1,0:T(8,128)(2,1)S(1)}, u32[]{:S(2)}, u32[]{:S(2)}) collective-permute-start(bf16[256,256]{1,0:T(8,128)(2,1)S(1)} %add_convert_fusion.5), channel_id=1, source_target_pairs={{0,8},{1,9},{2,10},{3,11},{4,12},{5,13},{6,14},{7,15},{8,0},{9,1},... | collective-permute-start | bytes 393224 | tf_op jit(solution)/shard_map/ppermute | solution.py:204
  33.5 6.6 %collective-permute-start.16 = (bf16[256,256]{1,0:T(8,128)(2,1)S(1)}, bf16[256,256]{1,0:T(8,128)(2,1)S(1)}, u32[]{:S(2)}, u32[]{:S(2)}) collective-permute-start(bf16[256,256]{1,0:T(8,128)(2,1)S(1)} %add_convert_fusion.4), channel_id=1, source_target_pairs={{0,2},{1,3},{2,0},{3,1},{4,6},{5,7},{6,4},{7,5},{8,10},{9,11},{10,... | collective-permute-start | bytes 393224 | tf_op jit(solution)/shard_map/ppermute | solution.py:204
  40.2 7.5 %collective-permute-start.20 = (bf16[256,256]{1,0:T(8,128)(2,1)S(1)}, bf16[256,256]{1,0:T(8,128)(2,1)S(1)}, u32[]{:S(2)}, u32[]{:S(2)}) collective-permute-start(bf16[256,256]{1,0:T(8,128)(2,1)S(1)} %add_convert_fusion.3.refs_0_), channel_id=1, source_target_pairs={{0,8},{1,9},{2,10},{3,11},{4,12},{5,13},{6,14},{7,15},{8,0},{9,1},... | collective-permute-start | bytes 393224 | tf_op jit(solution)/shard_map/ppermute | solution.py:204
  40.6 8.6 %collective-permute-start.17 = (bf16[256,256]{1,0:T(8,128)(2,1)S(1)}, bf16[256,256]{1,0:T(8,128)(2,1)S(1)}, u32[]{:S(2)}, u32[]{:S(2)}) collective-permute-start(bf16[256,256]{1,0:T(8,128)(2,1)S(1)} %add_convert_fusion.3.refs_0_), channel_id=1, source_target_pairs={{0,2},{1,3},{2,0},{3,1},{4,6},{5,7},{6,4},{7,5},{8,10},{9,11},{10,... | collective-permute-start | bytes 393224 | tf_op jit(solution)/shard_map/ppermute | solution.py:204
  42.3 8.6 %collective-permute-start.22 = (bf16[256,256]{1,0:T(8,128)(2,1)S(1)}, bf16[256,256]{1,0:T(8,128)(2,1)S(1)}, u32[]{:S(2)}, u32[]{:S(2)}) collective-permute-start(bf16[256,256]{1,0:T(8,128)(2,1)S(1)} %add_convert_fusion.3.refs_0_), channel_id=1, source_target_pairs={{0,12},{1,13},{2,14},{3,15},{4,8},{5,9},{6,10},{7,11},{8,4},{9,5},... | collective-permute-start | bytes 393224 | tf_op jit(solution)/shard_map/ppermute | solution.py:204
  43.9 7.0 %collective-permute-start.18 = (bf16[256,256]{1,0:T(8,128)(2,1)S(1)}, bf16[256,256]{1,0:T(8,128)(2,1)S(1)}, u32[]{:S(2)}, u32[]{:S(2)}) collective-permute-start(bf16[256,256]{1,0:T(8,128)(2,1)S(1)} %add_convert_fusion.3.refs_0_), channel_id=1, source_target_pairs={{0,4},{1,5},{2,6},{3,7},{4,0},{5,1},{6,2},{7,3},{8,12},{9,13},{10,... | collective-permute-start | bytes 393224 | tf_op jit(solution)/shard_map/ppermute | solution.py:204
  47.7 6.5 %collective-permute-start.21 = (bf16[256,256]{1,0:T(8,128)(2,1)S(1)}, bf16[256,256]{1,0:T(8,128)(2,1)S(1)}, u32[]{:S(2)}, u32[]{:S(2)}) collective-permute-start(bf16[256,256]{1,0:T(8,128)(2,1)S(1)} %collective-permute-done.20.refs_4_), channel_id=1, source_target_pairs={{0,2},{1,3},{2,0},{3,1},{4,6},{5,7},{6,4},{7,5},{8,10},{9,11},{10,... | collective-permute-start | bytes 393224 | tf_op jit(solution)/shard_map/ppermute | solution.py:204
  49.2 6.2 %collective-permute-start.23 = (bf16[256,256]{1,0:T(8,128)(2,1)S(1)}, bf16[256,256]{1,0:T(8,128)(2,1)S(1)}, u32[]{:S(2)}, u32[]{:S(2)}) collective-permute-start(bf16[256,256]{1,0:T(8,128)(2,1)S(1)} %collective-permute-done.17.refs_1_), channel_id=1, source_target_pairs={{0,12},{1,13},{2,14},{3,15},{4,8},{5,9},{6,10},{7,11},{8,4},{9,5},... | collective-permute-start | bytes 393224 | tf_op jit(solution)/shard_map/ppermute | solution.py:204
  50.6 5.0 %collective-permute-start.19 = (bf16[256,256]{1,0:T(8,128)(2,1)S(1)}, bf16[256,256]{1,0:T(8,128)(2,1)S(1)}, u32[]{:S(2)}, u32[]{:S(2)}) collective-permute-start(bf16[256,256]{1,0:T(8,128)(2,1)S(1)} %collective-permute-done.17.refs_1_), channel_id=1, source_target_pairs={{0,4},{1,5},{2,6},{3,7},{4,0},{5,1},{6,2},{7,3},{8,12},{9,13},{10,... | collective-permute-start | bytes 393224 | tf_op jit(solution)/shard_map/ppermute | solution.py:204
  55.7 2.9 %collective-permute-start.25 = (bf16[4,256,256]{2,1,0:T(8,128)(2,1)S(1)}, bf16[4,256,256]{2,1,0:T(8,128)(2,1)S(1)}, u32[]{:S(2)}, u32[]{:S(2)}) collective-permute-start(bf16[4,256,256]{2,1,0:T(8,128)(2,1)S(1)} %pack.1), channel_id=1, source_target_pairs={{0,1},{1,0},{2,3},{3,2},{4,5},{5,4},{6,7},{7,6},{8,9},{9,8},{10,11... | collective-permute-start | bytes 1572872 | tf_op jit(solution)/shard_map/ppermute | solution.py:204
  59.5 6.4 %collective-permute-start.28 = (bf16[256,256]{1,0:T(8,128)(2,1)S(1)}, bf16[256,256]{1,0:T(8,128)(2,1)S(1)}, u32[]{:S(2)}, u32[]{:S(2)}) collective-permute-start(bf16[256,256]{1,0:T(8,128)(2,1)S(1)} %get-tuple-element.38), channel_id=1, source_target_pairs={{0,64},{16,80},{32,96},{48,112},{64,0},{80,16},{96,32},{112,48},{1... | collective-permute-start | bytes 393224 | tf_op jit(solution)/shard_map/ppermute | solution.py:204
  59.7 8.7 %collective-permute-start.30 = (bf16[256,256]{1,0:T(8,128)(2,1)S(1)}, bf16[256,256]{1,0:T(8,128)(2,1)S(1)}, u32[]{:S(2)}, u32[]{:S(2)}) collective-permute-start(bf16[256,256]{1,0:T(8,128)(2,1)S(1)} %get-tuple-element.40), channel_id=1, source_target_pairs={{0,16},{16,0},{32,48},{48,32},{64,80},{80,64},{96,112},{112,96},{1... | collective-permute-start | bytes 393224 | tf_op jit(solution)/shard_map/ppermute | solution.py:204
  61.3 7.2 %collective-permute-start.31 = (bf16[256,256]{1,0:T(8,128)(2,1)S(1)}, bf16[256,256]{1,0:T(8,128)(2,1)S(1)}, u32[]{:S(2)}, u32[]{:S(2)}) collective-permute-start(bf16[256,256]{1,0:T(8,128)(2,1)S(1)} %get-tuple-element.41), channel_id=1, source_target_pairs={{0,48},{16,32},{32,16},{48,0},{64,112},{80,96},{96,80},{112,64},{1... | collective-permute-start | bytes 393224 | tf_op jit(solution)/shard_map/ppermute | solution.py:204
  63.7 6.1 %collective-permute-start.26 = (bf16[256,256]{1,0:T(8,128)(2,1)S(1)}, bf16[256,256]{1,0:T(8,128)(2,1)S(1)}, u32[]{:S(2)}, u32[]{:S(2)}) collective-permute-start(bf16[256,256]{1,0:T(8,128)(2,1)S(1)} %get-tuple-element.35), channel_id=1, source_target_pairs={{0,16},{16,0},{32,48},{48,32},{64,80},{80,64},{96,112},{112,96},{1... | collective-permute-start | bytes 393224 | tf_op jit(solution)/shard_map/ppermute | solution.py:204
  64.2 9.1 %collective-permute-start.27 = (bf16[256,256]{1,0:T(8,128)(2,1)S(1)}, bf16[256,256]{1,0:T(8,128)(2,1)S(1)}, u32[]{:S(2)}, u32[]{:S(2)}) collective-permute-start(bf16[256,256]{1,0:T(8,128)(2,1)S(1)} %get-tuple-element.36), channel_id=1, source_target_pairs={{0,48},{16,32},{32,16},{48,0},{64,112},{80,96},{96,80},{112,64},{1... | collective-permute-start | bytes 393224 | tf_op jit(solution)/shard_map/ppermute | solution.py:204
  65.9 7.4 %collective-permute-start.29 = (bf16[256,256]{1,0:T(8,128)(2,1)S(1)}, bf16[256,256]{1,0:T(8,128)(2,1)S(1)}, u32[]{:S(2)}, u32[]{:S(2)}) collective-permute-start(bf16[256,256]{1,0:T(8,128)(2,1)S(1)} %add_convert_fusion.2), channel_id=1, source_target_pairs={{0,32},{16,48},{32,0},{48,16},{64,96},{80,112},{96,64},{112,80},{1... | collective-permute-start | bytes 393224 | tf_op jit(solution)/shard_map/ppermute | solution.py:204
  68.5 5.0 %collective-permute-start.32 = (bf16[256,256]{1,0:T(8,128)(2,1)S(1)}, bf16[256,256]{1,0:T(8,128)(2,1)S(1)}, u32[]{:S(2)}, u32[]{:S(2)}) collective-permute-start(bf16[256,256]{1,0:T(8,128)(2,1)S(1)} %add_convert_fusion.1), channel_id=1, source_target_pairs={{0,64},{16,80},{32,96},{48,112},{64,0},{80,16},{96,32},{112,48},{1... | collective-permute-start | bytes 393224 | tf_op jit(solution)/shard_map/ppermute | solution.py:204
  (6 other events, 46.1 us)
